TPU v7x, 32 devices: a whole 2x2x4 slice. The times are simulated.
32 devices in a mesh: scene: 2 (over y), az: 8 (over z, x), rg: 2 (over core).
Axes of the slice: x: 2, y: 2, z: 4, core: 2. Of those that a mesh axis runs over, the one named last changes fastest.
Arguments:
- raw_re: float32 [64, 32768], P('rg', ('scene', 'az')), parts along dimension 1, may hold values from -6 to 6
- raw_im: float32 [64, 32768], P('rg', ('scene', 'az')), parts along dimension 1, may hold values from -6 to 6
- ref_blocks: float32 [16, 64, 64], P(('scene', 'az'), None, 'rg'), parts along dimension 0, may hold values from -3.140625 to 3.140625
- owners: int32 [4], P('scene'), parts along dimension 0, may hold values from 0 to 7, as said below
- offsets: int32 [4], P('rg'), may hold values from -8 to 8
- taps: float32 [64, 8], P('rg'), may hold values from -3 to 3
Outputs:
- image_re: float32 [64, 32768], P('rg', ('scene', 'az')), parts along dimension 1
- image_im: float32 [64, 32768], P('rg', ('scene', 'az')), parts along dimension 1
There are 2 independent parts, one for each index of `scene`. A program takes and returns all parts, laid end to end along the dimension named above; an argument that names none is the same for every part. Nothing has to cross between parts.
Inputs may be any that keep to these rules, and one draw needn't show every extreme that they name: The two sub-apertures have different owners.
All inputs are finite; a program needn't handle non-finite values.
Results may differ from a plain program's by a relative error of at most 0.00014.
Values sent between devices are 32-bit elements; how exact they have to be, the bound alone decides.
No kernel may reach another device: no remote copies, remote signals or barrier semaphores. Data moves between devices by JAX's collectives and lax.ppermute only.
A program may use at most 64 MiB of HBM per device.

v0:
```python
import functools
import math

import jax
import jax.numpy as jnp
import numpy as np
from jax import lax
from jax.experimental import pallas as pl
from jax.experimental.pallas import tpu as pltpu
from jax.sharding import PartitionSpec as P

SPLIT = 4
TAPS = 8
REACH = 8
BLOCK = 16


PRECISE = lax.Precision.HIGHEST
PHASE_GAIN = 50.0


def partner_2(value, axis, stride):
    return lax.ppermute(value, axis, [(i, i ^ 1 << stride) for i in range(lax.axis_size(axis))])


def from_root(block, axis, source):
    block = jnp.where(lax.axis_index(axis) == source, block, jnp.zeros_like(block))
    return lax.psum(block, axis)


def padded_2(value, sides, width):
    for axis, dim in sides:
        size, length = (lax.axis_size(axis), value.shape[dim])
        up = [(i, (i + 1) % size) for i in range(size - 1)]
        down = [(j, i) for i, j in up]
        last = lax.slice_in_dim(value, length - width, length, axis=dim)
        initial = lax.slice_in_dim(value, 0, width, axis=dim)
        before = lax.ppermute(last, axis, up)
        after = lax.ppermute(initial, axis, down)
        value = jnp.concatenate([before, value, after], axis=dim)
    return value


def angles(numerator, denominator, sign_value):
    return sign_value * 2.0 * math.pi * numerator.astype(jnp.float32) / denominator


def rotate(signal, cosine, sine_part):
    real_part = signal[0] * cosine - signal[1] * sine_part
    imag_part = signal[0] * sine_part + signal[1] * cosine
    return jnp.stack([real_part, imag_part])


def dft_table(length_n, sign_value):
    counter = jnp.arange(length_n, dtype=jnp.int32)
    turn_count = counter[:, None] * counter[None, :] % length_n
    angle_set = angles(turn_count, length_n, sign_value)
    return (jnp.cos(angle_set), jnp.sin(angle_set))


def complex_apply(einsum_form, cosine, sine_part, signal):
    real_part = jnp.einsum(einsum_form, cosine, signal[0], precision=PRECISE) - jnp.einsum(
        einsum_form, sine_part, signal[1], precision=PRECISE
    )
    imag_part = jnp.einsum(einsum_form, cosine, signal[1], precision=PRECISE) + jnp.einsum(
        einsum_form, sine_part, signal[0], precision=PRECISE
    )
    return jnp.stack([real_part, imag_part])


def local_dft(signal, sign_value):
    rg_cols = signal.shape[1]
    az_rows = signal.shape[2]
    inner_len = az_rows // SPLIT
    shaped = signal.reshape(2, rg_cols, SPLIT, inner_len)
    first_cos, first_sin = dft_table(SPLIT, sign_value)
    first_pass = complex_apply("aj,cjk->cak", first_cos, first_sin, shaped)
    outer_idx = jnp.arange(SPLIT, dtype=jnp.int32)
    inner_idx = jnp.arange(inner_len, dtype=jnp.int32)
    twist = angles(outer_idx[:, None] * inner_idx[None, :] % az_rows, az_rows, sign_value)
    first_pass = rotate(first_pass, jnp.cos(twist)[None, :, :], jnp.sin(twist)[None, :, :])
    second_cos, second_sin = dft_table(inner_len, sign_value)
    second_pass = complex_apply("bk,cak->cba", second_cos, second_sin, first_pass)
    return second_pass.reshape(2, rg_cols, az_rows)


def butterfly_down(signal, az_place, bit_count):
    for bit_num in reversed(range(bit_count)):
        half_span = 1 << bit_num
        partner = partner_2(signal, "az", bit_num)
        is_upper = az_place >> bit_num & 1 == 1
        angle_set = angles(az_place % half_span, 2 * half_span, -1.0)
        difference = rotate(partner - signal, jnp.cos(angle_set), jnp.sin(angle_set))
        signal = jnp.where(is_upper, difference, signal + partner)
    return signal


def butterfly_up(signal, az_place, bit_count):
    for bit_num in range(bit_count):
        half_span = 1 << bit_num
        partner = partner_2(signal, "az", bit_num)
        is_upper = az_place >> bit_num & 1 == 1
        angle_set = angles(az_place % half_span, 2 * half_span, 1.0)
        cosine = jnp.cos(angle_set)
        sine_part = jnp.sin(angle_set)
        lower_new = (signal + rotate(partner, cosine, sine_part)) * 0.5
        upper_new = (partner - rotate(signal, cosine, sine_part)) * 0.5
        signal = jnp.where(is_upper, upper_new, lower_new)
    return signal


def butterfly_shards(raw_re, raw_im, ref_blocks, owners, offsets, taps):
    rg_cols = raw_re.shape[0]
    az_rows = raw_re.shape[1]
    az_count = lax.axis_size("az")
    az_place = lax.axis_index("az")
    bit_count = az_count.bit_length() - 1
    az_total = az_rows * az_count
    rg_total = rg_cols * lax.axis_size("rg")
    own_block = ref_blocks[0]
    lower_ref = from_root(own_block, "az", owners[0])
    upper_ref = from_root(own_block, "az", owners[1])
    signal = jnp.stack([raw_re, raw_im])
    signal = butterfly_down(signal, az_place, bit_count)
    column = jnp.zeros((), jnp.int32)
    for bit_num in range(bit_count):
        column = column + ((az_place >> bit_num & 1) << bit_count - 1 - bit_num)
    row_index = jnp.arange(az_rows, dtype=jnp.int32)
    twist = angles(row_index * column % az_total, az_total, -1.0)
    signal = rotate(signal, jnp.cos(twist)[None, :], jnp.sin(twist)[None, :])
    signal = local_dft(signal, -1.0)
    frequency = column + az_count * row_index
    signed = (frequency + az_total // 2) % az_total - az_total // 2
    az_freq = signed.astype(jnp.float32) / az_total
    rg_index = lax.axis_index("rg") * rg_cols + jnp.arange(rg_cols, dtype=jnp.int32)
    rg_freq = (rg_index.astype(jnp.float32) + 0.5) / (2 * rg_total) - 0.25
    model_phase = PHASE_GAIN * jnp.sqrt((1.0 + rg_freq)[:, None] ** 2 - az_freq[None, :] ** 2)
    ref_rows = own_block.shape[0]
    coarse = frequency * ref_rows // az_total
    slot_index = jnp.where(signed >= 0, ref_rows + coarse, coarse)
    one_hot = (jnp.arange(2 * ref_rows, dtype=jnp.int32)[:, None] == slot_index[None, :]).astype(
        jnp.float32
    )
    both_refs = jnp.concatenate([lower_ref, upper_ref], axis=0)
    picked = jnp.dot(both_refs.T, one_hot, precision=PRECISE)
    phase_all = model_phase + picked
    signal = rotate(signal, jnp.cos(phase_all), jnp.sin(phase_all))
    rim_width = REACH + TAPS // 2
    padded = padded_2(signal, (("rg", 1),), rim_width)
    offset_cols = jnp.repeat(offsets, BLOCK)
    local_cols = jnp.arange(rg_cols, dtype=jnp.int32)
    tap_index = jnp.arange(TAPS, dtype=jnp.int32)
    target = local_cols[:, None] + rim_width + offset_cols[:, None] + tap_index[None, :] - TAPS // 2
    padded_index = jnp.arange(rg_cols + 2 * rim_width, dtype=jnp.int32)
    hits = (padded_index[:, None, None] == target[None, :, :]).astype(jnp.float32)
    band_matrix = jnp.sum(hits * taps[None, :, :], axis=2)
    signal = jnp.einsum("zma,mi->zia", padded, band_matrix, precision=PRECISE)
    signal = local_dft(signal, 1.0) / az_rows
    twist_back = angles(row_index * column % az_total, az_total, 1.0)
    signal = rotate(signal, jnp.cos(twist_back)[None, :], jnp.sin(twist_back)[None, :])
    signal = butterfly_up(signal, az_place, bit_count)
    return (signal[0], signal[1])


FACTOR = 128
PLACES = 8
PART = FACTOR // PLACES
HALF = FACTOR // 2
OUT_BINS = 8
WINDOW = OUT_BINS + TAPS - 1
REF_LINES = 8
EDGE = 16
CHUNKS = (((0, WINDOW), (0, OUT_BINS)),)


def split_bf16(value):
    high = value.astype(jnp.bfloat16)
    low = (value - high.astype(jnp.float32)).astype(jnp.bfloat16)
    return high, low


def dot_split(left, right):
    left_high, left_low = left
    right_high, right_low = right
    dot = functools.partial(jnp.dot, preferred_element_type=jnp.float32)
    return dot(left_high, right_high) + (dot(left_high, right_low) + dot(left_low, right_high))


def both_bf16(matrix):
    high = matrix.astype(jnp.bfloat16)
    return high, (matrix - high.astype(np.float64)).astype(jnp.bfloat16)


def dft_constants():
    counter = np.arange(FACTOR)
    kappa = np.arange(HALF)
    first, last, twists = [], [], []
    for side in range(2):
        order = [(middle, low, line) for low in (side, 1 - side) for middle in range(2) for line in range(PART)]
        mine = np.array([(2 * middle + low) * PART + line for middle, low, line in order])
        angle = 2 * np.pi * (np.outer(2 * kappa + side, mine) % FACTOR) / FACTOR
        cosine, sine = np.cos(angle), np.sin(angle)
        first.append(np.block([[cosine, sine], [-sine, cosine]]))
        back_re, back_im = np.block([cosine.T, -sine.T]), np.block([sine.T, cosine.T])
        own, other = slice(0, HALF // 2), slice(HALF // 2, HALF)
        last.append(np.concatenate([back_re[own], back_im[own], back_re[other], back_im[other]]))
        twist = 2 * np.pi * np.outer(2 * kappa + side, counter) / FACTOR**2
        twists.append(np.stack([np.cos(twist), np.sin(twist)]))
    angle = 2 * np.pi * (np.outer(counter, counter) % FACTOR) / FACTOR
    cosine, sine = np.cos(angle), np.sin(angle)
    there = np.block([[cosine, -sine], [sine, cosine]])
    back = np.block([[cosine, sine], [-sine, cosine]])
    matrices = [both_bf16(matrix) for matrix in (np.stack(first), there, back, np.stack(last))]
    return [part for pair in matrices for part in pair], np.stack(twists).astype(np.float32)


def cos_sin_quarters(quarters):
    whole = jnp.floor(quarters + 0.5)
    rest = (quarters - whole) * (math.pi / 2)
    square = rest * rest
    sine = rest + rest * square * (
        -1.6666654611e-1 + square * (8.3321608736e-3 + square * (-1.9515295891e-4))
    )
    cosine = 1.0 - 0.5 * square + square * square * (
        4.166664568298827e-2 + square * (-1.388731625493765e-3 + square * 2.443315711809948e-5)
    )
    number = whole.astype(jnp.int32)
    odd = (number & 1) == 1
    turned_cos = jnp.where(odd, sine, cosine)
    turned_sin = jnp.where(odd, cosine, sine)
    cos_sign = jnp.where(((number + 1) & 2) == 2, -1.0, 1.0)
    sin_sign = jnp.where((number & 2) == 2, -1.0, 1.0)
    return turned_cos * cos_sign, turned_sin * sin_sign


def window_start(chip, side, offsets_own, offsets_other):
    block = chip * OUT_BINS // BLOCK
    blocks = offsets_own.shape[0]
    local = lax.rem(block, blocks)
    shift = jnp.where(lax.div(block, blocks) == side, offsets_own[local], offsets_other[local])
    return chip * OUT_BINS + shift - TAPS // 2


def spread_lines(target, base, source):
    bins, samples = source.shape
    part_rows = samples // FACTOR
    for tile in range(0, bins, 8):
        for row in range(part_rows):
            target[pl.ds((base + tile) * part_rows + row, 8, stride=part_rows), :] = source[
                tile : tile + 8, row * FACTOR : (row + 1) * FACTOR
            ]


def spread_kernel(re_own, im_own, re_lines, im_lines):
    spread_lines(re_lines, 0, re_own)
    spread_lines(im_lines, 0, im_own)


def pack_kernel(re_lines, im_lines, re_other, im_other, ref_own, ref_other, off_own, off_other, *refs):
    messages, (re_all, im_all, ref_all) = refs[:-3], refs[-3:]
    bins, samples = re_other.shape
    part_rows = samples // FACTOR
    place, side = lax.axis_index("az"), lax.axis_index("rg")
    own_at, other_at = EDGE + side * bins, EDGE + (1 - side) * bins
    zeros = jnp.zeros((EDGE * part_rows, FACTOR), jnp.float32)
    for all_ref, own, other in ((re_all, re_lines, re_other), (im_all, im_lines, im_other)):
        all_ref[: EDGE * part_rows, :] = zeros
        all_ref[(EDGE + 2 * bins) * part_rows :, :] = zeros
        all_ref[pl.ds(pl.multiple_of(own_at * part_rows, 8), bins * part_rows), :] = own[...]
        spread_lines(all_ref, other_at, other)
    ref_rows = ref_own.shape[0]
    row = lax.broadcasted_iota(jnp.int32, (ref_rows, FACTOR), 0)
    column = lax.broadcasted_iota(jnp.int32, (ref_rows, FACTOR), 1)
    twice = (lax.rem(column, ref_rows) == row).astype(jnp.float32)
    ref_all[:EDGE, :] = jnp.zeros((EDGE, FACTOR), jnp.float32)
    ref_all[EDGE + 2 * bins :, :] = jnp.zeros((EDGE, FACTOR), jnp.float32)
    for at, ref in ((own_at, ref_own), (other_at, ref_other)):
        ref_all[pl.ds(pl.multiple_of(at, 16), bins), :] = lax.dot_general(
            ref[...], twice, (((0,), (0,)), ((), ())), precision=PRECISE, preferred_element_type=jnp.float32
        )
    lane = lax.broadcasted_iota(jnp.int32, (1, FACTOR), 1)
    for at, message in enumerate(messages):
        step = at % (PLACES // 2)
        (first_bin, last_bin), _ = CHUNKS[at // (PLACES // 2)]
        body = (last_bin - first_bin) * part_rows
        start = window_start(((place >> 1) ^ step) * 2 + side, side, off_own, off_other) + EDGE
        rows = pl.ds(pl.multiple_of((start + first_bin) * part_rows, 8), body)
        message[:body, :] = re_all[rows, :]
        message[body : 2 * body, :] = im_all[rows, :]
        if first_bin == 0:
            for bin_num in range(REF_LINES):
                low = ref_all[pl.ds(start + bin_num, 1), :]
                high = ref_all[pl.ds(start + REF_LINES + bin_num, 1), :]
                message[2 * body + bin_num : 2 * body + bin_num + 1, :] = jnp.where(lane < HALF, low, high)


def phase_kernel(bins_total, off_own, off_other, out):
    place, side = lax.axis_index("az"), lax.axis_index("rg")
    start = window_start(place, side, off_own, off_other)
    shape = (HALF, FACTOR)
    kappa = lax.broadcasted_iota(jnp.int32, shape, 0)
    frequency = 2 * kappa + side + FACTOR * lax.broadcasted_iota(jnp.int32, shape, 1)
    total = FACTOR * FACTOR
    signed = jnp.where(frequency >= total // 2, frequency - total, frequency)
    az_freq = signed.astype(jnp.float32) / total
    az_square = az_freq * az_freq
    for bin_num in range(WINDOW):
        rg_index = (start + bin_num).astype(jnp.float32)
        rg_freq = (rg_index + 0.5) / (2 * bins_total) - 0.25
        base = (1.0 + rg_freq) * (1.0 + rg_freq)
        root = jnp.sqrt(base - az_square)
        cosine, sine = cos_sin_quarters(root * (PHASE_GAIN * 2 / math.pi))
        out[bin_num, 0] = cosine
        out[bin_num, 1] = sine


def parity_kernel(bins, has_ref, *refs):
    chunks, refs = refs[: PLACES // 2], refs[PLACES // 2 :]
    place, side = lax.axis_index("az"), lax.axis_index("rg")
    if has_ref:
        owners, keep, give, keep_ref = refs
    else:
        keep, give = refs
    sign = jnp.where(place >= PLACES // 2, -1.0, 1.0)
    even = side == 0
    keep_near, keep_far = jnp.where(even, 1.0, sign), jnp.where(even, 1.0, -sign)
    give_near, give_far = jnp.where(even, sign, 1.0), jnp.where(even, -sign, 1.0)
    middle = (place >> 1) & 1
    for step in range(2):
        near, far = chunks[step], chunks[step + 2]
        for line in range(2 * bins):
            read = slice(line * PART, (line + 1) * PART)
            write = pl.ds(pl.multiple_of(line * 2 * PART + (middle ^ step) * PART, 8), PART)
            near_value, far_value = near[read, :], far[read, :]
            keep[write, :] = near_value * keep_near + far_value * keep_far
            give[write, :] = near_value * give_near + far_value * give_far
    if has_ref:
        for which in range(2):
            step = (owners[which] >> 1) ^ (place >> 1)
            for other in range(PLACES // 2):

                @pl.when(step == other)
                def _():
                    value = chunks[other][2 * bins * PART :, :]
                    give[pl.ds(2 * bins * 2 * PART + which * REF_LINES, REF_LINES), :] = value
                    keep_ref[which] = value


def band_kernel(chunk, *refs):
    (first_bin, last_bin), (first_out, last_out) = CHUNKS[chunk]
    bins = last_bin - first_bin
    keep, got, keep_ref, got_ref, owners, phase, taps_own, taps_other = refs[:8]
    first_high, first_low, there_high, there_low, back_high, back_low, last_high, last_low, twists = refs[8:17]
    refs = refs[17:]
    if chunk:
        earlier, refs = refs[0], refs[1:]
    keep_out, give_out, spectra, band, picked = refs
    place, side = lax.axis_index("az"), lax.axis_index("rg")

    row = lax.broadcasted_iota(jnp.int32, (FACTOR, FACTOR), 0)
    column = lax.broadcasted_iota(jnp.int32, (FACTOR, FACTOR), 1)
    lane = lax.broadcasted_iota(jnp.int32, (REF_LINES, FACTOR), 1)
    ref_at = got_ref.shape[0] - 2 * REF_LINES
    lines = [
        jnp.where(
            (owners[which] & 1) == side,
            keep_ref[which],
            got_ref[ref_at + which * REF_LINES : ref_at + (which + 1) * REF_LINES, :],
        )
        for which in range(2)
    ]
    for block in range(2):
        spread = (row == column // 2 + block * HALF).astype(jnp.float32)
        wide = [
            jnp.dot(lines[which], spread, precision=PRECISE, preferred_element_type=jnp.float32) for which in range(2)
        ]
        ref_phase = jnp.where(lane < HALF, wide[1], wide[0])
        ref_cos, ref_sin = cos_sin_quarters(ref_phase * (2 / math.pi))
        picked[0, block * REF_LINES : (block + 1) * REF_LINES, :] = ref_cos
        picked[1, block * REF_LINES : (block + 1) * REF_LINES, :] = ref_sin

    first, last = (first_high[side], first_low[side]), (last_high[side], last_low[side])
    there, back = (there_high[...], there_low[...]), (back_high[...], back_low[...])
    twist_cos, twist_sin = twists[side, 0], twists[side, 1]
    width = 2 * PART
    for at in range(0, bins, 4):
        group = range(at, min(at + 4, bins))
        columns = [
            jnp.concatenate(
                [
                    ref[(part * bins + bin_num) * width : (part * bins + bin_num + 1) * width, :]
                    for part in range(2)
                    for ref in (keep, got)
                ],
                axis=0,
            )
            for bin_num in group
        ]
        passed = dot_split(first, split_bf16(jnp.concatenate(columns, axis=1)))
        rows = []
        for index in range(len(group)):
            real = passed[:HALF, index * FACTOR : (index + 1) * FACTOR]
            imag = passed[HALF:, index * FACTOR : (index + 1) * FACTOR]
            rows.append(
                jnp.concatenate([real * twist_cos + imag * twist_sin, imag * twist_cos - real * twist_sin], axis=1)
            )
        passed = dot_split(split_bf16(jnp.concatenate(rows, axis=0)), there)
        for index, bin_num in enumerate(group):
            real = passed[index * HALF : (index + 1) * HALF, :FACTOR]
            imag = passed[index * HALF : (index + 1) * HALF, FACTOR:]
            whole = first_bin + bin_num
            model_cos, model_sin = phase[whole, 0], phase[whole, 1]
            row_cos, row_sin = picked[0, whole : whole + 1, :], picked[1, whole : whole + 1, :]
            cosine = model_cos * row_cos - model_sin * row_sin
            sine = model_sin * row_cos + model_cos * row_sin
            spectra[bin_num, 0] = real * cosine - imag * sine
            spectra[bin_num, 1] = real * sine + imag * cosine

    bins_held = taps_own.shape[0]
    held = lax.div(place * OUT_BINS, bins_held) == side
    local = lax.rem(place * OUT_BINS, bins_held)
    outs = range(first_out, last_out)
    weights = {
        out: [jnp.where(held, taps_own[local + out, tap], taps_other[local + out, tap]) for tap in range(TAPS)]
        for out in outs
    }
    strip = 8
    for part in range(2):
        for at in range(0, HALF, strip):
            rows = slice(at, at + strip)
            sums = {}
            for bin_num in range(first_out, last_out + TAPS - 1):
                if bin_num < first_bin:
                    value = earlier[bin_num, part, rows]
                else:
                    value = spectra[bin_num - first_bin, part, rows]
                for out in outs:
                    if 0 <= bin_num - out < TAPS:
                        term = value * weights[out][bin_num - out]
                        sums[out] = sums[out] + term if out in sums else term
            for out in outs:
                line = (out - first_out) * HALF + at
                band[line : line + strip, part * FACTOR : (part + 1) * FACTOR] = sums[out]

    scale = 1.0 / (FACTOR * FACTOR)
    cos_table, sin_table = twist_cos * scale, twist_sin * scale
    for at in range(0, last_out - first_out, 4):
        passed = dot_split(split_bf16(band[at * HALF : (at + 4) * HALF, :]), back)
        columns = []
        for index in range(4):
            real = passed[index * HALF : (index + 1) * HALF, :FACTOR]
            imag = passed[index * HALF : (index + 1) * HALF, FACTOR:]
            columns.append(
                jnp.concatenate([real * cos_table - imag * sin_table, imag * cos_table + real * sin_table], axis=0)
            )
        passed = dot_split(last, split_bf16(jnp.concatenate(columns, axis=1)))
        for index in range(4):
            lines = slice((at + index) * HALF, (at + index + 1) * HALF)
            keep_out[lines, :] = passed[:HALF, index * FACTOR : (index + 1) * FACTOR]
            give_out[lines, :] = passed[HALF:, index * FACTOR : (index + 1) * FACTOR]


def join_kernel(outs, keep, got, *messages):
    place, side = lax.axis_index("az"), lax.axis_index("rg")
    quarter = lax.rem(place, PLACES // 2)
    sign = jnp.where(side == 0, 1.0, -1.0)
    for step, message in enumerate(messages):
        target = quarter ^ step
        top, middle = target >> 1, target & 1
        keep_factor, got_factor = jnp.where(top == 0, 1.0, sign), jnp.where(top == 0, 1.0, -sign)
        for line in range(2 * outs):
            read = pl.ds(pl.multiple_of(line * 2 * PART + middle * PART, 8), PART)
            message[line * PART : (line + 1) * PART, :] = keep[read, :] * keep_factor + got[read, :] * got_factor


def place_kernel(*refs):
    messages, (out_re, out_im, re_all, im_all) = refs[:-4], refs[-4:]
    bins, samples = out_re.shape
    place = lax.axis_index("az")
    for at, message in enumerate(messages):
        sender = (place >> 1) ^ (at % (PLACES // 2))
        _, (first_out, last_out) = CHUNKS[at // (PLACES // 2)]
        for out in range(last_out - first_out):
            line = pl.multiple_of((sender * OUT_BINS + first_out + out) * PART, 8)
            re_all[pl.ds(line, PART), :] = message[2 * out * PART : (2 * out + 1) * PART, :]
            im_all[pl.ds(line, PART), :] = message[(2 * out + 1) * PART : (2 * out + 2) * PART, :]
    for out, all_ref in ((out_re, re_all), (out_im, im_all)):
        for tile in range(0, bins, 8):
            for row in range(PART):
                out[tile : tile + 8, row * FACTOR : (row + 1) * FACTOR] = all_ref[
                    pl.ds(tile * PART + row, 8, stride=PART), :
                ]


VMEM = pl.BlockSpec(memory_space=pltpu.VMEM)
SMEM = pl.BlockSpec(memory_space=pltpu.SMEM)


def kernel_call(body, name, out_shape, operands, scratch=(), flops=0, count=10**6, limit=8):
    specs = [SMEM if operand.size <= 1024 else VMEM for operand in operands]
    return pl.pallas_call(
        body,
        out_shape=out_shape,
        in_specs=specs,
        out_specs=jax.tree.map(lambda _: VMEM, out_shape),
        scratch_shapes=[pltpu.VMEM(shape, jnp.float32) for shape in scratch],
        compiler_params=pltpu.CompilerParams(vmem_limit_bytes=limit * 1024 * 1024),
        cost_estimate=pl.CostEstimate(flops=flops, bytes_accessed=count, transcendentals=0),
        name=name,
    )(*operands)


def transposed_shards(raw_re, raw_im, ref_blocks, owners, offsets, taps):
    bins, samples = raw_re.shape

    def array(*shape):
        return jax.ShapeDtypeStruct(shape, jnp.float32)

    matrices, twists = dft_constants()
    tables = [jnp.asarray(part) for part in matrices] + [jnp.asarray(twists)]
    swap = functools.partial(lax.ppermute, axis_name="rg", perm=[(0, 1), (1, 0)])
    half = PLACES // 2
    ref_own = ref_blocks[0]
    offsets_other = swap(offsets)
    ref_other, re_other, im_other, taps_other = swap(ref_own), swap(raw_re), swap(raw_im), swap(taps)

    lines = kernel_call(spread_kernel, "spread", [array(bins * PART, FACTOR)] * 2, [raw_re, raw_im], count=2 * 10**6)
    shapes = []
    for (first_bin, last_bin), _ in CHUNKS:
        ref_lines = REF_LINES if first_bin == 0 else 0
        shapes += [array(2 * (last_bin - first_bin) * PART + ref_lines, FACTOR)] * half
    all_lines = (2 * bins + 2 * EDGE) * PART
    messages = kernel_call(
        pack_kernel,
        "pack",
        shapes,
        [*lines, re_other, im_other, ref_own, ref_other, offsets, offsets_other],
        scratch=[(all_lines, FACTOR), (all_lines, FACTOR), (2 * bins + 2 * EDGE, FACTOR)],
        count=4 * 10**6,
    )
    phases = kernel_call(
        functools.partial(phase_kernel, 2 * bins),
        "phase",
        array(WINDOW, 2, HALF, FACTOR),
        [offsets, offsets_other],
        flops=10**7,
    )

    routes = [
        [
            (chip * 2 + core, (((chip >> 1) ^ step) * 2 + core) * 2 + (chip & 1))
            for chip in range(PLACES)
            for core in range(2)
        ]
        for step in range(half)
    ]
    routes_back = [
        [
            (chip * 2 + core, (((chip % half) ^ step) * 2 + core) * 2 + chip // half)
            for chip in range(PLACES)
            for core in range(2)
        ]
        for step in range(half)
    ]
    arrived = [lax.ppermute(message, ("az", "rg"), routes[at % half]) for at, message in enumerate(messages)]

    results = []
    refs, earlier = None, []
    for chunk, ((first_bin, last_bin), (first_out, last_out)) in enumerate(CHUNKS):
        count, outs = last_bin - first_bin, last_out - first_out
        has_ref = chunk == 0
        size = 2 * count * 2 * PART
        shapes = [array(size, FACTOR), array(size + (2 * REF_LINES if has_ref else 0), FACTOR)]
        operands = arrived[chunk * half : (chunk + 1) * half]
        if has_ref:
            shapes.append(array(2, REF_LINES, FACTOR))
            operands = operands + [owners]
        parity = kernel_call(functools.partial(parity_kernel, count, has_ref), "parity", shapes, operands)
        keep, give = parity[:2]
        got = swap(give)
        if has_ref:
            refs = [parity[2], got]
        pieces = kernel_call(
            functools.partial(band_kernel, chunk),
            "band",
            [array(outs * HALF, FACTOR), array(outs * HALF, FACTOR), array(count, 2, HALF, FACTOR)],
            [keep, got, *refs, owners, phases, taps, taps_other, *tables, *earlier],
            scratch=[(outs * HALF, 2 * FACTOR), (2, 2 * REF_LINES, FACTOR)],
            flops=10**9,
            count=4 * 10**6,
            limit=16,
        )
        keep, give, spectra = pieces
        earlier = [spectra]
        sent = kernel_call(
            functools.partial(join_kernel, outs),
            "join",
            [array(2 * outs * PART, FACTOR)] * half,
            [keep, swap(give)],
        )
        results += [lax.ppermute(message, ("az", "rg"), route) for message, route in zip(sent, routes_back)]
    return kernel_call(
        place_kernel, "place", [array(bins, samples)] * 2, results, scratch=[(bins * PART, FACTOR)] * 2
    )


def solution(mesh):
    sizes = mesh.shape

    def whole(raw_re, raw_im, ref_blocks, owners, offsets, taps):
        line = raw_re.shape[1] // sizes["scene"]
        fits = (
            sizes["rg"] == 2
            and sizes["az"] == PLACES
            and raw_re.shape[0] == OUT_BINS * PLACES
            and line == FACTOR * FACTOR
            and ref_blocks.shape[1] == HALF
        )
        return jax.shard_map(
            transposed_shards if fits else butterfly_shards,
            mesh=mesh,
            in_specs=(
                P("rg", ("scene", "az")),
                P("rg", ("scene", "az")),
                P(("scene", "az"), None, "rg"),
                P("scene"),
                P("rg"),
                P("rg", None),
            ),
            out_specs=(P("rg", ("scene", "az")), P("rg", ("scene", "az"))),
            check_vma=False,
        )(raw_re, raw_im, ref_blocks, owners, offsets, taps)

    return whole
```

profile of v0, /device:TPU:0, one launch (start us, length us, event | category | flops | bytes accessed | tf_op | source)
XLA Modules:
  0.0 63.1 jit_solution(7706228963902279912)
XLA Ops:
  0.6 0.5 collective-permute-start
  1.1 0.1 collective-permute-start.1
  1.2 0.8 %copy.17 = f32[1,64,32]{2,1,0:T(8,128)S(1)} copy(f32[1,64,32]{1,2,0:T(8,128)} %param.17) | data formatting | bytes 16384 | tf_op args[2]
  2.0 0.5 collective-permute-start.2
  2.5 0.2 copy-done.2
  2.7 0.4 collective-permute-start.3
  3.1 0.9 %copy-done = f32[32,2048]{1,0:T(8,128)S(1)} copy-done((f32[32,2048]{1,0:T(8,128)S(1)}, f32[32,2048]{1,0:T(8,128)}, u32[]{:S(2)}) %copy-start) | copy-done | bytes 262168
  4.1 0.9 %copy-done.1 = f32[32,2048]{1,0:T(8,128)S(1)} copy-done((f32[32,2048]{1,0:T(8,128)S(1)}, f32[32,2048]{1,0:T(8,128)}, u32[]{:S(2)}) %copy-start.1) | copy-done | bytes 262168
  5.0 0.1 spread.1
  5.2 0.9 %pack.1 = (f32[488,128]{1,0:T(8,128)S(1)}, f32[488,128]{1,0:T(8,128)S(1)}, f32[488,128]{1,0:T(8,128)S(1)}, f32[488,128]{1,0:T(8,128)S(1)}) custom-call(f32[512,128]{1,0:T(8,128)S(1)} %get-tuple-element.17.re_lines, f32[512,128]{1,0:T(8,128)S(1)} %get-tuple-element.18.im_lines, f32[32,2048]{1,0:T(8,128)S(1)} %collective-permute-done.re_other, ...), custom_call_target="tpu_custom_call" | custom-call | bytes 4000000 | tf_op jit(solution)/shard_map/pack/pallas_call | solution.py:501
  6.1 0.7 %collective-permute-start.4 = (f32[488,128]{1,0:T(8,128)S(1)}, f32[488,128]{1,0:T(8,128)S(1)}, u32[]{:S(2)}, u32[]{:S(2)}) collective-permute-start(f32[488,128]{1,0:T(8,128)S(1)} %get-tuple-element.19), channel_id=1, source_target_pairs={{0,0},{1,2},{2,1},{3,3},{4,4},{5,6},{6,5},{7,7},{8,8},{9,10},{10,9... | collective-permute-start | bytes 749576 | tf_op jit(solution)/shard_map/ppermute | solution.py:565
  6.8 2.7 %collective-permute-start.5 = (f32[488,128]{1,0:T(8,128)S(1)}, f32[488,128]{1,0:T(8,128)S(1)}, u32[]{:S(2)}, u32[]{:S(2)}) collective-permute-start(f32[488,128]{1,0:T(8,128)S(1)} %get-tuple-element.20), channel_id=1, source_target_pairs={{0,4},{1,6},{2,5},{3,7},{4,0},{5,2},{6,1},{7,3},{8,12},{9,14},{10,... | collective-permute-start | bytes 749576 | tf_op jit(solution)/shard_map/ppermute | solution.py:565
  9.5 2.6 %collective-permute-start.6 = (f32[488,128]{1,0:T(8,128)S(1)}, f32[488,128]{1,0:T(8,128)S(1)}, u32[]{:S(2)}, u32[]{:S(2)}) collective-permute-start(f32[488,128]{1,0:T(8,128)S(1)} %get-tuple-element.21), channel_id=1, source_target_pairs={{0,8},{1,10},{2,9},{3,11},{4,12},{5,14},{6,13},{7,15},{8,0},{9,2},... | collective-permute-start | bytes 749576 | tf_op jit(solution)/shard_map/ppermute | solution.py:565
  12.1 4.8 %collective-permute-done.5.refs_1_ = f32[488,128]{1,0:T(8,128)S(1)} collective-permute-done((f32[488,128]{1,0:T(8,128)S(1)}, f32[488,128]{1,0:T(8,128)S(1)}, u32[]{:S(2)}, u32[]{:S(2)}) %collective-permute-start.5) | collective-permute-done | bytes 249888 | tf_op jit(solution)/shard_map/ppermute | solution.py:565
  16.9 2.2 %collective-permute-done.6.refs_2_ = f32[488,128]{1,0:T(8,128)S(1)} collective-permute-done((f32[488,128]{1,0:T(8,128)S(1)}, f32[488,128]{1,0:T(8,128)S(1)}, u32[]{:S(2)}, u32[]{:S(2)}) %collective-permute-start.6) | collective-permute-done | bytes 249888 | tf_op jit(solution)/shard_map/ppermute | solution.py:565
  19.1 8.4 %collective-permute-done.7.refs_3_ = f32[488,128]{1,0:T(8,128)S(1)} collective-permute-done((f32[488,128]{1,0:T(8,128)S(1)}, f32[488,128]{1,0:T(8,128)S(1)}, u32[]{:S(2)}, u32[]{:S(2)}) %collective-permute-start.7) | collective-permute-done | bytes 249888 | tf_op jit(solution)/shard_map/ppermute | solution.py:565
  27.5 0.7 %parity.1 = (f32[960,128]{1,0:T(8,128)S(1)}, f32[976,128]{1,0:T(8,128)S(1)}, f32[2,8,128]{2,1,0:T(8,128)S(1)}) custom-call(f32[488,128]{1,0:T(8,128)S(1)} %collective-permute-done.4.refs_0_, f32[488,128]{1,0:T(8,128)S(1)} %collective-permute-done.5.refs_1_, f32[488,128]{1,0:T(8,128)S(1)} %collective-permute-done.6.refs_2_, ...), custom_call_target="tpu_custom_call" | custom-call | bytes 1000000 | tf_op jit(solution)/shard_map/parity/pallas_call | solution.py:501
  28.2 5.3 %collective-permute-start.8 = (f32[976,128]{1,0:T(8,128)S(1)}, f32[976,128]{1,0:T(8,128)S(1)}, u32[]{:S(2)}, u32[]{:S(2)}) collective-permute-start(f32[976,128]{1,0:T(8,128)S(1)} %get-tuple-element.24), channel_id=1, source_target_pairs={{0,1},{1,0},{2,3},{3,2},{4,5},{5,4},{6,7},{7,6},{8,9},{9,8},{10,11... | collective-permute-start | bytes 1499144 | tf_op jit(solution)/shard_map/ppermute | solution.py:580
  33.5 0.1 copy.19.refs_6_
  33.6 0.1 collective-permute-start.9
  33.7 1.3 %phase.1.refs_5_ = f32[15,2,64,128]{3,2,1,0:T(8,128)S(1)} custom-call(s32[2]{0:T(128)S(1)} %copy-done.2, s32[2]{0:T(128)S(1)} %collective-permute-done.3.off_other), custom_call_target="tpu_custom_call" | custom-call | flops 10000000 | bytes 1000000 | tf_op jit(solution)/shard_map/phase/pallas_call | solution.py:501
  35.1 3.6 %band.1 = (f32[512,128]{1,0:T(8,128)S(1)}, f32[512,128]{1,0:T(8,128)S(1)}, f32[15,2,64,128]{3,2,1,0:T(8,128)}) custom-call(f32[960,128]{1,0:T(8,128)S(1)} %get-tuple-element.23.refs_0_, f32[976,128]{1,0:T(8,128)S(1)} %collective-permute-done.8.refs_1_.refs_3_, f32[2,8,128]{2,1,0:T(8,128)S(1)} %get-tuple-element.25.refs_2_, ...), custom_call_target="tpu_custom_call" | custom-call | flops 1000000000 | bytes 4000000 | tf_op jit(solution)/shard_map/band/pallas_call | solution.py:501
  38.7 0.5 collective-permute-start.10
  39.2 1.2 %collective-permute-done.10.got = f32[512,128]{1,0:T(8,128)S(1)} collective-permute-done((f32[512,128]{1,0:T(8,128)S(1)}, f32[512,128]{1,0:T(8,128)S(1)}, u32[]{:S(2)}, u32[]{:S(2)}) %collective-permute-start.10) | collective-permute-done | bytes 262176 | tf_op jit(solution)/shard_map/ppermute | solution.py:599
  40.4 0.1 join.1
  40.4 0.7 %collective-permute-start.11 = (f32[256,128]{1,0:T(8,128)S(1)}, f32[256,128]{1,0:T(8,128)S(1)}, u32[]{:S(2)}, u32[]{:S(2)}) collective-permute-start(f32[256,128]{1,0:T(8,128)S(1)} %get-tuple-element.28), channel_id=1, source_target_pairs={{0,0},{1,2},{2,4},{3,6},{4,8},{5,10},{6,12},{7,14},{8,1},{9,3},{10... | collective-permute-start | bytes 393224 | tf_op jit(solution)/shard_map/ppermute | solution.py:601
  41.1 6.1 %collective-permute-start.12 = (f32[256,128]{1,0:T(8,128)S(1)}, f32[256,128]{1,0:T(8,128)S(1)}, u32[]{:S(2)}, u32[]{:S(2)}) collective-permute-start(f32[256,128]{1,0:T(8,128)S(1)} %get-tuple-element.29), channel_id=1, source_target_pairs={{0,4},{1,6},{2,0},{3,2},{4,12},{5,14},{6,8},{7,10},{8,5},{9,7},{10... | collective-permute-start | bytes 393224 | tf_op jit(solution)/shard_map/ppermute | solution.py:601
  47.2 2.5 %collective-permute-start.13 = (f32[256,128]{1,0:T(8,128)S(1)}, f32[256,128]{1,0:T(8,128)S(1)}, u32[]{:S(2)}, u32[]{:S(2)}) collective-permute-start(f32[256,128]{1,0:T(8,128)S(1)} %get-tuple-element.30), channel_id=1, source_target_pairs={{0,8},{1,10},{2,12},{3,14},{4,0},{5,2},{6,4},{7,6},{8,9},{9,11},{1... | collective-permute-start | bytes 393224 | tf_op jit(solution)/shard_map/ppermute | solution.py:601
  49.8 2.7 %collective-permute-start.14 = (f32[256,128]{1,0:T(8,128)S(1)}, f32[256,128]{1,0:T(8,128)S(1)}, u32[]{:S(2)}, u32[]{:S(2)}) collective-permute-start(f32[256,128]{1,0:T(8,128)S(1)} %get-tuple-element.31), channel_id=1, source_target_pairs={{0,12},{1,14},{2,8},{3,10},{4,4},{5,6},{6,0},{7,2},{8,13},{9,15},{... | collective-permute-start | bytes 393224 | tf_op jit(solution)/shard_map/ppermute | solution.py:601
  52.5 3.8 %collective-permute-done.13.refs_2_ = f32[256,128]{1,0:T(8,128)S(1)} collective-permute-done((f32[256,128]{1,0:T(8,128)S(1)}, f32[256,128]{1,0:T(8,128)S(1)}, u32[]{:S(2)}, u32[]{:S(2)}) %collective-permute-start.13) | collective-permute-done | bytes 131104 | tf_op jit(solution)/shard_map/ppermute | solution.py:601
  56.3 5.9 %collective-permute-done.14.refs_3_ = f32[256,128]{1,0:T(8,128)S(1)} collective-permute-done((f32[256,128]{1,0:T(8,128)S(1)}, f32[256,128]{1,0:T(8,128)S(1)}, u32[]{:S(2)}, u32[]{:S(2)}) %collective-permute-start.14) | collective-permute-done | bytes 131104 | tf_op jit(solution)/shard_map/ppermute | solution.py:601
  62.2 0.9 %place.1 = (f32[32,2048]{1,0:T(8,128)}, f32[32,2048]{1,0:T(8,128)}) custom-call(f32[256,128]{1,0:T(8,128)S(1)} %collective-permute-done.11.refs_0_, f32[256,128]{1,0:T(8,128)S(1)} %collective-permute-done.12.refs_1_, f32[256,128]{1,0:T(8,128)S(1)} %collective-permute-done.13.refs_2_, f32[256,128]{1,0:T(8,128)S(1)} %collective-permute-done.14.refs_3_), custom_call_target="tpu_custom_call" | custom-call | bytes 1000000 | tf_op jit(solution)/shard_map/place/pallas_call | solution.py:501
  (35 shorter events, 0.1 us)
Async XLA Ops:
  0.6 4.6 %collective-permute-start = (f32[32,2048]{1,0:T(8,128)}, f32[32,2048]{1,0:T(8,128)S(1)}, u32[]{:S(2)}, u32[]{:S(2)}) collective-permute-start(f32[32,2048]{1,0:T(8,128)} %re_own.1), channel_id=1, source_target_pairs={{0,1},{1,0},{2,3},{3,2},{4,5},{5,4},{6,7},{7,6},{8,9},{9,8},{10,11... | collective-permute-start | bytes 786440 | tf_op jit(solution)/shard_map/ppermute | solution.py:525
  1.1 4.1 %collective-permute-start.1 = (f32[32,2048]{1,0:T(8,128)}, f32[32,2048]{1,0:T(8,128)S(1)}, u32[]{:S(2)}, u32[]{:S(2)}) collective-permute-start(f32[32,2048]{1,0:T(8,128)} %im_own.1), channel_id=1, source_target_pairs={{0,1},{1,0},{2,3},{3,2},{4,5},{5,4},{6,7},{7,6},{8,9},{9,8},{10,11... | collective-permute-start | bytes 786440 | tf_op jit(solution)/shard_map/ppermute | solution.py:525
  2.0 0.7 %copy-start.2 = (s32[2]{0:T(128)S(1)}, s32[2]{0:T(128)}, u32[]{:S(2)}) copy-start(s32[2]{0:T(128)} %off_own.3) | copy-start | bytes 28
  2.0 3.1 %collective-permute-start.2 = (f32[64,32]{1,0:T(8,128)S(1)}, f32[64,32]{1,0:T(8,128)S(1)}, u32[]{:S(2)}, u32[]{:S(2)}) collective-permute-start(f32[64,32]{1,0:T(8,128)S(1)} %bitcast.1), channel_id=1, source_target_pairs={{0,1},{1,0},{2,3},{3,2},{4,5},{5,4},{6,7},{7,6},{8,9},{9,8},{10,11... | collective-permute-start | bytes 24584 | tf_op jit(solution)/shard_map/ppermute | solution.py:525
  2.7 2.5 %collective-permute-start.3 = (s32[2]{0:T(128)S(1)}, s32[2]{0:T(128)S(1)}, u32[]{:S(2)}, u32[]{:S(2)}) collective-permute-start(s32[2]{0:T(128)S(1)} %copy-done.2), channel_id=1, source_target_pairs={{0,1},{1,0},{2,3},{3,2},{4,5},{5,4},{6,7},{7,6},{8,9},{9,8},{10,11... | collective-permute-start | bytes 32 | tf_op jit(solution)/shard_map/ppermute | solution.py:524
  3.1 0.9 %copy-start = (f32[32,2048]{1,0:T(8,128)S(1)}, f32[32,2048]{1,0:T(8,128)}, u32[]{:S(2)}) copy-start(f32[32,2048]{1,0:T(8,128)} %re_own.1) | copy-start | bytes 786436
  4.1 0.9 %copy-start.1 = (f32[32,2048]{1,0:T(8,128)S(1)}, f32[32,2048]{1,0:T(8,128)}, u32[]{:S(2)}) copy-start(f32[32,2048]{1,0:T(8,128)} %im_own.1) | copy-start | bytes 786436
  6.1 6.0 %collective-permute-start.4 = (f32[488,128]{1,0:T(8,128)S(1)}, f32[488,128]{1,0:T(8,128)S(1)}, u32[]{:S(2)}, u32[]{:S(2)}) collective-permute-start(f32[488,128]{1,0:T(8,128)S(1)} %get-tuple-element.19), channel_id=1, source_target_pairs={{0,0},{1,2},{2,1},{3,3},{4,4},{5,6},{6,5},{7,7},{8,8},{9,10},{10,9... | collective-permute-start | bytes 749576 | tf_op jit(solution)/shard_map/ppermute | solution.py:565
  6.8 10.1 %collective-permute-start.5 = (f32[488,128]{1,0:T(8,128)S(1)}, f32[488,128]{1,0:T(8,128)S(1)}, u32[]{:S(2)}, u32[]{:S(2)}) collective-permute-start(f32[488,128]{1,0:T(8,128)S(1)} %get-tuple-element.20), channel_id=1, source_target_pairs={{0,4},{1,6},{2,5},{3,7},{4,0},{5,2},{6,1},{7,3},{8,12},{9,14},{10,... | collective-permute-start | bytes 749576 | tf_op jit(solution)/shard_map/ppermute | solution.py:565
  9.5 18.0 %copy-start.3 = (s32[2]{0:T(128)S(1)}, s32[2]{0:T(128)}, u32[]{:S(2)}) copy-start(s32[2]{0:T(128)} %refs_4_.3) | copy-start | bytes 28
  9.5 9.6 %collective-permute-start.6 = (f32[488,128]{1,0:T(8,128)S(1)}, f32[488,128]{1,0:T(8,128)S(1)}, u32[]{:S(2)}, u32[]{:S(2)}) collective-permute-start(f32[488,128]{1,0:T(8,128)S(1)} %get-tuple-element.21), channel_id=1, source_target_pairs={{0,8},{1,10},{2,9},{3,11},{4,12},{5,14},{6,13},{7,15},{8,0},{9,2},... | collective-permute-start | bytes 749576 | tf_op jit(solution)/shard_map/ppermute | solution.py:565
  12.1 15.4 %collective-permute-start.7 = (f32[488,128]{1,0:T(8,128)S(1)}, f32[488,128]{1,0:T(8,128)S(1)}, u32[]{:S(2)}, u32[]{:S(2)}) collective-permute-start(f32[488,128]{1,0:T(8,128)S(1)} %get-tuple-element.22), channel_id=1, source_target_pairs={{0,12},{1,14},{2,13},{3,15},{4,8},{5,10},{6,9},{7,11},{8,4},{9,6},... | collective-permute-start | bytes 749576 | tf_op jit(solution)/shard_map/ppermute | solution.py:565
  27.5 6.0 %copy-start.13 = (f32[32,8]{0,1:T(8,128)S(1)}, f32[32,8]{0,1:T(8,128)}, u32[]{:S(2)}) copy-start(f32[32,8]{0,1:T(8,128)} %param.20) | copy-start | bytes 3076
  28.2 6.9 %collective-permute-start.8 = (f32[976,128]{1,0:T(8,128)S(1)}, f32[976,128]{1,0:T(8,128)S(1)}, u32[]{:S(2)}, u32[]{:S(2)}) collective-permute-start(f32[976,128]{1,0:T(8,128)S(1)} %get-tuple-element.24), channel_id=1, source_target_pairs={{0,1},{1,0},{2,3},{3,2},{4,5},{5,4},{6,7},{7,6},{8,9},{9,8},{10,11... | collective-permute-start | bytes 1499144 | tf_op jit(solution)/shard_map/ppermute | solution.py:580
  33.5 1.5 %copy-start.4 = (f32[2,2,64,128]{3,2,1,0:T(8,128)S(1)}, f32[2,2,64,128]{3,2,1,0:T(8,128)}, u32[]{:S(2)}) copy-start(f32[2,2,64,128]{3,2,1,0:T(8,128)} %constant.26.clone.refs_16_) | copy-start | bytes 393220
  33.5 1.5 %copy-start.5 = (bf16[256,256]{1,0:T(8,128)(2,1)S(1)}, bf16[256,256]{1,0:T(8,128)(2,1)}, u32[]{:S(2)}) copy-start(bf16[256,256]{1,0:T(8,128)(2,1)} %constant.23.clone.refs_13_) | copy-start | bytes 393220
  33.5 1.5 %copy-start.6 = (bf16[256,256]{1,0:T(8,128)(2,1)S(1)}, bf16[256,256]{1,0:T(8,128)(2,1)}, u32[]{:S(2)}) copy-start(bf16[256,256]{1,0:T(8,128)(2,1)} %constant.22.clone.refs_12_) | copy-start | bytes 393220
  33.5 1.5 %copy-start.7 = (bf16[256,256]{1,0:T(8,128)(2,1)S(1)}, bf16[256,256]{1,0:T(8,128)(2,1)}, u32[]{:S(2)}) copy-start(bf16[256,256]{1,0:T(8,128)(2,1)} %constant.21.clone.refs_11_) | copy-start | bytes 393220
  33.6 1.5 %copy-start.8 = (bf16[256,256]{1,0:T(8,128)(2,1)S(1)}, bf16[256,256]{1,0:T(8,128)(2,1)}, u32[]{:S(2)}) copy-start(bf16[256,256]{1,0:T(8,128)(2,1)} %constant.20.clone.refs_10_) | copy-start | bytes 393220
  33.6 1.5 %copy-start.9 = (bf16[2,128,128]{2,1,0:T(8,128)(2,1)S(1)}, bf16[2,128,128]{2,1,0:T(8,128)(2,1)}, u32[]{:S(2)}) copy-start(bf16[2,128,128]{2,1,0:T(8,128)(2,1)} %constant.25.clone.refs_15_) | copy-start | bytes 196612
  33.6 1.5 %copy-start.10 = (bf16[2,128,128]{2,1,0:T(8,128)(2,1)S(1)}, bf16[2,128,128]{2,1,0:T(8,128)(2,1)}, u32[]{:S(2)}) copy-start(bf16[2,128,128]{2,1,0:T(8,128)(2,1)} %constant.24.clone.refs_14_) | copy-start | bytes 196612
  33.6 1.5 %copy-start.11 = (bf16[2,128,128]{2,1,0:T(8,128)(2,1)S(1)}, bf16[2,128,128]{2,1,0:T(8,128)(2,1)}, u32[]{:S(2)}) copy-start(bf16[2,128,128]{2,1,0:T(8,128)(2,1)} %constant.19.clone.refs_9_) | copy-start | bytes 196612
  33.6 1.5 %copy-start.12 = (bf16[2,128,128]{2,1,0:T(8,128)(2,1)S(1)}, bf16[2,128,128]{2,1,0:T(8,128)(2,1)}, u32[]{:S(2)}) copy-start(bf16[2,128,128]{2,1,0:T(8,128)(2,1)} %constant.18.clone.refs_8_) | copy-start | bytes 196612
  33.6 1.4 %collective-permute-start.9 = (f32[32,8]{1,0:T(8,128)S(1)}, f32[32,8]{1,0:T(8,128)S(1)}, u32[]{:S(2)}, u32[]{:S(2)}) collective-permute-start(f32[32,8]{1,0:T(8,128)S(1)} %copy.19.refs_6_), channel_id=1, source_target_pairs={{0,1},{1,0},{2,3},{3,2},{4,5},{5,4},{6,7},{7,6},{8,9},{9,8},{10,11... | collective-permute-start | bytes 3080 | tf_op jit(solution)/shard_map/ppermute | solution.py:525
  38.7 1.7 %collective-permute-start.10 = (f32[512,128]{1,0:T(8,128)S(1)}, f32[512,128]{1,0:T(8,128)S(1)}, u32[]{:S(2)}, u32[]{:S(2)}) collective-permute-start(f32[512,128]{1,0:T(8,128)S(1)} %get-tuple-element.27), channel_id=1, source_target_pairs={{0,1},{1,0},{2,3},{3,2},{4,5},{5,4},{6,7},{7,6},{8,9},{9,8},{10,11... | collective-permute-start | bytes 786440 | tf_op jit(solution)/shard_map/ppermute | solution.py:599
  40.4 12.0 %collective-permute-start.11 = (f32[256,128]{1,0:T(8,128)S(1)}, f32[256,128]{1,0:T(8,128)S(1)}, u32[]{:S(2)}, u32[]{:S(2)}) collective-permute-start(f32[256,128]{1,0:T(8,128)S(1)} %get-tuple-element.28), channel_id=1, source_target_pairs={{0,0},{1,2},{2,4},{3,6},{4,8},{5,10},{6,12},{7,14},{8,1},{9,3},{10... | collective-permute-start | bytes 393224 | tf_op jit(solution)/shard_map/ppermute | solution.py:601
  41.1 11.3 %collective-permute-start.12 = (f32[256,128]{1,0:T(8,128)S(1)}, f32[256,128]{1,0:T(8,128)S(1)}, u32[]{:S(2)}, u32[]{:S(2)}) collective-permute-start(f32[256,128]{1,0:T(8,128)S(1)} %get-tuple-element.29), channel_id=1, source_target_pairs={{0,4},{1,6},{2,0},{3,2},{4,12},{5,14},{6,8},{7,10},{8,5},{9,7},{10... | collective-permute-start | bytes 393224 | tf_op jit(solution)/shard_map/ppermute | solution.py:601
  47.2 9.0 %collective-permute-start.13 = (f32[256,128]{1,0:T(8,128)S(1)}, f32[256,128]{1,0:T(8,128)S(1)}, u32[]{:S(2)}, u32[]{:S(2)}) collective-permute-start(f32[256,128]{1,0:T(8,128)S(1)} %get-tuple-element.30), channel_id=1, source_target_pairs={{0,8},{1,10},{2,12},{3,14},{4,0},{5,2},{6,4},{7,6},{8,9},{9,11},{1... | collective-permute-start | bytes 393224 | tf_op jit(solution)/shard_map/ppermute | solution.py:601
  49.8 12.4 %collective-permute-start.14 = (f32[256,128]{1,0:T(8,128)S(1)}, f32[256,128]{1,0:T(8,128)S(1)}, u32[]{:S(2)}, u32[]{:S(2)}) collective-permute-start(f32[256,128]{1,0:T(8,128)S(1)} %get-tuple-element.31), channel_id=1, source_target_pairs={{0,12},{1,14},{2,8},{3,10},{4,4},{5,6},{6,0},{7,2},{8,13},{9,15},{... | collective-permute-start | bytes 393224 | tf_op jit(solution)/shard_map/ppermute | solution.py:601
where the time goes:
time: 63.4 us; the launch traced here: 63.1 us
  waiting for transfers between devices  26.2 us (41%)
  starting transfers between devices  25.4 us (40%)
  Pallas kernels  7.61 us (12%)
  local copies, waits for them, and re-layouts  2.99 us (5%)
  between operations  0.88 us (1%)
    ppermute x4, waiting for transfers between devices, transposed_shards(): lax.ppermute(message, ('az', 'rg'), routes[at % half])  15.4 us
    ppermute x4, starting transfers between devices, transposed_shards(): lax.ppermute(message, ('az', 'rg'), route)  12 us
    ppermute x4, waiting for transfers between devices, transposed_shards(): lax.ppermute(message, ('az', 'rg'), route)  9.69 us
    pallas_call x7, Pallas kernels, kernel_call(): pl.pallas_call(body, out_shape=out_shape, in_specs=specs, out_specs=jax.t...  7.61 us
    ppermute x4, starting transfers between devices, transposed_shards(): lax.ppermute(message, ('az', 'rg'), routes[at % half])  5.99 us
    ppermute x1, starting transfers between devices, transposed_shards(): got = swap(give)  5.29 us
    unnamed x30, local copies, waits for them, and re-layouts  2.99 us
  transfers between devices with their start and end apart: 15, of which 6 were waited for; matrix products, arithmetic and copies ran while one was open for 1% of the time, Pallas kernels for 2%

commit v1 on v0

--- a/solution.py
+++ b/solution.py
@@ -251,40 +251,52 @@
             ]
 
 
-def spread_kernel(re_own, im_own, re_lines, im_lines):
-    spread_lines(re_lines, 0, re_own)
-    spread_lines(im_lines, 0, im_own)
-
-
-def pack_kernel(re_lines, im_lines, re_other, im_other, ref_own, ref_other, off_own, off_other, *refs):
-    messages, (re_all, im_all, ref_all) = refs[:-3], refs[-3:]
-    bins, samples = re_other.shape
-    part_rows = samples // FACTOR
-    place, side = lax.axis_index("az"), lax.axis_index("rg")
-    own_at, other_at = EDGE + side * bins, EDGE + (1 - side) * bins
-    zeros = jnp.zeros((EDGE * part_rows, FACTOR), jnp.float32)
-    for all_ref, own, other in ((re_all, re_lines, re_other), (im_all, im_lines, im_other)):
-        all_ref[: EDGE * part_rows, :] = zeros
-        all_ref[(EDGE + 2 * bins) * part_rows :, :] = zeros
-        all_ref[pl.ds(pl.multiple_of(own_at * part_rows, 8), bins * part_rows), :] = own[...]
-        spread_lines(all_ref, other_at, other)
+def spread_kernel(re_raw, im_raw, ref_own, lines, halo, held, sems):
+    bins = re_raw.shape[0]
+    side = lax.axis_index("rg")
+    copies = []
+    for part, raw in enumerate((re_raw, im_raw)):
+        for tile in range(bins // 8):
+            at = part * (bins // 8) + tile
+            copies.append(pltpu.make_async_copy(raw.at[pl.ds(tile * 8, 8)], held.at[at], sems.at[at]))
+            copies[-1].start()
     ref_rows = ref_own.shape[0]
     row = lax.broadcasted_iota(jnp.int32, (ref_rows, FACTOR), 0)
     column = lax.broadcasted_iota(jnp.int32, (ref_rows, FACTOR), 1)
     twice = (lax.rem(column, ref_rows) == row).astype(jnp.float32)
-    ref_all[:EDGE, :] = jnp.zeros((EDGE, FACTOR), jnp.float32)
-    ref_all[EDGE + 2 * bins :, :] = jnp.zeros((EDGE, FACTOR), jnp.float32)
-    for at, ref in ((own_at, ref_own), (other_at, ref_other)):
-        ref_all[pl.ds(pl.multiple_of(at, 16), bins), :] = lax.dot_general(
-            ref[...], twice, (((0,), (0,)), ((), ())), precision=PRECISE, preferred_element_type=jnp.float32
-        )
+    lines[2 * bins * PART :, :] = lax.dot_general(
+        ref_own[...], twice, (((0,), (0,)), ((), ())), precision=PRECISE, preferred_element_type=jnp.float32
+    )
+    for at, copy in enumerate(copies):
+        copy.wait()
+        spread_lines(lines, at * 8, held.at[at])
+    first = (1 - side) * (bins - EDGE)
+    for part in range(2):
+        rows = pl.ds(pl.multiple_of((part * bins + first) * PART, 8), EDGE * PART)
+        halo[part * EDGE * PART : (part + 1) * EDGE * PART, :] = lines[rows, :]
+    halo[2 * EDGE * PART :, :] = lines[pl.ds(pl.multiple_of(2 * bins * PART + first, 8), EDGE), :]
+
+
+def pack_kernel(lines, halo, offsets, *refs):
+    messages, (re_all, im_all, ref_all) = refs[:-3], refs[-3:]
+    bins = re_all.shape[0] // PART - 2 * EDGE
+    place, side = lax.axis_index("az"), lax.axis_index("rg")
+    halo_at, empty_at = (1 - side) * (EDGE + bins), side * (EDGE + bins)
+    for part, all_ref in enumerate((re_all, im_all, ref_all)):
+        size = PART if part < 2 else 1
+        edge = EDGE * size
+        all_ref[edge : edge + bins * size, :] = lines[part * bins * PART : part * bins * PART + bins * size, :]
+        halo_rows = slice(part * EDGE * PART, part * EDGE * PART + edge)
+        all_ref[pl.ds(pl.multiple_of(halo_at * size, 8), edge), :] = halo[halo_rows, :]
+        all_ref[pl.ds(pl.multiple_of(empty_at * size, 8), edge), :] = jnp.zeros((edge, FACTOR), jnp.float32)
     lane = lax.broadcasted_iota(jnp.int32, (1, FACTOR), 1)
     for at, message in enumerate(messages):
         step = at % (PLACES // 2)
         (first_bin, last_bin), _ = CHUNKS[at // (PLACES // 2)]
-        body = (last_bin - first_bin) * part_rows
-        start = window_start(((place >> 1) ^ step) * 2 + side, side, off_own, off_other) + EDGE
-        rows = pl.ds(pl.multiple_of((start + first_bin) * part_rows, 8), body)
+        body = (last_bin - first_bin) * PART
+        chip = side * (PLACES // 2) + ((place >> 1) ^ step)
+        start = window_start(chip, side, offsets, offsets) - side * bins + EDGE
+        rows = pl.ds(pl.multiple_of((start + first_bin) * PART, 8), body)
         message[:body, :] = re_all[rows, :]
         message[body : 2 * body, :] = im_all[rows, :]
         if first_bin == 0:
@@ -321,11 +333,11 @@
         owners, keep, give, keep_ref = refs
     else:
         keep, give = refs
-    sign = jnp.where(place >= PLACES // 2, -1.0, 1.0)
+    sign = jnp.where(((place >> 1) & 1) == 1, -1.0, 1.0)
     even = side == 0
     keep_near, keep_far = jnp.where(even, 1.0, sign), jnp.where(even, 1.0, -sign)
     give_near, give_far = jnp.where(even, sign, 1.0), jnp.where(even, -sign, 1.0)
-    middle = (place >> 1) & 1
+    middle = place & 1
     for step in range(2):
         near, far = chunks[step], chunks[step + 2]
         for line in range(2 * bins):
@@ -336,7 +348,7 @@
             give[write, :] = near_value * give_near + far_value * give_far
     if has_ref:
         for which in range(2):
-            step = (owners[which] >> 1) ^ (place >> 1)
+            step = (owners[which] >> 1) ^ (place & (PLACES // 2 - 1))
             for other in range(PLACES // 2):
 
                 @pl.when(step == other)
@@ -496,7 +508,7 @@
 SMEM = pl.BlockSpec(memory_space=pltpu.SMEM)
 
 
-def kernel_call(body, name, out_shape, operands, scratch=(), flops=0, count=10**6, limit=8):
+def kernel_call(body, name, out_shape, operands, scratch=(), limit=8):
     specs = [SMEM if operand.size <= 1024 else VMEM for operand in operands]
     return pl.pallas_call(
         body,
@@ -505,7 +517,7 @@
         out_specs=jax.tree.map(lambda _: VMEM, out_shape),
         scratch_shapes=[pltpu.VMEM(shape, jnp.float32) for shape in scratch],
         compiler_params=pltpu.CompilerParams(vmem_limit_bytes=limit * 1024 * 1024),
-        cost_estimate=pl.CostEstimate(flops=flops, bytes_accessed=count, transcendentals=0),
+        cost_estimate=pl.CostEstimate(flops=1, bytes_accessed=1, transcendentals=0),
         name=name,
     )(*operands)
 
@@ -520,35 +532,44 @@
     tables = [jnp.asarray(part) for part in matrices] + [jnp.asarray(twists)]
     swap = functools.partial(lax.ppermute, axis_name="rg", perm=[(0, 1), (1, 0)])
     half = PLACES // 2
-    ref_own = ref_blocks[0]
-    offsets_other = swap(offsets)
-    ref_other, re_other, im_other, taps_other = swap(ref_own), swap(raw_re), swap(raw_im), swap(taps)
-
-    lines = kernel_call(spread_kernel, "spread", [array(bins * PART, FACTOR)] * 2, [raw_re, raw_im], count=2 * 10**6)
+    lines, halo = pl.pallas_call(
+        spread_kernel,
+        out_shape=[array(2 * bins * PART + bins, FACTOR), array(2 * EDGE * PART + EDGE, FACTOR)],
+        in_specs=[pl.BlockSpec(memory_space=pl.ANY)] * 2 + [VMEM],
+        out_specs=[VMEM] * 2,
+        scratch_shapes=[
+            pltpu.VMEM((2 * bins // 8, 8, samples), jnp.float32),
+            pltpu.SemaphoreType.DMA((2 * bins // 8,)),
+        ],
+        compiler_params=pltpu.CompilerParams(vmem_limit_bytes=8 * 1024 * 1024),
+        cost_estimate=pl.CostEstimate(flops=1, bytes_accessed=1, transcendentals=0),
+        name="spread",
+    )(raw_re, raw_im, ref_blocks[0])
+    halo = swap(halo)
+    offsets_other, taps_other = swap(offsets), swap(taps)
+
     shapes = []
     for (first_bin, last_bin), _ in CHUNKS:
         ref_lines = REF_LINES if first_bin == 0 else 0
         shapes += [array(2 * (last_bin - first_bin) * PART + ref_lines, FACTOR)] * half
-    all_lines = (2 * bins + 2 * EDGE) * PART
+    all_bins = bins + 2 * EDGE
     messages = kernel_call(
         pack_kernel,
         "pack",
         shapes,
-        [*lines, re_other, im_other, ref_own, ref_other, offsets, offsets_other],
-        scratch=[(all_lines, FACTOR), (all_lines, FACTOR), (2 * bins + 2 * EDGE, FACTOR)],
-        count=4 * 10**6,
+        [lines, halo, offsets],
+        scratch=[(all_bins * PART, FACTOR), (all_bins * PART, FACTOR), (all_bins, FACTOR)],
     )
     phases = kernel_call(
         functools.partial(phase_kernel, 2 * bins),
         "phase",
         array(WINDOW, 2, HALF, FACTOR),
         [offsets, offsets_other],
-        flops=10**7,
     )
 
     routes = [
         [
-            (chip * 2 + core, (((chip >> 1) ^ step) * 2 + core) * 2 + (chip & 1))
+            (chip * 2 + core, (core * half + ((chip >> 1) ^ step)) * 2 + (chip & 1))
             for chip in range(PLACES)
             for core in range(2)
         ]
@@ -564,6 +585,9 @@
     ]
     arrived = [lax.ppermute(message, ("az", "rg"), routes[at % half]) for at, message in enumerate(messages)]
 
+    def send_back(sent):
+        return [lax.ppermute(message, ("az", "rg"), route) for message, route in zip(sent, routes_back)]
+
     results = []
     refs, earlier = None, []
     for chunk, ((first_bin, last_bin), (first_out, last_out)) in enumerate(CHUNKS):
@@ -572,6 +596,11 @@
         size = 2 * count * 2 * PART
         shapes = [array(size, FACTOR), array(size + (2 * REF_LINES if has_ref else 0), FACTOR)]
         operands = arrived[chunk * half : (chunk + 1) * half]
+        if chunk == 0:
+            *operands, phases = lax.optimization_barrier((*operands, phases))
+        else:
+            *operands, _ = lax.optimization_barrier((*operands, sent[0]))
+            results += send_back(sent)
         if has_ref:
             shapes.append(array(2, REF_LINES, FACTOR))
             operands = operands + [owners]
@@ -586,9 +615,7 @@
             [array(outs * HALF, FACTOR), array(outs * HALF, FACTOR), array(count, 2, HALF, FACTOR)],
             [keep, got, *refs, owners, phases, taps, taps_other, *tables, *earlier],
             scratch=[(outs * HALF, 2 * FACTOR), (2, 2 * REF_LINES, FACTOR)],
-            flops=10**9,
-            count=4 * 10**6,
-            limit=16,
+                limit=16,
         )
         keep, give, spectra = pieces
         earlier = [spectra]
@@ -598,7 +625,7 @@
             [array(2 * outs * PART, FACTOR)] * half,
             [keep, swap(give)],
         )
-        results += [lax.ppermute(message, ("az", "rg"), route) for message, route in zip(sent, routes_back)]
+    results += send_back(sent)
     return kernel_call(
         place_kernel, "place", [array(bins, samples)] * 2, results, scratch=[(bins * PART, FACTOR)] * 2
     )

time: 63.4 us -> 62.9 us (level)
  waiting for transfers between devices: 26.2 us -> 19.7 us
  starting transfers between devices: 25.4 us -> 30.7 us
  Pallas kernels: 7.61 us -> 8.4 us
    ppermute x9 -> x7, starting transfers between devices: 13.6 us -> 19 us  [the longest x4 15.6 us: send_back(): lax.ppermute(message, ('az', 'rg'), route)]
    ppermute x4, starting transfers between devices: 5.99 us -> 10.8 us  [transposed_shards(): lax.ppermute(message, ('az', 'rg'), routes[at % half])]
    ppermute x1, starting transfers between devices: 5.29 us -> 0.53 us  [transposed_shards(): got = swap(give)]
    ppermute x4, waiting for transfers between devices: 15.4 us -> 10.7 us  [transposed_shards(): lax.ppermute(message, ('az', 'rg'), routes[at % half])]
    ppermute x9 -> x7, waiting for transfers between devices: 9.71 us -> 7.83 us  [the longest x4 4.44 us: send_back(): lax.ppermute(message, ('az', 'rg'), route)]
    pallas_call x0 -> x1, Pallas kernels: none -> 1.1 us  [transposed_shards(): pl.pallas_call(spread_kernel, out_shape=[array(2 * bins * PART + bins, FA...]
    pallas_call x7 -> x6, Pallas kernels: 7.61 us -> 7.3 us  [kernel_call(): pl.pallas_call(body, out_shape=out_shape, in_specs=specs, out_specs=jax.t...]
  transfers between devices with their start and end apart: 15 -> 13, of which waited for: 6 -> 6; matrix products, arithmetic and copies ran while one was open for 1% -> 0% of each run, Pallas kernels for 2% -> 2%
where the time goes in v1:
time: 62.9 us; the launch traced here: 62.6 us
  starting transfers between devices  30.7 us (49%)
  waiting for transfers between devices  19.7 us (31%)
  Pallas kernels  8.4 us (13%)
  local copies, waits for them, and re-layouts  2.85 us (5%)
  between operations  0.88 us (1%)
    ppermute x4, starting transfers between devices, send_back(): lax.ppermute(message, ('az', 'rg'), route)  15.6 us
    ppermute x4, starting transfers between devices, transposed_shards(): lax.ppermute(message, ('az', 'rg'), routes[at % half])  10.8 us
    ppermute x4, waiting for transfers between devices, transposed_shards(): lax.ppermute(message, ('az', 'rg'), routes[at % half])  10.7 us
    pallas_call x6, Pallas kernels, kernel_call(): pl.pallas_call(body, out_shape=out_shape, in_specs=specs, out_specs=jax.t...  7.3 us
    ppermute x4, waiting for transfers between devices, send_back(): lax.ppermute(message, ('az', 'rg'), route)  4.44 us
    unnamed x30, local copies, waits for them, and re-layouts  2.85 us
    ppermute x2, starting transfers between devices, transposed_shards(): offsets_other, taps_other = (swap(offsets), swap(taps))  2.84 us
    ppermute x2, waiting for transfers between devices, transposed_shards(): offsets_other, taps_other = (swap(offsets), swap(taps))  2.22 us
  transfers between devices with their start and end apart: 13, of which 6 were waited for; matrix products, arithmetic and copies ran while one was open for 0% of the time, Pallas kernels for 2%

profile of v1, /device:TPU:0, one launch (start us, length us, event | category | flops | bytes accessed | tf_op | source)
XLA Modules:
  0.0 62.6 jit_solution(3543002455421737445)
XLA Ops:
  0.6 0.8 %copy.17 = f32[1,64,32]{2,1,0:T(8,128)S(1)} copy(f32[1,64,32]{1,2,0:T(8,128)} %param.17) | data formatting | bytes 16384 | tf_op args[2]
  1.4 0.9 %copy-done = f32[32,2048]{1,0:T(8,128)S(1)} copy-done((f32[32,2048]{1,0:T(8,128)S(1)}, f32[32,2048]{1,0:T(8,128)}, u32[]{:S(2)}) %copy-start) | copy-done | bytes 262168
  2.4 0.9 %copy-done.1 = f32[32,2048]{1,0:T(8,128)S(1)} copy-done((f32[32,2048]{1,0:T(8,128)S(1)}, f32[32,2048]{1,0:T(8,128)}, u32[]{:S(2)}) %copy-start.1) | copy-done | bytes 262168
  3.3 1.1 %spread.1 = (f32[1056,128]{1,0:T(8,128)S(1)}, f32[528,128]{1,0:T(8,128)S(1)}) custom-call(f32[32,2048]{1,0:T(8,128)S(1)} %copy-done, f32[32,2048]{1,0:T(8,128)S(1)} %copy-done.1, f32[64,32]{1,0:T(8,128)S(1)} %bitcast.1), custom_call_target="tpu_custom_call" | custom-call | flops 1 | bytes 1 | tf_op jit(solution)/shard_map/spread/pallas_call | solution.py:535
  4.5 0.5 collective-permute-start
  5.0 1.2 %collective-permute-done.halo = f32[528,128]{1,0:T(8,128)S(1)} collective-permute-done((f32[528,128]{1,0:T(8,128)S(1)}, f32[528,128]{1,0:T(8,128)S(1)}, u32[]{:S(2)}, u32[]{:S(2)}) %collective-permute-start) | collective-permute-done | bytes 270368 | tf_op jit(solution)/shard_map/ppermute | solution.py:548
  6.2 0.7 %pack.1 = (f32[488,128]{1,0:T(8,128)S(1)}, f32[488,128]{1,0:T(8,128)S(1)}, f32[488,128]{1,0:T(8,128)S(1)}, f32[488,128]{1,0:T(8,128)S(1)}) custom-call(f32[1056,128]{1,0:T(8,128)S(1)} %get-tuple-element.22.lines, f32[528,128]{1,0:T(8,128)S(1)} %collective-permute-done.halo, s32[2]{0:T(128)S(1)} %copy-done.12), custom_call_target="tpu_custom_call" | custom-call | flops 1 | bytes 1 | tf_op jit(solution)/shard_map/pack/pallas_call | solution.py:513
  6.8 0.7 %collective-permute-start.1 = (f32[488,128]{1,0:T(8,128)S(1)}, f32[488,128]{1,0:T(8,128)S(1)}, u32[]{:S(2)}, u32[]{:S(2)}) collective-permute-start(f32[488,128]{1,0:T(8,128)S(1)} %get-tuple-element.24), channel_id=1, source_target_pairs={{0,0},{1,8},{2,1},{3,9},{4,2},{5,10},{6,3},{7,11},{8,4},{9,12},{10... | collective-permute-start | bytes 749576 | tf_op jit(solution)/shard_map/ppermute | solution.py:586
  7.5 4.2 %collective-permute-start.2 = (f32[488,128]{1,0:T(8,128)S(1)}, f32[488,128]{1,0:T(8,128)S(1)}, u32[]{:S(2)}, u32[]{:S(2)}) collective-permute-start(f32[488,128]{1,0:T(8,128)S(1)} %get-tuple-element.25), channel_id=1, source_target_pairs={{0,2},{1,10},{2,3},{3,11},{4,0},{5,8},{6,1},{7,9},{8,6},{9,14},{10... | collective-permute-start | bytes 749576 | tf_op jit(solution)/shard_map/ppermute | solution.py:586
  11.7 1.5 %collective-permute-start.3 = (f32[488,128]{1,0:T(8,128)S(1)}, f32[488,128]{1,0:T(8,128)S(1)}, u32[]{:S(2)}, u32[]{:S(2)}) collective-permute-start(f32[488,128]{1,0:T(8,128)S(1)} %get-tuple-element.26), channel_id=1, source_target_pairs={{0,4},{1,12},{2,5},{3,13},{4,6},{5,14},{6,7},{7,15},{8,0},{9,8},{1... | collective-permute-start | bytes 749576 | tf_op jit(solution)/shard_map/ppermute | solution.py:586
  13.2 4.5 %collective-permute-start.4 = (f32[488,128]{1,0:T(8,128)S(1)}, f32[488,128]{1,0:T(8,128)S(1)}, u32[]{:S(2)}, u32[]{:S(2)}) collective-permute-start(f32[488,128]{1,0:T(8,128)S(1)} %get-tuple-element.27), channel_id=1, source_target_pairs={{0,6},{1,14},{2,7},{3,15},{4,4},{5,12},{6,5},{7,13},{8,2},{9,10},{... | collective-permute-start | bytes 749576 | tf_op jit(solution)/shard_map/ppermute | solution.py:586
  17.7 2.8 %collective-permute-start.5 = (s32[2]{0:T(128)S(1)}, s32[2]{0:T(128)S(1)}, u32[]{:S(2)}, u32[]{:S(2)}) collective-permute-start(s32[2]{0:T(128)S(1)} %copy-done.12), channel_id=1, source_target_pairs={{0,1},{1,0},{2,3},{3,2},{4,5},{5,4},{6,7},{7,6},{8,9},{9,8},{10,11... | collective-permute-start | bytes 32 | tf_op jit(solution)/shard_map/ppermute | solution.py:549
  20.5 0.8 %collective-permute-done.5.off_other = s32[2]{0:T(128)S(1)} collective-permute-done((s32[2]{0:T(128)S(1)}, s32[2]{0:T(128)S(1)}, u32[]{:S(2)}, u32[]{:S(2)}) %collective-permute-start.5) | collective-permute-done | bytes 40 | tf_op jit(solution)/shard_map/ppermute | solution.py:549
  21.3 1.3 %phase.1.refs_5_ = f32[15,2,64,128]{3,2,1,0:T(8,128)S(1)} custom-call(s32[2]{0:T(128)S(1)} %copy-done.12, s32[2]{0:T(128)S(1)} %collective-permute-done.5.off_other), custom_call_target="tpu_custom_call" | custom-call | flops 1 | bytes 1 | tf_op jit(solution)/shard_map/phase/pallas_call | solution.py:513
  22.6 0.0 copy-start.2
  22.6 0.0 copy-start.3
  22.7 10.7 %collective-permute-done.3.refs_2_ = f32[488,128]{1,0:T(8,128)S(1)} collective-permute-done((f32[488,128]{1,0:T(8,128)S(1)}, f32[488,128]{1,0:T(8,128)S(1)}, u32[]{:S(2)}, u32[]{:S(2)}) %collective-permute-start.3) | collective-permute-done | bytes 249888 | tf_op jit(solution)/shard_map/ppermute | solution.py:586
  33.5 0.7 %parity.1 = (f32[960,128]{1,0:T(8,128)S(1)}, f32[976,128]{1,0:T(8,128)S(1)}, f32[2,8,128]{2,1,0:T(8,128)S(1)}) custom-call(f32[488,128]{1,0:T(8,128)S(1)} %collective-permute-done.1.refs_0_, f32[488,128]{1,0:T(8,128)S(1)} %collective-permute-done.2.refs_1_, f32[488,128]{1,0:T(8,128)S(1)} %collective-permute-done.3.refs_2_, ...), custom_call_target="tpu_custom_call" | custom-call | flops 1 | bytes 1 | tf_op jit(solution)/shard_map/parity/pallas_call | solution.py:513
  34.2 0.5 collective-permute-start.6
  34.7 0.1 copy.19.refs_6_
  34.8 0.0 collective-permute-start.7
  34.9 1.4 %collective-permute-done.7.refs_7_ = f32[32,8]{1,0:T(8,128)S(1)} collective-permute-done((f32[32,8]{1,0:T(8,128)S(1)}, f32[32,8]{1,0:T(8,128)S(1)}, u32[]{:S(2)}, u32[]{:S(2)}) %collective-permute-start.7) | collective-permute-done | bytes 1056 | tf_op jit(solution)/shard_map/ppermute | solution.py:549
  36.3 3.6 %band.1 = (f32[512,128]{1,0:T(8,128)S(1)}, f32[512,128]{1,0:T(8,128)S(1)}, f32[15,2,64,128]{3,2,1,0:T(8,128)}) custom-call(f32[960,128]{1,0:T(8,128)S(1)} %get-tuple-element.32.refs_0_, f32[976,128]{1,0:T(8,128)S(1)} %collective-permute-done.6.refs_1_.refs_3_, f32[2,8,128]{2,1,0:T(8,128)S(1)} %get-tuple-element.34.refs_2_, ...), custom_call_target="tpu_custom_call" | custom-call | flops 1 | bytes 1 | tf_op jit(solution)/shard_map/band/pallas_call | solution.py:513
  39.9 0.4 collective-permute-start.8
  40.3 1.2 %collective-permute-done.8.got = f32[512,128]{1,0:T(8,128)S(1)} collective-permute-done((f32[512,128]{1,0:T(8,128)S(1)}, f32[512,128]{1,0:T(8,128)S(1)}, u32[]{:S(2)}, u32[]{:S(2)}) %collective-permute-start.8) | collective-permute-done | bytes 262176 | tf_op jit(solution)/shard_map/ppermute | solution.py:626
  41.5 0.1 join.1
  41.5 0.7 %collective-permute-start.9 = (f32[256,128]{1,0:T(8,128)S(1)}, f32[256,128]{1,0:T(8,128)S(1)}, u32[]{:S(2)}, u32[]{:S(2)}) collective-permute-start(f32[256,128]{1,0:T(8,128)S(1)} %get-tuple-element.38), channel_id=1, source_target_pairs={{0,0},{1,2},{2,4},{3,6},{4,8},{5,10},{6,12},{7,14},{8,1},{9,3},{10... | collective-permute-start | bytes 393224 | tf_op jit(solution)/shard_map/ppermute | solution.py:589
  42.2 5.0 %collective-permute-start.10 = (f32[256,128]{1,0:T(8,128)S(1)}, f32[256,128]{1,0:T(8,128)S(1)}, u32[]{:S(2)}, u32[]{:S(2)}) collective-permute-start(f32[256,128]{1,0:T(8,128)S(1)} %get-tuple-element.39), channel_id=1, source_target_pairs={{0,4},{1,6},{2,0},{3,2},{4,12},{5,14},{6,8},{7,10},{8,5},{9,7},{10... | collective-permute-start | bytes 393224 | tf_op jit(solution)/shard_map/ppermute | solution.py:589
  47.2 1.4 %collective-permute-start.11 = (f32[256,128]{1,0:T(8,128)S(1)}, f32[256,128]{1,0:T(8,128)S(1)}, u32[]{:S(2)}, u32[]{:S(2)}) collective-permute-start(f32[256,128]{1,0:T(8,128)S(1)} %get-tuple-element.40), channel_id=1, source_target_pairs={{0,8},{1,10},{2,12},{3,14},{4,0},{5,2},{6,4},{7,6},{8,9},{9,11},{1... | collective-permute-start | bytes 393224 | tf_op jit(solution)/shard_map/ppermute | solution.py:589
  48.7 8.5 %collective-permute-start.12 = (f32[256,128]{1,0:T(8,128)S(1)}, f32[256,128]{1,0:T(8,128)S(1)}, u32[]{:S(2)}, u32[]{:S(2)}) collective-permute-start(f32[256,128]{1,0:T(8,128)S(1)} %get-tuple-element.41), channel_id=1, source_target_pairs={{0,12},{1,14},{2,8},{3,10},{4,4},{5,6},{6,0},{7,2},{8,13},{9,15},{... | collective-permute-start | bytes 393224 | tf_op jit(solution)/shard_map/ppermute | solution.py:589
  57.2 4.4 %collective-permute-done.12.refs_3_ = f32[256,128]{1,0:T(8,128)S(1)} collective-permute-done((f32[256,128]{1,0:T(8,128)S(1)}, f32[256,128]{1,0:T(8,128)S(1)}, u32[]{:S(2)}, u32[]{:S(2)}) %collective-permute-start.12) | collective-permute-done | bytes 131104 | tf_op jit(solution)/shard_map/ppermute | solution.py:589
  61.7 0.9 %place.1 = (f32[32,2048]{1,0:T(8,128)}, f32[32,2048]{1,0:T(8,128)}) custom-call(f32[256,128]{1,0:T(8,128)S(1)} %collective-permute-done.9.refs_0_, f32[256,128]{1,0:T(8,128)S(1)} %collective-permute-done.10.refs_1_, f32[256,128]{1,0:T(8,128)S(1)} %collective-permute-done.11.refs_2_, f32[256,128]{1,0:T(8,128)S(1)} %collective-permute-done.12.refs_3_), custom_call_target="tpu_custom_call" | custom-call | flops 1 | bytes 1 | tf_op jit(solution)/shard_map/place/pallas_call | solution.py:513
  (31 shorter events, 0.1 us)
Async XLA Ops:
  1.4 1.0 %copy-start = (f32[32,2048]{1,0:T(8,128)S(1)}, f32[32,2048]{1,0:T(8,128)}, u32[]{:S(2)}) copy-start(f32[32,2048]{1,0:T(8,128)} %re_raw.1) | copy-start | bytes 786436
  2.4 0.9 %copy-start.1 = (f32[32,2048]{1,0:T(8,128)S(1)}, f32[32,2048]{1,0:T(8,128)}, u32[]{:S(2)}) copy-start(f32[32,2048]{1,0:T(8,128)} %im_raw.1) | copy-start | bytes 786436
  4.4 1.7 %copy-start.12 = (s32[2]{0:T(128)S(1)}, s32[2]{0:T(128)}, u32[]{:S(2)}) copy-start(s32[2]{0:T(128)} %off_own.1) | copy-start | bytes 28
  4.5 1.7 %collective-permute-start = (f32[528,128]{1,0:T(8,128)S(1)}, f32[528,128]{1,0:T(8,128)S(1)}, u32[]{:S(2)}, u32[]{:S(2)}) collective-permute-start(f32[528,128]{1,0:T(8,128)S(1)} %get-tuple-element.23), channel_id=1, source_target_pairs={{0,1},{1,0},{2,3},{3,2},{4,5},{5,4},{6,7},{7,6},{8,9},{9,8},{10,11... | collective-permute-start | bytes 811016 | tf_op jit(solution)/shard_map/ppermute | solution.py:548
  6.8 15.8 %collective-permute-start.1 = (f32[488,128]{1,0:T(8,128)S(1)}, f32[488,128]{1,0:T(8,128)S(1)}, u32[]{:S(2)}, u32[]{:S(2)}) collective-permute-start(f32[488,128]{1,0:T(8,128)S(1)} %get-tuple-element.24), channel_id=1, source_target_pairs={{0,0},{1,8},{2,1},{3,9},{4,2},{5,10},{6,3},{7,11},{8,4},{9,12},{10... | collective-permute-start | bytes 749576 | tf_op jit(solution)/shard_map/ppermute | solution.py:586
  7.5 15.2 %collective-permute-start.2 = (f32[488,128]{1,0:T(8,128)S(1)}, f32[488,128]{1,0:T(8,128)S(1)}, u32[]{:S(2)}, u32[]{:S(2)}) collective-permute-start(f32[488,128]{1,0:T(8,128)S(1)} %get-tuple-element.25), channel_id=1, source_target_pairs={{0,2},{1,10},{2,3},{3,11},{4,0},{5,8},{6,1},{7,9},{8,6},{9,14},{10... | collective-permute-start | bytes 749576 | tf_op jit(solution)/shard_map/ppermute | solution.py:586
  11.7 21.7 %collective-permute-start.3 = (f32[488,128]{1,0:T(8,128)S(1)}, f32[488,128]{1,0:T(8,128)S(1)}, u32[]{:S(2)}, u32[]{:S(2)}) collective-permute-start(f32[488,128]{1,0:T(8,128)S(1)} %get-tuple-element.26), channel_id=1, source_target_pairs={{0,4},{1,12},{2,5},{3,13},{4,6},{5,14},{6,7},{7,15},{8,0},{9,8},{1... | collective-permute-start | bytes 749576 | tf_op jit(solution)/shard_map/ppermute | solution.py:586
  13.2 20.2 %copy-start.11 = (s32[2]{0:T(128)S(1)}, s32[2]{0:T(128)}, u32[]{:S(2)}) copy-start(s32[2]{0:T(128)} %refs_4_.3) | copy-start | bytes 28
  13.2 20.2 %collective-permute-start.4 = (f32[488,128]{1,0:T(8,128)S(1)}, f32[488,128]{1,0:T(8,128)S(1)}, u32[]{:S(2)}, u32[]{:S(2)}) collective-permute-start(f32[488,128]{1,0:T(8,128)S(1)} %get-tuple-element.27), channel_id=1, source_target_pairs={{0,6},{1,14},{2,7},{3,15},{4,4},{5,12},{6,5},{7,13},{8,2},{9,10},{... | collective-permute-start | bytes 749576 | tf_op jit(solution)/shard_map/ppermute | solution.py:586
  17.7 3.6 %collective-permute-start.5 = (s32[2]{0:T(128)S(1)}, s32[2]{0:T(128)S(1)}, u32[]{:S(2)}, u32[]{:S(2)}) collective-permute-start(s32[2]{0:T(128)S(1)} %copy-done.12), channel_id=1, source_target_pairs={{0,1},{1,0},{2,3},{3,2},{4,5},{5,4},{6,7},{7,6},{8,9},{9,8},{10,11... | collective-permute-start | bytes 32 | tf_op jit(solution)/shard_map/ppermute | solution.py:549
  22.6 13.6 %copy-start.2 = (f32[2,2,64,128]{3,2,1,0:T(8,128)S(1)}, f32[2,2,64,128]{3,2,1,0:T(8,128)}, u32[]{:S(2)}) copy-start(f32[2,2,64,128]{3,2,1,0:T(8,128)} %constant.26.clone.refs_16_) | copy-start | bytes 393220
  22.6 13.6 %copy-start.3 = (bf16[256,256]{1,0:T(8,128)(2,1)S(1)}, bf16[256,256]{1,0:T(8,128)(2,1)}, u32[]{:S(2)}) copy-start(bf16[256,256]{1,0:T(8,128)(2,1)} %constant.23.clone.refs_13_) | copy-start | bytes 393220
  22.6 13.6 %copy-start.4 = (bf16[256,256]{1,0:T(8,128)(2,1)S(1)}, bf16[256,256]{1,0:T(8,128)(2,1)}, u32[]{:S(2)}) copy-start(bf16[256,256]{1,0:T(8,128)(2,1)} %constant.22.clone.refs_12_) | copy-start | bytes 393220
  22.6 13.6 %copy-start.5 = (bf16[256,256]{1,0:T(8,128)(2,1)S(1)}, bf16[256,256]{1,0:T(8,128)(2,1)}, u32[]{:S(2)}) copy-start(bf16[256,256]{1,0:T(8,128)(2,1)} %constant.21.clone.refs_11_) | copy-start | bytes 393220
  22.7 13.6 %copy-start.6 = (bf16[256,256]{1,0:T(8,128)(2,1)S(1)}, bf16[256,256]{1,0:T(8,128)(2,1)}, u32[]{:S(2)}) copy-start(bf16[256,256]{1,0:T(8,128)(2,1)} %constant.20.clone.refs_10_) | copy-start | bytes 393220
  33.4 1.3 %copy-start.13 = (f32[32,8]{0,1:T(8,128)S(1)}, f32[32,8]{0,1:T(8,128)}, u32[]{:S(2)}) copy-start(f32[32,8]{0,1:T(8,128)} %param.20) | copy-start | bytes 3076
  33.4 2.8 %copy-start.7 = (bf16[2,128,128]{2,1,0:T(8,128)(2,1)S(1)}, bf16[2,128,128]{2,1,0:T(8,128)(2,1)}, u32[]{:S(2)}) copy-start(bf16[2,128,128]{2,1,0:T(8,128)(2,1)} %constant.25.clone.refs_15_) | copy-start | bytes 196612
  33.5 2.8 %copy-start.8 = (bf16[2,128,128]{2,1,0:T(8,128)(2,1)S(1)}, bf16[2,128,128]{2,1,0:T(8,128)(2,1)}, u32[]{:S(2)}) copy-start(bf16[2,128,128]{2,1,0:T(8,128)(2,1)} %constant.24.clone.refs_14_) | copy-start | bytes 196612
  33.5 2.8 %copy-start.9 = (bf16[2,128,128]{2,1,0:T(8,128)(2,1)S(1)}, bf16[2,128,128]{2,1,0:T(8,128)(2,1)}, u32[]{:S(2)}) copy-start(bf16[2,128,128]{2,1,0:T(8,128)(2,1)} %constant.19.clone.refs_9_) | copy-start | bytes 196612
  33.5 2.8 %copy-start.10 = (bf16[2,128,128]{2,1,0:T(8,128)(2,1)S(1)}, bf16[2,128,128]{2,1,0:T(8,128)(2,1)}, u32[]{:S(2)}) copy-start(bf16[2,128,128]{2,1,0:T(8,128)(2,1)} %constant.18.clone.refs_8_) | copy-start | bytes 196612
  34.2 2.1 %collective-permute-start.6 = (f32[976,128]{1,0:T(8,128)S(1)}, f32[976,128]{1,0:T(8,128)S(1)}, u32[]{:S(2)}, u32[]{:S(2)}) collective-permute-start(f32[976,128]{1,0:T(8,128)S(1)} %get-tuple-element.33), channel_id=1, source_target_pairs={{0,1},{1,0},{2,3},{3,2},{4,5},{5,4},{6,7},{7,6},{8,9},{9,8},{10,11... | collective-permute-start | bytes 1499144 | tf_op jit(solution)/shard_map/ppermute | solution.py:609
  34.8 1.4 %collective-permute-start.7 = (f32[32,8]{1,0:T(8,128)S(1)}, f32[32,8]{1,0:T(8,128)S(1)}, u32[]{:S(2)}, u32[]{:S(2)}) collective-permute-start(f32[32,8]{1,0:T(8,128)S(1)} %copy.19.refs_6_), channel_id=1, source_target_pairs={{0,1},{1,0},{2,3},{3,2},{4,5},{5,4},{6,7},{7,6},{8,9},{9,8},{10,11... | collective-permute-start | bytes 3080 | tf_op jit(solution)/shard_map/ppermute | solution.py:549
  39.9 1.5 %collective-permute-start.8 = (f32[512,128]{1,0:T(8,128)S(1)}, f32[512,128]{1,0:T(8,128)S(1)}, u32[]{:S(2)}, u32[]{:S(2)}) collective-permute-start(f32[512,128]{1,0:T(8,128)S(1)} %get-tuple-element.37), channel_id=1, source_target_pairs={{0,1},{1,0},{2,3},{3,2},{4,5},{5,4},{6,7},{7,6},{8,9},{9,8},{10,11... | collective-permute-start | bytes 786440 | tf_op jit(solution)/shard_map/ppermute | solution.py:626
  41.5 15.6 %collective-permute-start.9 = (f32[256,128]{1,0:T(8,128)S(1)}, f32[256,128]{1,0:T(8,128)S(1)}, u32[]{:S(2)}, u32[]{:S(2)}) collective-permute-start(f32[256,128]{1,0:T(8,128)S(1)} %get-tuple-element.38), channel_id=1, source_target_pairs={{0,0},{1,2},{2,4},{3,6},{4,8},{5,10},{6,12},{7,14},{8,1},{9,3},{10... | collective-permute-start | bytes 393224 | tf_op jit(solution)/shard_map/ppermute | solution.py:589
  42.2 15.0 %collective-permute-start.10 = (f32[256,128]{1,0:T(8,128)S(1)}, f32[256,128]{1,0:T(8,128)S(1)}, u32[]{:S(2)}, u32[]{:S(2)}) collective-permute-start(f32[256,128]{1,0:T(8,128)S(1)} %get-tuple-element.39), channel_id=1, source_target_pairs={{0,4},{1,6},{2,0},{3,2},{4,12},{5,14},{6,8},{7,10},{8,5},{9,7},{10... | collective-permute-start | bytes 393224 | tf_op jit(solution)/shard_map/ppermute | solution.py:589
  47.2 10.0 %collective-permute-start.11 = (f32[256,128]{1,0:T(8,128)S(1)}, f32[256,128]{1,0:T(8,128)S(1)}, u32[]{:S(2)}, u32[]{:S(2)}) collective-permute-start(f32[256,128]{1,0:T(8,128)S(1)} %get-tuple-element.40), channel_id=1, source_target_pairs={{0,8},{1,10},{2,12},{3,14},{4,0},{5,2},{6,4},{7,6},{8,9},{9,11},{1... | collective-permute-start | bytes 393224 | tf_op jit(solution)/shard_map/ppermute | solution.py:589
  48.7 13.0 %collective-permute-start.12 = (f32[256,128]{1,0:T(8,128)S(1)}, f32[256,128]{1,0:T(8,128)S(1)}, u32[]{:S(2)}, u32[]{:S(2)}) collective-permute-start(f32[256,128]{1,0:T(8,128)S(1)} %get-tuple-element.41), channel_id=1, source_target_pairs={{0,12},{1,14},{2,8},{3,10},{4,4},{5,6},{6,0},{7,2},{8,13},{9,15},{... | collective-permute-start | bytes 393224 | tf_op jit(solution)/shard_map/ppermute | solution.py:589

commit v2 on v0

--- a/solution.py
+++ b/solution.py
@@ -170,6 +170,7 @@
 WINDOW = OUT_BINS + TAPS - 1
 REF_LINES = 8
 EDGE = 16
+STEPS = (2, 3, 1, 0)
 CHUNKS = (((0, WINDOW), (0, OUT_BINS)),)
 
 
@@ -252,8 +253,10 @@
 
 
 def spread_kernel(re_own, im_own, re_lines, im_lines):
-    spread_lines(re_lines, 0, re_own)
-    spread_lines(im_lines, 0, im_own)
+    at = pl.program_id(0) * 8
+    for target, source in ((re_lines, re_own), (im_lines, im_own)):
+        for row in range(PART):
+            target[pl.ds(at * PART + row, 8, stride=PART), :] = source[:, row * FACTOR : (row + 1) * FACTOR]
 
 
 def pack_kernel(re_lines, im_lines, re_other, im_other, ref_own, ref_other, off_own, off_other, *refs):
@@ -315,7 +318,8 @@
 
 
 def parity_kernel(bins, has_ref, *refs):
-    chunks, refs = refs[: PLACES // 2], refs[PLACES // 2 :]
+    chunks = dict(zip(STEPS, refs))
+    refs = refs[PLACES // 2 :]
     place, side = lax.axis_index("az"), lax.axis_index("rg")
     if has_ref:
         owners, keep, give, keep_ref = refs
@@ -524,7 +528,15 @@
     offsets_other = swap(offsets)
     ref_other, re_other, im_other, taps_other = swap(ref_own), swap(raw_re), swap(raw_im), swap(taps)
 
-    lines = kernel_call(spread_kernel, "spread", [array(bins * PART, FACTOR)] * 2, [raw_re, raw_im], count=2 * 10**6)
+    lines = pl.pallas_call(
+        spread_kernel,
+        out_shape=[array(bins * PART, FACTOR)] * 2,
+        grid=(bins // 8,),
+        in_specs=[pl.BlockSpec((8, samples), lambda i: (i, 0))] * 2,
+        out_specs=[pl.BlockSpec((bins * PART, FACTOR), lambda i: (0, 0))] * 2,
+        cost_estimate=pl.CostEstimate(flops=1, bytes_accessed=2 * 10**6, transcendentals=0),
+        name="spread",
+    )(raw_re, raw_im)
     shapes = []
     for (first_bin, last_bin), _ in CHUNKS:
         ref_lines = REF_LINES if first_bin == 0 else 0
@@ -562,7 +574,11 @@
         ]
         for step in range(half)
     ]
-    arrived = [lax.ppermute(message, ("az", "rg"), routes[at % half]) for at, message in enumerate(messages)]
+    arrived = [
+        lax.ppermute(messages[chunk * half + step], ("az", "rg"), routes[step])
+        for chunk in range(len(CHUNKS))
+        for step in STEPS
+    ]
 
     results = []
     refs, earlier = None, []
@@ -572,6 +588,8 @@
         size = 2 * count * 2 * PART
         shapes = [array(size, FACTOR), array(size + (2 * REF_LINES if has_ref else 0), FACTOR)]
         operands = arrived[chunk * half : (chunk + 1) * half]
+        if chunk == 0:
+            *operands, phases, taps_other = lax.optimization_barrier((*operands, phases, taps_other))
         if has_ref:
             shapes.append(array(2, REF_LINES, FACTOR))
             operands = operands + [owners]

time: 63.4 us -> 64.6 us (1.019)
  Pallas kernels: 7.61 us -> 10.2 us
  waiting for transfers between devices: 26.2 us -> 24.5 us
    ppermute x1, starting transfers between devices: 5.29 us -> 1.03 us  [transposed_shards(): got = swap(give)]
    ppermute x4, waiting for transfers between devices: 15.4 us -> 11.3 us  [transposed_shards(): lax.ppermute(messages[chunk * half + step], ('az', 'rg'), routes[step])]
    ppermute x1, starting transfers between devices: 0.09 us -> 3.47 us  [transposed_shards(): swap(taps)]
    pallas_call x0 -> x1, Pallas kernels: none -> 2.69 us  [transposed_shards(): pl.pallas_call(spread_kernel, out_shape=[array(bins * PART, FACTOR)] * 2,...]
    ppermute x1, waiting for transfers between devices: 0.01 us -> 1.5 us  [transposed_shards(): got = swap(give)]
    ppermute x4, starting transfers between devices: 12 us -> 13.3 us  [transposed_shards(): lax.ppermute(message, ('az', 'rg'), route)]
    ppermute x4, waiting for transfers between devices: 9.69 us -> 10.5 us  [transposed_shards(): lax.ppermute(message, ('az', 'rg'), route)]
    pallas_call x7 -> x6, Pallas kernels: 7.61 us -> 7.47 us  [kernel_call(): pl.pallas_call(body, out_shape=out_shape, in_specs=specs, out_specs=jax.t...]
  transfers between devices with their start and end apart: 15 -> 15, of which waited for: 6 -> 6; matrix products, arithmetic and copies ran while one was open for 1% -> 1% of each run, Pallas kernels for 2% -> 6%
where the time goes in v2:
time: 64.6 us; the launch traced here: 64.2 us
  starting transfers between devices  25.7 us (40%)
  waiting for transfers between devices  24.5 us (38%)
  Pallas kernels  10.2 us (16%)
  local copies, waits for them, and re-layouts  3 us (5%)
  between operations  0.88 us (1%)
    ppermute x4, starting transfers between devices, transposed_shards(): lax.ppermute(message, ('az', 'rg'), route)  13.3 us
    ppermute x4, waiting for transfers between devices, transposed_shards(): lax.ppermute(messages[chunk * half + step], ('az', 'rg'), routes[step])  11.3 us
    ppermute x4, waiting for transfers between devices, transposed_shards(): lax.ppermute(message, ('az', 'rg'), route)  10.5 us
    pallas_call x6, Pallas kernels, kernel_call(): pl.pallas_call(body, out_shape=out_shape, in_specs=specs, out_specs=jax.t...  7.47 us
    ppermute x4, starting transfers between devices, transposed_shards(): lax.ppermute(messages[chunk * half + step], ('az', 'rg'), routes[step])  5.97 us
    ppermute x1, starting transfers between devices, transposed_shards(): swap(taps)  3.47 us
    unnamed x30, local copies, waits for them, and re-layouts  3 us
    pallas_call x1, Pallas kernels, transposed_shards(): pl.pallas_call(spread_kernel, out_shape=[array(bins * PART, FACTOR)] * 2,...  2.69 us
  transfers between devices with their start and end apart: 15, of which 6 were waited for; matrix products, arithmetic and copies ran while one was open for 1% of the time, Pallas kernels for 6%

profile of v2, /device:TPU:0, one launch (start us, length us, event | category | flops | bytes accessed | tf_op | source)
XLA Modules:
  0.0 64.2 jit_solution(14790919321946207666)
XLA Ops:
  0.6 0.5 collective-permute-start
  1.1 0.1 collective-permute-start.1
  1.2 0.8 %copy.17 = f32[1,64,32]{2,1,0:T(8,128)S(1)} copy(f32[1,64,32]{1,2,0:T(8,128)} %param.17) | data formatting | bytes 16384 | tf_op args[2]
  2.0 0.5 collective-permute-start.2
  2.5 0.2 copy-done.2
  2.7 0.4 collective-permute-start.3
  3.1 2.7 %spread.1 = (f32[512,128]{1,0:T(8,128)}, f32[512,128]{1,0:T(8,128)}) custom-call(f32[32,2048]{1,0:T(8,128)} %re_own.1, f32[32,2048]{1,0:T(8,128)} %im_own.1), custom_call_target="tpu_custom_call" | custom-call | flops 1 | bytes 2000000 | tf_op jit(solution)/shard_map/spread/pallas_call | solution.py:531
  5.8 0.9 %copy-done = f32[512,128]{1,0:T(8,128)S(1)} copy-done((f32[512,128]{1,0:T(8,128)S(1)}, f32[512,128]{1,0:T(8,128)}, u32[]{:S(2)}) %copy-start) | copy-done | bytes 262168
  6.8 0.9 %copy-done.1 = f32[512,128]{1,0:T(8,128)S(1)} copy-done((f32[512,128]{1,0:T(8,128)S(1)}, f32[512,128]{1,0:T(8,128)}, u32[]{:S(2)}) %copy-start.1) | copy-done | bytes 262168
  7.7 0.9 %pack.1 = (f32[488,128]{1,0:T(8,128)S(1)}, f32[488,128]{1,0:T(8,128)S(1)}, f32[488,128]{1,0:T(8,128)S(1)}, f32[488,128]{1,0:T(8,128)S(1)}) custom-call(f32[512,128]{1,0:T(8,128)S(1)} %copy-done, f32[512,128]{1,0:T(8,128)S(1)} %copy-done.1, f32[32,2048]{1,0:T(8,128)S(1)} %collective-permute-done.re_other, f32[32,2048]{1,0:T(8,128)S(1)} %collective-permute-done.1.im_other, ...), custom_call_target="tpu_custom_call" | custom-call | bytes 4000000 | tf_op jit(solution)/shard_map/pack/pallas_call | solution.py:505
  8.6 3.7 %collective-permute-start.4 = (f32[488,128]{1,0:T(8,128)S(1)}, f32[488,128]{1,0:T(8,128)S(1)}, u32[]{:S(2)}, u32[]{:S(2)}) collective-permute-start(f32[488,128]{1,0:T(8,128)S(1)} %get-tuple-element.25), channel_id=1, source_target_pairs={{0,8},{1,10},{2,9},{3,11},{4,12},{5,14},{6,13},{7,15},{8,0},{9,2},... | collective-permute-start | bytes 749576 | tf_op jit(solution)/shard_map/ppermute | solution.py:578
  12.4 1.3 %collective-permute-start.5 = (f32[488,128]{1,0:T(8,128)S(1)}, f32[488,128]{1,0:T(8,128)S(1)}, u32[]{:S(2)}, u32[]{:S(2)}) collective-permute-start(f32[488,128]{1,0:T(8,128)S(1)} %get-tuple-element.26), channel_id=1, source_target_pairs={{0,12},{1,14},{2,13},{3,15},{4,8},{5,10},{6,9},{7,11},{8,4},{9,6},... | collective-permute-start | bytes 749576 | tf_op jit(solution)/shard_map/ppermute | solution.py:578
  13.7 0.2 collective-permute-start.6
  14.0 0.7 %collective-permute-start.7 = (f32[488,128]{1,0:T(8,128)S(1)}, f32[488,128]{1,0:T(8,128)S(1)}, u32[]{:S(2)}, u32[]{:S(2)}) collective-permute-start(f32[488,128]{1,0:T(8,128)S(1)} %get-tuple-element.28), channel_id=1, source_target_pairs={{0,0},{1,2},{2,1},{3,3},{4,4},{5,6},{6,5},{7,7},{8,8},{9,10},{10,9... | collective-permute-start | bytes 749576 | tf_op jit(solution)/shard_map/ppermute | solution.py:578
  14.6 0.1 copy.18.refs_6_
  14.7 3.5 %collective-permute-start.8 = (f32[32,8]{1,0:T(8,128)S(1)}, f32[32,8]{1,0:T(8,128)S(1)}, u32[]{:S(2)}, u32[]{:S(2)}) collective-permute-start(f32[32,8]{1,0:T(8,128)S(1)} %copy.18.refs_6_), channel_id=1, source_target_pairs={{0,1},{1,0},{2,3},{3,2},{4,5},{5,4},{6,7},{7,6},{8,9},{9,8},{10,11... | collective-permute-start | bytes 3080 | tf_op jit(solution)/shard_map/ppermute | solution.py:529
  18.2 1.3 %phase.1.refs_5_ = f32[15,2,64,128]{3,2,1,0:T(8,128)S(1)} custom-call(s32[2]{0:T(128)S(1)} %copy-done.2, s32[2]{0:T(128)S(1)} %collective-permute-done.3.off_other), custom_call_target="tpu_custom_call" | custom-call | flops 10000000 | bytes 1000000 | tf_op jit(solution)/shard_map/phase/pallas_call | solution.py:505
  19.6 9.8 %collective-permute-done.4.refs_0_ = f32[488,128]{1,0:T(8,128)S(1)} collective-permute-done((f32[488,128]{1,0:T(8,128)S(1)}, f32[488,128]{1,0:T(8,128)S(1)}, u32[]{:S(2)}, u32[]{:S(2)}) %collective-permute-start.4) | collective-permute-done | bytes 249888 | tf_op jit(solution)/shard_map/ppermute | solution.py:578
  29.4 1.5 %collective-permute-done.6.refs_2_ = f32[488,128]{1,0:T(8,128)S(1)} collective-permute-done((f32[488,128]{1,0:T(8,128)S(1)}, f32[488,128]{1,0:T(8,128)S(1)}, u32[]{:S(2)}, u32[]{:S(2)}) %collective-permute-start.6) | collective-permute-done | bytes 249888 | tf_op jit(solution)/shard_map/ppermute | solution.py:578
  30.9 0.7 %parity.1 = (f32[960,128]{1,0:T(8,128)S(1)}, f32[976,128]{1,0:T(8,128)S(1)}, f32[2,8,128]{2,1,0:T(8,128)S(1)}) custom-call(f32[488,128]{1,0:T(8,128)S(1)} %collective-permute-done.4.refs_0_, f32[488,128]{1,0:T(8,128)S(1)} %collective-permute-done.5.refs_1_, f32[488,128]{1,0:T(8,128)S(1)} %collective-permute-done.6.refs_2_, ...), custom_call_target="tpu_custom_call" | custom-call | bytes 1000000 | tf_op jit(solution)/shard_map/parity/pallas_call | solution.py:505
  31.7 1.0 %collective-permute-start.9 = (f32[976,128]{1,0:T(8,128)S(1)}, f32[976,128]{1,0:T(8,128)S(1)}, u32[]{:S(2)}, u32[]{:S(2)}) collective-permute-start(f32[976,128]{1,0:T(8,128)S(1)} %get-tuple-element.34), channel_id=1, source_target_pairs={{0,1},{1,0},{2,3},{3,2},{4,5},{5,4},{6,7},{7,6},{8,9},{9,8},{10,11... | collective-permute-start | bytes 1499144 | tf_op jit(solution)/shard_map/ppermute | solution.py:598
  32.7 1.5 %collective-permute-done.9.refs_1_.refs_3_ = f32[976,128]{1,0:T(8,128)S(1)} collective-permute-done((f32[976,128]{1,0:T(8,128)S(1)}, f32[976,128]{1,0:T(8,128)S(1)}, u32[]{:S(2)}, u32[]{:S(2)}) %collective-permute-start.9) | collective-permute-done | bytes 499744 | tf_op jit(solution)/shard_map/ppermute | solution.py:598
  34.3 3.6 %band.1 = (f32[512,128]{1,0:T(8,128)S(1)}, f32[512,128]{1,0:T(8,128)S(1)}, f32[15,2,64,128]{3,2,1,0:T(8,128)}) custom-call(f32[960,128]{1,0:T(8,128)S(1)} %get-tuple-element.33.refs_0_, f32[976,128]{1,0:T(8,128)S(1)} %collective-permute-done.9.refs_1_.refs_3_, f32[2,8,128]{2,1,0:T(8,128)S(1)} %get-tuple-element.35.refs_2_, ...), custom_call_target="tpu_custom_call" | custom-call | flops 1000000000 | bytes 4000000 | tf_op jit(solution)/shard_map/band/pallas_call | solution.py:505
  37.8 0.4 collective-permute-start.10
  38.2 1.2 %collective-permute-done.10.got = f32[512,128]{1,0:T(8,128)S(1)} collective-permute-done((f32[512,128]{1,0:T(8,128)S(1)}, f32[512,128]{1,0:T(8,128)S(1)}, u32[]{:S(2)}, u32[]{:S(2)}) %collective-permute-start.10) | collective-permute-done | bytes 262176 | tf_op jit(solution)/shard_map/ppermute | solution.py:617
  39.5 0.7 %collective-permute-start.11 = (f32[256,128]{1,0:T(8,128)S(1)}, f32[256,128]{1,0:T(8,128)S(1)}, u32[]{:S(2)}, u32[]{:S(2)}) collective-permute-start(f32[256,128]{1,0:T(8,128)S(1)} %get-tuple-element.40), channel_id=1, source_target_pairs={{0,0},{1,2},{2,4},{3,6},{4,8},{5,10},{6,12},{7,14},{8,1},{9,3},{10... | collective-permute-start | bytes 393224 | tf_op jit(solution)/shard_map/ppermute | solution.py:619
  40.1 8.6 %collective-permute-start.12 = (f32[256,128]{1,0:T(8,128)S(1)}, f32[256,128]{1,0:T(8,128)S(1)}, u32[]{:S(2)}, u32[]{:S(2)}) collective-permute-start(f32[256,128]{1,0:T(8,128)S(1)} %get-tuple-element.41), channel_id=1, source_target_pairs={{0,4},{1,6},{2,0},{3,2},{4,12},{5,14},{6,8},{7,10},{8,5},{9,7},{10... | collective-permute-start | bytes 393224 | tf_op jit(solution)/shard_map/ppermute | solution.py:619
  48.7 2.1 %collective-permute-start.13 = (f32[256,128]{1,0:T(8,128)S(1)}, f32[256,128]{1,0:T(8,128)S(1)}, u32[]{:S(2)}, u32[]{:S(2)}) collective-permute-start(f32[256,128]{1,0:T(8,128)S(1)} %get-tuple-element.42), channel_id=1, source_target_pairs={{0,8},{1,10},{2,12},{3,14},{4,0},{5,2},{6,4},{7,6},{8,9},{9,11},{1... | collective-permute-start | bytes 393224 | tf_op jit(solution)/shard_map/ppermute | solution.py:619
  50.8 1.9 %collective-permute-start.14 = (f32[256,128]{1,0:T(8,128)S(1)}, f32[256,128]{1,0:T(8,128)S(1)}, u32[]{:S(2)}, u32[]{:S(2)}) collective-permute-start(f32[256,128]{1,0:T(8,128)S(1)} %get-tuple-element.43), channel_id=1, source_target_pairs={{0,12},{1,14},{2,8},{3,10},{4,4},{5,6},{6,0},{7,2},{8,13},{9,15},{... | collective-permute-start | bytes 393224 | tf_op jit(solution)/shard_map/ppermute | solution.py:619
  52.8 4.8 %collective-permute-done.13.refs_2_ = f32[256,128]{1,0:T(8,128)S(1)} collective-permute-done((f32[256,128]{1,0:T(8,128)S(1)}, f32[256,128]{1,0:T(8,128)S(1)}, u32[]{:S(2)}, u32[]{:S(2)}) %collective-permute-start.13) | collective-permute-done | bytes 131104 | tf_op jit(solution)/shard_map/ppermute | solution.py:619
  57.6 5.6 %collective-permute-done.14.refs_3_ = f32[256,128]{1,0:T(8,128)S(1)} collective-permute-done((f32[256,128]{1,0:T(8,128)S(1)}, f32[256,128]{1,0:T(8,128)S(1)}, u32[]{:S(2)}, u32[]{:S(2)}) %collective-permute-start.14) | collective-permute-done | bytes 131104 | tf_op jit(solution)/shard_map/ppermute | solution.py:619
  63.3 0.9 %place.1 = (f32[32,2048]{1,0:T(8,128)}, f32[32,2048]{1,0:T(8,128)}) custom-call(f32[256,128]{1,0:T(8,128)S(1)} %collective-permute-done.11.refs_0_, f32[256,128]{1,0:T(8,128)S(1)} %collective-permute-done.12.refs_1_, f32[256,128]{1,0:T(8,128)S(1)} %collective-permute-done.13.refs_2_, f32[256,128]{1,0:T(8,128)S(1)} %collective-permute-done.14.refs_3_), custom_call_target="tpu_custom_call" | custom-call | bytes 1000000 | tf_op jit(solution)/shard_map/place/pallas_call | solution.py:505
  (35 shorter events, 0.2 us)
Async XLA Ops:
  0.6 5.2 %collective-permute-start = (f32[32,2048]{1,0:T(8,128)}, f32[32,2048]{1,0:T(8,128)S(1)}, u32[]{:S(2)}, u32[]{:S(2)}) collective-permute-start(f32[32,2048]{1,0:T(8,128)} %re_own.1), channel_id=1, source_target_pairs={{0,1},{1,0},{2,3},{3,2},{4,5},{5,4},{6,7},{7,6},{8,9},{9,8},{10,11... | collective-permute-start | bytes 786440 | tf_op jit(solution)/shard_map/ppermute | solution.py:529
  1.1 4.7 %collective-permute-start.1 = (f32[32,2048]{1,0:T(8,128)}, f32[32,2048]{1,0:T(8,128)S(1)}, u32[]{:S(2)}, u32[]{:S(2)}) collective-permute-start(f32[32,2048]{1,0:T(8,128)} %im_own.1), channel_id=1, source_target_pairs={{0,1},{1,0},{2,3},{3,2},{4,5},{5,4},{6,7},{7,6},{8,9},{9,8},{10,11... | collective-permute-start | bytes 786440 | tf_op jit(solution)/shard_map/ppermute | solution.py:529
  2.0 0.7 %copy-start.2 = (s32[2]{0:T(128)S(1)}, s32[2]{0:T(128)}, u32[]{:S(2)}) copy-start(s32[2]{0:T(128)} %off_own.3) | copy-start | bytes 28
  2.0 3.8 %collective-permute-start.2 = (f32[64,32]{1,0:T(8,128)S(1)}, f32[64,32]{1,0:T(8,128)S(1)}, u32[]{:S(2)}, u32[]{:S(2)}) collective-permute-start(f32[64,32]{1,0:T(8,128)S(1)} %bitcast.1), channel_id=1, source_target_pairs={{0,1},{1,0},{2,3},{3,2},{4,5},{5,4},{6,7},{7,6},{8,9},{9,8},{10,11... | collective-permute-start | bytes 24584 | tf_op jit(solution)/shard_map/ppermute | solution.py:529
  2.7 3.1 %collective-permute-start.3 = (s32[2]{0:T(128)S(1)}, s32[2]{0:T(128)S(1)}, u32[]{:S(2)}, u32[]{:S(2)}) collective-permute-start(s32[2]{0:T(128)S(1)} %copy-done.2), channel_id=1, source_target_pairs={{0,1},{1,0},{2,3},{3,2},{4,5},{5,4},{6,7},{7,6},{8,9},{9,8},{10,11... | collective-permute-start | bytes 32 | tf_op jit(solution)/shard_map/ppermute | solution.py:528
  5.8 1.0 %copy-start = (f32[512,128]{1,0:T(8,128)S(1)}, f32[512,128]{1,0:T(8,128)}, u32[]{:S(2)}) copy-start(f32[512,128]{1,0:T(8,128)} %get-tuple-element.23.re_lines) | copy-start | bytes 786436
  6.8 0.9 %copy-start.1 = (f32[512,128]{1,0:T(8,128)S(1)}, f32[512,128]{1,0:T(8,128)}, u32[]{:S(2)}) copy-start(f32[512,128]{1,0:T(8,128)} %get-tuple-element.24.im_lines) | copy-start | bytes 786436
  8.6 6.0 %copy-start.13 = (f32[32,8]{0,1:T(8,128)S(1)}, f32[32,8]{0,1:T(8,128)}, u32[]{:S(2)}) copy-start(f32[32,8]{0,1:T(8,128)} %param.20) | copy-start | bytes 3076
  8.6 20.8 %collective-permute-start.4 = (f32[488,128]{1,0:T(8,128)S(1)}, f32[488,128]{1,0:T(8,128)S(1)}, u32[]{:S(2)}, u32[]{:S(2)}) collective-permute-start(f32[488,128]{1,0:T(8,128)S(1)} %get-tuple-element.25), channel_id=1, source_target_pairs={{0,8},{1,10},{2,9},{3,11},{4,12},{5,14},{6,13},{7,15},{8,0},{9,2},... | collective-permute-start | bytes 749576 | tf_op jit(solution)/shard_map/ppermute | solution.py:578
  12.4 17.1 %collective-permute-start.5 = (f32[488,128]{1,0:T(8,128)S(1)}, f32[488,128]{1,0:T(8,128)S(1)}, u32[]{:S(2)}, u32[]{:S(2)}) collective-permute-start(f32[488,128]{1,0:T(8,128)S(1)} %get-tuple-element.26), channel_id=1, source_target_pairs={{0,12},{1,14},{2,13},{3,15},{4,8},{5,10},{6,9},{7,11},{8,4},{9,6},... | collective-permute-start | bytes 749576 | tf_op jit(solution)/shard_map/ppermute | solution.py:578
  13.7 17.2 %collective-permute-start.6 = (f32[488,128]{1,0:T(8,128)S(1)}, f32[488,128]{1,0:T(8,128)S(1)}, u32[]{:S(2)}, u32[]{:S(2)}) collective-permute-start(f32[488,128]{1,0:T(8,128)S(1)} %get-tuple-element.27), channel_id=1, source_target_pairs={{0,4},{1,6},{2,5},{3,7},{4,0},{5,2},{6,1},{7,3},{8,12},{9,14},{10,... | collective-permute-start | bytes 749576 | tf_op jit(solution)/shard_map/ppermute | solution.py:578
  14.0 17.0 %collective-permute-start.7 = (f32[488,128]{1,0:T(8,128)S(1)}, f32[488,128]{1,0:T(8,128)S(1)}, u32[]{:S(2)}, u32[]{:S(2)}) collective-permute-start(f32[488,128]{1,0:T(8,128)S(1)} %get-tuple-element.28), channel_id=1, source_target_pairs={{0,0},{1,2},{2,1},{3,3},{4,4},{5,6},{6,5},{7,7},{8,8},{9,10},{10,9... | collective-permute-start | bytes 749576 | tf_op jit(solution)/shard_map/ppermute | solution.py:578
  14.7 16.2 %copy-start.3 = (s32[2]{0:T(128)S(1)}, s32[2]{0:T(128)}, u32[]{:S(2)}) copy-start(s32[2]{0:T(128)} %refs_4_.3) | copy-start | bytes 28
  14.7 4.9 %collective-permute-start.8 = (f32[32,8]{1,0:T(8,128)S(1)}, f32[32,8]{1,0:T(8,128)S(1)}, u32[]{:S(2)}, u32[]{:S(2)}) collective-permute-start(f32[32,8]{1,0:T(8,128)S(1)} %copy.18.refs_6_), channel_id=1, source_target_pairs={{0,1},{1,0},{2,3},{3,2},{4,5},{5,4},{6,7},{7,6},{8,9},{9,8},{10,11... | collective-permute-start | bytes 3080 | tf_op jit(solution)/shard_map/ppermute | solution.py:529
  19.5 14.7 %copy-start.4 = (f32[2,2,64,128]{3,2,1,0:T(8,128)S(1)}, f32[2,2,64,128]{3,2,1,0:T(8,128)}, u32[]{:S(2)}) copy-start(f32[2,2,64,128]{3,2,1,0:T(8,128)} %constant.26.clone.refs_16_) | copy-start | bytes 393220
  19.5 14.7 %copy-start.5 = (bf16[256,256]{1,0:T(8,128)(2,1)S(1)}, bf16[256,256]{1,0:T(8,128)(2,1)}, u32[]{:S(2)}) copy-start(bf16[256,256]{1,0:T(8,128)(2,1)} %constant.23.clone.refs_13_) | copy-start | bytes 393220
  19.5 14.7 %copy-start.6 = (bf16[256,256]{1,0:T(8,128)(2,1)S(1)}, bf16[256,256]{1,0:T(8,128)(2,1)}, u32[]{:S(2)}) copy-start(bf16[256,256]{1,0:T(8,128)(2,1)} %constant.22.clone.refs_12_) | copy-start | bytes 393220
  19.5 14.7 %copy-start.7 = (bf16[256,256]{1,0:T(8,128)(2,1)S(1)}, bf16[256,256]{1,0:T(8,128)(2,1)}, u32[]{:S(2)}) copy-start(bf16[256,256]{1,0:T(8,128)(2,1)} %constant.21.clone.refs_11_) | copy-start | bytes 393220
  19.5 14.7 %copy-start.8 = (bf16[256,256]{1,0:T(8,128)(2,1)S(1)}, bf16[256,256]{1,0:T(8,128)(2,1)}, u32[]{:S(2)}) copy-start(bf16[256,256]{1,0:T(8,128)(2,1)} %constant.20.clone.refs_10_) | copy-start | bytes 393220
  19.6 14.7 %copy-start.9 = (bf16[2,128,128]{2,1,0:T(8,128)(2,1)S(1)}, bf16[2,128,128]{2,1,0:T(8,128)(2,1)}, u32[]{:S(2)}) copy-start(bf16[2,128,128]{2,1,0:T(8,128)(2,1)} %constant.25.clone.refs_15_) | copy-start | bytes 196612
  19.6 14.7 %copy-start.10 = (bf16[2,128,128]{2,1,0:T(8,128)(2,1)S(1)}, bf16[2,128,128]{2,1,0:T(8,128)(2,1)}, u32[]{:S(2)}) copy-start(bf16[2,128,128]{2,1,0:T(8,128)(2,1)} %constant.24.clone.refs_14_) | copy-start | bytes 196612
  19.6 14.7 %copy-start.11 = (bf16[2,128,128]{2,1,0:T(8,128)(2,1)S(1)}, bf16[2,128,128]{2,1,0:T(8,128)(2,1)}, u32[]{:S(2)}) copy-start(bf16[2,128,128]{2,1,0:T(8,128)(2,1)} %constant.19.clone.refs_9_) | copy-start | bytes 196612
  19.6 14.6 %copy-start.12 = (bf16[2,128,128]{2,1,0:T(8,128)(2,1)S(1)}, bf16[2,128,128]{2,1,0:T(8,128)(2,1)}, u32[]{:S(2)}) copy-start(bf16[2,128,128]{2,1,0:T(8,128)(2,1)} %constant.18.clone.refs_8_) | copy-start | bytes 196612
  31.7 2.5 %collective-permute-start.9 = (f32[976,128]{1,0:T(8,128)S(1)}, f32[976,128]{1,0:T(8,128)S(1)}, u32[]{:S(2)}, u32[]{:S(2)}) collective-permute-start(f32[976,128]{1,0:T(8,128)S(1)} %get-tuple-element.34), channel_id=1, source_target_pairs={{0,1},{1,0},{2,3},{3,2},{4,5},{5,4},{6,7},{7,6},{8,9},{9,8},{10,11... | collective-permute-start | bytes 1499144 | tf_op jit(solution)/shard_map/ppermute | solution.py:598
  37.8 1.5 %collective-permute-start.10 = (f32[512,128]{1,0:T(8,128)S(1)}, f32[512,128]{1,0:T(8,128)S(1)}, u32[]{:S(2)}, u32[]{:S(2)}) collective-permute-start(f32[512,128]{1,0:T(8,128)S(1)} %get-tuple-element.39), channel_id=1, source_target_pairs={{0,1},{1,0},{2,3},{3,2},{4,5},{5,4},{6,7},{7,6},{8,9},{9,8},{10,11... | collective-permute-start | bytes 786440 | tf_op jit(solution)/shard_map/ppermute | solution.py:617
  39.5 13.3 %collective-permute-start.11 = (f32[256,128]{1,0:T(8,128)S(1)}, f32[256,128]{1,0:T(8,128)S(1)}, u32[]{:S(2)}, u32[]{:S(2)}) collective-permute-start(f32[256,128]{1,0:T(8,128)S(1)} %get-tuple-element.40), channel_id=1, source_target_pairs={{0,0},{1,2},{2,4},{3,6},{4,8},{5,10},{6,12},{7,14},{8,1},{9,3},{10... | collective-permute-start | bytes 393224 | tf_op jit(solution)/shard_map/ppermute | solution.py:619
  40.1 12.6 %collective-permute-start.12 = (f32[256,128]{1,0:T(8,128)S(1)}, f32[256,128]{1,0:T(8,128)S(1)}, u32[]{:S(2)}, u32[]{:S(2)}) collective-permute-start(f32[256,128]{1,0:T(8,128)S(1)} %get-tuple-element.41), channel_id=1, source_target_pairs={{0,4},{1,6},{2,0},{3,2},{4,12},{5,14},{6,8},{7,10},{8,5},{9,7},{10... | collective-permute-start | bytes 393224 | tf_op jit(solution)/shard_map/ppermute | solution.py:619
  48.7 8.9 %collective-permute-start.13 = (f32[256,128]{1,0:T(8,128)S(1)}, f32[256,128]{1,0:T(8,128)S(1)}, u32[]{:S(2)}, u32[]{:S(2)}) collective-permute-start(f32[256,128]{1,0:T(8,128)S(1)} %get-tuple-element.42), channel_id=1, source_target_pairs={{0,8},{1,10},{2,12},{3,14},{4,0},{5,2},{6,4},{7,6},{8,9},{9,11},{1... | collective-permute-start | bytes 393224 | tf_op jit(solution)/shard_map/ppermute | solution.py:619
  50.8 12.4 %collective-permute-start.14 = (f32[256,128]{1,0:T(8,128)S(1)}, f32[256,128]{1,0:T(8,128)S(1)}, u32[]{:S(2)}, u32[]{:S(2)}) collective-permute-start(f32[256,128]{1,0:T(8,128)S(1)} %get-tuple-element.43), channel_id=1, source_target_pairs={{0,12},{1,14},{2,8},{3,10},{4,4},{5,6},{6,0},{7,2},{8,13},{9,15},{... | collective-permute-start | bytes 393224 | tf_op jit(solution)/shard_map/ppermute | solution.py:619

commit v3 on v2

--- a/solution.py
+++ b/solution.py
@@ -174,34 +174,35 @@
 CHUNKS = (((0, WINDOW), (0, OUT_BINS)),)
 
 
-def split_bf16(value):
+def split_bf16(value, axis):
     high = value.astype(jnp.bfloat16)
     low = (value - high.astype(jnp.float32)).astype(jnp.bfloat16)
-    return high, low
-
-
-def dot_split(left, right):
-    left_high, left_low = left
-    right_high, right_low = right
-    dot = functools.partial(jnp.dot, preferred_element_type=jnp.float32)
-    return dot(left_high, right_high) + (dot(left_high, right_low) + dot(left_low, right_high))
-
-
-def both_bf16(matrix):
+    return jnp.concatenate([high, low, high], axis=axis)
+
+
+def dot(left, right):
+    return jnp.dot(left, right, preferred_element_type=jnp.float32)
+
+
+def both_bf16(matrix, axis):
     high = matrix.astype(jnp.bfloat16)
-    return high, (matrix - high.astype(np.float64)).astype(jnp.bfloat16)
+    low = (matrix - high.astype(np.float64)).astype(jnp.bfloat16)
+    return np.concatenate([high, high, low], axis=axis)
 
 
 def dft_constants():
     counter = np.arange(FACTOR)
     kappa = np.arange(HALF)
-    first, last, twists = [], [], []
+    near, far, last, twists = [], [], [], []
     for side in range(2):
         order = [(middle, low, line) for low in (side, 1 - side) for middle in range(2) for line in range(PART)]
         mine = np.array([(2 * middle + low) * PART + line for middle, low, line in order])
         angle = 2 * np.pi * (np.outer(2 * kappa + side, mine) % FACTOR) / FACTOR
         cosine, sine = np.cos(angle), np.sin(angle)
-        first.append(np.block([[cosine, sine], [-sine, cosine]]))
+        whole = np.block([[cosine, sine], [-sine, cosine]])
+        quarters = np.split(whole, 4, axis=1)
+        near.append(np.concatenate(quarters[0::2], axis=1))
+        far.append(np.concatenate(quarters[1::2], axis=1))
         back_re, back_im = np.block([cosine.T, -sine.T]), np.block([sine.T, cosine.T])
         own, other = slice(0, HALF // 2), slice(HALF // 2, HALF)
         last.append(np.concatenate([back_re[own], back_im[own], back_re[other], back_im[other]]))
@@ -211,8 +212,14 @@
     cosine, sine = np.cos(angle), np.sin(angle)
     there = np.block([[cosine, -sine], [sine, cosine]])
     back = np.block([[cosine, sine], [-sine, cosine]])
-    matrices = [both_bf16(matrix) for matrix in (np.stack(first), there, back, np.stack(last))]
-    return [part for pair in matrices for part in pair], np.stack(twists).astype(np.float32)
+    matrices = [
+        both_bf16(np.stack(near), 2),
+        both_bf16(np.stack(far), 2),
+        both_bf16(there, 0),
+        both_bf16(back, 0),
+        both_bf16(np.stack(last), 2),
+    ]
+    return matrices, np.stack(twists).astype(np.float32)
 
 
 def cos_sin_quarters(quarters):
@@ -250,13 +257,6 @@
             target[pl.ds((base + tile) * part_rows + row, 8, stride=part_rows), :] = source[
                 tile : tile + 8, row * FACTOR : (row + 1) * FACTOR
             ]
-
-
-def spread_kernel(re_own, im_own, re_lines, im_lines):
-    at = pl.program_id(0) * 8
-    for target, source in ((re_lines, re_own), (im_lines, im_own)):
-        for row in range(PART):
-            target[pl.ds(at * PART + row, 8, stride=PART), :] = source[:, row * FACTOR : (row + 1) * FACTOR]
 
 
 def pack_kernel(re_lines, im_lines, re_other, im_other, ref_own, ref_other, off_own, off_other, *refs):
@@ -271,16 +271,10 @@
         all_ref[(EDGE + 2 * bins) * part_rows :, :] = zeros
         all_ref[pl.ds(pl.multiple_of(own_at * part_rows, 8), bins * part_rows), :] = own[...]
         spread_lines(all_ref, other_at, other)
-    ref_rows = ref_own.shape[0]
-    row = lax.broadcasted_iota(jnp.int32, (ref_rows, FACTOR), 0)
-    column = lax.broadcasted_iota(jnp.int32, (ref_rows, FACTOR), 1)
-    twice = (lax.rem(column, ref_rows) == row).astype(jnp.float32)
     ref_all[:EDGE, :] = jnp.zeros((EDGE, FACTOR), jnp.float32)
     ref_all[EDGE + 2 * bins :, :] = jnp.zeros((EDGE, FACTOR), jnp.float32)
     for at, ref in ((own_at, ref_own), (other_at, ref_other)):
-        ref_all[pl.ds(pl.multiple_of(at, 16), bins), :] = lax.dot_general(
-            ref[...], twice, (((0,), (0,)), ((), ())), precision=PRECISE, preferred_element_type=jnp.float32
-        )
+        ref_all[pl.ds(pl.multiple_of(at, 16), bins), :] = jnp.concatenate([ref[...], ref[...]], axis=1)
     lane = lax.broadcasted_iota(jnp.int32, (1, FACTOR), 1)
     for at, message in enumerate(messages):
         step = at % (PLACES // 2)
@@ -350,12 +344,33 @@
                     keep_ref[which] = value
 
 
+def gather_lines(ref, bins, group):
+    width = 2 * PART
+    columns = [
+        jnp.concatenate(
+            [ref[(part * bins + bin_num) * width : (part * bins + bin_num + 1) * width, :] for part in range(2)], axis=0
+        )
+        for bin_num in group
+    ]
+    return jnp.concatenate(columns, axis=1)
+
+
+def bin_groups(bins):
+    return [range(at, min(at + 4, bins)) for at in range(0, bins, 4)]
+
+
+def near_kernel(bins, keep, near, out):
+    matrix = near[lax.axis_index("rg")]
+    for index, group in enumerate(bin_groups(bins)):
+        out[index, :, : len(group) * FACTOR] = dot(matrix, split_bf16(gather_lines(keep, bins, group), 0))
+
+
 def band_kernel(chunk, *refs):
     (first_bin, last_bin), (first_out, last_out) = CHUNKS[chunk]
     bins = last_bin - first_bin
-    keep, got, keep_ref, got_ref, owners, phase, taps_own, taps_other = refs[:8]
-    first_high, first_low, there_high, there_low, back_high, back_low, last_high, last_low, twists = refs[8:17]
-    refs = refs[17:]
+    partial, got, keep_ref, got_ref, owners, phase, taps_own, taps_other = refs[:8]
+    far, there, back, last, twists = refs[8:13]
+    refs = refs[13:]
     if chunk:
         earlier, refs = refs[0], refs[1:]
     keep_out, give_out, spectra, band, picked = refs
@@ -383,24 +398,10 @@
         picked[0, block * REF_LINES : (block + 1) * REF_LINES, :] = ref_cos
         picked[1, block * REF_LINES : (block + 1) * REF_LINES, :] = ref_sin
 
-    first, last = (first_high[side], first_low[side]), (last_high[side], last_low[side])
-    there, back = (there_high[...], there_low[...]), (back_high[...], back_low[...])
+    far, last, there, back = far[side], last[side], there[...], back[...]
     twist_cos, twist_sin = twists[side, 0], twists[side, 1]
-    width = 2 * PART
-    for at in range(0, bins, 4):
-        group = range(at, min(at + 4, bins))
-        columns = [
-            jnp.concatenate(
-                [
-                    ref[(part * bins + bin_num) * width : (part * bins + bin_num + 1) * width, :]
-                    for part in range(2)
-                    for ref in (keep, got)
-                ],
-                axis=0,
-            )
-            for bin_num in group
-        ]
-        passed = dot_split(first, split_bf16(jnp.concatenate(columns, axis=1)))
+    for number, group in enumerate(bin_groups(bins)):
+        passed = partial[number, :, : len(group) * FACTOR] + dot(far, split_bf16(gather_lines(got, bins, group), 0))
         rows = []
         for index in range(len(group)):
             real = passed[:HALF, index * FACTOR : (index + 1) * FACTOR]
@@ -408,7 +409,7 @@
             rows.append(
                 jnp.concatenate([real * twist_cos + imag * twist_sin, imag * twist_cos - real * twist_sin], axis=1)
             )
-        passed = dot_split(split_bf16(jnp.concatenate(rows, axis=0)), there)
+        passed = dot(split_bf16(jnp.concatenate(rows, axis=0), 1), there)
         for index, bin_num in enumerate(group):
             real = passed[index * HALF : (index + 1) * HALF, :FACTOR]
             imag = passed[index * HALF : (index + 1) * HALF, FACTOR:]
@@ -449,7 +450,7 @@
     scale = 1.0 / (FACTOR * FACTOR)
     cos_table, sin_table = twist_cos * scale, twist_sin * scale
     for at in range(0, last_out - first_out, 4):
-        passed = dot_split(split_bf16(band[at * HALF : (at + 4) * HALF, :]), back)
+        passed = dot(split_bf16(band[at * HALF : (at + 4) * HALF, :], 1), back)
         columns = []
         for index in range(4):
             real = passed[index * HALF : (index + 1) * HALF, :FACTOR]
@@ -457,7 +458,7 @@
             columns.append(
                 jnp.concatenate([real * cos_table - imag * sin_table, imag * cos_table + real * sin_table], axis=0)
             )
-        passed = dot_split(last, split_bf16(jnp.concatenate(columns, axis=1)))
+        passed = dot(last, split_bf16(jnp.concatenate(columns, axis=1), 0))
         for index in range(4):
             lines = slice((at + index) * HALF, (at + index + 1) * HALF)
             keep_out[lines, :] = passed[:HALF, index * FACTOR : (index + 1) * FACTOR]
@@ -521,22 +522,14 @@
         return jax.ShapeDtypeStruct(shape, jnp.float32)
 
     matrices, twists = dft_constants()
-    tables = [jnp.asarray(part) for part in matrices] + [jnp.asarray(twists)]
+    near_table, *tables = [jnp.asarray(table) for table in (*matrices, twists)]
     swap = functools.partial(lax.ppermute, axis_name="rg", perm=[(0, 1), (1, 0)])
     half = PLACES // 2
-    ref_own = ref_blocks[0]
+    ref_own = ref_blocks[0].T
     offsets_other = swap(offsets)
     ref_other, re_other, im_other, taps_other = swap(ref_own), swap(raw_re), swap(raw_im), swap(taps)
 
-    lines = pl.pallas_call(
-        spread_kernel,
-        out_shape=[array(bins * PART, FACTOR)] * 2,
-        grid=(bins // 8,),
-        in_specs=[pl.BlockSpec((8, samples), lambda i: (i, 0))] * 2,
-        out_specs=[pl.BlockSpec((bins * PART, FACTOR), lambda i: (0, 0))] * 2,
-        cost_estimate=pl.CostEstimate(flops=1, bytes_accessed=2 * 10**6, transcendentals=0),
-        name="spread",
-    )(raw_re, raw_im)
+    lines = [raw_re.reshape(bins * PART, FACTOR), raw_im.reshape(bins * PART, FACTOR)]
     shapes = []
     for (first_bin, last_bin), _ in CHUNKS:
         ref_lines = REF_LINES if first_bin == 0 else 0
@@ -596,13 +589,17 @@
         parity = kernel_call(functools.partial(parity_kernel, count, has_ref), "parity", shapes, operands)
         keep, give = parity[:2]
         got = swap(give)
+        groups = len(bin_groups(count))
+        partial = kernel_call(
+            functools.partial(near_kernel, count), "near", array(groups, FACTOR, 4 * FACTOR), [keep, near_table]
+        )
         if has_ref:
             refs = [parity[2], got]
         pieces = kernel_call(
             functools.partial(band_kernel, chunk),
             "band",
             [array(outs * HALF, FACTOR), array(outs * HALF, FACTOR), array(count, 2, HALF, FACTOR)],
-            [keep, got, *refs, owners, phases, taps, taps_other, *tables, *earlier],
+            [partial, got, *refs, owners, phases, taps, taps_other, *tables, *earlier],
             scratch=[(outs * HALF, 2 * FACTOR), (2, 2 * REF_LINES, FACTOR)],
             flops=10**9,
             count=4 * 10**6,

time: 64.6 us -> 60.6 us (0.938)
  Pallas kernels: 10.2 us -> 7.82 us
  local copies, waits for them, and re-layouts: 3 us -> 1.72 us
    pallas_call x1 -> x0, Pallas kernels: 2.69 us -> none  [transposed_shards(): pl.pallas_call(spread_kernel, out_shape=[array(bins * PART, FACTOR)] * 2,...]
    unnamed x30 -> x23, local copies, waits for them, and re-layouts: 3 us -> 0.67 us
    reshape x0 -> x2, local copies, waits for them, and re-layouts: none -> 1.04 us  [the longest x1 1 us: transposed_shards(): raw_re.reshape(bins * PART, FACTOR)]
    pallas_call x6 -> x7, Pallas kernels: 7.47 us -> 7.82 us  [kernel_call(): pl.pallas_call(body, out_shape=out_shape, in_specs=specs, out_specs=jax.t...]
  transfers between devices with their start and end apart: 15 -> 15, of which waited for: 6 -> 7; matrix products, arithmetic and copies ran while one was open for 1% -> 2% of each run, Pallas kernels for 6% -> 3%
where the time goes in v3:
time: 60.6 us; the launch traced here: 60.3 us
  starting transfers between devices  25.6 us (42%)
  waiting for transfers between devices  24.3 us (40%)
  Pallas kernels  7.82 us (13%)
  local copies, waits for them, and re-layouts  1.72 us (3%)
  between operations  0.82 us (1%)
    ppermute x4, starting transfers between devices, transposed_shards(): lax.ppermute(message, ('az', 'rg'), route)  13.6 us
    ppermute x4, waiting for transfers between devices, transposed_shards(): lax.ppermute(messages[chunk * half + step], ('az', 'rg'), routes[step])  11.4 us
    ppermute x4, waiting for transfers between devices, transposed_shards(): lax.ppermute(message, ('az', 'rg'), route)  10.5 us
    pallas_call x7, Pallas kernels, kernel_call(): pl.pallas_call(body, out_shape=out_shape, in_specs=specs, out_specs=jax.t...  7.82 us
    ppermute x4, starting transfers between devices, transposed_shards(): lax.ppermute(messages[chunk * half + step], ('az', 'rg'), routes[step])  6.32 us
    ppermute x1, starting transfers between devices, transposed_shards(): swap(taps)  3.47 us
  transfers between devices with their start and end apart: 15, of which 7 were waited for; matrix products, arithmetic and copies ran while one was open for 2% of the time, Pallas kernels for 3%

profile of v3, /device:TPU:0, one launch (start us, length us, event | category | flops | bytes accessed | tf_op | source)
XLA Modules:
  0.0 60.3 jit_solution(17934156462690891266)
XLA Ops:
  0.6 0.5 collective-permute-start
  1.2 0.1 collective-permute-start.1
  1.2 0.4 collective-permute-start.2
  1.7 0.1 collective-permute-start.3
  1.8 1.0 %reshape.10.re_lines = f32[512,128]{1,0:T(8,128)S(1)} reshape(f32[32,2048]{1,0:T(8,128)} %param.12) | data formatting | bytes 524288 | tf_op jit(solution)/shard_map/reshape | solution.py:532
  2.8 0.1 collective-permute-done.2.ref_other
  2.9 0.5 copy-done.6
  3.5 0.8 %pack.1 = (f32[488,128]{1,0:T(8,128)S(1)}, f32[488,128]{1,0:T(8,128)S(1)}, f32[488,128]{1,0:T(8,128)S(1)}, f32[488,128]{1,0:T(8,128)S(1)}) custom-call(f32[512,128]{1,0:T(8,128)S(1)} %reshape.10.re_lines, f32[512,128]{1,0:T(8,128)S(1)} %reshape.11.im_lines, f32[32,2048]{1,0:T(8,128)S(1)} %collective-permute-done.re_other, ...), custom_call_target="tpu_custom_call" | custom-call | bytes 4000000 | tf_op jit(solution)/shard_map/pack/pallas_call | solution.py:506
  4.3 4.1 %collective-permute-start.4 = (f32[488,128]{1,0:T(8,128)S(1)}, f32[488,128]{1,0:T(8,128)S(1)}, u32[]{:S(2)}, u32[]{:S(2)}) collective-permute-start(f32[488,128]{1,0:T(8,128)S(1)} %get-tuple-element.21), channel_id=1, source_target_pairs={{0,8},{1,10},{2,9},{3,11},{4,12},{5,14},{6,13},{7,15},{8,0},{9,2},... | collective-permute-start | bytes 749576 | tf_op jit(solution)/shard_map/ppermute | solution.py:571
  8.4 1.3 %collective-permute-start.5 = (f32[488,128]{1,0:T(8,128)S(1)}, f32[488,128]{1,0:T(8,128)S(1)}, u32[]{:S(2)}, u32[]{:S(2)}) collective-permute-start(f32[488,128]{1,0:T(8,128)S(1)} %get-tuple-element.22), channel_id=1, source_target_pairs={{0,12},{1,14},{2,13},{3,15},{4,8},{5,10},{6,9},{7,11},{8,4},{9,6},... | collective-permute-start | bytes 749576 | tf_op jit(solution)/shard_map/ppermute | solution.py:571
  9.8 0.2 collective-permute-start.6
  10.0 0.7 %collective-permute-start.7 = (f32[488,128]{1,0:T(8,128)S(1)}, f32[488,128]{1,0:T(8,128)S(1)}, u32[]{:S(2)}, u32[]{:S(2)}) collective-permute-start(f32[488,128]{1,0:T(8,128)S(1)} %get-tuple-element.24), channel_id=1, source_target_pairs={{0,0},{1,2},{2,1},{3,3},{4,4},{5,6},{6,5},{7,7},{8,8},{9,10},{10,9... | collective-permute-start | bytes 749576 | tf_op jit(solution)/shard_map/ppermute | solution.py:571
  10.7 0.1 copy.14.refs_6_
  10.8 3.5 %collective-permute-start.8 = (f32[32,8]{1,0:T(8,128)S(1)}, f32[32,8]{1,0:T(8,128)S(1)}, u32[]{:S(2)}, u32[]{:S(2)}) collective-permute-start(f32[32,8]{1,0:T(8,128)S(1)} %copy.14.refs_6_), channel_id=1, source_target_pairs={{0,1},{1,0},{2,3},{3,2},{4,5},{5,4},{6,7},{7,6},{8,9},{9,8},{10,11... | collective-permute-start | bytes 3080 | tf_op jit(solution)/shard_map/ppermute | solution.py:530
  14.2 1.3 %phase.1.refs_5_ = f32[15,2,64,128]{3,2,1,0:T(8,128)S(1)} custom-call(s32[2]{0:T(128)S(1)} %copy-done.7, s32[2]{0:T(128)S(1)} %collective-permute-done.3.off_other), custom_call_target="tpu_custom_call" | custom-call | flops 10000000 | bytes 1000000 | tf_op jit(solution)/shard_map/phase/pallas_call | solution.py:506
  15.6 9.9 %collective-permute-done.4.refs_0_ = f32[488,128]{1,0:T(8,128)S(1)} collective-permute-done((f32[488,128]{1,0:T(8,128)S(1)}, f32[488,128]{1,0:T(8,128)S(1)}, u32[]{:S(2)}, u32[]{:S(2)}) %collective-permute-start.4) | collective-permute-done | bytes 249888 | tf_op jit(solution)/shard_map/ppermute | solution.py:571
  25.5 1.5 %collective-permute-done.6.refs_2_ = f32[488,128]{1,0:T(8,128)S(1)} collective-permute-done((f32[488,128]{1,0:T(8,128)S(1)}, f32[488,128]{1,0:T(8,128)S(1)}, u32[]{:S(2)}, u32[]{:S(2)}) %collective-permute-start.6) | collective-permute-done | bytes 249888 | tf_op jit(solution)/shard_map/ppermute | solution.py:571
  27.0 0.7 %parity.1 = (f32[960,128]{1,0:T(8,128)S(1)}, f32[976,128]{1,0:T(8,128)S(1)}, f32[2,8,128]{2,1,0:T(8,128)S(1)}) custom-call(f32[488,128]{1,0:T(8,128)S(1)} %collective-permute-done.4.refs_0_, f32[488,128]{1,0:T(8,128)S(1)} %collective-permute-done.5.refs_1_, f32[488,128]{1,0:T(8,128)S(1)} %collective-permute-done.6.refs_2_, ...), custom_call_target="tpu_custom_call" | custom-call | bytes 1000000 | tf_op jit(solution)/shard_map/parity/pallas_call | solution.py:506
  27.7 0.7 %collective-permute-start.9 = (f32[976,128]{1,0:T(8,128)S(1)}, f32[976,128]{1,0:T(8,128)S(1)}, u32[]{:S(2)}, u32[]{:S(2)}) collective-permute-start(f32[976,128]{1,0:T(8,128)S(1)} %get-tuple-element.30), channel_id=1, source_target_pairs={{0,1},{1,0},{2,3},{3,2},{4,5},{5,4},{6,7},{7,6},{8,9},{9,8},{10,11... | collective-permute-start | bytes 1499144 | tf_op jit(solution)/shard_map/ppermute | solution.py:591
  28.4 0.3 near.2.refs_0_
  28.7 1.2 %collective-permute-done.9.refs_1_.refs_3_ = f32[976,128]{1,0:T(8,128)S(1)} collective-permute-done((f32[976,128]{1,0:T(8,128)S(1)}, f32[976,128]{1,0:T(8,128)S(1)}, u32[]{:S(2)}, u32[]{:S(2)}) %collective-permute-start.9) | collective-permute-done | bytes 499744 | tf_op jit(solution)/shard_map/ppermute | solution.py:591
  29.9 3.7 %band.1 = (f32[512,128]{1,0:T(8,128)S(1)}, f32[512,128]{1,0:T(8,128)S(1)}, f32[15,2,64,128]{3,2,1,0:T(8,128)}) custom-call(f32[4,128,512]{2,1,0:T(8,128)S(1)} %near.2.refs_0_, f32[976,128]{1,0:T(8,128)S(1)} %collective-permute-done.9.refs_1_.refs_3_, f32[2,8,128]{2,1,0:T(8,128)S(1)} %get-tuple-element.31.refs_2_, ...), custom_call_target="tpu_custom_call" | custom-call | flops 1000000000 | bytes 4000000 | tf_op jit(solution)/shard_map/band/pallas_call | solution.py:506
  33.6 0.4 collective-permute-start.10
  34.0 1.2 %collective-permute-done.10.got = f32[512,128]{1,0:T(8,128)S(1)} collective-permute-done((f32[512,128]{1,0:T(8,128)S(1)}, f32[512,128]{1,0:T(8,128)S(1)}, u32[]{:S(2)}, u32[]{:S(2)}) %collective-permute-start.10) | collective-permute-done | bytes 262176 | tf_op jit(solution)/shard_map/ppermute | solution.py:614
  35.1 0.1 join.1
  35.2 0.7 %collective-permute-start.11 = (f32[256,128]{1,0:T(8,128)S(1)}, f32[256,128]{1,0:T(8,128)S(1)}, u32[]{:S(2)}, u32[]{:S(2)}) collective-permute-start(f32[256,128]{1,0:T(8,128)S(1)} %get-tuple-element.36), channel_id=1, source_target_pairs={{0,0},{1,2},{2,4},{3,6},{4,8},{5,10},{6,12},{7,14},{8,1},{9,3},{10... | collective-permute-start | bytes 393224 | tf_op jit(solution)/shard_map/ppermute | solution.py:616
  35.9 9.0 %collective-permute-start.12 = (f32[256,128]{1,0:T(8,128)S(1)}, f32[256,128]{1,0:T(8,128)S(1)}, u32[]{:S(2)}, u32[]{:S(2)}) collective-permute-start(f32[256,128]{1,0:T(8,128)S(1)} %get-tuple-element.37), channel_id=1, source_target_pairs={{0,4},{1,6},{2,0},{3,2},{4,12},{5,14},{6,8},{7,10},{8,5},{9,7},{10... | collective-permute-start | bytes 393224 | tf_op jit(solution)/shard_map/ppermute | solution.py:616
  44.8 2.1 %collective-permute-start.13 = (f32[256,128]{1,0:T(8,128)S(1)}, f32[256,128]{1,0:T(8,128)S(1)}, u32[]{:S(2)}, u32[]{:S(2)}) collective-permute-start(f32[256,128]{1,0:T(8,128)S(1)} %get-tuple-element.38), channel_id=1, source_target_pairs={{0,8},{1,10},{2,12},{3,14},{4,0},{5,2},{6,4},{7,6},{8,9},{9,11},{1... | collective-permute-start | bytes 393224 | tf_op jit(solution)/shard_map/ppermute | solution.py:616
  47.0 1.9 %collective-permute-start.14 = (f32[256,128]{1,0:T(8,128)S(1)}, f32[256,128]{1,0:T(8,128)S(1)}, u32[]{:S(2)}, u32[]{:S(2)}) collective-permute-start(f32[256,128]{1,0:T(8,128)S(1)} %get-tuple-element.39), channel_id=1, source_target_pairs={{0,12},{1,14},{2,8},{3,10},{4,4},{5,6},{6,0},{7,2},{8,13},{9,15},{... | collective-permute-start | bytes 393224 | tf_op jit(solution)/shard_map/ppermute | solution.py:616
  48.9 4.7 %collective-permute-done.13.refs_2_ = f32[256,128]{1,0:T(8,128)S(1)} collective-permute-done((f32[256,128]{1,0:T(8,128)S(1)}, f32[256,128]{1,0:T(8,128)S(1)}, u32[]{:S(2)}, u32[]{:S(2)}) %collective-permute-start.13) | collective-permute-done | bytes 131104 | tf_op jit(solution)/shard_map/ppermute | solution.py:616
  53.6 5.7 %collective-permute-done.14.refs_3_ = f32[256,128]{1,0:T(8,128)S(1)} collective-permute-done((f32[256,128]{1,0:T(8,128)S(1)}, f32[256,128]{1,0:T(8,128)S(1)}, u32[]{:S(2)}, u32[]{:S(2)}) %collective-permute-start.14) | collective-permute-done | bytes 131104 | tf_op jit(solution)/shard_map/ppermute | solution.py:616
  59.4 0.9 %place.1 = (f32[32,2048]{1,0:T(8,128)}, f32[32,2048]{1,0:T(8,128)}) custom-call(f32[256,128]{1,0:T(8,128)S(1)} %collective-permute-done.11.refs_0_, f32[256,128]{1,0:T(8,128)S(1)} %collective-permute-done.12.refs_1_, f32[256,128]{1,0:T(8,128)S(1)} %collective-permute-done.13.refs_2_, f32[256,128]{1,0:T(8,128)S(1)} %collective-permute-done.14.refs_3_), custom_call_target="tpu_custom_call" | custom-call | bytes 1000000 | tf_op jit(solution)/shard_map/place/pallas_call | solution.py:506
  (30 shorter events, 0.1 us)
Async XLA Ops:
  0.6 1.0 %copy-start.7 = (s32[2]{0:T(128)S(1)}, s32[2]{0:T(128)}, u32[]{:S(2)}) copy-start(s32[2]{0:T(128)} %off_own.3) | copy-start | bytes 28
  0.6 2.3 %collective-permute-start = (f32[32,2048]{1,0:T(8,128)}, f32[32,2048]{1,0:T(8,128)S(1)}, u32[]{:S(2)}, u32[]{:S(2)}) collective-permute-start(f32[32,2048]{1,0:T(8,128)} %param.12), channel_id=1, source_target_pairs={{0,1},{1,0},{2,3},{3,2},{4,5},{5,4},{6,7},{7,6},{8,9},{9,8},{10,11... | collective-permute-start | bytes 786440 | tf_op jit(solution)/shard_map/ppermute | solution.py:530
  1.2 1.8 %collective-permute-start.1 = (f32[32,2048]{1,0:T(8,128)}, f32[32,2048]{1,0:T(8,128)S(1)}, u32[]{:S(2)}, u32[]{:S(2)}) collective-permute-start(f32[32,2048]{1,0:T(8,128)} %param.13), channel_id=1, source_target_pairs={{0,1},{1,0},{2,3},{3,2},{4,5},{5,4},{6,7},{7,6},{8,9},{9,8},{10,11... | collective-permute-start | bytes 786440 | tf_op jit(solution)/shard_map/ppermute | solution.py:530
  1.2 1.5 %copy-start.9 = (f32[32,2048]{1,0:T(8,128)S(1)}, f32[32,2048]{1,0:T(8,128)}, u32[]{:S(2)}) copy-start(f32[32,2048]{1,0:T(8,128)} %param.13) | copy-start | bytes 786436
  1.2 1.7 %collective-permute-start.2 = (f32[32,64]{1,0:T(8,128)}, f32[32,64]{1,0:T(8,128)S(1)}, u32[]{:S(2)}, u32[]{:S(2)}) collective-permute-start(f32[32,64]{1,0:T(8,128)} %bitcast.3), channel_id=1, source_target_pairs={{0,1},{1,0},{2,3},{3,2},{4,5},{5,4},{6,7},{7,6},{8,9},{9,8},{10,11... | collective-permute-start | bytes 24584 | tf_op jit(solution)/shard_map/ppermute | solution.py:530
  1.7 1.2 %collective-permute-start.3 = (s32[2]{0:T(128)S(1)}, s32[2]{0:T(128)S(1)}, u32[]{:S(2)}, u32[]{:S(2)}) collective-permute-start(s32[2]{0:T(128)S(1)} %copy-done.7), channel_id=1, source_target_pairs={{0,1},{1,0},{2,3},{3,2},{4,5},{5,4},{6,7},{7,6},{8,9},{9,8},{10,11... | collective-permute-start | bytes 32 | tf_op jit(solution)/shard_map/ppermute | solution.py:529
  2.8 0.7 %copy-start.6 = (f32[1,64,32]{1,2,0:T(8,128)S(1)}, f32[1,64,32]{1,2,0:T(8,128)}, u32[]{:S(2)}) copy-start(f32[1,64,32]{1,2,0:T(8,128)} %param.14) | copy-start | bytes 24580
  4.3 6.3 %copy-start.10 = (f32[32,8]{0,1:T(8,128)S(1)}, f32[32,8]{0,1:T(8,128)}, u32[]{:S(2)}) copy-start(f32[32,8]{0,1:T(8,128)} %param.17) | copy-start | bytes 3076
  4.3 21.2 %collective-permute-start.4 = (f32[488,128]{1,0:T(8,128)S(1)}, f32[488,128]{1,0:T(8,128)S(1)}, u32[]{:S(2)}, u32[]{:S(2)}) collective-permute-start(f32[488,128]{1,0:T(8,128)S(1)} %get-tuple-element.21), channel_id=1, source_target_pairs={{0,8},{1,10},{2,9},{3,11},{4,12},{5,14},{6,13},{7,15},{8,0},{9,2},... | collective-permute-start | bytes 749576 | tf_op jit(solution)/shard_map/ppermute | solution.py:571
  8.4 17.1 %collective-permute-start.5 = (f32[488,128]{1,0:T(8,128)S(1)}, f32[488,128]{1,0:T(8,128)S(1)}, u32[]{:S(2)}, u32[]{:S(2)}) collective-permute-start(f32[488,128]{1,0:T(8,128)S(1)} %get-tuple-element.22), channel_id=1, source_target_pairs={{0,12},{1,14},{2,13},{3,15},{4,8},{5,10},{6,9},{7,11},{8,4},{9,6},... | collective-permute-start | bytes 749576 | tf_op jit(solution)/shard_map/ppermute | solution.py:571
  9.8 17.2 %collective-permute-start.6 = (f32[488,128]{1,0:T(8,128)S(1)}, f32[488,128]{1,0:T(8,128)S(1)}, u32[]{:S(2)}, u32[]{:S(2)}) collective-permute-start(f32[488,128]{1,0:T(8,128)S(1)} %get-tuple-element.23), channel_id=1, source_target_pairs={{0,4},{1,6},{2,5},{3,7},{4,0},{5,2},{6,1},{7,3},{8,12},{9,14},{10,... | collective-permute-start | bytes 749576 | tf_op jit(solution)/shard_map/ppermute | solution.py:571
  10.0 17.0 %collective-permute-start.7 = (f32[488,128]{1,0:T(8,128)S(1)}, f32[488,128]{1,0:T(8,128)S(1)}, u32[]{:S(2)}, u32[]{:S(2)}) collective-permute-start(f32[488,128]{1,0:T(8,128)S(1)} %get-tuple-element.24), channel_id=1, source_target_pairs={{0,0},{1,2},{2,1},{3,3},{4,4},{5,6},{6,5},{7,7},{8,8},{9,10},{10,9... | collective-permute-start | bytes 749576 | tf_op jit(solution)/shard_map/ppermute | solution.py:571
  10.8 16.2 %copy-start.8 = (s32[2]{0:T(128)S(1)}, s32[2]{0:T(128)}, u32[]{:S(2)}) copy-start(s32[2]{0:T(128)} %refs_4_.3) | copy-start | bytes 28
  10.8 4.8 %collective-permute-start.8 = (f32[32,8]{1,0:T(8,128)S(1)}, f32[32,8]{1,0:T(8,128)S(1)}, u32[]{:S(2)}, u32[]{:S(2)}) collective-permute-start(f32[32,8]{1,0:T(8,128)S(1)} %copy.14.refs_6_), channel_id=1, source_target_pairs={{0,1},{1,0},{2,3},{3,2},{4,5},{5,4},{6,7},{7,6},{8,9},{9,8},{10,11... | collective-permute-start | bytes 3080 | tf_op jit(solution)/shard_map/ppermute | solution.py:530
  15.5 12.8 %copy-start.5 = (bf16[2,128,192]{2,1,0:T(8,128)(2,1)S(1)}, bf16[2,128,192]{2,1,0:T(8,128)(2,1)}, u32[]{:S(2)}) copy-start(bf16[2,128,192]{2,1,0:T(8,128)(2,1)} %constant.12.clone.near) | copy-start | bytes 294916
  27.7 2.2 %collective-permute-start.9 = (f32[976,128]{1,0:T(8,128)S(1)}, f32[976,128]{1,0:T(8,128)S(1)}, u32[]{:S(2)}, u32[]{:S(2)}) collective-permute-start(f32[976,128]{1,0:T(8,128)S(1)} %get-tuple-element.30), channel_id=1, source_target_pairs={{0,1},{1,0},{2,3},{3,2},{4,5},{5,4},{6,7},{7,6},{8,9},{9,8},{10,11... | collective-permute-start | bytes 1499144 | tf_op jit(solution)/shard_map/ppermute | solution.py:591
  28.4 1.5 %copy-start = (bf16[768,256]{1,0:T(8,128)(2,1)S(1)}, bf16[768,256]{1,0:T(8,128)(2,1)}, u32[]{:S(2)}) copy-start(bf16[768,256]{1,0:T(8,128)(2,1)} %constant.15.clone.refs_10_) | copy-start | bytes 1179652
  28.4 1.5 %copy-start.1 = (bf16[768,256]{1,0:T(8,128)(2,1)S(1)}, bf16[768,256]{1,0:T(8,128)(2,1)}, u32[]{:S(2)}) copy-start(bf16[768,256]{1,0:T(8,128)(2,1)} %constant.14.clone.refs_9_) | copy-start | bytes 1179652
  28.4 1.5 %copy-start.2 = (bf16[2,128,384]{2,1,0:T(8,128)(2,1)S(1)}, bf16[2,128,384]{2,1,0:T(8,128)(2,1)}, u32[]{:S(2)}) copy-start(bf16[2,128,384]{2,1,0:T(8,128)(2,1)} %constant.16.clone.refs_11_) | copy-start | bytes 589828
  28.4 1.5 %copy-start.3 = (f32[2,2,64,128]{3,2,1,0:T(8,128)S(1)}, f32[2,2,64,128]{3,2,1,0:T(8,128)}, u32[]{:S(2)}) copy-start(f32[2,2,64,128]{3,2,1,0:T(8,128)} %constant.17.clone.refs_12_) | copy-start | bytes 393220
  28.4 1.5 %copy-start.4 = (bf16[2,128,192]{2,1,0:T(8,128)(2,1)S(1)}, bf16[2,128,192]{2,1,0:T(8,128)(2,1)}, u32[]{:S(2)}) copy-start(bf16[2,128,192]{2,1,0:T(8,128)(2,1)} %constant.13.clone.refs_8_) | copy-start | bytes 294916
  33.6 1.5 %collective-permute-start.10 = (f32[512,128]{1,0:T(8,128)S(1)}, f32[512,128]{1,0:T(8,128)S(1)}, u32[]{:S(2)}, u32[]{:S(2)}) collective-permute-start(f32[512,128]{1,0:T(8,128)S(1)} %get-tuple-element.35), channel_id=1, source_target_pairs={{0,1},{1,0},{2,3},{3,2},{4,5},{5,4},{6,7},{7,6},{8,9},{9,8},{10,11... | collective-permute-start | bytes 786440 | tf_op jit(solution)/shard_map/ppermute | solution.py:614
  35.2 13.7 %collective-permute-start.11 = (f32[256,128]{1,0:T(8,128)S(1)}, f32[256,128]{1,0:T(8,128)S(1)}, u32[]{:S(2)}, u32[]{:S(2)}) collective-permute-start(f32[256,128]{1,0:T(8,128)S(1)} %get-tuple-element.36), channel_id=1, source_target_pairs={{0,0},{1,2},{2,4},{3,6},{4,8},{5,10},{6,12},{7,14},{8,1},{9,3},{10... | collective-permute-start | bytes 393224 | tf_op jit(solution)/shard_map/ppermute | solution.py:616
  35.9 13.0 %collective-permute-start.12 = (f32[256,128]{1,0:T(8,128)S(1)}, f32[256,128]{1,0:T(8,128)S(1)}, u32[]{:S(2)}, u32[]{:S(2)}) collective-permute-start(f32[256,128]{1,0:T(8,128)S(1)} %get-tuple-element.37), channel_id=1, source_target_pairs={{0,4},{1,6},{2,0},{3,2},{4,12},{5,14},{6,8},{7,10},{8,5},{9,7},{10... | collective-permute-start | bytes 393224 | tf_op jit(solution)/shard_map/ppermute | solution.py:616
  44.8 8.8 %collective-permute-start.13 = (f32[256,128]{1,0:T(8,128)S(1)}, f32[256,128]{1,0:T(8,128)S(1)}, u32[]{:S(2)}, u32[]{:S(2)}) collective-permute-start(f32[256,128]{1,0:T(8,128)S(1)} %get-tuple-element.38), channel_id=1, source_target_pairs={{0,8},{1,10},{2,12},{3,14},{4,0},{5,2},{6,4},{7,6},{8,9},{9,11},{1... | collective-permute-start | bytes 393224 | tf_op jit(solution)/shard_map/ppermute | solution.py:616
  47.0 12.4 %collective-permute-start.14 = (f32[256,128]{1,0:T(8,128)S(1)}, f32[256,128]{1,0:T(8,128)S(1)}, u32[]{:S(2)}, u32[]{:S(2)}) collective-permute-start(f32[256,128]{1,0:T(8,128)S(1)} %get-tuple-element.39), channel_id=1, source_target_pairs={{0,12},{1,14},{2,8},{3,10},{4,4},{5,6},{6,0},{7,2},{8,13},{9,15},{... | collective-permute-start | bytes 393224 | tf_op jit(solution)/shard_map/ppermute | solution.py:616

commit v4 on v3

--- a/solution.py
+++ b/solution.py
@@ -174,20 +174,20 @@
 CHUNKS = (((0, WINDOW), (0, OUT_BINS)),)
 
 
-def split_bf16(value, axis):
+def split_bf16(value):
     high = value.astype(jnp.bfloat16)
     low = (value - high.astype(jnp.float32)).astype(jnp.bfloat16)
-    return jnp.concatenate([high, low, high], axis=axis)
-
-
-def dot(left, right):
-    return jnp.dot(left, right, preferred_element_type=jnp.float32)
-
-
-def both_bf16(matrix, axis):
+    return high, low
+
+
+def dot_split(left, right):
+    dot = functools.partial(jnp.dot, preferred_element_type=jnp.float32)
+    return dot(left[0], right[0]) + (dot(left[0], right[1]) + dot(left[1], right[0]))
+
+
+def both_bf16(matrix):
     high = matrix.astype(jnp.bfloat16)
-    low = (matrix - high.astype(np.float64)).astype(jnp.bfloat16)
-    return np.concatenate([high, high, low], axis=axis)
+    return np.stack([high, (matrix - high.astype(np.float64)).astype(jnp.bfloat16)])
 
 
 def dft_constants():
@@ -213,11 +213,11 @@
     there = np.block([[cosine, -sine], [sine, cosine]])
     back = np.block([[cosine, sine], [-sine, cosine]])
     matrices = [
-        both_bf16(np.stack(near), 2),
-        both_bf16(np.stack(far), 2),
-        both_bf16(there, 0),
-        both_bf16(back, 0),
-        both_bf16(np.stack(last), 2),
+        both_bf16(np.stack(near)),
+        both_bf16(np.stack(far)),
+        both_bf16(there),
+        both_bf16(back),
+        both_bf16(np.stack(last)),
     ]
     return matrices, np.stack(twists).astype(np.float32)
 
@@ -335,13 +335,11 @@
     if has_ref:
         for which in range(2):
             step = (owners[which] >> 1) ^ (place >> 1)
-            for other in range(PLACES // 2):
-
-                @pl.when(step == other)
-                def _():
-                    value = chunks[other][2 * bins * PART :, :]
-                    give[pl.ds(2 * bins * 2 * PART + which * REF_LINES, REF_LINES), :] = value
-                    keep_ref[which] = value
+            value = chunks[0][2 * bins * PART :, :]
+            for other in range(1, PLACES // 2):
+                value = jnp.where(step == other, chunks[other][2 * bins * PART :, :], value)
+            give[2 * bins * 2 * PART + which * REF_LINES : 2 * bins * 2 * PART + (which + 1) * REF_LINES, :] = value
+            keep_ref[which] = value
 
 
 def gather_lines(ref, bins, group):
@@ -360,9 +358,10 @@
 
 
 def near_kernel(bins, keep, near, out):
-    matrix = near[lax.axis_index("rg")]
+    side = lax.axis_index("rg")
+    matrix = (near[0, side], near[1, side])
     for index, group in enumerate(bin_groups(bins)):
-        out[index, :, : len(group) * FACTOR] = dot(matrix, split_bf16(gather_lines(keep, bins, group), 0))
+        out[index, :, : len(group) * FACTOR] = dot_split(matrix, split_bf16(gather_lines(keep, bins, group)))
 
 
 def band_kernel(chunk, *refs):
@@ -376,8 +375,6 @@
     keep_out, give_out, spectra, band, picked = refs
     place, side = lax.axis_index("az"), lax.axis_index("rg")
 
-    row = lax.broadcasted_iota(jnp.int32, (FACTOR, FACTOR), 0)
-    column = lax.broadcasted_iota(jnp.int32, (FACTOR, FACTOR), 1)
     lane = lax.broadcasted_iota(jnp.int32, (REF_LINES, FACTOR), 1)
     ref_at = got_ref.shape[0] - 2 * REF_LINES
     lines = [
@@ -389,19 +386,18 @@
         for which in range(2)
     ]
     for block in range(2):
-        spread = (row == column // 2 + block * HALF).astype(jnp.float32)
-        wide = [
-            jnp.dot(lines[which], spread, precision=PRECISE, preferred_element_type=jnp.float32) for which in range(2)
-        ]
+        coarse = (lane >> 1) + block * HALF
+        wide = [jnp.take_along_axis(lines[which], coarse, axis=1) for which in range(2)]
         ref_phase = jnp.where(lane < HALF, wide[1], wide[0])
         ref_cos, ref_sin = cos_sin_quarters(ref_phase * (2 / math.pi))
         picked[0, block * REF_LINES : (block + 1) * REF_LINES, :] = ref_cos
         picked[1, block * REF_LINES : (block + 1) * REF_LINES, :] = ref_sin
 
-    far, last, there, back = far[side], last[side], there[...], back[...]
+    far, last = (far[0, side], far[1, side]), (last[0, side], last[1, side])
+    there, back = (there[0], there[1]), (back[0], back[1])
     twist_cos, twist_sin = twists[side, 0], twists[side, 1]
     for number, group in enumerate(bin_groups(bins)):
-        passed = partial[number, :, : len(group) * FACTOR] + dot(far, split_bf16(gather_lines(got, bins, group), 0))
+        passed = partial[number, :, : len(group) * FACTOR] + dot_split(far, split_bf16(gather_lines(got, bins, group)))
         rows = []
         for index in range(len(group)):
             real = passed[:HALF, index * FACTOR : (index + 1) * FACTOR]
@@ -409,7 +405,7 @@
             rows.append(
                 jnp.concatenate([real * twist_cos + imag * twist_sin, imag * twist_cos - real * twist_sin], axis=1)
             )
-        passed = dot(split_bf16(jnp.concatenate(rows, axis=0), 1), there)
+        passed = dot_split(split_bf16(jnp.concatenate(rows, axis=0)), there)
         for index, bin_num in enumerate(group):
             real = passed[index * HALF : (index + 1) * HALF, :FACTOR]
             imag = passed[index * HALF : (index + 1) * HALF, FACTOR:]
@@ -450,7 +446,7 @@
     scale = 1.0 / (FACTOR * FACTOR)
     cos_table, sin_table = twist_cos * scale, twist_sin * scale
     for at in range(0, last_out - first_out, 4):
-        passed = dot(split_bf16(band[at * HALF : (at + 4) * HALF, :], 1), back)
+        passed = dot_split(split_bf16(band[at * HALF : (at + 4) * HALF, :]), back)
         columns = []
         for index in range(4):
             real = passed[index * HALF : (index + 1) * HALF, :FACTOR]
@@ -458,7 +454,7 @@
             columns.append(
                 jnp.concatenate([real * cos_table - imag * sin_table, imag * cos_table + real * sin_table], axis=0)
             )
-        passed = dot(last, split_bf16(jnp.concatenate(columns, axis=1), 0))
+        passed = dot_split(last, split_bf16(jnp.concatenate(columns, axis=1)))
         for index in range(4):
             lines = slice((at + index) * HALF, (at + index + 1) * HALF)
             keep_out[lines, :] = passed[:HALF, index * FACTOR : (index + 1) * FACTOR]

time: 60.6 us -> 60.2 us (level)
  no operation moved by 1% of the time
where the time goes in v4:
time: 60.2 us; the launch traced here: 60 us
  starting transfers between devices  25.6 us (43%)
  waiting for transfers between devices  24.1 us (40%)
  Pallas kernels  7.72 us (13%)
  local copies, waits for them, and re-layouts  1.72 us (3%)
  between operations  0.81 us (1%)
    ppermute x4, starting transfers between devices, transposed_shards(): lax.ppermute(message, ('az', 'rg'), route)  13.6 us
    ppermute x4, waiting for transfers between devices, transposed_shards(): lax.ppermute(messages[chunk * half + step], ('az', 'rg'), routes[step])  11.4 us
    ppermute x4, waiting for transfers between devices, transposed_shards(): lax.ppermute(message, ('az', 'rg'), route)  10.5 us
    pallas_call x7, Pallas kernels, kernel_call(): pl.pallas_call(body, out_shape=out_shape, in_specs=specs, out_specs=jax.t...  7.72 us
    ppermute x4, starting transfers between devices, transposed_shards(): lax.ppermute(messages[chunk * half + step], ('az', 'rg'), routes[step])  6.32 us
    ppermute x1, starting transfers between devices, transposed_shards(): swap(taps)  3.47 us
  transfers between devices with their start and end apart: 15, of which 7 were waited for; matrix products, arithmetic and copies ran while one was open for 2% of the time, Pallas kernels for 3%

profile of v4, /device:TPU:0, one launch (start us, length us, event | category | flops | bytes accessed | tf_op | source)
XLA Modules:
  0.0 60.0 jit_solution(3202117730627434066)
XLA Ops:
  0.6 0.5 collective-permute-start
  1.2 0.1 collective-permute-start.1
  1.2 0.4 collective-permute-start.2
  1.7 0.1 collective-permute-start.3
  1.8 1.0 %reshape.10.re_lines = f32[512,128]{1,0:T(8,128)S(1)} reshape(f32[32,2048]{1,0:T(8,128)} %param.12) | data formatting | bytes 524288 | tf_op jit(solution)/shard_map/reshape | solution.py:528
  2.8 0.1 collective-permute-done.2.ref_other
  2.9 0.5 copy-done.6
  3.5 0.8 %pack.1 = (f32[488,128]{1,0:T(8,128)S(1)}, f32[488,128]{1,0:T(8,128)S(1)}, f32[488,128]{1,0:T(8,128)S(1)}, f32[488,128]{1,0:T(8,128)S(1)}) custom-call(f32[512,128]{1,0:T(8,128)S(1)} %reshape.10.re_lines, f32[512,128]{1,0:T(8,128)S(1)} %reshape.11.im_lines, f32[32,2048]{1,0:T(8,128)S(1)} %collective-permute-done.re_other, ...), custom_call_target="tpu_custom_call" | custom-call | bytes 4000000 | tf_op jit(solution)/shard_map/pack/pallas_call | solution.py:502
  4.3 4.1 %collective-permute-start.4 = (f32[488,128]{1,0:T(8,128)S(1)}, f32[488,128]{1,0:T(8,128)S(1)}, u32[]{:S(2)}, u32[]{:S(2)}) collective-permute-start(f32[488,128]{1,0:T(8,128)S(1)} %get-tuple-element.21), channel_id=1, source_target_pairs={{0,8},{1,10},{2,9},{3,11},{4,12},{5,14},{6,13},{7,15},{8,0},{9,2},... | collective-permute-start | bytes 749576 | tf_op jit(solution)/shard_map/ppermute | solution.py:567
  8.4 1.3 %collective-permute-start.5 = (f32[488,128]{1,0:T(8,128)S(1)}, f32[488,128]{1,0:T(8,128)S(1)}, u32[]{:S(2)}, u32[]{:S(2)}) collective-permute-start(f32[488,128]{1,0:T(8,128)S(1)} %get-tuple-element.22), channel_id=1, source_target_pairs={{0,12},{1,14},{2,13},{3,15},{4,8},{5,10},{6,9},{7,11},{8,4},{9,6},... | collective-permute-start | bytes 749576 | tf_op jit(solution)/shard_map/ppermute | solution.py:567
  9.8 0.2 collective-permute-start.6
  10.0 0.7 %collective-permute-start.7 = (f32[488,128]{1,0:T(8,128)S(1)}, f32[488,128]{1,0:T(8,128)S(1)}, u32[]{:S(2)}, u32[]{:S(2)}) collective-permute-start(f32[488,128]{1,0:T(8,128)S(1)} %get-tuple-element.24), channel_id=1, source_target_pairs={{0,0},{1,2},{2,1},{3,3},{4,4},{5,6},{6,5},{7,7},{8,8},{9,10},{10,9... | collective-permute-start | bytes 749576 | tf_op jit(solution)/shard_map/ppermute | solution.py:567
  10.7 0.1 copy.14.refs_6_
  10.8 3.5 %collective-permute-start.8 = (f32[32,8]{1,0:T(8,128)S(1)}, f32[32,8]{1,0:T(8,128)S(1)}, u32[]{:S(2)}, u32[]{:S(2)}) collective-permute-start(f32[32,8]{1,0:T(8,128)S(1)} %copy.14.refs_6_), channel_id=1, source_target_pairs={{0,1},{1,0},{2,3},{3,2},{4,5},{5,4},{6,7},{7,6},{8,9},{9,8},{10,11... | collective-permute-start | bytes 3080 | tf_op jit(solution)/shard_map/ppermute | solution.py:526
  14.2 1.3 %phase.1.refs_5_ = f32[15,2,64,128]{3,2,1,0:T(8,128)S(1)} custom-call(s32[2]{0:T(128)S(1)} %copy-done.7, s32[2]{0:T(128)S(1)} %collective-permute-done.3.off_other), custom_call_target="tpu_custom_call" | custom-call | flops 10000000 | bytes 1000000 | tf_op jit(solution)/shard_map/phase/pallas_call | solution.py:502
  15.6 9.9 %collective-permute-done.4.refs_0_ = f32[488,128]{1,0:T(8,128)S(1)} collective-permute-done((f32[488,128]{1,0:T(8,128)S(1)}, f32[488,128]{1,0:T(8,128)S(1)}, u32[]{:S(2)}, u32[]{:S(2)}) %collective-permute-start.4) | collective-permute-done | bytes 249888 | tf_op jit(solution)/shard_map/ppermute | solution.py:567
  25.5 1.5 %collective-permute-done.6.refs_2_ = f32[488,128]{1,0:T(8,128)S(1)} collective-permute-done((f32[488,128]{1,0:T(8,128)S(1)}, f32[488,128]{1,0:T(8,128)S(1)}, u32[]{:S(2)}, u32[]{:S(2)}) %collective-permute-start.6) | collective-permute-done | bytes 249888 | tf_op jit(solution)/shard_map/ppermute | solution.py:567
  27.0 0.7 %parity.1 = (f32[960,128]{1,0:T(8,128)S(1)}, f32[976,128]{1,0:T(8,128)S(1)}, f32[2,8,128]{2,1,0:T(8,128)S(1)}) custom-call(f32[488,128]{1,0:T(8,128)S(1)} %collective-permute-done.4.refs_0_, f32[488,128]{1,0:T(8,128)S(1)} %collective-permute-done.5.refs_1_, f32[488,128]{1,0:T(8,128)S(1)} %collective-permute-done.6.refs_2_, ...), custom_call_target="tpu_custom_call" | custom-call | bytes 1000000 | tf_op jit(solution)/shard_map/parity/pallas_call | solution.py:502
  27.7 0.7 %collective-permute-start.9 = (f32[976,128]{1,0:T(8,128)S(1)}, f32[976,128]{1,0:T(8,128)S(1)}, u32[]{:S(2)}, u32[]{:S(2)}) collective-permute-start(f32[976,128]{1,0:T(8,128)S(1)} %get-tuple-element.30), channel_id=1, source_target_pairs={{0,1},{1,0},{2,3},{3,2},{4,5},{5,4},{6,7},{7,6},{8,9},{9,8},{10,11... | collective-permute-start | bytes 1499144 | tf_op jit(solution)/shard_map/ppermute | solution.py:587
  28.4 0.5 near.2.refs_0_
  28.9 0.9 %collective-permute-done.9.refs_1_.refs_3_ = f32[976,128]{1,0:T(8,128)S(1)} collective-permute-done((f32[976,128]{1,0:T(8,128)S(1)}, f32[976,128]{1,0:T(8,128)S(1)}, u32[]{:S(2)}, u32[]{:S(2)}) %collective-permute-start.9) | collective-permute-done | bytes 499744 | tf_op jit(solution)/shard_map/ppermute | solution.py:587
  29.9 3.4 %band.1 = (f32[512,128]{1,0:T(8,128)S(1)}, f32[512,128]{1,0:T(8,128)S(1)}, f32[15,2,64,128]{3,2,1,0:T(8,128)}) custom-call(f32[4,128,512]{2,1,0:T(8,128)S(1)} %near.2.refs_0_, f32[976,128]{1,0:T(8,128)S(1)} %collective-permute-done.9.refs_1_.refs_3_, f32[2,8,128]{2,1,0:T(8,128)S(1)} %get-tuple-element.31.refs_2_, ...), custom_call_target="tpu_custom_call" | custom-call | flops 1000000000 | bytes 4000000 | tf_op jit(solution)/shard_map/band/pallas_call | solution.py:502
  33.3 0.4 collective-permute-start.10
  33.6 1.2 %collective-permute-done.10.got = f32[512,128]{1,0:T(8,128)S(1)} collective-permute-done((f32[512,128]{1,0:T(8,128)S(1)}, f32[512,128]{1,0:T(8,128)S(1)}, u32[]{:S(2)}, u32[]{:S(2)}) %collective-permute-start.10) | collective-permute-done | bytes 262176 | tf_op jit(solution)/shard_map/ppermute | solution.py:610
  34.8 0.1 join.1
  34.9 0.7 %collective-permute-start.11 = (f32[256,128]{1,0:T(8,128)S(1)}, f32[256,128]{1,0:T(8,128)S(1)}, u32[]{:S(2)}, u32[]{:S(2)}) collective-permute-start(f32[256,128]{1,0:T(8,128)S(1)} %get-tuple-element.36), channel_id=1, source_target_pairs={{0,0},{1,2},{2,4},{3,6},{4,8},{5,10},{6,12},{7,14},{8,1},{9,3},{10... | collective-permute-start | bytes 393224 | tf_op jit(solution)/shard_map/ppermute | solution.py:612
  35.6 9.0 %collective-permute-start.12 = (f32[256,128]{1,0:T(8,128)S(1)}, f32[256,128]{1,0:T(8,128)S(1)}, u32[]{:S(2)}, u32[]{:S(2)}) collective-permute-start(f32[256,128]{1,0:T(8,128)S(1)} %get-tuple-element.37), channel_id=1, source_target_pairs={{0,4},{1,6},{2,0},{3,2},{4,12},{5,14},{6,8},{7,10},{8,5},{9,7},{10... | collective-permute-start | bytes 393224 | tf_op jit(solution)/shard_map/ppermute | solution.py:612
  44.5 2.1 %collective-permute-start.13 = (f32[256,128]{1,0:T(8,128)S(1)}, f32[256,128]{1,0:T(8,128)S(1)}, u32[]{:S(2)}, u32[]{:S(2)}) collective-permute-start(f32[256,128]{1,0:T(8,128)S(1)} %get-tuple-element.38), channel_id=1, source_target_pairs={{0,8},{1,10},{2,12},{3,14},{4,0},{5,2},{6,4},{7,6},{8,9},{9,11},{1... | collective-permute-start | bytes 393224 | tf_op jit(solution)/shard_map/ppermute | solution.py:612
  46.6 1.9 %collective-permute-start.14 = (f32[256,128]{1,0:T(8,128)S(1)}, f32[256,128]{1,0:T(8,128)S(1)}, u32[]{:S(2)}, u32[]{:S(2)}) collective-permute-start(f32[256,128]{1,0:T(8,128)S(1)} %get-tuple-element.39), channel_id=1, source_target_pairs={{0,12},{1,14},{2,8},{3,10},{4,4},{5,6},{6,0},{7,2},{8,13},{9,15},{... | collective-permute-start | bytes 393224 | tf_op jit(solution)/shard_map/ppermute | solution.py:612
  48.6 4.7 %collective-permute-done.13.refs_2_ = f32[256,128]{1,0:T(8,128)S(1)} collective-permute-done((f32[256,128]{1,0:T(8,128)S(1)}, f32[256,128]{1,0:T(8,128)S(1)}, u32[]{:S(2)}, u32[]{:S(2)}) %collective-permute-start.13) | collective-permute-done | bytes 131104 | tf_op jit(solution)/shard_map/ppermute | solution.py:612
  53.3 5.7 %collective-permute-done.14.refs_3_ = f32[256,128]{1,0:T(8,128)S(1)} collective-permute-done((f32[256,128]{1,0:T(8,128)S(1)}, f32[256,128]{1,0:T(8,128)S(1)}, u32[]{:S(2)}, u32[]{:S(2)}) %collective-permute-start.14) | collective-permute-done | bytes 131104 | tf_op jit(solution)/shard_map/ppermute | solution.py:612
  59.0 0.9 %place.1 = (f32[32,2048]{1,0:T(8,128)}, f32[32,2048]{1,0:T(8,128)}) custom-call(f32[256,128]{1,0:T(8,128)S(1)} %collective-permute-done.11.refs_0_, f32[256,128]{1,0:T(8,128)S(1)} %collective-permute-done.12.refs_1_, f32[256,128]{1,0:T(8,128)S(1)} %collective-permute-done.13.refs_2_, f32[256,128]{1,0:T(8,128)S(1)} %collective-permute-done.14.refs_3_), custom_call_target="tpu_custom_call" | custom-call | bytes 1000000 | tf_op jit(solution)/shard_map/place/pallas_call | solution.py:502
  (30 shorter events, 0.1 us)
Async XLA Ops:
  0.6 1.0 %copy-start.7 = (s32[2]{0:T(128)S(1)}, s32[2]{0:T(128)}, u32[]{:S(2)}) copy-start(s32[2]{0:T(128)} %off_own.3) | copy-start | bytes 28
  0.6 2.3 %collective-permute-start = (f32[32,2048]{1,0:T(8,128)}, f32[32,2048]{1,0:T(8,128)S(1)}, u32[]{:S(2)}, u32[]{:S(2)}) collective-permute-start(f32[32,2048]{1,0:T(8,128)} %param.12), channel_id=1, source_target_pairs={{0,1},{1,0},{2,3},{3,2},{4,5},{5,4},{6,7},{7,6},{8,9},{9,8},{10,11... | collective-permute-start | bytes 786440 | tf_op jit(solution)/shard_map/ppermute | solution.py:526
  1.2 1.8 %collective-permute-start.1 = (f32[32,2048]{1,0:T(8,128)}, f32[32,2048]{1,0:T(8,128)S(1)}, u32[]{:S(2)}, u32[]{:S(2)}) collective-permute-start(f32[32,2048]{1,0:T(8,128)} %param.13), channel_id=1, source_target_pairs={{0,1},{1,0},{2,3},{3,2},{4,5},{5,4},{6,7},{7,6},{8,9},{9,8},{10,11... | collective-permute-start | bytes 786440 | tf_op jit(solution)/shard_map/ppermute | solution.py:526
  1.2 1.5 %copy-start.9 = (f32[32,2048]{1,0:T(8,128)S(1)}, f32[32,2048]{1,0:T(8,128)}, u32[]{:S(2)}) copy-start(f32[32,2048]{1,0:T(8,128)} %param.13) | copy-start | bytes 786436
  1.2 1.7 %collective-permute-start.2 = (f32[32,64]{1,0:T(8,128)}, f32[32,64]{1,0:T(8,128)S(1)}, u32[]{:S(2)}, u32[]{:S(2)}) collective-permute-start(f32[32,64]{1,0:T(8,128)} %bitcast.3), channel_id=1, source_target_pairs={{0,1},{1,0},{2,3},{3,2},{4,5},{5,4},{6,7},{7,6},{8,9},{9,8},{10,11... | collective-permute-start | bytes 24584 | tf_op jit(solution)/shard_map/ppermute | solution.py:526
  1.7 1.2 %collective-permute-start.3 = (s32[2]{0:T(128)S(1)}, s32[2]{0:T(128)S(1)}, u32[]{:S(2)}, u32[]{:S(2)}) collective-permute-start(s32[2]{0:T(128)S(1)} %copy-done.7), channel_id=1, source_target_pairs={{0,1},{1,0},{2,3},{3,2},{4,5},{5,4},{6,7},{7,6},{8,9},{9,8},{10,11... | collective-permute-start | bytes 32 | tf_op jit(solution)/shard_map/ppermute | solution.py:525
  2.8 0.7 %copy-start.6 = (f32[1,64,32]{1,2,0:T(8,128)S(1)}, f32[1,64,32]{1,2,0:T(8,128)}, u32[]{:S(2)}) copy-start(f32[1,64,32]{1,2,0:T(8,128)} %param.14) | copy-start | bytes 24580
  4.3 6.3 %copy-start.10 = (f32[32,8]{0,1:T(8,128)S(1)}, f32[32,8]{0,1:T(8,128)}, u32[]{:S(2)}) copy-start(f32[32,8]{0,1:T(8,128)} %param.17) | copy-start | bytes 3076
  4.3 21.2 %collective-permute-start.4 = (f32[488,128]{1,0:T(8,128)S(1)}, f32[488,128]{1,0:T(8,128)S(1)}, u32[]{:S(2)}, u32[]{:S(2)}) collective-permute-start(f32[488,128]{1,0:T(8,128)S(1)} %get-tuple-element.21), channel_id=1, source_target_pairs={{0,8},{1,10},{2,9},{3,11},{4,12},{5,14},{6,13},{7,15},{8,0},{9,2},... | collective-permute-start | bytes 749576 | tf_op jit(solution)/shard_map/ppermute | solution.py:567
  8.4 17.1 %collective-permute-start.5 = (f32[488,128]{1,0:T(8,128)S(1)}, f32[488,128]{1,0:T(8,128)S(1)}, u32[]{:S(2)}, u32[]{:S(2)}) collective-permute-start(f32[488,128]{1,0:T(8,128)S(1)} %get-tuple-element.22), channel_id=1, source_target_pairs={{0,12},{1,14},{2,13},{3,15},{4,8},{5,10},{6,9},{7,11},{8,4},{9,6},... | collective-permute-start | bytes 749576 | tf_op jit(solution)/shard_map/ppermute | solution.py:567
  9.8 17.2 %collective-permute-start.6 = (f32[488,128]{1,0:T(8,128)S(1)}, f32[488,128]{1,0:T(8,128)S(1)}, u32[]{:S(2)}, u32[]{:S(2)}) collective-permute-start(f32[488,128]{1,0:T(8,128)S(1)} %get-tuple-element.23), channel_id=1, source_target_pairs={{0,4},{1,6},{2,5},{3,7},{4,0},{5,2},{6,1},{7,3},{8,12},{9,14},{10,... | collective-permute-start | bytes 749576 | tf_op jit(solution)/shard_map/ppermute | solution.py:567
  10.0 17.0 %collective-permute-start.7 = (f32[488,128]{1,0:T(8,128)S(1)}, f32[488,128]{1,0:T(8,128)S(1)}, u32[]{:S(2)}, u32[]{:S(2)}) collective-permute-start(f32[488,128]{1,0:T(8,128)S(1)} %get-tuple-element.24), channel_id=1, source_target_pairs={{0,0},{1,2},{2,1},{3,3},{4,4},{5,6},{6,5},{7,7},{8,8},{9,10},{10,9... | collective-permute-start | bytes 749576 | tf_op jit(solution)/shard_map/ppermute | solution.py:567
  10.8 16.2 %copy-start.8 = (s32[2]{0:T(128)S(1)}, s32[2]{0:T(128)}, u32[]{:S(2)}) copy-start(s32[2]{0:T(128)} %refs_4_.3) | copy-start | bytes 28
  10.8 4.8 %collective-permute-start.8 = (f32[32,8]{1,0:T(8,128)S(1)}, f32[32,8]{1,0:T(8,128)S(1)}, u32[]{:S(2)}, u32[]{:S(2)}) collective-permute-start(f32[32,8]{1,0:T(8,128)S(1)} %copy.14.refs_6_), channel_id=1, source_target_pairs={{0,1},{1,0},{2,3},{3,2},{4,5},{5,4},{6,7},{7,6},{8,9},{9,8},{10,11... | collective-permute-start | bytes 3080 | tf_op jit(solution)/shard_map/ppermute | solution.py:526
  15.5 12.8 %copy-start.5 = (bf16[2,2,128,64]{3,2,1,0:T(8,128)(2,1)S(1)}, bf16[2,2,128,64]{3,2,1,0:T(8,128)(2,1)}, u32[]{:S(2)}) copy-start(bf16[2,2,128,64]{3,2,1,0:T(8,128)(2,1)} %constant.12.clone.near) | copy-start | bytes 196612
  27.7 2.2 %collective-permute-start.9 = (f32[976,128]{1,0:T(8,128)S(1)}, f32[976,128]{1,0:T(8,128)S(1)}, u32[]{:S(2)}, u32[]{:S(2)}) collective-permute-start(f32[976,128]{1,0:T(8,128)S(1)} %get-tuple-element.30), channel_id=1, source_target_pairs={{0,1},{1,0},{2,3},{3,2},{4,5},{5,4},{6,7},{7,6},{8,9},{9,8},{10,11... | collective-permute-start | bytes 1499144 | tf_op jit(solution)/shard_map/ppermute | solution.py:587
  28.4 1.5 %copy-start = (bf16[2,256,256]{2,1,0:T(8,128)(2,1)S(1)}, bf16[2,256,256]{2,1,0:T(8,128)(2,1)}, u32[]{:S(2)}) copy-start(bf16[2,256,256]{2,1,0:T(8,128)(2,1)} %constant.15.clone.refs_10_) | copy-start | bytes 786436
  28.4 1.5 %copy-start.1 = (bf16[2,256,256]{2,1,0:T(8,128)(2,1)S(1)}, bf16[2,256,256]{2,1,0:T(8,128)(2,1)}, u32[]{:S(2)}) copy-start(bf16[2,256,256]{2,1,0:T(8,128)(2,1)} %constant.14.clone.refs_9_) | copy-start | bytes 786436
  28.4 1.5 %copy-start.2 = (f32[2,2,64,128]{3,2,1,0:T(8,128)S(1)}, f32[2,2,64,128]{3,2,1,0:T(8,128)}, u32[]{:S(2)}) copy-start(f32[2,2,64,128]{3,2,1,0:T(8,128)} %constant.17.clone.refs_12_) | copy-start | bytes 393220
  28.4 1.5 %copy-start.3 = (bf16[2,2,128,128]{3,2,1,0:T(8,128)(2,1)S(1)}, bf16[2,2,128,128]{3,2,1,0:T(8,128)(2,1)}, u32[]{:S(2)}) copy-start(bf16[2,2,128,128]{3,2,1,0:T(8,128)(2,1)} %constant.16.clone.refs_11_) | copy-start | bytes 393220
  28.4 1.5 %copy-start.4 = (bf16[2,2,128,64]{3,2,1,0:T(8,128)(2,1)S(1)}, bf16[2,2,128,64]{3,2,1,0:T(8,128)(2,1)}, u32[]{:S(2)}) copy-start(bf16[2,2,128,64]{3,2,1,0:T(8,128)(2,1)} %constant.13.clone.refs_8_) | copy-start | bytes 196612
  33.3 1.5 %collective-permute-start.10 = (f32[512,128]{1,0:T(8,128)S(1)}, f32[512,128]{1,0:T(8,128)S(1)}, u32[]{:S(2)}, u32[]{:S(2)}) collective-permute-start(f32[512,128]{1,0:T(8,128)S(1)} %get-tuple-element.35), channel_id=1, source_target_pairs={{0,1},{1,0},{2,3},{3,2},{4,5},{5,4},{6,7},{7,6},{8,9},{9,8},{10,11... | collective-permute-start | bytes 786440 | tf_op jit(solution)/shard_map/ppermute | solution.py:610
  34.9 13.7 %collective-permute-start.11 = (f32[256,128]{1,0:T(8,128)S(1)}, f32[256,128]{1,0:T(8,128)S(1)}, u32[]{:S(2)}, u32[]{:S(2)}) collective-permute-start(f32[256,128]{1,0:T(8,128)S(1)} %get-tuple-element.36), channel_id=1, source_target_pairs={{0,0},{1,2},{2,4},{3,6},{4,8},{5,10},{6,12},{7,14},{8,1},{9,3},{10... | collective-permute-start | bytes 393224 | tf_op jit(solution)/shard_map/ppermute | solution.py:612
  35.6 13.0 %collective-permute-start.12 = (f32[256,128]{1,0:T(8,128)S(1)}, f32[256,128]{1,0:T(8,128)S(1)}, u32[]{:S(2)}, u32[]{:S(2)}) collective-permute-start(f32[256,128]{1,0:T(8,128)S(1)} %get-tuple-element.37), channel_id=1, source_target_pairs={{0,4},{1,6},{2,0},{3,2},{4,12},{5,14},{6,8},{7,10},{8,5},{9,7},{10... | collective-permute-start | bytes 393224 | tf_op jit(solution)/shard_map/ppermute | solution.py:612
  44.5 8.8 %collective-permute-start.13 = (f32[256,128]{1,0:T(8,128)S(1)}, f32[256,128]{1,0:T(8,128)S(1)}, u32[]{:S(2)}, u32[]{:S(2)}) collective-permute-start(f32[256,128]{1,0:T(8,128)S(1)} %get-tuple-element.38), channel_id=1, source_target_pairs={{0,8},{1,10},{2,12},{3,14},{4,0},{5,2},{6,4},{7,6},{8,9},{9,11},{1... | collective-permute-start | bytes 393224 | tf_op jit(solution)/shard_map/ppermute | solution.py:612
  46.6 12.4 %collective-permute-start.14 = (f32[256,128]{1,0:T(8,128)S(1)}, f32[256,128]{1,0:T(8,128)S(1)}, u32[]{:S(2)}, u32[]{:S(2)}) collective-permute-start(f32[256,128]{1,0:T(8,128)S(1)} %get-tuple-element.39), channel_id=1, source_target_pairs={{0,12},{1,14},{2,8},{3,10},{4,4},{5,6},{6,0},{7,2},{8,13},{9,15},{... | collective-permute-start | bytes 393224 | tf_op jit(solution)/shard_map/ppermute | solution.py:612

commit v5 on v4

--- a/solution.py
+++ b/solution.py
@@ -180,14 +180,27 @@
     return high, low
 
 
+def dot(left, right):
+    return jnp.dot(left, right, preferred_element_type=jnp.float32)
+
+
 def dot_split(left, right):
-    dot = functools.partial(jnp.dot, preferred_element_type=jnp.float32)
     return dot(left[0], right[0]) + (dot(left[0], right[1]) + dot(left[1], right[0]))
 
 
 def both_bf16(matrix):
     high = matrix.astype(jnp.bfloat16)
     return np.stack([high, (matrix - high.astype(np.float64)).astype(jnp.bfloat16)])
+
+
+def long_bf16(matrix):
+    high, low = both_bf16(matrix)
+    return np.concatenate([high, high, low], axis=-1)
+
+
+def long_rows(value):
+    high, low = split_bf16(value)
+    return jnp.concatenate([high, low, high], axis=0)
 
 
 def dft_constants():
@@ -213,11 +226,11 @@
     there = np.block([[cosine, -sine], [sine, cosine]])
     back = np.block([[cosine, sine], [-sine, cosine]])
     matrices = [
-        both_bf16(np.stack(near)),
-        both_bf16(np.stack(far)),
+        long_bf16(np.stack(near)),
+        long_bf16(np.stack(far)),
         both_bf16(there),
         both_bf16(back),
-        both_bf16(np.stack(last)),
+        long_bf16(np.stack(last)),
     ]
     return matrices, np.stack(twists).astype(np.float32)
 
@@ -323,15 +336,15 @@
     even = side == 0
     keep_near, keep_far = jnp.where(even, 1.0, sign), jnp.where(even, 1.0, -sign)
     give_near, give_far = jnp.where(even, sign, 1.0), jnp.where(even, -sign, 1.0)
-    middle = (place >> 1) & 1
-    for step in range(2):
-        near, far = chunks[step], chunks[step + 2]
-        for line in range(2 * bins):
-            read = slice(line * PART, (line + 1) * PART)
-            write = pl.ds(pl.multiple_of(line * 2 * PART + (middle ^ step) * PART, 8), PART)
-            near_value, far_value = near[read, :], far[read, :]
-            keep[write, :] = near_value * keep_near + far_value * keep_far
-            give[write, :] = near_value * give_near + far_value * give_far
+    plain = ((place >> 1) & 1) == 0
+    for line in range(2 * bins):
+        read = slice(line * PART, (line + 1) * PART)
+        write = line * 2 * PART
+        values = [chunks[step][read, :] for step in range(4)]
+        for target, near_factor, far_factor in ((keep, keep_near, keep_far), (give, give_near, give_far)):
+            pair = [values[step] * near_factor + values[step + 2] * far_factor for step in range(2)]
+            target[write : write + PART, :] = jnp.where(plain, pair[0], pair[1])
+            target[write + PART : write + 2 * PART, :] = jnp.where(plain, pair[1], pair[0])
     if has_ref:
         for which in range(2):
             step = (owners[which] >> 1) ^ (place >> 1)
@@ -358,10 +371,9 @@
 
 
 def near_kernel(bins, keep, near, out):
-    side = lax.axis_index("rg")
-    matrix = (near[0, side], near[1, side])
+    matrix = near[lax.axis_index("rg")]
     for index, group in enumerate(bin_groups(bins)):
-        out[index, :, : len(group) * FACTOR] = dot_split(matrix, split_bf16(gather_lines(keep, bins, group)))
+        out[index, :, : len(group) * FACTOR] = dot(matrix, long_rows(gather_lines(keep, bins, group)))
 
 
 def band_kernel(chunk, *refs):
@@ -393,11 +405,11 @@
         picked[0, block * REF_LINES : (block + 1) * REF_LINES, :] = ref_cos
         picked[1, block * REF_LINES : (block + 1) * REF_LINES, :] = ref_sin
 
-    far, last = (far[0, side], far[1, side]), (last[0, side], last[1, side])
+    far, last = far[side], last[side]
     there, back = (there[0], there[1]), (back[0], back[1])
     twist_cos, twist_sin = twists[side, 0], twists[side, 1]
     for number, group in enumerate(bin_groups(bins)):
-        passed = partial[number, :, : len(group) * FACTOR] + dot_split(far, split_bf16(gather_lines(got, bins, group)))
+        passed = partial[number, :, : len(group) * FACTOR] + dot(far, long_rows(gather_lines(got, bins, group)))
         rows = []
         for index in range(len(group)):
             real = passed[:HALF, index * FACTOR : (index + 1) * FACTOR]
@@ -454,11 +466,15 @@
             columns.append(
                 jnp.concatenate([real * cos_table - imag * sin_table, imag * cos_table + real * sin_table], axis=0)
             )
-        passed = dot_split(last, split_bf16(jnp.concatenate(columns, axis=1)))
+        passed = dot(last, long_rows(jnp.concatenate(columns, axis=1)))
         for index in range(4):
             lines = slice((at + index) * HALF, (at + index + 1) * HALF)
             keep_out[lines, :] = passed[:HALF, index * FACTOR : (index + 1) * FACTOR]
             give_out[lines, :] = passed[HALF:, index * FACTOR : (index + 1) * FACTOR]
+
+
+def crossed(quarter):
+    return ((quarter & 1) << 1) | (quarter >> 1)
 
 
 def join_kernel(outs, keep, got, *messages):
@@ -466,7 +482,7 @@
     quarter = lax.rem(place, PLACES // 2)
     sign = jnp.where(side == 0, 1.0, -1.0)
     for step, message in enumerate(messages):
-        target = quarter ^ step
+        target = crossed(quarter) ^ step
         top, middle = target >> 1, target & 1
         keep_factor, got_factor = jnp.where(top == 0, 1.0, sign), jnp.where(top == 0, 1.0, -sign)
         for line in range(2 * outs):
@@ -479,7 +495,7 @@
     bins, samples = out_re.shape
     place = lax.axis_index("az")
     for at, message in enumerate(messages):
-        sender = (place >> 1) ^ (at % (PLACES // 2))
+        sender = crossed((place >> 1) ^ (at % (PLACES // 2)))
         _, (first_out, last_out) = CHUNKS[at // (PLACES // 2)]
         for out in range(last_out - first_out):
             line = pl.multiple_of((sender * OUT_BINS + first_out + out) * PART, 8)
@@ -557,7 +573,7 @@
     ]
     routes_back = [
         [
-            (chip * 2 + core, (((chip % half) ^ step) * 2 + core) * 2 + chip // half)
+            (chip * 2 + core, ((crossed(chip % half) ^ step) * 2 + core) * 2 + chip // half)
             for chip in range(PLACES)
             for core in range(2)
         ]

time: 60.2 us -> 57.6 us (0.957)
  the two profiles are of different devices: /device:TPU:0 before, /device:TPU:13 now
where the time goes in v5:
time: 57.6 us; the launch traced here: 57.3 us
  waiting for transfers between devices  29.9 us (52%)
  starting transfers between devices  17.2 us (30%)
  Pallas kernels  7.71 us (13%)
  local copies, waits for them, and re-layouts  1.72 us (3%)
  between operations  0.81 us (1%)
    ppermute x4, waiting for transfers between devices, transposed_shards(): lax.ppermute(messages[chunk * half + step], ('az', 'rg'), routes[step])  15.5 us
    ppermute x4, waiting for transfers between devices, transposed_shards(): lax.ppermute(message, ('az', 'rg'), route)  11.9 us
    ppermute x4, starting transfers between devices, transposed_shards(): lax.ppermute(messages[chunk * half + step], ('az', 'rg'), routes[step])  8.24 us
    pallas_call x7, Pallas kernels, kernel_call(): pl.pallas_call(body, out_shape=out_shape, in_specs=specs, out_specs=jax.t...  7.71 us
    ppermute x4, starting transfers between devices, transposed_shards(): lax.ppermute(message, ('az', 'rg'), route)  6.84 us
    ppermute x1, waiting for transfers between devices, transposed_shards(): got = swap(give)  1.21 us
    ppermute x1, waiting for transfers between devices, transposed_shards(): swap(give)  1.2 us
  transfers between devices with their start and end apart: 15, of which 8 were waited for; matrix products, arithmetic and copies ran while one was open for 2% of the time, Pallas kernels for 3%

profile of v5, /device:TPU:13, one launch (start us, length us, event | category | flops | bytes accessed | tf_op | source)
XLA Modules:
  0.0 57.3 jit_solution(6723756855978500257)
XLA Ops:
  0.6 0.7 %collective-permute-start = (f32[32,2048]{1,0:T(8,128)}, f32[32,2048]{1,0:T(8,128)S(1)}, u32[]{:S(2)}, u32[]{:S(2)}) collective-permute-start(f32[32,2048]{1,0:T(8,128)} %param.12), channel_id=1, source_target_pairs={{0,1},{1,0},{2,3},{3,2},{4,5},{5,4},{6,7},{7,6},{8,9},{9,8},{10,11... | collective-permute-start | bytes 786440 | tf_op jit(solution)/shard_map/ppermute | solution.py:542
  1.4 0.1 collective-permute-start.1
  1.5 0.4 collective-permute-start.2
  1.9 0.1 collective-permute-start.3
  2.0 1.0 %reshape.10.re_lines = f32[512,128]{1,0:T(8,128)S(1)} reshape(f32[32,2048]{1,0:T(8,128)} %param.12) | data formatting | bytes 524288 | tf_op jit(solution)/shard_map/reshape | solution.py:544
  3.1 0.1 collective-permute-done.2.ref_other
  3.2 0.5 copy-done.6
  3.7 0.8 %pack.1 = (f32[488,128]{1,0:T(8,128)S(1)}, f32[488,128]{1,0:T(8,128)S(1)}, f32[488,128]{1,0:T(8,128)S(1)}, f32[488,128]{1,0:T(8,128)S(1)}) custom-call(f32[512,128]{1,0:T(8,128)S(1)} %reshape.10.re_lines, f32[512,128]{1,0:T(8,128)S(1)} %reshape.11.im_lines, f32[32,2048]{1,0:T(8,128)S(1)} %collective-permute-done.re_other, ...), custom_call_target="tpu_custom_call" | custom-call | bytes 4000000 | tf_op jit(solution)/shard_map/pack/pallas_call | solution.py:518
  4.6 3.6 %collective-permute-start.4 = (f32[488,128]{1,0:T(8,128)S(1)}, f32[488,128]{1,0:T(8,128)S(1)}, u32[]{:S(2)}, u32[]{:S(2)}) collective-permute-start(f32[488,128]{1,0:T(8,128)S(1)} %get-tuple-element.21), channel_id=1, source_target_pairs={{0,8},{1,10},{2,9},{3,11},{4,12},{5,14},{6,13},{7,15},{8,0},{9,2},... | collective-permute-start | bytes 749576 | tf_op jit(solution)/shard_map/ppermute | solution.py:583
  8.2 2.4 %collective-permute-start.6 = (f32[488,128]{1,0:T(8,128)S(1)}, f32[488,128]{1,0:T(8,128)S(1)}, u32[]{:S(2)}, u32[]{:S(2)}) collective-permute-start(f32[488,128]{1,0:T(8,128)S(1)} %get-tuple-element.23), channel_id=1, source_target_pairs={{0,4},{1,6},{2,5},{3,7},{4,0},{5,2},{6,1},{7,3},{8,12},{9,14},{10,... | collective-permute-start | bytes 749576 | tf_op jit(solution)/shard_map/ppermute | solution.py:583
  10.6 2.2 %collective-permute-start.7 = (f32[488,128]{1,0:T(8,128)S(1)}, f32[488,128]{1,0:T(8,128)S(1)}, u32[]{:S(2)}, u32[]{:S(2)}) collective-permute-start(f32[488,128]{1,0:T(8,128)S(1)} %get-tuple-element.24), channel_id=1, source_target_pairs={{0,0},{1,2},{2,1},{3,3},{4,4},{5,6},{6,5},{7,7},{8,8},{9,10},{10,9... | collective-permute-start | bytes 749576 | tf_op jit(solution)/shard_map/ppermute | solution.py:583
  12.8 0.1 copy.14.refs_6_
  12.9 0.0 collective-permute-start.8
  12.9 1.3 %phase.1.refs_5_ = f32[15,2,64,128]{3,2,1,0:T(8,128)S(1)} custom-call(s32[2]{0:T(128)S(1)} %copy-done.7, s32[2]{0:T(128)S(1)} %collective-permute-done.3.off_other), custom_call_target="tpu_custom_call" | custom-call | flops 10000000 | bytes 1000000 | tf_op jit(solution)/shard_map/phase/pallas_call | solution.py:518
  14.2 0.0 copy-start.5
  14.3 10.1 %collective-permute-done.4.refs_0_ = f32[488,128]{1,0:T(8,128)S(1)} collective-permute-done((f32[488,128]{1,0:T(8,128)S(1)}, f32[488,128]{1,0:T(8,128)S(1)}, u32[]{:S(2)}, u32[]{:S(2)}) %collective-permute-start.4) | collective-permute-done | bytes 249888 | tf_op jit(solution)/shard_map/ppermute | solution.py:583
  24.4 5.4 %collective-permute-done.5.refs_1_ = f32[488,128]{1,0:T(8,128)S(1)} collective-permute-done((f32[488,128]{1,0:T(8,128)S(1)}, f32[488,128]{1,0:T(8,128)S(1)}, u32[]{:S(2)}, u32[]{:S(2)}) %collective-permute-start.5) | collective-permute-done | bytes 249888 | tf_op jit(solution)/shard_map/ppermute | solution.py:583
  29.7 0.7 %parity.1 = (f32[960,128]{1,0:T(8,128)S(1)}, f32[976,128]{1,0:T(8,128)S(1)}, f32[2,8,128]{2,1,0:T(8,128)S(1)}) custom-call(f32[488,128]{1,0:T(8,128)S(1)} %collective-permute-done.4.refs_0_, f32[488,128]{1,0:T(8,128)S(1)} %collective-permute-done.5.refs_1_, f32[488,128]{1,0:T(8,128)S(1)} %collective-permute-done.6.refs_2_, ...), custom_call_target="tpu_custom_call" | custom-call | bytes 1000000 | tf_op jit(solution)/shard_map/parity/pallas_call | solution.py:518
  30.4 0.4 collective-permute-start.9
  30.9 0.3 near.2.refs_0_
  31.2 1.2 %collective-permute-done.9.refs_1_.refs_3_ = f32[976,128]{1,0:T(8,128)S(1)} collective-permute-done((f32[976,128]{1,0:T(8,128)S(1)}, f32[976,128]{1,0:T(8,128)S(1)}, u32[]{:S(2)}, u32[]{:S(2)}) %collective-permute-start.9) | collective-permute-done | bytes 499744 | tf_op jit(solution)/shard_map/ppermute | solution.py:603
  32.4 3.6 %band.1 = (f32[512,128]{1,0:T(8,128)S(1)}, f32[512,128]{1,0:T(8,128)S(1)}, f32[15,2,64,128]{3,2,1,0:T(8,128)}) custom-call(f32[4,128,512]{2,1,0:T(8,128)S(1)} %near.2.refs_0_, f32[976,128]{1,0:T(8,128)S(1)} %collective-permute-done.9.refs_1_.refs_3_, f32[2,8,128]{2,1,0:T(8,128)S(1)} %get-tuple-element.31.refs_2_, ...), custom_call_target="tpu_custom_call" | custom-call | flops 1000000000 | bytes 4000000 | tf_op jit(solution)/shard_map/band/pallas_call | solution.py:518
  36.0 0.3 collective-permute-start.10
  36.3 1.2 %collective-permute-done.10.got = f32[512,128]{1,0:T(8,128)S(1)} collective-permute-done((f32[512,128]{1,0:T(8,128)S(1)}, f32[512,128]{1,0:T(8,128)S(1)}, u32[]{:S(2)}, u32[]{:S(2)}) %collective-permute-start.10) | collective-permute-done | bytes 262176 | tf_op jit(solution)/shard_map/ppermute | solution.py:626
  37.5 0.1 join.1
  37.6 3.2 %collective-permute-start.11 = (f32[256,128]{1,0:T(8,128)S(1)}, f32[256,128]{1,0:T(8,128)S(1)}, u32[]{:S(2)}, u32[]{:S(2)}) collective-permute-start(f32[256,128]{1,0:T(8,128)S(1)} %get-tuple-element.36), channel_id=1, source_target_pairs={{0,0},{1,2},{2,8},{3,10},{4,4},{5,6},{6,12},{7,14},{8,1},{9,3},{10... | collective-permute-start | bytes 393224 | tf_op jit(solution)/shard_map/ppermute | solution.py:628
  40.8 3.5 %collective-permute-start.12 = (f32[256,128]{1,0:T(8,128)S(1)}, f32[256,128]{1,0:T(8,128)S(1)}, u32[]{:S(2)}, u32[]{:S(2)}) collective-permute-start(f32[256,128]{1,0:T(8,128)S(1)} %get-tuple-element.37), channel_id=1, source_target_pairs={{0,4},{1,6},{2,12},{3,14},{4,0},{5,2},{6,8},{7,10},{8,5},{9,7},{10... | collective-permute-start | bytes 393224 | tf_op jit(solution)/shard_map/ppermute | solution.py:628
  44.4 0.1 collective-permute-start.14
  44.5 1.6 %collective-permute-done.11.refs_0_ = f32[256,128]{1,0:T(8,128)S(1)} collective-permute-done((f32[256,128]{1,0:T(8,128)S(1)}, f32[256,128]{1,0:T(8,128)S(1)}, u32[]{:S(2)}, u32[]{:S(2)}) %collective-permute-start.11) | collective-permute-done | bytes 131104 | tf_op jit(solution)/shard_map/ppermute | solution.py:628
  46.1 7.8 %collective-permute-done.12.refs_1_ = f32[256,128]{1,0:T(8,128)S(1)} collective-permute-done((f32[256,128]{1,0:T(8,128)S(1)}, f32[256,128]{1,0:T(8,128)S(1)}, u32[]{:S(2)}, u32[]{:S(2)}) %collective-permute-start.12) | collective-permute-done | bytes 131104 | tf_op jit(solution)/shard_map/ppermute | solution.py:628
  53.9 2.5 %collective-permute-done.14.refs_3_ = f32[256,128]{1,0:T(8,128)S(1)} collective-permute-done((f32[256,128]{1,0:T(8,128)S(1)}, f32[256,128]{1,0:T(8,128)S(1)}, u32[]{:S(2)}, u32[]{:S(2)}) %collective-permute-start.14) | collective-permute-done | bytes 131104 | tf_op jit(solution)/shard_map/ppermute | solution.py:628
  56.4 0.9 %place.1 = (f32[32,2048]{1,0:T(8,128)}, f32[32,2048]{1,0:T(8,128)}) custom-call(f32[256,128]{1,0:T(8,128)S(1)} %collective-permute-done.11.refs_0_, f32[256,128]{1,0:T(8,128)S(1)} %collective-permute-done.12.refs_1_, f32[256,128]{1,0:T(8,128)S(1)} %collective-permute-done.13.refs_2_, f32[256,128]{1,0:T(8,128)S(1)} %collective-permute-done.14.refs_3_), custom_call_target="tpu_custom_call" | custom-call | bytes 1000000 | tf_op jit(solution)/shard_map/place/pallas_call | solution.py:518
  (30 shorter events, 0.1 us)
Async XLA Ops:
  0.6 1.3 %copy-start.7 = (s32[2]{0:T(128)S(1)}, s32[2]{0:T(128)}, u32[]{:S(2)}) copy-start(s32[2]{0:T(128)} %off_own.3) | copy-start | bytes 28
  0.6 2.5 %collective-permute-start = (f32[32,2048]{1,0:T(8,128)}, f32[32,2048]{1,0:T(8,128)S(1)}, u32[]{:S(2)}, u32[]{:S(2)}) collective-permute-start(f32[32,2048]{1,0:T(8,128)} %param.12), channel_id=1, source_target_pairs={{0,1},{1,0},{2,3},{3,2},{4,5},{5,4},{6,7},{7,6},{8,9},{9,8},{10,11... | collective-permute-start | bytes 786440 | tf_op jit(solution)/shard_map/ppermute | solution.py:542
  1.4 1.8 %collective-permute-start.1 = (f32[32,2048]{1,0:T(8,128)}, f32[32,2048]{1,0:T(8,128)S(1)}, u32[]{:S(2)}, u32[]{:S(2)}) collective-permute-start(f32[32,2048]{1,0:T(8,128)} %param.13), channel_id=1, source_target_pairs={{0,1},{1,0},{2,3},{3,2},{4,5},{5,4},{6,7},{7,6},{8,9},{9,8},{10,11... | collective-permute-start | bytes 786440 | tf_op jit(solution)/shard_map/ppermute | solution.py:542
  1.5 1.5 %copy-start.9 = (f32[32,2048]{1,0:T(8,128)S(1)}, f32[32,2048]{1,0:T(8,128)}, u32[]{:S(2)}) copy-start(f32[32,2048]{1,0:T(8,128)} %param.13) | copy-start | bytes 786436
  1.5 1.7 %collective-permute-start.2 = (f32[32,64]{1,0:T(8,128)}, f32[32,64]{1,0:T(8,128)S(1)}, u32[]{:S(2)}, u32[]{:S(2)}) collective-permute-start(f32[32,64]{1,0:T(8,128)} %bitcast.3), channel_id=1, source_target_pairs={{0,1},{1,0},{2,3},{3,2},{4,5},{5,4},{6,7},{7,6},{8,9},{9,8},{10,11... | collective-permute-start | bytes 24584 | tf_op jit(solution)/shard_map/ppermute | solution.py:542
  1.9 1.2 %collective-permute-start.3 = (s32[2]{0:T(128)S(1)}, s32[2]{0:T(128)S(1)}, u32[]{:S(2)}, u32[]{:S(2)}) collective-permute-start(s32[2]{0:T(128)S(1)} %copy-done.7), channel_id=1, source_target_pairs={{0,1},{1,0},{2,3},{3,2},{4,5},{5,4},{6,7},{7,6},{8,9},{9,8},{10,11... | collective-permute-start | bytes 32 | tf_op jit(solution)/shard_map/ppermute | solution.py:541
  3.0 0.7 %copy-start.6 = (f32[1,64,32]{1,2,0:T(8,128)S(1)}, f32[1,64,32]{1,2,0:T(8,128)}, u32[]{:S(2)}) copy-start(f32[1,64,32]{1,2,0:T(8,128)} %param.14) | copy-start | bytes 24580
  4.5 8.3 %copy-start.10 = (f32[32,8]{0,1:T(8,128)S(1)}, f32[32,8]{0,1:T(8,128)}, u32[]{:S(2)}) copy-start(f32[32,8]{0,1:T(8,128)} %param.17) | copy-start | bytes 3076
  4.6 19.8 %collective-permute-start.4 = (f32[488,128]{1,0:T(8,128)S(1)}, f32[488,128]{1,0:T(8,128)S(1)}, u32[]{:S(2)}, u32[]{:S(2)}) collective-permute-start(f32[488,128]{1,0:T(8,128)S(1)} %get-tuple-element.21), channel_id=1, source_target_pairs={{0,8},{1,10},{2,9},{3,11},{4,12},{5,14},{6,13},{7,15},{8,0},{9,2},... | collective-permute-start | bytes 749576 | tf_op jit(solution)/shard_map/ppermute | solution.py:583
  8.2 21.5 %collective-permute-start.5 = (f32[488,128]{1,0:T(8,128)S(1)}, f32[488,128]{1,0:T(8,128)S(1)}, u32[]{:S(2)}, u32[]{:S(2)}) collective-permute-start(f32[488,128]{1,0:T(8,128)S(1)} %get-tuple-element.22), channel_id=1, source_target_pairs={{0,12},{1,14},{2,13},{3,15},{4,8},{5,10},{6,9},{7,11},{8,4},{9,6},... | collective-permute-start | bytes 749576 | tf_op jit(solution)/shard_map/ppermute | solution.py:583
  8.2 21.5 %collective-permute-start.6 = (f32[488,128]{1,0:T(8,128)S(1)}, f32[488,128]{1,0:T(8,128)S(1)}, u32[]{:S(2)}, u32[]{:S(2)}) collective-permute-start(f32[488,128]{1,0:T(8,128)S(1)} %get-tuple-element.23), channel_id=1, source_target_pairs={{0,4},{1,6},{2,5},{3,7},{4,0},{5,2},{6,1},{7,3},{8,12},{9,14},{10,... | collective-permute-start | bytes 749576 | tf_op jit(solution)/shard_map/ppermute | solution.py:583
  10.6 19.1 %collective-permute-start.7 = (f32[488,128]{1,0:T(8,128)S(1)}, f32[488,128]{1,0:T(8,128)S(1)}, u32[]{:S(2)}, u32[]{:S(2)}) collective-permute-start(f32[488,128]{1,0:T(8,128)S(1)} %get-tuple-element.24), channel_id=1, source_target_pairs={{0,0},{1,2},{2,1},{3,3},{4,4},{5,6},{6,5},{7,7},{8,8},{9,10},{10,9... | collective-permute-start | bytes 749576 | tf_op jit(solution)/shard_map/ppermute | solution.py:583
  12.9 16.8 %copy-start.8 = (s32[2]{0:T(128)S(1)}, s32[2]{0:T(128)}, u32[]{:S(2)}) copy-start(s32[2]{0:T(128)} %refs_4_.3) | copy-start | bytes 28
  12.9 1.3 %collective-permute-start.8 = (f32[32,8]{1,0:T(8,128)S(1)}, f32[32,8]{1,0:T(8,128)S(1)}, u32[]{:S(2)}, u32[]{:S(2)}) collective-permute-start(f32[32,8]{1,0:T(8,128)S(1)} %copy.14.refs_6_), channel_id=1, source_target_pairs={{0,1},{1,0},{2,3},{3,2},{4,5},{5,4},{6,7},{7,6},{8,9},{9,8},{10,11... | collective-permute-start | bytes 3080 | tf_op jit(solution)/shard_map/ppermute | solution.py:542
  14.2 16.6 %copy-start.5 = (bf16[2,128,192]{2,1,0:T(8,128)(2,1)S(1)}, bf16[2,128,192]{2,1,0:T(8,128)(2,1)}, u32[]{:S(2)}) copy-start(bf16[2,128,192]{2,1,0:T(8,128)(2,1)} %constant.12.clone.near) | copy-start | bytes 294916
  30.4 1.9 %collective-permute-start.9 = (f32[976,128]{1,0:T(8,128)S(1)}, f32[976,128]{1,0:T(8,128)S(1)}, u32[]{:S(2)}, u32[]{:S(2)}) collective-permute-start(f32[976,128]{1,0:T(8,128)S(1)} %get-tuple-element.30), channel_id=1, source_target_pairs={{0,1},{1,0},{2,3},{3,2},{4,5},{5,4},{6,7},{7,6},{8,9},{9,8},{10,11... | collective-permute-start | bytes 1499144 | tf_op jit(solution)/shard_map/ppermute | solution.py:603
  30.8 1.5 %copy-start = (bf16[2,256,256]{2,1,0:T(8,128)(2,1)S(1)}, bf16[2,256,256]{2,1,0:T(8,128)(2,1)}, u32[]{:S(2)}) copy-start(bf16[2,256,256]{2,1,0:T(8,128)(2,1)} %constant.15.clone.refs_10_) | copy-start | bytes 786436
  30.8 1.5 %copy-start.1 = (bf16[2,256,256]{2,1,0:T(8,128)(2,1)S(1)}, bf16[2,256,256]{2,1,0:T(8,128)(2,1)}, u32[]{:S(2)}) copy-start(bf16[2,256,256]{2,1,0:T(8,128)(2,1)} %constant.14.clone.refs_9_) | copy-start | bytes 786436
  30.8 1.5 %copy-start.2 = (bf16[2,128,384]{2,1,0:T(8,128)(2,1)S(1)}, bf16[2,128,384]{2,1,0:T(8,128)(2,1)}, u32[]{:S(2)}) copy-start(bf16[2,128,384]{2,1,0:T(8,128)(2,1)} %constant.16.clone.refs_11_) | copy-start | bytes 589828
  30.8 1.5 %copy-start.3 = (f32[2,2,64,128]{3,2,1,0:T(8,128)S(1)}, f32[2,2,64,128]{3,2,1,0:T(8,128)}, u32[]{:S(2)}) copy-start(f32[2,2,64,128]{3,2,1,0:T(8,128)} %constant.17.clone.refs_12_) | copy-start | bytes 393220
  30.9 1.5 %copy-start.4 = (bf16[2,128,192]{2,1,0:T(8,128)(2,1)S(1)}, bf16[2,128,192]{2,1,0:T(8,128)(2,1)}, u32[]{:S(2)}) copy-start(bf16[2,128,192]{2,1,0:T(8,128)(2,1)} %constant.13.clone.refs_8_) | copy-start | bytes 294916
  36.0 1.5 %collective-permute-start.10 = (f32[512,128]{1,0:T(8,128)S(1)}, f32[512,128]{1,0:T(8,128)S(1)}, u32[]{:S(2)}, u32[]{:S(2)}) collective-permute-start(f32[512,128]{1,0:T(8,128)S(1)} %get-tuple-element.35), channel_id=1, source_target_pairs={{0,1},{1,0},{2,3},{3,2},{4,5},{5,4},{6,7},{7,6},{8,9},{9,8},{10,11... | collective-permute-start | bytes 786440 | tf_op jit(solution)/shard_map/ppermute | solution.py:626
  37.6 8.5 %collective-permute-start.11 = (f32[256,128]{1,0:T(8,128)S(1)}, f32[256,128]{1,0:T(8,128)S(1)}, u32[]{:S(2)}, u32[]{:S(2)}) collective-permute-start(f32[256,128]{1,0:T(8,128)S(1)} %get-tuple-element.36), channel_id=1, source_target_pairs={{0,0},{1,2},{2,8},{3,10},{4,4},{5,6},{6,12},{7,14},{8,1},{9,3},{10... | collective-permute-start | bytes 393224 | tf_op jit(solution)/shard_map/ppermute | solution.py:628
  40.8 13.1 %collective-permute-start.12 = (f32[256,128]{1,0:T(8,128)S(1)}, f32[256,128]{1,0:T(8,128)S(1)}, u32[]{:S(2)}, u32[]{:S(2)}) collective-permute-start(f32[256,128]{1,0:T(8,128)S(1)} %get-tuple-element.37), channel_id=1, source_target_pairs={{0,4},{1,6},{2,12},{3,14},{4,0},{5,2},{6,8},{7,10},{8,5},{9,7},{10... | collective-permute-start | bytes 393224 | tf_op jit(solution)/shard_map/ppermute | solution.py:628
  44.4 9.5 %collective-permute-start.13 = (f32[256,128]{1,0:T(8,128)S(1)}, f32[256,128]{1,0:T(8,128)S(1)}, u32[]{:S(2)}, u32[]{:S(2)}) collective-permute-start(f32[256,128]{1,0:T(8,128)S(1)} %get-tuple-element.38), channel_id=1, source_target_pairs={{0,8},{1,10},{2,0},{3,2},{4,12},{5,14},{6,4},{7,6},{8,9},{9,11},{1... | collective-permute-start | bytes 393224 | tf_op jit(solution)/shard_map/ppermute | solution.py:628
  44.4 12.0 %collective-permute-start.14 = (f32[256,128]{1,0:T(8,128)S(1)}, f32[256,128]{1,0:T(8,128)S(1)}, u32[]{:S(2)}, u32[]{:S(2)}) collective-permute-start(f32[256,128]{1,0:T(8,128)S(1)} %get-tuple-element.39), channel_id=1, source_target_pairs={{0,12},{1,14},{2,4},{3,6},{4,8},{5,10},{6,0},{7,2},{8,13},{9,15},{... | collective-permute-start | bytes 393224 | tf_op jit(solution)/shard_map/ppermute | solution.py:628

commit v6 on v5

--- a/solution.py
+++ b/solution.py
@@ -171,7 +171,6 @@
 REF_LINES = 8
 EDGE = 16
 STEPS = (2, 3, 1, 0)
-CHUNKS = (((0, WINDOW), (0, OUT_BINS)),)
 
 
 def split_bf16(value):
@@ -230,7 +229,7 @@
         long_bf16(np.stack(far)),
         both_bf16(there),
         both_bf16(back),
-        long_bf16(np.stack(last)),
+        both_bf16(np.stack(last)),
     ]
     return matrices, np.stack(twists).astype(np.float32)
 
@@ -290,22 +289,33 @@
         ref_all[pl.ds(pl.multiple_of(at, 16), bins), :] = jnp.concatenate([ref[...], ref[...]], axis=1)
     lane = lax.broadcasted_iota(jnp.int32, (1, FACTOR), 1)
     for at, message in enumerate(messages):
-        step = at % (PLACES // 2)
-        (first_bin, last_bin), _ = CHUNKS[at // (PLACES // 2)]
-        body = (last_bin - first_bin) * part_rows
-        start = window_start(((place >> 1) ^ step) * 2 + side, side, off_own, off_other) + EDGE
-        rows = pl.ds(pl.multiple_of((start + first_bin) * part_rows, 8), body)
+        body = WINDOW * part_rows
+        start = window_start(((place >> 1) ^ at) * 2 + side, side, off_own, off_other) + EDGE
+        rows = pl.ds(pl.multiple_of(start * part_rows, 8), body)
         message[:body, :] = re_all[rows, :]
         message[body : 2 * body, :] = im_all[rows, :]
-        if first_bin == 0:
-            for bin_num in range(REF_LINES):
-                low = ref_all[pl.ds(start + bin_num, 1), :]
-                high = ref_all[pl.ds(start + REF_LINES + bin_num, 1), :]
-                message[2 * body + bin_num : 2 * body + bin_num + 1, :] = jnp.where(lane < HALF, low, high)
-
-
-def phase_kernel(bins_total, off_own, off_other, out):
+        for bin_num in range(REF_LINES):
+            low = ref_all[pl.ds(start + bin_num, 1), :]
+            high = ref_all[pl.ds(start + REF_LINES + bin_num, 1), :]
+            message[2 * body + bin_num : 2 * body + bin_num + 1, :] = jnp.where(lane < HALF, low, high)
+
+
+def phase_kernel(bins_total, off_own, off_other, owners, taps_own, taps_other, out, weights, choice):
     place, side = lax.axis_index("az"), lax.axis_index("rg")
+    bins_held = taps_own.shape[0]
+    held = lax.div(place * OUT_BINS, bins_held) == side
+    local = lax.rem(place * OUT_BINS, bins_held)
+    for bin_num in range(OUT_BINS):
+        for tap in range(TAPS):
+            weight = jnp.where(held, taps_own[local + bin_num, tap], taps_other[local + bin_num, tap])
+            line = bin_num * TAPS + tap
+            weights[line : line + 1, :] = jnp.full((1, FACTOR), weight, jnp.float32)
+    line = lax.broadcasted_iota(jnp.int32, (2 * len(STEPS), FACTOR), 0)
+    for which in range(2):
+        owner = owners[which]
+        step = (owner >> 1) ^ (place >> 1)
+        wanted = jnp.where((owner & 1) == side, step, step + len(STEPS))
+        choice[which] = jnp.where(line == wanted, 1.0, 0.0)
     start = window_start(place, side, off_own, off_other)
     shape = (HALF, FACTOR)
     kappa = lax.broadcasted_iota(jnp.int32, shape, 0)
@@ -324,20 +334,16 @@
         out[bin_num, 1] = sine
 
 
-def parity_kernel(bins, has_ref, *refs):
+def parity_kernel(*refs):
     chunks = dict(zip(STEPS, refs))
-    refs = refs[PLACES // 2 :]
+    keep, give = refs[len(STEPS) :]
     place, side = lax.axis_index("az"), lax.axis_index("rg")
-    if has_ref:
-        owners, keep, give, keep_ref = refs
-    else:
-        keep, give = refs
     sign = jnp.where(place >= PLACES // 2, -1.0, 1.0)
     even = side == 0
     keep_near, keep_far = jnp.where(even, 1.0, sign), jnp.where(even, 1.0, -sign)
     give_near, give_far = jnp.where(even, sign, 1.0), jnp.where(even, -sign, 1.0)
     plain = ((place >> 1) & 1) == 0
-    for line in range(2 * bins):
+    for line in range(2 * WINDOW):
         read = slice(line * PART, (line + 1) * PART)
         write = line * 2 * PART
         values = [chunks[step][read, :] for step in range(4)]
@@ -345,14 +351,11 @@
             pair = [values[step] * near_factor + values[step + 2] * far_factor for step in range(2)]
             target[write : write + PART, :] = jnp.where(plain, pair[0], pair[1])
             target[write + PART : write + 2 * PART, :] = jnp.where(plain, pair[1], pair[0])
-    if has_ref:
-        for which in range(2):
-            step = (owners[which] >> 1) ^ (place >> 1)
-            value = chunks[0][2 * bins * PART :, :]
-            for other in range(1, PLACES // 2):
-                value = jnp.where(step == other, chunks[other][2 * bins * PART :, :], value)
-            give[2 * bins * 2 * PART + which * REF_LINES : 2 * bins * 2 * PART + (which + 1) * REF_LINES, :] = value
-            keep_ref[which] = value
+    for step in range(len(STEPS)):
+        value = chunks[step][2 * WINDOW * PART :, :]
+        at = 2 * WINDOW * 2 * PART + step * REF_LINES
+        keep[at : at + REF_LINES, :] = value
+        give[at : at + REF_LINES, :] = value
 
 
 def gather_lines(ref, bins, group):
@@ -370,33 +373,27 @@
     return [range(at, min(at + 4, bins)) for at in range(0, bins, 4)]
 
 
-def near_kernel(bins, keep, near, out):
+def near_kernel(keep, near, out):
     matrix = near[lax.axis_index("rg")]
-    for index, group in enumerate(bin_groups(bins)):
-        out[index, :, : len(group) * FACTOR] = dot(matrix, long_rows(gather_lines(keep, bins, group)))
-
-
-def band_kernel(chunk, *refs):
-    (first_bin, last_bin), (first_out, last_out) = CHUNKS[chunk]
-    bins = last_bin - first_bin
-    partial, got, keep_ref, got_ref, owners, phase, taps_own, taps_other = refs[:8]
-    far, there, back, last, twists = refs[8:13]
-    refs = refs[13:]
-    if chunk:
-        earlier, refs = refs[0], refs[1:]
-    keep_out, give_out, spectra, band, picked = refs
-    place, side = lax.axis_index("az"), lax.axis_index("rg")
+    for index, group in enumerate(bin_groups(WINDOW)):
+        out[index, :, : len(group) * FACTOR] = dot(matrix, long_rows(gather_lines(keep, WINDOW, group)))
+
+
+def band_kernel(
+    partial, keep, got, phase, weights, choice, far, there, back, last, twists, keep_out, give_out, spectra, band, picked
+):
+    side = lax.axis_index("rg")
+    bins = WINDOW
 
     lane = lax.broadcasted_iota(jnp.int32, (REF_LINES, FACTOR), 1)
-    ref_at = got_ref.shape[0] - 2 * REF_LINES
-    lines = [
-        jnp.where(
-            (owners[which] & 1) == side,
-            keep_ref[which],
-            got_ref[ref_at + which * REF_LINES : ref_at + (which + 1) * REF_LINES, :],
-        )
-        for which in range(2)
-    ]
+    lines = []
+    for which in range(2):
+        value = jnp.zeros((REF_LINES, FACTOR), jnp.float32)
+        for option in range(2 * len(STEPS)):
+            at = 2 * bins * 2 * PART + option % len(STEPS) * REF_LINES
+            candidate = (keep if option < len(STEPS) else got)[at : at + REF_LINES, :]
+            value = jnp.where(choice[which, option : option + 1, :] > 0.5, candidate, value)
+        lines.append(value)
     for block in range(2):
         coarse = (lane >> 1) + block * HALF
         wide = [jnp.take_along_axis(lines[which], coarse, axis=1) for which in range(2)]
@@ -405,7 +402,7 @@
         picked[0, block * REF_LINES : (block + 1) * REF_LINES, :] = ref_cos
         picked[1, block * REF_LINES : (block + 1) * REF_LINES, :] = ref_sin
 
-    far, last = far[side], last[side]
+    far, last = far[side], (last[0, side], last[1, side])
     there, back = (there[0], there[1]), (back[0], back[1])
     twist_cos, twist_sin = twists[side, 0], twists[side, 1]
     for number, group in enumerate(bin_groups(bins)):
@@ -421,43 +418,31 @@
         for index, bin_num in enumerate(group):
             real = passed[index * HALF : (index + 1) * HALF, :FACTOR]
             imag = passed[index * HALF : (index + 1) * HALF, FACTOR:]
-            whole = first_bin + bin_num
-            model_cos, model_sin = phase[whole, 0], phase[whole, 1]
-            row_cos, row_sin = picked[0, whole : whole + 1, :], picked[1, whole : whole + 1, :]
+            model_cos, model_sin = phase[bin_num, 0], phase[bin_num, 1]
+            row_cos, row_sin = picked[0, bin_num : bin_num + 1, :], picked[1, bin_num : bin_num + 1, :]
             cosine = model_cos * row_cos - model_sin * row_sin
             sine = model_sin * row_cos + model_cos * row_sin
             spectra[bin_num, 0] = real * cosine - imag * sine
             spectra[bin_num, 1] = real * sine + imag * cosine
 
-    bins_held = taps_own.shape[0]
-    held = lax.div(place * OUT_BINS, bins_held) == side
-    local = lax.rem(place * OUT_BINS, bins_held)
-    outs = range(first_out, last_out)
-    weights = {
-        out: [jnp.where(held, taps_own[local + out, tap], taps_other[local + out, tap]) for tap in range(TAPS)]
-        for out in outs
-    }
     strip = 8
     for part in range(2):
         for at in range(0, HALF, strip):
             rows = slice(at, at + strip)
             sums = {}
-            for bin_num in range(first_out, last_out + TAPS - 1):
-                if bin_num < first_bin:
-                    value = earlier[bin_num, part, rows]
-                else:
-                    value = spectra[bin_num - first_bin, part, rows]
-                for out in outs:
-                    if 0 <= bin_num - out < TAPS:
-                        term = value * weights[out][bin_num - out]
-                        sums[out] = sums[out] + term if out in sums else term
-            for out in outs:
-                line = (out - first_out) * HALF + at
+            for bin_num in range(bins):
+                value = spectra[bin_num, part, rows]
+                for out in range(max(0, bin_num - TAPS + 1), min(OUT_BINS, bin_num + 1)):
+                    weight = out * TAPS + bin_num - out
+                    term = value * weights[weight : weight + 1, :]
+                    sums[out] = sums[out] + term if out in sums else term
+            for out in range(OUT_BINS):
+                line = out * HALF + at
                 band[line : line + strip, part * FACTOR : (part + 1) * FACTOR] = sums[out]
 
     scale = 1.0 / (FACTOR * FACTOR)
     cos_table, sin_table = twist_cos * scale, twist_sin * scale
-    for at in range(0, last_out - first_out, 4):
+    for at in range(0, OUT_BINS, 4):
         passed = dot_split(split_bf16(band[at * HALF : (at + 4) * HALF, :]), back)
         columns = []
         for index in range(4):
@@ -466,7 +451,7 @@
             columns.append(
                 jnp.concatenate([real * cos_table - imag * sin_table, imag * cos_table + real * sin_table], axis=0)
             )
-        passed = dot(last, long_rows(jnp.concatenate(columns, axis=1)))
+        passed = dot_split(last, split_bf16(jnp.concatenate(columns, axis=1)))
         for index in range(4):
             lines = slice((at + index) * HALF, (at + index + 1) * HALF)
             keep_out[lines, :] = passed[:HALF, index * FACTOR : (index + 1) * FACTOR]
@@ -477,7 +462,7 @@
     return ((quarter & 1) << 1) | (quarter >> 1)
 
 
-def join_kernel(outs, keep, got, *messages):
+def join_kernel(keep, got, *messages):
     place, side = lax.axis_index("az"), lax.axis_index("rg")
     quarter = lax.rem(place, PLACES // 2)
     sign = jnp.where(side == 0, 1.0, -1.0)
@@ -485,7 +470,7 @@
         target = crossed(quarter) ^ step
         top, middle = target >> 1, target & 1
         keep_factor, got_factor = jnp.where(top == 0, 1.0, sign), jnp.where(top == 0, 1.0, -sign)
-        for line in range(2 * outs):
+        for line in range(2 * OUT_BINS):
             read = pl.ds(pl.multiple_of(line * 2 * PART + middle * PART, 8), PART)
             message[line * PART : (line + 1) * PART, :] = keep[read, :] * keep_factor + got[read, :] * got_factor
 
@@ -495,10 +480,9 @@
     bins, samples = out_re.shape
     place = lax.axis_index("az")
     for at, message in enumerate(messages):
-        sender = crossed((place >> 1) ^ (at % (PLACES // 2)))
-        _, (first_out, last_out) = CHUNKS[at // (PLACES // 2)]
-        for out in range(last_out - first_out):
-            line = pl.multiple_of((sender * OUT_BINS + first_out + out) * PART, 8)
+        sender = crossed((place >> 1) ^ at)
+        for out in range(OUT_BINS):
+            line = pl.multiple_of((sender * OUT_BINS + out) * PART, 8)
             re_all[pl.ds(line, PART), :] = message[2 * out * PART : (2 * out + 1) * PART, :]
             im_all[pl.ds(line, PART), :] = message[(2 * out + 1) * PART : (2 * out + 2) * PART, :]
     for out, all_ref in ((out_re, re_all), (out_im, im_all)):
@@ -514,7 +498,7 @@
 
 
 def kernel_call(body, name, out_shape, operands, scratch=(), flops=0, count=10**6, limit=8):
-    specs = [SMEM if operand.size <= 1024 else VMEM for operand in operands]
+    specs = [SMEM if operand.size <= 256 else VMEM for operand in operands]
     return pl.pallas_call(
         body,
         out_shape=out_shape,
@@ -542,25 +526,20 @@
     ref_other, re_other, im_other, taps_other = swap(ref_own), swap(raw_re), swap(raw_im), swap(taps)
 
     lines = [raw_re.reshape(bins * PART, FACTOR), raw_im.reshape(bins * PART, FACTOR)]
-    shapes = []
-    for (first_bin, last_bin), _ in CHUNKS:
-        ref_lines = REF_LINES if first_bin == 0 else 0
-        shapes += [array(2 * (last_bin - first_bin) * PART + ref_lines, FACTOR)] * half
-    all_lines = (2 * bins + 2 * EDGE) * PART
+    all_bins = 2 * bins + 2 * EDGE
     messages = kernel_call(
         pack_kernel,
         "pack",
-        shapes,
+        [array(2 * WINDOW * PART + REF_LINES, FACTOR)] * half,
         [*lines, re_other, im_other, ref_own, ref_other, offsets, offsets_other],
-        scratch=[(all_lines, FACTOR), (all_lines, FACTOR), (2 * bins + 2 * EDGE, FACTOR)],
+        scratch=[(all_bins * PART, FACTOR), (all_bins * PART, FACTOR), (all_bins, FACTOR)],
         count=4 * 10**6,
     )
-    phases = kernel_call(
+    prepared = kernel_call(
         functools.partial(phase_kernel, 2 * bins),
         "phase",
-        array(WINDOW, 2, HALF, FACTOR),
-        [offsets, offsets_other],
-        flops=10**7,
+        [array(WINDOW, 2, HALF, FACTOR), array(OUT_BINS * TAPS, FACTOR), array(2, 2 * half, FACTOR)],
+        [offsets, offsets_other, owners, taps, taps_other],
     )
 
     routes = [
@@ -579,53 +558,25 @@
         ]
         for step in range(half)
     ]
-    arrived = [
-        lax.ppermute(messages[chunk * half + step], ("az", "rg"), routes[step])
-        for chunk in range(len(CHUNKS))
-        for step in STEPS
-    ]
-
-    results = []
-    refs, earlier = None, []
-    for chunk, ((first_bin, last_bin), (first_out, last_out)) in enumerate(CHUNKS):
-        count, outs = last_bin - first_bin, last_out - first_out
-        has_ref = chunk == 0
-        size = 2 * count * 2 * PART
-        shapes = [array(size, FACTOR), array(size + (2 * REF_LINES if has_ref else 0), FACTOR)]
-        operands = arrived[chunk * half : (chunk + 1) * half]
-        if chunk == 0:
-            *operands, phases, taps_other = lax.optimization_barrier((*operands, phases, taps_other))
-        if has_ref:
-            shapes.append(array(2, REF_LINES, FACTOR))
-            operands = operands + [owners]
-        parity = kernel_call(functools.partial(parity_kernel, count, has_ref), "parity", shapes, operands)
-        keep, give = parity[:2]
-        got = swap(give)
-        groups = len(bin_groups(count))
-        partial = kernel_call(
-            functools.partial(near_kernel, count), "near", array(groups, FACTOR, 4 * FACTOR), [keep, near_table]
-        )
-        if has_ref:
-            refs = [parity[2], got]
-        pieces = kernel_call(
-            functools.partial(band_kernel, chunk),
-            "band",
-            [array(outs * HALF, FACTOR), array(outs * HALF, FACTOR), array(count, 2, HALF, FACTOR)],
-            [partial, got, *refs, owners, phases, taps, taps_other, *tables, *earlier],
-            scratch=[(outs * HALF, 2 * FACTOR), (2, 2 * REF_LINES, FACTOR)],
-            flops=10**9,
-            count=4 * 10**6,
-            limit=16,
-        )
-        keep, give, spectra = pieces
-        earlier = [spectra]
-        sent = kernel_call(
-            functools.partial(join_kernel, outs),
-            "join",
-            [array(2 * outs * PART, FACTOR)] * half,
-            [keep, swap(give)],
-        )
-        results += [lax.ppermute(message, ("az", "rg"), route) for message, route in zip(sent, routes_back)]
+    arrived = [lax.ppermute(messages[step], ("az", "rg"), routes[step]) for step in STEPS]
+    *arrived, phases, weights, choice = lax.optimization_barrier((*arrived, *prepared))
+
+    size = 2 * WINDOW * 2 * PART + half * REF_LINES
+    keep, give = kernel_call(parity_kernel, "parity", [array(size, FACTOR)] * 2, arrived)
+    got = swap(give)
+    partial = kernel_call(
+        near_kernel, "near", array(len(bin_groups(WINDOW)), FACTOR, 4 * FACTOR), [keep, near_table]
+    )
+    keep, give = kernel_call(
+        band_kernel,
+        "band",
+        [array(OUT_BINS * HALF, FACTOR)] * 2,
+        [partial, keep, got, phases, weights, choice, *tables],
+        scratch=[(WINDOW, 2, HALF, FACTOR), (OUT_BINS * HALF, 2 * FACTOR), (2, 2 * REF_LINES, FACTOR)],
+        limit=16,
+    )
+    sent = kernel_call(join_kernel, "join", [array(2 * OUT_BINS * PART, FACTOR)] * half, [keep, swap(give)])
+    results = [lax.ppermute(message, ("az", "rg"), route) for message, route in zip(sent, routes_back)]
     return kernel_call(
         place_kernel, "place", [array(bins, samples)] * 2, results, scratch=[(bins * PART, FACTOR)] * 2
     )

time: 57.6 us -> 55.4 us (0.962)
  Pallas kernels: 7.71 us -> 6.11 us
  waiting for transfers between devices: 29.9 us -> 28.9 us
    ppermute x4, waiting for transfers between devices: 15.5 us -> 13.6 us  [transposed_shards(): lax.ppermute(messages[step], ('az', 'rg'), routes[step])]
    pallas_call x7, Pallas kernels: 7.71 us -> 6.11 us  [kernel_call(): pl.pallas_call(body, out_shape=out_shape, in_specs=specs, out_specs=jax.t...]
    ppermute x1, waiting for transfers between devices: 0.01 us -> 1.17 us  [transposed_shards(): swap(taps)]
  transfers between devices with their start and end apart: 15 -> 15, of which waited for: 8 -> 9; matrix products, arithmetic and copies ran while one was open for 2% -> 2% of each run, Pallas kernels for 3% -> 4%
where the time goes in v6:
time: 55.4 us; the launch traced here: 55.2 us
  waiting for transfers between devices  28.9 us (52%)
  starting transfers between devices  17.4 us (31%)
  Pallas kernels  6.11 us (11%)
  local copies, waits for them, and re-layouts  2.05 us (4%)
  between operations  0.79 us (1%)
    ppermute x4, waiting for transfers between devices, transposed_shards(): lax.ppermute(messages[step], ('az', 'rg'), routes[step])  13.6 us
    ppermute x4, waiting for transfers between devices, transposed_shards(): lax.ppermute(message, ('az', 'rg'), route)  11.9 us
    ppermute x4, starting transfers between devices, transposed_shards(): lax.ppermute(messages[step], ('az', 'rg'), routes[step])  8.37 us
    ppermute x4, starting transfers between devices, transposed_shards(): lax.ppermute(message, ('az', 'rg'), route)  6.86 us
    pallas_call x7, Pallas kernels, kernel_call(): pl.pallas_call(body, out_shape=out_shape, in_specs=specs, out_specs=jax.t...  6.11 us
    ppermute x1, waiting for transfers between devices, transposed_shards(): swap(give)  1.2 us
    ppermute x1, waiting for transfers between devices, transposed_shards(): swap(taps)  1.17 us
  transfers between devices with their start and end apart: 15, of which 9 were waited for; matrix products, arithmetic and copies ran while one was open for 2% of the time, Pallas kernels for 4%

profile of v6, /device:TPU:13, one launch (start us, length us, event | category | flops | bytes accessed | tf_op | source)
XLA Modules:
  0.0 55.2 jit_solution(16655708564084996466)
XLA Ops:
  0.6 0.7 %collective-permute-start = (f32[32,2048]{1,0:T(8,128)}, f32[32,2048]{1,0:T(8,128)S(1)}, u32[]{:S(2)}, u32[]{:S(2)}) collective-permute-start(f32[32,2048]{1,0:T(8,128)} %param.12), channel_id=1, source_target_pairs={{0,1},{1,0},{2,3},{3,2},{4,5},{5,4},{6,7},{7,6},{8,9},{9,8},{10,11... | collective-permute-start | bytes 786440 | tf_op jit(solution)/shard_map/ppermute | solution.py:526
  1.4 0.1 collective-permute-start.1
  1.5 0.4 collective-permute-start.2
  1.9 0.1 collective-permute-start.3
  2.0 1.0 %reshape.10.re_lines = f32[512,128]{1,0:T(8,128)S(1)} reshape(f32[32,2048]{1,0:T(8,128)} %param.12) | data formatting | bytes 524288 | tf_op jit(solution)/shard_map/reshape | solution.py:528
  3.1 0.1 collective-permute-done.2.ref_other
  3.2 0.5 copy-done.6
  3.7 0.8 %pack.1 = (f32[488,128]{1,0:T(8,128)S(1)}, f32[488,128]{1,0:T(8,128)S(1)}, f32[488,128]{1,0:T(8,128)S(1)}, f32[488,128]{1,0:T(8,128)S(1)}) custom-call(f32[512,128]{1,0:T(8,128)S(1)} %reshape.10.re_lines, f32[512,128]{1,0:T(8,128)S(1)} %reshape.11.im_lines, f32[32,2048]{1,0:T(8,128)S(1)} %collective-permute-done.re_other, ...), custom_call_target="tpu_custom_call" | custom-call | bytes 4000000 | tf_op jit(solution)/shard_map/pack/pallas_call | solution.py:502
  4.6 3.6 %collective-permute-start.4 = (f32[488,128]{1,0:T(8,128)S(1)}, f32[488,128]{1,0:T(8,128)S(1)}, u32[]{:S(2)}, u32[]{:S(2)}) collective-permute-start(f32[488,128]{1,0:T(8,128)S(1)} %get-tuple-element.24), channel_id=1, source_target_pairs={{0,8},{1,10},{2,9},{3,11},{4,12},{5,14},{6,13},{7,15},{8,0},{9,2},... | collective-permute-start | bytes 749576 | tf_op jit(solution)/shard_map/ppermute | solution.py:561
  8.2 2.4 %collective-permute-start.6 = (f32[488,128]{1,0:T(8,128)S(1)}, f32[488,128]{1,0:T(8,128)S(1)}, u32[]{:S(2)}, u32[]{:S(2)}) collective-permute-start(f32[488,128]{1,0:T(8,128)S(1)} %get-tuple-element.26), channel_id=1, source_target_pairs={{0,4},{1,6},{2,5},{3,7},{4,0},{5,2},{6,1},{7,3},{8,12},{9,14},{10,... | collective-permute-start | bytes 749576 | tf_op jit(solution)/shard_map/ppermute | solution.py:561
  10.6 2.3 %collective-permute-start.7 = (f32[488,128]{1,0:T(8,128)S(1)}, f32[488,128]{1,0:T(8,128)S(1)}, u32[]{:S(2)}, u32[]{:S(2)}) collective-permute-start(f32[488,128]{1,0:T(8,128)S(1)} %get-tuple-element.27), channel_id=1, source_target_pairs={{0,0},{1,2},{2,1},{3,3},{4,4},{5,6},{6,5},{7,7},{8,8},{9,10},{10,9... | collective-permute-start | bytes 749576 | tf_op jit(solution)/shard_map/ppermute | solution.py:561
  13.0 0.1 copy.15.taps_own
  13.0 1.2 %collective-permute-done.8.taps_other = f32[32,8]{1,0:T(8,128)S(1)} collective-permute-done((f32[32,8]{1,0:T(8,128)S(1)}, f32[32,8]{1,0:T(8,128)S(1)}, u32[]{:S(2)}, u32[]{:S(2)}) %collective-permute-start.8) | collective-permute-done | bytes 1056 | tf_op jit(solution)/shard_map/ppermute | solution.py:526
  14.2 1.9 %phase.1 = (f32[15,2,64,128]{3,2,1,0:T(8,128)S(1)}, f32[64,128]{1,0:T(8,128)S(1)}, f32[2,8,128]{2,1,0:T(8,128)S(1)}) custom-call(s32[2]{0:T(128)S(1)} %copy-done.7, s32[2]{0:T(128)S(1)} %collective-permute-done.3.off_other, s32[2]{0:T(128)S(1)} %copy-done.8, f32[32,8]{1,0:T(8,128)S(1)} %copy.15.taps_own, f32[32,8]{1,0:T(8,128)S(1)} %collective-permute-done.8.taps_other), custom_call_target="tpu_custom_call" | custom-call | bytes 1000000 | tf_op jit(solution)/shard_map/phase/pallas_call | solution.py:502
  16.1 8.2 %collective-permute-done.4.refs_0_ = f32[488,128]{1,0:T(8,128)S(1)} collective-permute-done((f32[488,128]{1,0:T(8,128)S(1)}, f32[488,128]{1,0:T(8,128)S(1)}, u32[]{:S(2)}, u32[]{:S(2)}) %collective-permute-start.4) | collective-permute-done | bytes 249888 | tf_op jit(solution)/shard_map/ppermute | solution.py:561
  24.4 5.4 %collective-permute-done.5.refs_1_ = f32[488,128]{1,0:T(8,128)S(1)} collective-permute-done((f32[488,128]{1,0:T(8,128)S(1)}, f32[488,128]{1,0:T(8,128)S(1)}, u32[]{:S(2)}, u32[]{:S(2)}) %collective-permute-start.5) | collective-permute-done | bytes 249888 | tf_op jit(solution)/shard_map/ppermute | solution.py:561
  29.7 0.2 parity.1
  29.9 0.4 collective-permute-start.9
  30.3 0.3 copy-done.5
  30.7 0.3 near.2.partial
  31.0 0.9 %collective-permute-done.9.got = f32[992,128]{1,0:T(8,128)S(1)} collective-permute-done((f32[992,128]{1,0:T(8,128)S(1)}, f32[992,128]{1,0:T(8,128)S(1)}, u32[]{:S(2)}, u32[]{:S(2)}) %collective-permute-start.9) | collective-permute-done | bytes 507936 | tf_op jit(solution)/shard_map/ppermute | solution.py:566
  31.9 1.9 %band.1 = (f32[512,128]{1,0:T(8,128)S(1)}, f32[512,128]{1,0:T(8,128)S(1)}) custom-call(f32[4,128,512]{2,1,0:T(8,128)S(1)} %near.2.partial, f32[992,128]{1,0:T(8,128)S(1)} %get-tuple-element.35.keep, f32[992,128]{1,0:T(8,128)S(1)} %collective-permute-done.9.got, f32[15,2,64,128]{3,2,1,0:T(8,128)S(1)} %get-tuple-element.37.phase, ...), custom_call_target="tpu_custom_call" | custom-call | bytes 1000000 | tf_op jit(solution)/shard_map/band/pallas_call | solution.py:502
  33.8 0.4 collective-permute-start.10
  34.2 1.2 %collective-permute-done.10.got = f32[512,128]{1,0:T(8,128)S(1)} collective-permute-done((f32[512,128]{1,0:T(8,128)S(1)}, f32[512,128]{1,0:T(8,128)S(1)}, u32[]{:S(2)}, u32[]{:S(2)}) %collective-permute-start.10) | collective-permute-done | bytes 262176 | tf_op jit(solution)/shard_map/ppermute | solution.py:578
  35.4 0.1 join.1
  35.5 3.2 %collective-permute-start.11 = (f32[256,128]{1,0:T(8,128)S(1)}, f32[256,128]{1,0:T(8,128)S(1)}, u32[]{:S(2)}, u32[]{:S(2)}) collective-permute-start(f32[256,128]{1,0:T(8,128)S(1)} %get-tuple-element.42), channel_id=1, source_target_pairs={{0,0},{1,2},{2,8},{3,10},{4,4},{5,6},{6,12},{7,14},{8,1},{9,3},{10... | collective-permute-start | bytes 393224 | tf_op jit(solution)/shard_map/ppermute | solution.py:579
  38.7 3.5 %collective-permute-start.12 = (f32[256,128]{1,0:T(8,128)S(1)}, f32[256,128]{1,0:T(8,128)S(1)}, u32[]{:S(2)}, u32[]{:S(2)}) collective-permute-start(f32[256,128]{1,0:T(8,128)S(1)} %get-tuple-element.43), channel_id=1, source_target_pairs={{0,4},{1,6},{2,12},{3,14},{4,0},{5,2},{6,8},{7,10},{8,5},{9,7},{10... | collective-permute-start | bytes 393224 | tf_op jit(solution)/shard_map/ppermute | solution.py:579
  42.2 0.1 collective-permute-start.14
  42.3 1.6 %collective-permute-done.11.refs_0_ = f32[256,128]{1,0:T(8,128)S(1)} collective-permute-done((f32[256,128]{1,0:T(8,128)S(1)}, f32[256,128]{1,0:T(8,128)S(1)}, u32[]{:S(2)}, u32[]{:S(2)}) %collective-permute-start.11) | collective-permute-done | bytes 131104 | tf_op jit(solution)/shard_map/ppermute | solution.py:579
  43.9 7.8 %collective-permute-done.12.refs_1_ = f32[256,128]{1,0:T(8,128)S(1)} collective-permute-done((f32[256,128]{1,0:T(8,128)S(1)}, f32[256,128]{1,0:T(8,128)S(1)}, u32[]{:S(2)}, u32[]{:S(2)}) %collective-permute-start.12) | collective-permute-done | bytes 131104 | tf_op jit(solution)/shard_map/ppermute | solution.py:579
  51.8 2.5 %collective-permute-done.14.refs_3_ = f32[256,128]{1,0:T(8,128)S(1)} collective-permute-done((f32[256,128]{1,0:T(8,128)S(1)}, f32[256,128]{1,0:T(8,128)S(1)}, u32[]{:S(2)}, u32[]{:S(2)}) %collective-permute-start.14) | collective-permute-done | bytes 131104 | tf_op jit(solution)/shard_map/ppermute | solution.py:579
  54.3 0.9 %place.1 = (f32[32,2048]{1,0:T(8,128)}, f32[32,2048]{1,0:T(8,128)}) custom-call(f32[256,128]{1,0:T(8,128)S(1)} %collective-permute-done.11.refs_0_, f32[256,128]{1,0:T(8,128)S(1)} %collective-permute-done.12.refs_1_, f32[256,128]{1,0:T(8,128)S(1)} %collective-permute-done.13.refs_2_, f32[256,128]{1,0:T(8,128)S(1)} %collective-permute-done.14.refs_3_), custom_call_target="tpu_custom_call" | custom-call | bytes 1000000 | tf_op jit(solution)/shard_map/place/pallas_call | solution.py:502
  (30 shorter events, 0.1 us)
Async XLA Ops:
  0.6 1.3 %copy-start.7 = (s32[2]{0:T(128)S(1)}, s32[2]{0:T(128)}, u32[]{:S(2)}) copy-start(s32[2]{0:T(128)} %off_own.3) | copy-start | bytes 28
  0.6 2.5 %collective-permute-start = (f32[32,2048]{1,0:T(8,128)}, f32[32,2048]{1,0:T(8,128)S(1)}, u32[]{:S(2)}, u32[]{:S(2)}) collective-permute-start(f32[32,2048]{1,0:T(8,128)} %param.12), channel_id=1, source_target_pairs={{0,1},{1,0},{2,3},{3,2},{4,5},{5,4},{6,7},{7,6},{8,9},{9,8},{10,11... | collective-permute-start | bytes 786440 | tf_op jit(solution)/shard_map/ppermute | solution.py:526
  1.4 1.8 %collective-permute-start.1 = (f32[32,2048]{1,0:T(8,128)}, f32[32,2048]{1,0:T(8,128)S(1)}, u32[]{:S(2)}, u32[]{:S(2)}) collective-permute-start(f32[32,2048]{1,0:T(8,128)} %param.13), channel_id=1, source_target_pairs={{0,1},{1,0},{2,3},{3,2},{4,5},{5,4},{6,7},{7,6},{8,9},{9,8},{10,11... | collective-permute-start | bytes 786440 | tf_op jit(solution)/shard_map/ppermute | solution.py:526
  1.5 1.5 %copy-start.9 = (f32[32,2048]{1,0:T(8,128)S(1)}, f32[32,2048]{1,0:T(8,128)}, u32[]{:S(2)}) copy-start(f32[32,2048]{1,0:T(8,128)} %param.13) | copy-start | bytes 786436
  1.5 1.7 %collective-permute-start.2 = (f32[32,64]{1,0:T(8,128)}, f32[32,64]{1,0:T(8,128)S(1)}, u32[]{:S(2)}, u32[]{:S(2)}) collective-permute-start(f32[32,64]{1,0:T(8,128)} %bitcast.3), channel_id=1, source_target_pairs={{0,1},{1,0},{2,3},{3,2},{4,5},{5,4},{6,7},{7,6},{8,9},{9,8},{10,11... | collective-permute-start | bytes 24584 | tf_op jit(solution)/shard_map/ppermute | solution.py:526
  1.9 1.2 %collective-permute-start.3 = (s32[2]{0:T(128)S(1)}, s32[2]{0:T(128)S(1)}, u32[]{:S(2)}, u32[]{:S(2)}) collective-permute-start(s32[2]{0:T(128)S(1)} %copy-done.7), channel_id=1, source_target_pairs={{0,1},{1,0},{2,3},{3,2},{4,5},{5,4},{6,7},{7,6},{8,9},{9,8},{10,11... | collective-permute-start | bytes 32 | tf_op jit(solution)/shard_map/ppermute | solution.py:525
  3.0 0.7 %copy-start.6 = (f32[1,64,32]{1,2,0:T(8,128)S(1)}, f32[1,64,32]{1,2,0:T(8,128)}, u32[]{:S(2)}) copy-start(f32[1,64,32]{1,2,0:T(8,128)} %param.14) | copy-start | bytes 24580
  4.5 8.4 %copy-start.10 = (f32[32,8]{0,1:T(8,128)S(1)}, f32[32,8]{0,1:T(8,128)}, u32[]{:S(2)}) copy-start(f32[32,8]{0,1:T(8,128)} %param.17) | copy-start | bytes 3076
  4.6 19.8 %collective-permute-start.4 = (f32[488,128]{1,0:T(8,128)S(1)}, f32[488,128]{1,0:T(8,128)S(1)}, u32[]{:S(2)}, u32[]{:S(2)}) collective-permute-start(f32[488,128]{1,0:T(8,128)S(1)} %get-tuple-element.24), channel_id=1, source_target_pairs={{0,8},{1,10},{2,9},{3,11},{4,12},{5,14},{6,13},{7,15},{8,0},{9,2},... | collective-permute-start | bytes 749576 | tf_op jit(solution)/shard_map/ppermute | solution.py:561
  8.2 21.5 %collective-permute-start.5 = (f32[488,128]{1,0:T(8,128)S(1)}, f32[488,128]{1,0:T(8,128)S(1)}, u32[]{:S(2)}, u32[]{:S(2)}) collective-permute-start(f32[488,128]{1,0:T(8,128)S(1)} %get-tuple-element.25), channel_id=1, source_target_pairs={{0,12},{1,14},{2,13},{3,15},{4,8},{5,10},{6,9},{7,11},{8,4},{9,6},... | collective-permute-start | bytes 749576 | tf_op jit(solution)/shard_map/ppermute | solution.py:561
  8.2 21.5 %collective-permute-start.6 = (f32[488,128]{1,0:T(8,128)S(1)}, f32[488,128]{1,0:T(8,128)S(1)}, u32[]{:S(2)}, u32[]{:S(2)}) collective-permute-start(f32[488,128]{1,0:T(8,128)S(1)} %get-tuple-element.26), channel_id=1, source_target_pairs={{0,4},{1,6},{2,5},{3,7},{4,0},{5,2},{6,1},{7,3},{8,12},{9,14},{10,... | collective-permute-start | bytes 749576 | tf_op jit(solution)/shard_map/ppermute | solution.py:561
  10.6 3.6 %copy-start.8 = (s32[2]{0:T(128)S(1)}, s32[2]{0:T(128)}, u32[]{:S(2)}) copy-start(s32[2]{0:T(128)} %owners.1) | copy-start | bytes 28
  10.6 19.1 %collective-permute-start.7 = (f32[488,128]{1,0:T(8,128)S(1)}, f32[488,128]{1,0:T(8,128)S(1)}, u32[]{:S(2)}, u32[]{:S(2)}) collective-permute-start(f32[488,128]{1,0:T(8,128)S(1)} %get-tuple-element.27), channel_id=1, source_target_pairs={{0,0},{1,2},{2,1},{3,3},{4,4},{5,6},{6,5},{7,7},{8,8},{9,10},{10,9... | collective-permute-start | bytes 749576 | tf_op jit(solution)/shard_map/ppermute | solution.py:561
  13.0 1.2 %collective-permute-start.8 = (f32[32,8]{1,0:T(8,128)S(1)}, f32[32,8]{1,0:T(8,128)S(1)}, u32[]{:S(2)}, u32[]{:S(2)}) collective-permute-start(f32[32,8]{1,0:T(8,128)S(1)} %copy.15.taps_own), channel_id=1, source_target_pairs={{0,1},{1,0},{2,3},{3,2},{4,5},{5,4},{6,7},{7,6},{8,9},{9,8},{10,11... | collective-permute-start | bytes 3080 | tf_op jit(solution)/shard_map/ppermute | solution.py:526
  29.7 0.9 %copy-start.5 = (bf16[2,128,192]{2,1,0:T(8,128)(2,1)S(1)}, bf16[2,128,192]{2,1,0:T(8,128)(2,1)}, u32[]{:S(2)}) copy-start(bf16[2,128,192]{2,1,0:T(8,128)(2,1)} %constant.12.clone.near) | copy-start | bytes 294916
  29.9 2.0 %collective-permute-start.9 = (f32[992,128]{1,0:T(8,128)S(1)}, f32[992,128]{1,0:T(8,128)S(1)}, u32[]{:S(2)}, u32[]{:S(2)}) collective-permute-start(f32[992,128]{1,0:T(8,128)S(1)} %get-tuple-element.36), channel_id=1, source_target_pairs={{0,1},{1,0},{2,3},{3,2},{4,5},{5,4},{6,7},{7,6},{8,9},{9,8},{10,11... | collective-permute-start | bytes 1523720 | tf_op jit(solution)/shard_map/ppermute | solution.py:566
  30.6 1.2 %copy-start = (bf16[2,256,256]{2,1,0:T(8,128)(2,1)S(1)}, bf16[2,256,256]{2,1,0:T(8,128)(2,1)}, u32[]{:S(2)}) copy-start(bf16[2,256,256]{2,1,0:T(8,128)(2,1)} %constant.15.clone.back) | copy-start | bytes 786436
  30.6 1.2 %copy-start.1 = (bf16[2,256,256]{2,1,0:T(8,128)(2,1)S(1)}, bf16[2,256,256]{2,1,0:T(8,128)(2,1)}, u32[]{:S(2)}) copy-start(bf16[2,256,256]{2,1,0:T(8,128)(2,1)} %constant.14.clone.there) | copy-start | bytes 786436
  30.6 1.2 %copy-start.2 = (f32[2,2,64,128]{3,2,1,0:T(8,128)S(1)}, f32[2,2,64,128]{3,2,1,0:T(8,128)}, u32[]{:S(2)}) copy-start(f32[2,2,64,128]{3,2,1,0:T(8,128)} %constant.17.clone.twists) | copy-start | bytes 393220
  30.6 1.2 %copy-start.3 = (bf16[2,2,128,128]{3,2,1,0:T(8,128)(2,1)S(1)}, bf16[2,2,128,128]{3,2,1,0:T(8,128)(2,1)}, u32[]{:S(2)}) copy-start(bf16[2,2,128,128]{3,2,1,0:T(8,128)(2,1)} %constant.16.clone.last) | copy-start | bytes 393220
  30.6 1.2 %copy-start.4 = (bf16[2,128,192]{2,1,0:T(8,128)(2,1)S(1)}, bf16[2,128,192]{2,1,0:T(8,128)(2,1)}, u32[]{:S(2)}) copy-start(bf16[2,128,192]{2,1,0:T(8,128)(2,1)} %constant.13.clone.far) | copy-start | bytes 294916
  33.8 1.6 %collective-permute-start.10 = (f32[512,128]{1,0:T(8,128)S(1)}, f32[512,128]{1,0:T(8,128)S(1)}, u32[]{:S(2)}, u32[]{:S(2)}) collective-permute-start(f32[512,128]{1,0:T(8,128)S(1)} %get-tuple-element.41), channel_id=1, source_target_pairs={{0,1},{1,0},{2,3},{3,2},{4,5},{5,4},{6,7},{7,6},{8,9},{9,8},{10,11... | collective-permute-start | bytes 786440 | tf_op jit(solution)/shard_map/ppermute | solution.py:578
  35.5 8.5 %collective-permute-start.11 = (f32[256,128]{1,0:T(8,128)S(1)}, f32[256,128]{1,0:T(8,128)S(1)}, u32[]{:S(2)}, u32[]{:S(2)}) collective-permute-start(f32[256,128]{1,0:T(8,128)S(1)} %get-tuple-element.42), channel_id=1, source_target_pairs={{0,0},{1,2},{2,8},{3,10},{4,4},{5,6},{6,12},{7,14},{8,1},{9,3},{10... | collective-permute-start | bytes 393224 | tf_op jit(solution)/shard_map/ppermute | solution.py:579
  38.7 13.1 %collective-permute-start.12 = (f32[256,128]{1,0:T(8,128)S(1)}, f32[256,128]{1,0:T(8,128)S(1)}, u32[]{:S(2)}, u32[]{:S(2)}) collective-permute-start(f32[256,128]{1,0:T(8,128)S(1)} %get-tuple-element.43), channel_id=1, source_target_pairs={{0,4},{1,6},{2,12},{3,14},{4,0},{5,2},{6,8},{7,10},{8,5},{9,7},{10... | collective-permute-start | bytes 393224 | tf_op jit(solution)/shard_map/ppermute | solution.py:579
  42.2 9.5 %collective-permute-start.13 = (f32[256,128]{1,0:T(8,128)S(1)}, f32[256,128]{1,0:T(8,128)S(1)}, u32[]{:S(2)}, u32[]{:S(2)}) collective-permute-start(f32[256,128]{1,0:T(8,128)S(1)} %get-tuple-element.44), channel_id=1, source_target_pairs={{0,8},{1,10},{2,0},{3,2},{4,12},{5,14},{6,4},{7,6},{8,9},{9,11},{1... | collective-permute-start | bytes 393224 | tf_op jit(solution)/shard_map/ppermute | solution.py:579
  42.2 12.0 %collective-permute-start.14 = (f32[256,128]{1,0:T(8,128)S(1)}, f32[256,128]{1,0:T(8,128)S(1)}, u32[]{:S(2)}, u32[]{:S(2)}) collective-permute-start(f32[256,128]{1,0:T(8,128)S(1)} %get-tuple-element.45), channel_id=1, source_target_pairs={{0,12},{1,14},{2,4},{3,6},{4,8},{5,10},{6,0},{7,2},{8,13},{9,15},{... | collective-permute-start | bytes 393224 | tf_op jit(solution)/shard_map/ppermute | solution.py:579

commit v7 on v6

--- a/solution.py
+++ b/solution.py
@@ -170,7 +170,7 @@
 WINDOW = OUT_BINS + TAPS - 1
 REF_LINES = 8
 EDGE = 16
-STEPS = (2, 3, 1, 0)
+STEPS = (0, 1, 2, 3)
 
 
 def split_bf16(value):
@@ -271,8 +271,18 @@
             ]
 
 
-def pack_kernel(re_lines, im_lines, re_other, im_other, ref_own, ref_other, off_own, off_other, *refs):
-    messages, (re_all, im_all, ref_all) = refs[:-3], refs[-3:]
+def met(place, step, low):
+    return (place >> 1) ^ step ^ (2 * low)
+
+
+def pack_kernel(re_lines, im_lines, re_other, im_other, ref_own, ref_other, own_offsets, other_offsets, *refs):
+    messages, (re_all, im_all, ref_all, off_own, off_other, sems) = refs[:-6], refs[-6:]
+    copies = [
+        pltpu.make_async_copy(source, target, sems.at[at])
+        for at, (source, target) in enumerate(((own_offsets, off_own), (other_offsets, off_other)))
+    ]
+    for copy in copies:
+        copy.start()
     bins, samples = re_other.shape
     part_rows = samples // FACTOR
     place, side = lax.axis_index("az"), lax.axis_index("rg")
@@ -287,10 +297,12 @@
     ref_all[EDGE + 2 * bins :, :] = jnp.zeros((EDGE, FACTOR), jnp.float32)
     for at, ref in ((own_at, ref_own), (other_at, ref_other)):
         ref_all[pl.ds(pl.multiple_of(at, 16), bins), :] = jnp.concatenate([ref[...], ref[...]], axis=1)
+    for copy in copies:
+        copy.wait()
     lane = lax.broadcasted_iota(jnp.int32, (1, FACTOR), 1)
     for at, message in enumerate(messages):
         body = WINDOW * part_rows
-        start = window_start(((place >> 1) ^ at) * 2 + side, side, off_own, off_other) + EDGE
+        start = window_start(met(place, at, place & 1) * 2 + side, side, off_own, off_other) + EDGE
         rows = pl.ds(pl.multiple_of(start * part_rows, 8), body)
         message[:body, :] = re_all[rows, :]
         message[body : 2 * body, :] = im_all[rows, :]
@@ -313,7 +325,7 @@
     line = lax.broadcasted_iota(jnp.int32, (2 * len(STEPS), FACTOR), 0)
     for which in range(2):
         owner = owners[which]
-        step = (owner >> 1) ^ (place >> 1)
+        step = met(place, owner >> 1, owner & 1)
         wanted = jnp.where((owner & 1) == side, step, step + len(STEPS))
         choice[which] = jnp.where(line == wanted, 1.0, 0.0)
     start = window_start(place, side, off_own, off_other)
@@ -338,7 +350,7 @@
     chunks = dict(zip(STEPS, refs))
     keep, give = refs[len(STEPS) :]
     place, side = lax.axis_index("az"), lax.axis_index("rg")
-    sign = jnp.where(place >= PLACES // 2, -1.0, 1.0)
+    sign = jnp.where((place >> 2) ^ side == 1, -1.0, 1.0)
     even = side == 0
     keep_near, keep_far = jnp.where(even, 1.0, sign), jnp.where(even, 1.0, -sign)
     give_near, give_far = jnp.where(even, sign, 1.0), jnp.where(even, -sign, 1.0)
@@ -476,7 +488,7 @@
 
 
 def place_kernel(*refs):
-    messages, (out_re, out_im, re_all, im_all) = refs[:-4], refs[-4:]
+    messages, (out_re, out_im, re_all, im_all, tiles, sems) = refs[:-6], refs[-6:]
     bins, samples = out_re.shape
     place = lax.axis_index("az")
     for at, message in enumerate(messages):
@@ -485,12 +497,16 @@
             line = pl.multiple_of((sender * OUT_BINS + out) * PART, 8)
             re_all[pl.ds(line, PART), :] = message[2 * out * PART : (2 * out + 1) * PART, :]
             im_all[pl.ds(line, PART), :] = message[(2 * out + 1) * PART : (2 * out + 2) * PART, :]
+    copies = []
     for out, all_ref in ((out_re, re_all), (out_im, im_all)):
         for tile in range(0, bins, 8):
+            at = len(copies)
             for row in range(PART):
-                out[tile : tile + 8, row * FACTOR : (row + 1) * FACTOR] = all_ref[
-                    pl.ds(tile * PART + row, 8, stride=PART), :
-                ]
+                tiles[at, :, row * FACTOR : (row + 1) * FACTOR] = all_ref[pl.ds(tile * PART + row, 8, stride=PART), :]
+            copies.append(pltpu.make_async_copy(tiles.at[at], out.at[pl.ds(tile, 8)], sems.at[at]))
+            copies[-1].start()
+    for copy in copies:
+        copy.wait()
 
 
 VMEM = pl.BlockSpec(memory_space=pltpu.VMEM)
@@ -527,14 +543,24 @@
 
     lines = [raw_re.reshape(bins * PART, FACTOR), raw_im.reshape(bins * PART, FACTOR)]
     all_bins = 2 * bins + 2 * EDGE
-    messages = kernel_call(
+    anywhere = pl.BlockSpec(memory_space=pl.ANY)
+    messages = pl.pallas_call(
         pack_kernel,
-        "pack",
-        [array(2 * WINDOW * PART + REF_LINES, FACTOR)] * half,
-        [*lines, re_other, im_other, ref_own, ref_other, offsets, offsets_other],
-        scratch=[(all_bins * PART, FACTOR), (all_bins * PART, FACTOR), (all_bins, FACTOR)],
-        count=4 * 10**6,
-    )
+        out_shape=[array(2 * WINDOW * PART + REF_LINES, FACTOR)] * half,
+        in_specs=[VMEM] * 6 + [anywhere] * 2,
+        out_specs=[VMEM] * half,
+        scratch_shapes=[
+            pltpu.VMEM((all_bins * PART, FACTOR), jnp.float32),
+            pltpu.VMEM((all_bins * PART, FACTOR), jnp.float32),
+            pltpu.VMEM((all_bins, FACTOR), jnp.float32),
+            pltpu.SMEM(offsets.shape, jnp.int32),
+            pltpu.SMEM(offsets.shape, jnp.int32),
+            pltpu.SemaphoreType.DMA((2,)),
+        ],
+        compiler_params=pltpu.CompilerParams(vmem_limit_bytes=8 * 1024 * 1024),
+        cost_estimate=pl.CostEstimate(flops=1, bytes_accessed=1, transcendentals=0),
+        name="pack",
+    )(*lines, re_other, im_other, ref_own, ref_other, offsets, offsets_other)
     prepared = kernel_call(
         functools.partial(phase_kernel, 2 * bins),
         "phase",
@@ -544,7 +570,7 @@
 
     routes = [
         [
-            (chip * 2 + core, (((chip >> 1) ^ step) * 2 + core) * 2 + (chip & 1))
+            (chip * 2 + core, (met(chip, step, chip & 1) * 2 + core) * 2 + (chip & 1))
             for chip in range(PLACES)
             for core in range(2)
         ]
@@ -577,9 +603,22 @@
     )
     sent = kernel_call(join_kernel, "join", [array(2 * OUT_BINS * PART, FACTOR)] * half, [keep, swap(give)])
     results = [lax.ppermute(message, ("az", "rg"), route) for message, route in zip(sent, routes_back)]
-    return kernel_call(
-        place_kernel, "place", [array(bins, samples)] * 2, results, scratch=[(bins * PART, FACTOR)] * 2
-    )
+    tiles = 2 * bins // 8
+    return pl.pallas_call(
+        place_kernel,
+        out_shape=[array(bins, samples)] * 2,
+        in_specs=[VMEM] * half,
+        out_specs=[anywhere] * 2,
+        scratch_shapes=[
+            pltpu.VMEM((bins * PART, FACTOR), jnp.float32),
+            pltpu.VMEM((bins * PART, FACTOR), jnp.float32),
+            pltpu.VMEM((tiles, 8, samples), jnp.float32),
+            pltpu.SemaphoreType.DMA((tiles,)),
+        ],
+        compiler_params=pltpu.CompilerParams(vmem_limit_bytes=8 * 1024 * 1024),
+        cost_estimate=pl.CostEstimate(flops=1, bytes_accessed=1, transcendentals=0),
+        name="place",
+    )(*results)
 
 
 def solution(mesh):

time: 55.4 us -> 59.5 us (1.074)
  waiting for transfers between devices: 28.9 us -> 31.4 us
  starting transfers between devices: 17.4 us -> 18.7 us
    ppermute x4, waiting for transfers between devices: 13.6 us -> 15.8 us  [transposed_shards(): lax.ppermute(messages[step], ('az', 'rg'), routes[step])]
    pallas_call x7 -> x5, Pallas kernels: 6.11 us -> 4.34 us  [kernel_call(): pl.pallas_call(body, out_shape=out_shape, in_specs=specs, out_specs=jax.t...]
    pallas_call x0 -> x2, Pallas kernels: none -> 1.59 us  [the longest x1 0.92 us: transposed_shards(): pl.pallas_call(place_kernel, out_shape=[array(bins, samples)] * 2, in_spe...]
    ppermute x4, starting transfers between devices: 6.86 us -> 7.88 us  [transposed_shards(): lax.ppermute(message, ('az', 'rg'), route)]
    ppermute x4, starting transfers between devices: 8.37 us -> 9.22 us  [transposed_shards(): lax.ppermute(messages[step], ('az', 'rg'), routes[step])]
  transfers between devices with their start and end apart: 15 -> 15, of which waited for: 9 -> 10; matrix products, arithmetic and copies ran while one was open for 2% -> 2% of each run, Pallas kernels for 4% -> 4%
where the time goes in v7:
time: 59.5 us; the launch traced here: 59.3 us
  waiting for transfers between devices  31.4 us (53%)
  starting transfers between devices  18.7 us (31%)
  Pallas kernels  5.93 us (10%)
  local copies, waits for them, and re-layouts  2.38 us (4%)
  between operations  0.81 us (1%)
    ppermute x4, waiting for transfers between devices, transposed_shards(): lax.ppermute(messages[step], ('az', 'rg'), routes[step])  15.8 us
    ppermute x4, waiting for transfers between devices, transposed_shards(): lax.ppermute(message, ('az', 'rg'), route)  12.1 us
    ppermute x4, starting transfers between devices, transposed_shards(): lax.ppermute(messages[step], ('az', 'rg'), routes[step])  9.22 us
    ppermute x4, starting transfers between devices, transposed_shards(): lax.ppermute(message, ('az', 'rg'), route)  7.88 us
    pallas_call x5, Pallas kernels, kernel_call(): pl.pallas_call(body, out_shape=out_shape, in_specs=specs, out_specs=jax.t...  4.34 us
    ppermute x1, waiting for transfers between devices, transposed_shards(): swap(give)  1.41 us
    unnamed x23, local copies, waits for them, and re-layouts  1.34 us
  transfers between devices with their start and end apart: 15, of which 10 were waited for; matrix products, arithmetic and copies ran while one was open for 2% of the time, Pallas kernels for 4%

profile of v7, /device:TPU:13, one launch (start us, length us, event | category | flops | bytes accessed | tf_op | source)
XLA Modules:
  0.0 59.3 jit_solution(10511293810865939521)
XLA Ops:
  0.6 0.7 %collective-permute-start = (f32[32,2048]{1,0:T(8,128)}, f32[32,2048]{1,0:T(8,128)S(1)}, u32[]{:S(2)}, u32[]{:S(2)}) collective-permute-start(f32[32,2048]{1,0:T(8,128)} %param.12), channel_id=1, source_target_pairs={{0,1},{1,0},{2,3},{3,2},{4,5},{5,4},{6,7},{7,6},{8,9},{9,8},{10,11... | collective-permute-start | bytes 786440 | tf_op jit(solution)/shard_map/ppermute | solution.py:542
  1.4 0.1 collective-permute-start.1
  1.5 0.4 collective-permute-start.2
  1.9 0.1 collective-permute-start.3
  2.0 1.0 %reshape.10.re_lines = f32[512,128]{1,0:T(8,128)S(1)} reshape(f32[32,2048]{1,0:T(8,128)} %param.12) | data formatting | bytes 524288 | tf_op jit(solution)/shard_map/reshape | solution.py:544
  3.1 0.1 collective-permute-done.2.ref_other
  3.2 0.5 copy-done.6
  3.7 0.7 %pack.1 = (f32[488,128]{1,0:T(8,128)S(1)}, f32[488,128]{1,0:T(8,128)S(1)}, f32[488,128]{1,0:T(8,128)S(1)}, f32[488,128]{1,0:T(8,128)S(1)}) custom-call(f32[512,128]{1,0:T(8,128)S(1)} %reshape.10.re_lines, f32[512,128]{1,0:T(8,128)S(1)} %reshape.11.im_lines, f32[32,2048]{1,0:T(8,128)S(1)} %collective-permute-done.re_other, ...), custom_call_target="tpu_custom_call" | custom-call | flops 1 | bytes 1 | tf_op jit(solution)/shard_map/pack/pallas_call | solution.py:547
  4.4 3.4 %collective-permute-start.4 = (f32[488,128]{1,0:T(8,128)S(1)}, f32[488,128]{1,0:T(8,128)S(1)}, u32[]{:S(2)}, u32[]{:S(2)}) collective-permute-start(f32[488,128]{1,0:T(8,128)S(1)} %get-tuple-element.24), channel_id=1, source_target_pairs={{0,0},{1,2},{2,9},{3,11},{4,4},{5,6},{6,13},{7,15},{8,8},{9,10},{1... | collective-permute-start | bytes 749576 | tf_op jit(solution)/shard_map/ppermute | solution.py:587
  7.8 2.2 %collective-permute-start.5 = (f32[488,128]{1,0:T(8,128)S(1)}, f32[488,128]{1,0:T(8,128)S(1)}, u32[]{:S(2)}, u32[]{:S(2)}) collective-permute-start(f32[488,128]{1,0:T(8,128)S(1)} %get-tuple-element.25), channel_id=1, source_target_pairs={{0,4},{1,6},{2,13},{3,15},{4,0},{5,2},{6,9},{7,11},{8,12},{9,14},{... | collective-permute-start | bytes 749576 | tf_op jit(solution)/shard_map/ppermute | solution.py:587
  10.0 3.2 %collective-permute-start.6 = (f32[488,128]{1,0:T(8,128)S(1)}, f32[488,128]{1,0:T(8,128)S(1)}, u32[]{:S(2)}, u32[]{:S(2)}) collective-permute-start(f32[488,128]{1,0:T(8,128)S(1)} %get-tuple-element.26), channel_id=1, source_target_pairs={{0,8},{1,10},{2,1},{3,3},{4,12},{5,14},{6,5},{7,7},{8,0},{9,2},{10... | collective-permute-start | bytes 749576 | tf_op jit(solution)/shard_map/ppermute | solution.py:587
  13.2 0.4 collective-permute-start.7
  13.7 1.2 %collective-permute-done.8.taps_other = f32[32,8]{1,0:T(8,128)S(1)} collective-permute-done((f32[32,8]{1,0:T(8,128)S(1)}, f32[32,8]{1,0:T(8,128)S(1)}, u32[]{:S(2)}, u32[]{:S(2)}) %collective-permute-start.8) | collective-permute-done | bytes 1056 | tf_op jit(solution)/shard_map/ppermute | solution.py:542
  14.9 1.9 %phase.1 = (f32[15,2,64,128]{3,2,1,0:T(8,128)S(1)}, f32[64,128]{1,0:T(8,128)S(1)}, f32[2,8,128]{2,1,0:T(8,128)S(1)}) custom-call(s32[2]{0:T(128)S(1)} %copy-done.7, s32[2]{0:T(128)S(1)} %collective-permute-done.3.other_offsets.off_other, s32[2]{0:T(128)S(1)} %copy-done.8, f32[32,8]{1,0:T(8,128)S(1)} %copy.15.taps_own, ...), custom_call_target="tpu_custom_call" | custom-call | bytes 1000000 | tf_op jit(solution)/shard_map/phase/pallas_call | solution.py:518
  16.8 14.1 %collective-permute-done.5.refs_1_ = f32[488,128]{1,0:T(8,128)S(1)} collective-permute-done((f32[488,128]{1,0:T(8,128)S(1)}, f32[488,128]{1,0:T(8,128)S(1)}, u32[]{:S(2)}, u32[]{:S(2)}) %collective-permute-start.5) | collective-permute-done | bytes 249888 | tf_op jit(solution)/shard_map/ppermute | solution.py:587
  31.0 1.7 %collective-permute-done.7.refs_3_ = f32[488,128]{1,0:T(8,128)S(1)} collective-permute-done((f32[488,128]{1,0:T(8,128)S(1)}, f32[488,128]{1,0:T(8,128)S(1)}, u32[]{:S(2)}, u32[]{:S(2)}) %collective-permute-start.7) | collective-permute-done | bytes 249888 | tf_op jit(solution)/shard_map/ppermute | solution.py:587
  32.6 0.2 parity.1
  32.9 0.7 %copy-done.5 = bf16[2,128,192]{2,1,0:T(8,128)(2,1)S(1)} copy-done((bf16[2,128,192]{2,1,0:T(8,128)(2,1)S(1)}, bf16[2,128,192]{2,1,0:T(8,128)(2,1)}, u32[]{:S(2)}) %copy-start.5) | copy-done | bytes 98328
  33.6 0.3 near.2.partial
  33.9 0.9 %collective-permute-done.9.got = f32[992,128]{1,0:T(8,128)S(1)} collective-permute-done((f32[992,128]{1,0:T(8,128)S(1)}, f32[992,128]{1,0:T(8,128)S(1)}, u32[]{:S(2)}, u32[]{:S(2)}) %collective-permute-start.9) | collective-permute-done | bytes 507936 | tf_op jit(solution)/shard_map/ppermute | solution.py:592
  34.8 1.9 %band.1 = (f32[512,128]{1,0:T(8,128)S(1)}, f32[512,128]{1,0:T(8,128)S(1)}) custom-call(f32[4,128,512]{2,1,0:T(8,128)S(1)} %near.2.partial, f32[992,128]{1,0:T(8,128)S(1)} %get-tuple-element.35.keep, f32[992,128]{1,0:T(8,128)S(1)} %collective-permute-done.9.got, f32[15,2,64,128]{3,2,1,0:T(8,128)S(1)} %get-tuple-element.37.phase, ...), custom_call_target="tpu_custom_call" | custom-call | bytes 1000000 | tf_op jit(solution)/shard_map/band/pallas_call | solution.py:518
  36.7 0.2 collective-permute-start.10
  36.9 1.4 %collective-permute-done.10.got = f32[512,128]{1,0:T(8,128)S(1)} collective-permute-done((f32[512,128]{1,0:T(8,128)S(1)}, f32[512,128]{1,0:T(8,128)S(1)}, u32[]{:S(2)}, u32[]{:S(2)}) %collective-permute-start.10) | collective-permute-done | bytes 262176 | tf_op jit(solution)/shard_map/ppermute | solution.py:604
  38.4 4.3 %collective-permute-start.11 = (f32[256,128]{1,0:T(8,128)S(1)}, f32[256,128]{1,0:T(8,128)S(1)}, u32[]{:S(2)}, u32[]{:S(2)}) collective-permute-start(f32[256,128]{1,0:T(8,128)S(1)} %get-tuple-element.42), channel_id=1, source_target_pairs={{0,0},{1,2},{2,8},{3,10},{4,4},{5,6},{6,12},{7,14},{8,1},{9,3},{10... | collective-permute-start | bytes 393224 | tf_op jit(solution)/shard_map/ppermute | solution.py:605
  42.7 0.8 %collective-permute-start.12 = (f32[256,128]{1,0:T(8,128)S(1)}, f32[256,128]{1,0:T(8,128)S(1)}, u32[]{:S(2)}, u32[]{:S(2)}) collective-permute-start(f32[256,128]{1,0:T(8,128)S(1)} %get-tuple-element.43), channel_id=1, source_target_pairs={{0,4},{1,6},{2,12},{3,14},{4,0},{5,2},{6,8},{7,10},{8,5},{9,7},{10... | collective-permute-start | bytes 393224 | tf_op jit(solution)/shard_map/ppermute | solution.py:605
  43.4 0.8 %collective-permute-start.13 = (f32[256,128]{1,0:T(8,128)S(1)}, f32[256,128]{1,0:T(8,128)S(1)}, u32[]{:S(2)}, u32[]{:S(2)}) collective-permute-start(f32[256,128]{1,0:T(8,128)S(1)} %get-tuple-element.44), channel_id=1, source_target_pairs={{0,8},{1,10},{2,0},{3,2},{4,12},{5,14},{6,4},{7,6},{8,9},{9,11},{1... | collective-permute-start | bytes 393224 | tf_op jit(solution)/shard_map/ppermute | solution.py:605
  44.2 2.0 %collective-permute-start.14 = (f32[256,128]{1,0:T(8,128)S(1)}, f32[256,128]{1,0:T(8,128)S(1)}, u32[]{:S(2)}, u32[]{:S(2)}) collective-permute-start(f32[256,128]{1,0:T(8,128)S(1)} %get-tuple-element.45), channel_id=1, source_target_pairs={{0,12},{1,14},{2,4},{3,6},{4,8},{5,10},{6,0},{7,2},{8,13},{9,15},{... | collective-permute-start | bytes 393224 | tf_op jit(solution)/shard_map/ppermute | solution.py:605
  46.3 0.7 %collective-permute-done.11.refs_0_ = f32[256,128]{1,0:T(8,128)S(1)} collective-permute-done((f32[256,128]{1,0:T(8,128)S(1)}, f32[256,128]{1,0:T(8,128)S(1)}, u32[]{:S(2)}, u32[]{:S(2)}) %collective-permute-start.11) | collective-permute-done | bytes 131104 | tf_op jit(solution)/shard_map/ppermute | solution.py:605
  47.0 6.1 %collective-permute-done.12.refs_1_ = f32[256,128]{1,0:T(8,128)S(1)} collective-permute-done((f32[256,128]{1,0:T(8,128)S(1)}, f32[256,128]{1,0:T(8,128)S(1)}, u32[]{:S(2)}, u32[]{:S(2)}) %collective-permute-start.12) | collective-permute-done | bytes 131104 | tf_op jit(solution)/shard_map/ppermute | solution.py:605
  53.0 0.1 collective-permute-done.13.refs_2_
  53.2 5.2 %collective-permute-done.14.refs_3_ = f32[256,128]{1,0:T(8,128)S(1)} collective-permute-done((f32[256,128]{1,0:T(8,128)S(1)}, f32[256,128]{1,0:T(8,128)S(1)}, u32[]{:S(2)}, u32[]{:S(2)}) %collective-permute-start.14) | collective-permute-done | bytes 131104 | tf_op jit(solution)/shard_map/ppermute | solution.py:605
  58.3 0.9 %place.1 = (f32[32,2048]{1,0:T(8,128)}, f32[32,2048]{1,0:T(8,128)}) custom-call(f32[256,128]{1,0:T(8,128)S(1)} %collective-permute-done.11.refs_0_, f32[256,128]{1,0:T(8,128)S(1)} %collective-permute-done.12.refs_1_, f32[256,128]{1,0:T(8,128)S(1)} %collective-permute-done.13.refs_2_, f32[256,128]{1,0:T(8,128)S(1)} %collective-permute-done.14.refs_3_), custom_call_target="tpu_custom_call" | custom-call | flops 1 | bytes 1 | tf_op jit(solution)/shard_map/place/pallas_call | solution.py:607
  (30 shorter events, 0.3 us)
Async XLA Ops:
  0.6 1.3 %copy-start.7 = (s32[2]{0:T(128)S(1)}, s32[2]{0:T(128)}, u32[]{:S(2)}) copy-start(s32[2]{0:T(128)} %off_own.1) | copy-start | bytes 28
  0.6 2.5 %collective-permute-start = (f32[32,2048]{1,0:T(8,128)}, f32[32,2048]{1,0:T(8,128)S(1)}, u32[]{:S(2)}, u32[]{:S(2)}) collective-permute-start(f32[32,2048]{1,0:T(8,128)} %param.12), channel_id=1, source_target_pairs={{0,1},{1,0},{2,3},{3,2},{4,5},{5,4},{6,7},{7,6},{8,9},{9,8},{10,11... | collective-permute-start | bytes 786440 | tf_op jit(solution)/shard_map/ppermute | solution.py:542
  1.4 1.8 %collective-permute-start.1 = (f32[32,2048]{1,0:T(8,128)}, f32[32,2048]{1,0:T(8,128)S(1)}, u32[]{:S(2)}, u32[]{:S(2)}) collective-permute-start(f32[32,2048]{1,0:T(8,128)} %param.13), channel_id=1, source_target_pairs={{0,1},{1,0},{2,3},{3,2},{4,5},{5,4},{6,7},{7,6},{8,9},{9,8},{10,11... | collective-permute-start | bytes 786440 | tf_op jit(solution)/shard_map/ppermute | solution.py:542
  1.5 1.5 %copy-start.9 = (f32[32,2048]{1,0:T(8,128)S(1)}, f32[32,2048]{1,0:T(8,128)}, u32[]{:S(2)}) copy-start(f32[32,2048]{1,0:T(8,128)} %param.13) | copy-start | bytes 786436
  1.5 1.7 %collective-permute-start.2 = (f32[32,64]{1,0:T(8,128)}, f32[32,64]{1,0:T(8,128)S(1)}, u32[]{:S(2)}, u32[]{:S(2)}) collective-permute-start(f32[32,64]{1,0:T(8,128)} %bitcast.3), channel_id=1, source_target_pairs={{0,1},{1,0},{2,3},{3,2},{4,5},{5,4},{6,7},{7,6},{8,9},{9,8},{10,11... | collective-permute-start | bytes 24584 | tf_op jit(solution)/shard_map/ppermute | solution.py:542
  1.9 1.2 %collective-permute-start.3 = (s32[2]{0:T(128)S(1)}, s32[2]{0:T(128)S(1)}, u32[]{:S(2)}, u32[]{:S(2)}) collective-permute-start(s32[2]{0:T(128)S(1)} %copy-done.7), channel_id=1, source_target_pairs={{0,1},{1,0},{2,3},{3,2},{4,5},{5,4},{6,7},{7,6},{8,9},{9,8},{10,11... | collective-permute-start | bytes 32 | tf_op jit(solution)/shard_map/ppermute | solution.py:541
  3.0 0.7 %copy-start.6 = (f32[1,64,32]{1,2,0:T(8,128)S(1)}, f32[1,64,32]{1,2,0:T(8,128)}, u32[]{:S(2)}) copy-start(f32[1,64,32]{1,2,0:T(8,128)} %param.14) | copy-start | bytes 24580
  4.4 9.3 %copy-start.10 = (f32[32,8]{0,1:T(8,128)S(1)}, f32[32,8]{0,1:T(8,128)}, u32[]{:S(2)}) copy-start(f32[32,8]{0,1:T(8,128)} %param.17) | copy-start | bytes 3076
  4.4 12.4 %collective-permute-start.4 = (f32[488,128]{1,0:T(8,128)S(1)}, f32[488,128]{1,0:T(8,128)S(1)}, u32[]{:S(2)}, u32[]{:S(2)}) collective-permute-start(f32[488,128]{1,0:T(8,128)S(1)} %get-tuple-element.24), channel_id=1, source_target_pairs={{0,0},{1,2},{2,9},{3,11},{4,4},{5,6},{6,13},{7,15},{8,8},{9,10},{1... | collective-permute-start | bytes 749576 | tf_op jit(solution)/shard_map/ppermute | solution.py:587
  7.8 23.1 %collective-permute-start.5 = (f32[488,128]{1,0:T(8,128)S(1)}, f32[488,128]{1,0:T(8,128)S(1)}, u32[]{:S(2)}, u32[]{:S(2)}) collective-permute-start(f32[488,128]{1,0:T(8,128)S(1)} %get-tuple-element.25), channel_id=1, source_target_pairs={{0,4},{1,6},{2,13},{3,15},{4,0},{5,2},{6,9},{7,11},{8,12},{9,14},{... | collective-permute-start | bytes 749576 | tf_op jit(solution)/shard_map/ppermute | solution.py:587
  10.0 21.0 %collective-permute-start.6 = (f32[488,128]{1,0:T(8,128)S(1)}, f32[488,128]{1,0:T(8,128)S(1)}, u32[]{:S(2)}, u32[]{:S(2)}) collective-permute-start(f32[488,128]{1,0:T(8,128)S(1)} %get-tuple-element.26), channel_id=1, source_target_pairs={{0,8},{1,10},{2,1},{3,3},{4,12},{5,14},{6,5},{7,7},{8,0},{9,2},{10... | collective-permute-start | bytes 749576 | tf_op jit(solution)/shard_map/ppermute | solution.py:587
  13.2 1.7 %copy-start.8 = (s32[2]{0:T(128)S(1)}, s32[2]{0:T(128)}, u32[]{:S(2)}) copy-start(s32[2]{0:T(128)} %owners.1) | copy-start | bytes 28
  13.2 19.4 %collective-permute-start.7 = (f32[488,128]{1,0:T(8,128)S(1)}, f32[488,128]{1,0:T(8,128)S(1)}, u32[]{:S(2)}, u32[]{:S(2)}) collective-permute-start(f32[488,128]{1,0:T(8,128)S(1)} %get-tuple-element.27), channel_id=1, source_target_pairs={{0,12},{1,14},{2,5},{3,7},{4,8},{5,10},{6,1},{7,3},{8,4},{9,6},{10... | collective-permute-start | bytes 749576 | tf_op jit(solution)/shard_map/ppermute | solution.py:587
  13.7 1.2 %collective-permute-start.8 = (f32[32,8]{1,0:T(8,128)S(1)}, f32[32,8]{1,0:T(8,128)S(1)}, u32[]{:S(2)}, u32[]{:S(2)}) collective-permute-start(f32[32,8]{1,0:T(8,128)S(1)} %copy.15.taps_own), channel_id=1, source_target_pairs={{0,1},{1,0},{2,3},{3,2},{4,5},{5,4},{6,7},{7,6},{8,9},{9,8},{10,11... | collective-permute-start | bytes 3080 | tf_op jit(solution)/shard_map/ppermute | solution.py:542
  32.6 0.9 %copy-start.5 = (bf16[2,128,192]{2,1,0:T(8,128)(2,1)S(1)}, bf16[2,128,192]{2,1,0:T(8,128)(2,1)}, u32[]{:S(2)}) copy-start(bf16[2,128,192]{2,1,0:T(8,128)(2,1)} %constant.12.clone.near) | copy-start | bytes 294916
  32.8 2.0 %collective-permute-start.9 = (f32[992,128]{1,0:T(8,128)S(1)}, f32[992,128]{1,0:T(8,128)S(1)}, u32[]{:S(2)}, u32[]{:S(2)}) collective-permute-start(f32[992,128]{1,0:T(8,128)S(1)} %get-tuple-element.36), channel_id=1, source_target_pairs={{0,1},{1,0},{2,3},{3,2},{4,5},{5,4},{6,7},{7,6},{8,9},{9,8},{10,11... | collective-permute-start | bytes 1523720 | tf_op jit(solution)/shard_map/ppermute | solution.py:592
  33.5 1.2 %copy-start = (bf16[2,256,256]{2,1,0:T(8,128)(2,1)S(1)}, bf16[2,256,256]{2,1,0:T(8,128)(2,1)}, u32[]{:S(2)}) copy-start(bf16[2,256,256]{2,1,0:T(8,128)(2,1)} %constant.15.clone.back) | copy-start | bytes 786436
  33.5 1.2 %copy-start.1 = (bf16[2,256,256]{2,1,0:T(8,128)(2,1)S(1)}, bf16[2,256,256]{2,1,0:T(8,128)(2,1)}, u32[]{:S(2)}) copy-start(bf16[2,256,256]{2,1,0:T(8,128)(2,1)} %constant.14.clone.there) | copy-start | bytes 786436
  33.6 1.2 %copy-start.2 = (f32[2,2,64,128]{3,2,1,0:T(8,128)S(1)}, f32[2,2,64,128]{3,2,1,0:T(8,128)}, u32[]{:S(2)}) copy-start(f32[2,2,64,128]{3,2,1,0:T(8,128)} %constant.17.clone.twists) | copy-start | bytes 393220
  33.6 1.2 %copy-start.3 = (bf16[2,2,128,128]{3,2,1,0:T(8,128)(2,1)S(1)}, bf16[2,2,128,128]{3,2,1,0:T(8,128)(2,1)}, u32[]{:S(2)}) copy-start(bf16[2,2,128,128]{3,2,1,0:T(8,128)(2,1)} %constant.16.clone.last) | copy-start | bytes 393220
  33.6 1.2 %copy-start.4 = (bf16[2,128,192]{2,1,0:T(8,128)(2,1)S(1)}, bf16[2,128,192]{2,1,0:T(8,128)(2,1)}, u32[]{:S(2)}) copy-start(bf16[2,128,192]{2,1,0:T(8,128)(2,1)} %constant.13.clone.far) | copy-start | bytes 294916
  36.7 1.6 %collective-permute-start.10 = (f32[512,128]{1,0:T(8,128)S(1)}, f32[512,128]{1,0:T(8,128)S(1)}, u32[]{:S(2)}, u32[]{:S(2)}) collective-permute-start(f32[512,128]{1,0:T(8,128)S(1)} %get-tuple-element.41), channel_id=1, source_target_pairs={{0,1},{1,0},{2,3},{3,2},{4,5},{5,4},{6,7},{7,6},{8,9},{9,8},{10,11... | collective-permute-start | bytes 786440 | tf_op jit(solution)/shard_map/ppermute | solution.py:604
  38.4 8.6 %collective-permute-start.11 = (f32[256,128]{1,0:T(8,128)S(1)}, f32[256,128]{1,0:T(8,128)S(1)}, u32[]{:S(2)}, u32[]{:S(2)}) collective-permute-start(f32[256,128]{1,0:T(8,128)S(1)} %get-tuple-element.42), channel_id=1, source_target_pairs={{0,0},{1,2},{2,8},{3,10},{4,4},{5,6},{6,12},{7,14},{8,1},{9,3},{10... | collective-permute-start | bytes 393224 | tf_op jit(solution)/shard_map/ppermute | solution.py:605
  42.7 10.4 %collective-permute-start.12 = (f32[256,128]{1,0:T(8,128)S(1)}, f32[256,128]{1,0:T(8,128)S(1)}, u32[]{:S(2)}, u32[]{:S(2)}) collective-permute-start(f32[256,128]{1,0:T(8,128)S(1)} %get-tuple-element.43), channel_id=1, source_target_pairs={{0,4},{1,6},{2,12},{3,14},{4,0},{5,2},{6,8},{7,10},{8,5},{9,7},{10... | collective-permute-start | bytes 393224 | tf_op jit(solution)/shard_map/ppermute | solution.py:605
  43.4 9.7 %collective-permute-start.13 = (f32[256,128]{1,0:T(8,128)S(1)}, f32[256,128]{1,0:T(8,128)S(1)}, u32[]{:S(2)}, u32[]{:S(2)}) collective-permute-start(f32[256,128]{1,0:T(8,128)S(1)} %get-tuple-element.44), channel_id=1, source_target_pairs={{0,8},{1,10},{2,0},{3,2},{4,12},{5,14},{6,4},{7,6},{8,9},{9,11},{1... | collective-permute-start | bytes 393224 | tf_op jit(solution)/shard_map/ppermute | solution.py:605
  44.2 14.1 %collective-permute-start.14 = (f32[256,128]{1,0:T(8,128)S(1)}, f32[256,128]{1,0:T(8,128)S(1)}, u32[]{:S(2)}, u32[]{:S(2)}) collective-permute-start(f32[256,128]{1,0:T(8,128)S(1)} %get-tuple-element.45), channel_id=1, source_target_pairs={{0,12},{1,14},{2,4},{3,6},{4,8},{5,10},{6,0},{7,2},{8,13},{9,15},{... | collective-permute-start | bytes 393224 | tf_op jit(solution)/shard_map/ppermute | solution.py:605

commit v8 on v7

--- a/solution.py
+++ b/solution.py
@@ -170,7 +170,7 @@
 WINDOW = OUT_BINS + TAPS - 1
 REF_LINES = 8
 EDGE = 16
-STEPS = (0, 1, 2, 3)
+STEPS = (2, 3, 1, 0)
 
 
 def split_bf16(value):
@@ -271,10 +271,6 @@
             ]
 
 
-def met(place, step, low):
-    return (place >> 1) ^ step ^ (2 * low)
-
-
 def pack_kernel(re_lines, im_lines, re_other, im_other, ref_own, ref_other, own_offsets, other_offsets, *refs):
     messages, (re_all, im_all, ref_all, off_own, off_other, sems) = refs[:-6], refs[-6:]
     copies = [
@@ -302,7 +298,7 @@
     lane = lax.broadcasted_iota(jnp.int32, (1, FACTOR), 1)
     for at, message in enumerate(messages):
         body = WINDOW * part_rows
-        start = window_start(met(place, at, place & 1) * 2 + side, side, off_own, off_other) + EDGE
+        start = window_start(((place >> 1) ^ at) * 2 + side, side, off_own, off_other) + EDGE
         rows = pl.ds(pl.multiple_of(start * part_rows, 8), body)
         message[:body, :] = re_all[rows, :]
         message[body : 2 * body, :] = im_all[rows, :]
@@ -325,7 +321,7 @@
     line = lax.broadcasted_iota(jnp.int32, (2 * len(STEPS), FACTOR), 0)
     for which in range(2):
         owner = owners[which]
-        step = met(place, owner >> 1, owner & 1)
+        step = (owner >> 1) ^ (place >> 1)
         wanted = jnp.where((owner & 1) == side, step, step + len(STEPS))
         choice[which] = jnp.where(line == wanted, 1.0, 0.0)
     start = window_start(place, side, off_own, off_other)
@@ -350,7 +346,7 @@
     chunks = dict(zip(STEPS, refs))
     keep, give = refs[len(STEPS) :]
     place, side = lax.axis_index("az"), lax.axis_index("rg")
-    sign = jnp.where((place >> 2) ^ side == 1, -1.0, 1.0)
+    sign = jnp.where(place >= PLACES // 2, -1.0, 1.0)
     even = side == 0
     keep_near, keep_far = jnp.where(even, 1.0, sign), jnp.where(even, 1.0, -sign)
     give_near, give_far = jnp.where(even, sign, 1.0), jnp.where(even, -sign, 1.0)
@@ -487,24 +483,21 @@
             message[line * PART : (line + 1) * PART, :] = keep[read, :] * keep_factor + got[read, :] * got_factor
 
 
+def tile_kernel(message, re_tile, im_tile):
+    for part, tile in enumerate((re_tile, im_tile)):
+        for row in range(PART):
+            tile[:, row * FACTOR : (row + 1) * FACTOR] = message[pl.ds(part * PART + row, OUT_BINS, stride=2 * PART), :]
+
+
 def place_kernel(*refs):
-    messages, (out_re, out_im, re_all, im_all, tiles, sems) = refs[:-6], refs[-6:]
-    bins, samples = out_re.shape
+    tiles, (out_re, out_im, sems) = refs[:-3], refs[-3:]
     place = lax.axis_index("az")
-    for at, message in enumerate(messages):
-        sender = crossed((place >> 1) ^ at)
-        for out in range(OUT_BINS):
-            line = pl.multiple_of((sender * OUT_BINS + out) * PART, 8)
-            re_all[pl.ds(line, PART), :] = message[2 * out * PART : (2 * out + 1) * PART, :]
-            im_all[pl.ds(line, PART), :] = message[(2 * out + 1) * PART : (2 * out + 2) * PART, :]
     copies = []
-    for out, all_ref in ((out_re, re_all), (out_im, im_all)):
-        for tile in range(0, bins, 8):
-            at = len(copies)
-            for row in range(PART):
-                tiles[at, :, row * FACTOR : (row + 1) * FACTOR] = all_ref[pl.ds(tile * PART + row, 8, stride=PART), :]
-            copies.append(pltpu.make_async_copy(tiles.at[at], out.at[pl.ds(tile, 8)], sems.at[at]))
-            copies[-1].start()
+    for at, tile in enumerate(tiles):
+        sender = crossed((place >> 1) ^ (at // 2))
+        rows = pl.ds(pl.multiple_of(sender * OUT_BINS, 8), OUT_BINS)
+        copies.append(pltpu.make_async_copy(tile, (out_re, out_im)[at % 2].at[rows], sems.at[at]))
+        copies[-1].start()
     for copy in copies:
         copy.wait()
 
@@ -570,7 +563,7 @@
 
     routes = [
         [
-            (chip * 2 + core, (met(chip, step, chip & 1) * 2 + core) * 2 + (chip & 1))
+            (chip * 2 + core, (((chip >> 1) ^ step) * 2 + core) * 2 + (chip & 1))
             for chip in range(PLACES)
             for core in range(2)
         ]
@@ -603,22 +596,19 @@
     )
     sent = kernel_call(join_kernel, "join", [array(2 * OUT_BINS * PART, FACTOR)] * half, [keep, swap(give)])
     results = [lax.ppermute(message, ("az", "rg"), route) for message, route in zip(sent, routes_back)]
-    tiles = 2 * bins // 8
+    tiles = []
+    for message in results:
+        tiles += kernel_call(tile_kernel, "tile", [array(OUT_BINS, samples)] * 2, [message])
     return pl.pallas_call(
         place_kernel,
         out_shape=[array(bins, samples)] * 2,
-        in_specs=[VMEM] * half,
+        in_specs=[VMEM] * len(tiles),
         out_specs=[anywhere] * 2,
-        scratch_shapes=[
-            pltpu.VMEM((bins * PART, FACTOR), jnp.float32),
-            pltpu.VMEM((bins * PART, FACTOR), jnp.float32),
-            pltpu.VMEM((tiles, 8, samples), jnp.float32),
-            pltpu.SemaphoreType.DMA((tiles,)),
-        ],
+        scratch_shapes=[pltpu.SemaphoreType.DMA((len(tiles),))],
         compiler_params=pltpu.CompilerParams(vmem_limit_bytes=8 * 1024 * 1024),
         cost_estimate=pl.CostEstimate(flops=1, bytes_accessed=1, transcendentals=0),
         name="place",
-    )(*results)
+    )(*tiles)
 
 
 def solution(mesh):

time: 59.5 us -> 55.3 us (0.929)
  waiting for transfers between devices: 31.4 us -> 28.6 us
  starting transfers between devices: 18.7 us -> 17.4 us
    ppermute x4, waiting for transfers between devices: 15.8 us -> 13.6 us  [transposed_shards(): lax.ppermute(messages[step], ('az', 'rg'), routes[step])]
    ppermute x4, starting transfers between devices: 7.88 us -> 6.85 us  [transposed_shards(): lax.ppermute(message, ('az', 'rg'), route)]
    ppermute x4, starting transfers between devices: 9.22 us -> 8.37 us  [transposed_shards(): lax.ppermute(messages[step], ('az', 'rg'), routes[step])]
    pallas_call x5 -> x9, Pallas kernels: 4.34 us -> 4.67 us  [kernel_call(): pl.pallas_call(body, out_shape=out_shape, in_specs=specs, out_specs=jax.t...]
  transfers between devices with their start and end apart: 15 -> 15, of which waited for: 10 -> 9; matrix products, arithmetic and copies ran while one was open for 2% -> 2% of each run, Pallas kernels for 4% -> 4%
where the time goes in v8:
time: 55.3 us; the launch traced here: 55 us
  waiting for transfers between devices  28.6 us (52%)
  starting transfers between devices  17.4 us (31%)
  Pallas kernels  6.21 us (11%)
  local copies, waits for them, and re-layouts  2.05 us (4%)
  between operations  0.81 us (1%)
    ppermute x4, waiting for transfers between devices, transposed_shards(): lax.ppermute(messages[step], ('az', 'rg'), routes[step])  13.6 us
    ppermute x4, waiting for transfers between devices, transposed_shards(): lax.ppermute(message, ('az', 'rg'), route)  11.7 us
    ppermute x4, starting transfers between devices, transposed_shards(): lax.ppermute(messages[step], ('az', 'rg'), routes[step])  8.37 us
    ppermute x4, starting transfers between devices, transposed_shards(): lax.ppermute(message, ('az', 'rg'), route)  6.85 us
    pallas_call x9, Pallas kernels, kernel_call(): pl.pallas_call(body, out_shape=out_shape, in_specs=specs, out_specs=jax.t...  4.67 us
    ppermute x1, waiting for transfers between devices, transposed_shards(): swap(give)  1.2 us
    ppermute x1, waiting for transfers between devices, transposed_shards(): swap(taps)  1.17 us
  transfers between devices with their start and end apart: 15, of which 9 were waited for; matrix products, arithmetic and copies ran while one was open for 2% of the time, Pallas kernels for 4%

profile of v8, /device:TPU:13, one launch (start us, length us, event | category | flops | bytes accessed | tf_op | source)
XLA Modules:
  0.0 55.0 jit_solution(3808718800054389165)
XLA Ops:
  0.6 0.7 %collective-permute-start = (f32[32,2048]{1,0:T(8,128)}, f32[32,2048]{1,0:T(8,128)S(1)}, u32[]{:S(2)}, u32[]{:S(2)}) collective-permute-start(f32[32,2048]{1,0:T(8,128)} %param.12), channel_id=1, source_target_pairs={{0,1},{1,0},{2,3},{3,2},{4,5},{5,4},{6,7},{7,6},{8,9},{9,8},{10,11... | collective-permute-start | bytes 786440 | tf_op jit(solution)/shard_map/ppermute | solution.py:535
  1.5 0.4 collective-permute-start.2
  2.0 1.0 %reshape.10.re_lines = f32[512,128]{1,0:T(8,128)S(1)} reshape(f32[32,2048]{1,0:T(8,128)} %param.12) | data formatting | bytes 524288 | tf_op jit(solution)/shard_map/reshape | solution.py:537
  3.1 0.1 collective-permute-done.2.ref_other
  3.2 0.5 copy-done.6
  3.7 0.7 %pack.1 = (f32[488,128]{1,0:T(8,128)S(1)}, f32[488,128]{1,0:T(8,128)S(1)}, f32[488,128]{1,0:T(8,128)S(1)}, f32[488,128]{1,0:T(8,128)S(1)}) custom-call(f32[512,128]{1,0:T(8,128)S(1)} %reshape.10.re_lines, f32[512,128]{1,0:T(8,128)S(1)} %reshape.11.im_lines, f32[32,2048]{1,0:T(8,128)S(1)} %collective-permute-done.re_other, ...), custom_call_target="tpu_custom_call" | custom-call | flops 1 | bytes 1 | tf_op jit(solution)/shard_map/pack/pallas_call | solution.py:540
  4.4 3.6 %collective-permute-start.4 = (f32[488,128]{1,0:T(8,128)S(1)}, f32[488,128]{1,0:T(8,128)S(1)}, u32[]{:S(2)}, u32[]{:S(2)}) collective-permute-start(f32[488,128]{1,0:T(8,128)S(1)} %get-tuple-element.32), channel_id=1, source_target_pairs={{0,8},{1,10},{2,9},{3,11},{4,12},{5,14},{6,13},{7,15},{8,0},{9,2},... | collective-permute-start | bytes 749576 | tf_op jit(solution)/shard_map/ppermute | solution.py:580
  8.0 2.4 %collective-permute-start.6 = (f32[488,128]{1,0:T(8,128)S(1)}, f32[488,128]{1,0:T(8,128)S(1)}, u32[]{:S(2)}, u32[]{:S(2)}) collective-permute-start(f32[488,128]{1,0:T(8,128)S(1)} %get-tuple-element.34), channel_id=1, source_target_pairs={{0,4},{1,6},{2,5},{3,7},{4,0},{5,2},{6,1},{7,3},{8,12},{9,14},{10,... | collective-permute-start | bytes 749576 | tf_op jit(solution)/shard_map/ppermute | solution.py:580
  10.4 2.3 %collective-permute-start.7 = (f32[488,128]{1,0:T(8,128)S(1)}, f32[488,128]{1,0:T(8,128)S(1)}, u32[]{:S(2)}, u32[]{:S(2)}) collective-permute-start(f32[488,128]{1,0:T(8,128)S(1)} %get-tuple-element.35), channel_id=1, source_target_pairs={{0,0},{1,2},{2,1},{3,3},{4,4},{5,6},{6,5},{7,7},{8,8},{9,10},{10,9... | collective-permute-start | bytes 749576 | tf_op jit(solution)/shard_map/ppermute | solution.py:580
  12.9 1.2 %collective-permute-done.8.taps_other = f32[32,8]{1,0:T(8,128)S(1)} collective-permute-done((f32[32,8]{1,0:T(8,128)S(1)}, f32[32,8]{1,0:T(8,128)S(1)}, u32[]{:S(2)}, u32[]{:S(2)}) %collective-permute-start.8) | collective-permute-done | bytes 1056 | tf_op jit(solution)/shard_map/ppermute | solution.py:535
  14.1 1.9 %phase.1 = (f32[15,2,64,128]{3,2,1,0:T(8,128)S(1)}, f32[64,128]{1,0:T(8,128)S(1)}, f32[2,8,128]{2,1,0:T(8,128)S(1)}) custom-call(s32[2]{0:T(128)S(1)} %copy-done.7, s32[2]{0:T(128)S(1)} %collective-permute-done.3.other_offsets.off_other, s32[2]{0:T(128)S(1)} %copy-done.8, f32[32,8]{1,0:T(8,128)S(1)} %copy.15.taps_own, ...), custom_call_target="tpu_custom_call" | custom-call | bytes 1000000 | tf_op jit(solution)/shard_map/phase/pallas_call | solution.py:511
  16.0 8.2 %collective-permute-done.4.refs_0_ = f32[488,128]{1,0:T(8,128)S(1)} collective-permute-done((f32[488,128]{1,0:T(8,128)S(1)}, f32[488,128]{1,0:T(8,128)S(1)}, u32[]{:S(2)}, u32[]{:S(2)}) %collective-permute-start.4) | collective-permute-done | bytes 249888 | tf_op jit(solution)/shard_map/ppermute | solution.py:580
  24.2 5.4 %collective-permute-done.5.refs_1_ = f32[488,128]{1,0:T(8,128)S(1)} collective-permute-done((f32[488,128]{1,0:T(8,128)S(1)}, f32[488,128]{1,0:T(8,128)S(1)}, u32[]{:S(2)}, u32[]{:S(2)}) %collective-permute-start.5) | collective-permute-done | bytes 249888 | tf_op jit(solution)/shard_map/ppermute | solution.py:580
  29.6 0.2 parity.1
  29.7 0.4 collective-permute-start.9
  30.1 0.3 copy-done.5
  30.5 0.3 near.2.partial
  30.8 0.9 %collective-permute-done.9.got = f32[992,128]{1,0:T(8,128)S(1)} collective-permute-done((f32[992,128]{1,0:T(8,128)S(1)}, f32[992,128]{1,0:T(8,128)S(1)}, u32[]{:S(2)}, u32[]{:S(2)}) %collective-permute-start.9) | collective-permute-done | bytes 507936 | tf_op jit(solution)/shard_map/ppermute | solution.py:585
  31.7 1.9 %band.1 = (f32[512,128]{1,0:T(8,128)S(1)}, f32[512,128]{1,0:T(8,128)S(1)}) custom-call(f32[4,128,512]{2,1,0:T(8,128)S(1)} %near.2.partial, f32[992,128]{1,0:T(8,128)S(1)} %get-tuple-element.43.keep, f32[992,128]{1,0:T(8,128)S(1)} %collective-permute-done.9.got, f32[15,2,64,128]{3,2,1,0:T(8,128)S(1)} %get-tuple-element.45.phase, ...), custom_call_target="tpu_custom_call" | custom-call | bytes 1000000 | tf_op jit(solution)/shard_map/band/pallas_call | solution.py:511
  33.6 0.4 collective-permute-start.10
  34.0 1.2 %collective-permute-done.10.got = f32[512,128]{1,0:T(8,128)S(1)} collective-permute-done((f32[512,128]{1,0:T(8,128)S(1)}, f32[512,128]{1,0:T(8,128)S(1)}, u32[]{:S(2)}, u32[]{:S(2)}) %collective-permute-start.10) | collective-permute-done | bytes 262176 | tf_op jit(solution)/shard_map/ppermute | solution.py:597
  35.3 3.2 %collective-permute-start.11 = (f32[256,128]{1,0:T(8,128)S(1)}, f32[256,128]{1,0:T(8,128)S(1)}, u32[]{:S(2)}, u32[]{:S(2)}) collective-permute-start(f32[256,128]{1,0:T(8,128)S(1)} %get-tuple-element.50), channel_id=1, source_target_pairs={{0,0},{1,2},{2,8},{3,10},{4,4},{5,6},{6,12},{7,14},{8,1},{9,3},{10... | collective-permute-start | bytes 393224 | tf_op jit(solution)/shard_map/ppermute | solution.py:598
  38.5 3.5 %collective-permute-start.12 = (f32[256,128]{1,0:T(8,128)S(1)}, f32[256,128]{1,0:T(8,128)S(1)}, u32[]{:S(2)}, u32[]{:S(2)}) collective-permute-start(f32[256,128]{1,0:T(8,128)S(1)} %get-tuple-element.53), channel_id=1, source_target_pairs={{0,4},{1,6},{2,12},{3,14},{4,0},{5,2},{6,8},{7,10},{8,5},{9,7},{10... | collective-permute-start | bytes 393224 | tf_op jit(solution)/shard_map/ppermute | solution.py:598
  42.1 0.1 collective-permute-start.14
  42.2 1.6 %collective-permute-done.11.message = f32[256,128]{1,0:T(8,128)S(1)} collective-permute-done((f32[256,128]{1,0:T(8,128)S(1)}, f32[256,128]{1,0:T(8,128)S(1)}, u32[]{:S(2)}, u32[]{:S(2)}) %collective-permute-start.11) | collective-permute-done | bytes 131104 | tf_op jit(solution)/shard_map/ppermute | solution.py:598
  43.8 0.1 tile.4
  43.8 7.7 %collective-permute-done.12.message = f32[256,128]{1,0:T(8,128)S(1)} collective-permute-done((f32[256,128]{1,0:T(8,128)S(1)}, f32[256,128]{1,0:T(8,128)S(1)}, u32[]{:S(2)}, u32[]{:S(2)}) %collective-permute-start.12) | collective-permute-done | bytes 131104 | tf_op jit(solution)/shard_map/ppermute | solution.py:598
  51.6 0.1 tile.5
  51.7 0.1 tile.6
  51.8 2.3 %collective-permute-done.14.message = f32[256,128]{1,0:T(8,128)S(1)} collective-permute-done((f32[256,128]{1,0:T(8,128)S(1)}, f32[256,128]{1,0:T(8,128)S(1)}, u32[]{:S(2)}, u32[]{:S(2)}) %collective-permute-start.14) | collective-permute-done | bytes 131104 | tf_op jit(solution)/shard_map/ppermute | solution.py:598
  54.1 0.1 tile.7
  54.2 0.9 %place.1 = (f32[32,2048]{1,0:T(8,128)}, f32[32,2048]{1,0:T(8,128)}) custom-call(f32[8,2048]{1,0:T(8,128)S(1)} %get-tuple-element.51.refs_0_, f32[8,2048]{1,0:T(8,128)S(1)} %get-tuple-element.52.refs_1_, f32[8,2048]{1,0:T(8,128)S(1)} %get-tuple-element.54.refs_2_, f32[8,2048]{1,0:T(8,128)S(1)} %get-tuple-element.55.refs_3_, ...), custom_call_target="tpu_custom_call" | custom-call | flops 1 | bytes 1 | tf_op jit(solution)/shard_map/place/pallas_call | solution.py:602
  (34 shorter events, 0.4 us)
Async XLA Ops:
  0.6 1.3 %copy-start.7 = (s32[2]{0:T(128)S(1)}, s32[2]{0:T(128)}, u32[]{:S(2)}) copy-start(s32[2]{0:T(128)} %off_own.1) | copy-start | bytes 28
  0.6 2.5 %collective-permute-start = (f32[32,2048]{1,0:T(8,128)}, f32[32,2048]{1,0:T(8,128)S(1)}, u32[]{:S(2)}, u32[]{:S(2)}) collective-permute-start(f32[32,2048]{1,0:T(8,128)} %param.12), channel_id=1, source_target_pairs={{0,1},{1,0},{2,3},{3,2},{4,5},{5,4},{6,7},{7,6},{8,9},{9,8},{10,11... | collective-permute-start | bytes 786440 | tf_op jit(solution)/shard_map/ppermute | solution.py:535
  1.4 1.8 %collective-permute-start.1 = (f32[32,2048]{1,0:T(8,128)}, f32[32,2048]{1,0:T(8,128)S(1)}, u32[]{:S(2)}, u32[]{:S(2)}) collective-permute-start(f32[32,2048]{1,0:T(8,128)} %param.13), channel_id=1, source_target_pairs={{0,1},{1,0},{2,3},{3,2},{4,5},{5,4},{6,7},{7,6},{8,9},{9,8},{10,11... | collective-permute-start | bytes 786440 | tf_op jit(solution)/shard_map/ppermute | solution.py:535
  1.5 1.5 %copy-start.9 = (f32[32,2048]{1,0:T(8,128)S(1)}, f32[32,2048]{1,0:T(8,128)}, u32[]{:S(2)}) copy-start(f32[32,2048]{1,0:T(8,128)} %param.13) | copy-start | bytes 786436
  1.5 1.7 %collective-permute-start.2 = (f32[32,64]{1,0:T(8,128)}, f32[32,64]{1,0:T(8,128)S(1)}, u32[]{:S(2)}, u32[]{:S(2)}) collective-permute-start(f32[32,64]{1,0:T(8,128)} %bitcast.3), channel_id=1, source_target_pairs={{0,1},{1,0},{2,3},{3,2},{4,5},{5,4},{6,7},{7,6},{8,9},{9,8},{10,11... | collective-permute-start | bytes 24584 | tf_op jit(solution)/shard_map/ppermute | solution.py:535
  1.9 1.2 %collective-permute-start.3 = (s32[2]{0:T(128)S(1)}, s32[2]{0:T(128)S(1)}, u32[]{:S(2)}, u32[]{:S(2)}) collective-permute-start(s32[2]{0:T(128)S(1)} %copy-done.7), channel_id=1, source_target_pairs={{0,1},{1,0},{2,3},{3,2},{4,5},{5,4},{6,7},{7,6},{8,9},{9,8},{10,11... | collective-permute-start | bytes 32 | tf_op jit(solution)/shard_map/ppermute | solution.py:534
  3.0 0.7 %copy-start.6 = (f32[1,64,32]{1,2,0:T(8,128)S(1)}, f32[1,64,32]{1,2,0:T(8,128)}, u32[]{:S(2)}) copy-start(f32[1,64,32]{1,2,0:T(8,128)} %param.14) | copy-start | bytes 24580
  4.4 8.4 %copy-start.10 = (f32[32,8]{0,1:T(8,128)S(1)}, f32[32,8]{0,1:T(8,128)}, u32[]{:S(2)}) copy-start(f32[32,8]{0,1:T(8,128)} %param.17) | copy-start | bytes 3076
  4.4 19.8 %collective-permute-start.4 = (f32[488,128]{1,0:T(8,128)S(1)}, f32[488,128]{1,0:T(8,128)S(1)}, u32[]{:S(2)}, u32[]{:S(2)}) collective-permute-start(f32[488,128]{1,0:T(8,128)S(1)} %get-tuple-element.32), channel_id=1, source_target_pairs={{0,8},{1,10},{2,9},{3,11},{4,12},{5,14},{6,13},{7,15},{8,0},{9,2},... | collective-permute-start | bytes 749576 | tf_op jit(solution)/shard_map/ppermute | solution.py:580
  8.0 21.5 %collective-permute-start.5 = (f32[488,128]{1,0:T(8,128)S(1)}, f32[488,128]{1,0:T(8,128)S(1)}, u32[]{:S(2)}, u32[]{:S(2)}) collective-permute-start(f32[488,128]{1,0:T(8,128)S(1)} %get-tuple-element.33), channel_id=1, source_target_pairs={{0,12},{1,14},{2,13},{3,15},{4,8},{5,10},{6,9},{7,11},{8,4},{9,6},... | collective-permute-start | bytes 749576 | tf_op jit(solution)/shard_map/ppermute | solution.py:580
  8.0 21.5 %collective-permute-start.6 = (f32[488,128]{1,0:T(8,128)S(1)}, f32[488,128]{1,0:T(8,128)S(1)}, u32[]{:S(2)}, u32[]{:S(2)}) collective-permute-start(f32[488,128]{1,0:T(8,128)S(1)} %get-tuple-element.34), channel_id=1, source_target_pairs={{0,4},{1,6},{2,5},{3,7},{4,0},{5,2},{6,1},{7,3},{8,12},{9,14},{10,... | collective-permute-start | bytes 749576 | tf_op jit(solution)/shard_map/ppermute | solution.py:580
  10.4 3.6 %copy-start.8 = (s32[2]{0:T(128)S(1)}, s32[2]{0:T(128)}, u32[]{:S(2)}) copy-start(s32[2]{0:T(128)} %owners.1) | copy-start | bytes 28
  10.4 19.1 %collective-permute-start.7 = (f32[488,128]{1,0:T(8,128)S(1)}, f32[488,128]{1,0:T(8,128)S(1)}, u32[]{:S(2)}, u32[]{:S(2)}) collective-permute-start(f32[488,128]{1,0:T(8,128)S(1)} %get-tuple-element.35), channel_id=1, source_target_pairs={{0,0},{1,2},{2,1},{3,3},{4,4},{5,6},{6,5},{7,7},{8,8},{9,10},{10,9... | collective-permute-start | bytes 749576 | tf_op jit(solution)/shard_map/ppermute | solution.py:580
  12.9 1.2 %collective-permute-start.8 = (f32[32,8]{1,0:T(8,128)S(1)}, f32[32,8]{1,0:T(8,128)S(1)}, u32[]{:S(2)}, u32[]{:S(2)}) collective-permute-start(f32[32,8]{1,0:T(8,128)S(1)} %copy.15.taps_own), channel_id=1, source_target_pairs={{0,1},{1,0},{2,3},{3,2},{4,5},{5,4},{6,7},{7,6},{8,9},{9,8},{10,11... | collective-permute-start | bytes 3080 | tf_op jit(solution)/shard_map/ppermute | solution.py:535
  29.6 0.9 %copy-start.5 = (bf16[2,128,192]{2,1,0:T(8,128)(2,1)S(1)}, bf16[2,128,192]{2,1,0:T(8,128)(2,1)}, u32[]{:S(2)}) copy-start(bf16[2,128,192]{2,1,0:T(8,128)(2,1)} %constant.12.clone.near) | copy-start | bytes 294916
  29.7 2.0 %collective-permute-start.9 = (f32[992,128]{1,0:T(8,128)S(1)}, f32[992,128]{1,0:T(8,128)S(1)}, u32[]{:S(2)}, u32[]{:S(2)}) collective-permute-start(f32[992,128]{1,0:T(8,128)S(1)} %get-tuple-element.44), channel_id=1, source_target_pairs={{0,1},{1,0},{2,3},{3,2},{4,5},{5,4},{6,7},{7,6},{8,9},{9,8},{10,11... | collective-permute-start | bytes 1523720 | tf_op jit(solution)/shard_map/ppermute | solution.py:585
  30.5 1.2 %copy-start = (bf16[2,256,256]{2,1,0:T(8,128)(2,1)S(1)}, bf16[2,256,256]{2,1,0:T(8,128)(2,1)}, u32[]{:S(2)}) copy-start(bf16[2,256,256]{2,1,0:T(8,128)(2,1)} %constant.15.clone.back) | copy-start | bytes 786436
  30.5 1.2 %copy-start.1 = (bf16[2,256,256]{2,1,0:T(8,128)(2,1)S(1)}, bf16[2,256,256]{2,1,0:T(8,128)(2,1)}, u32[]{:S(2)}) copy-start(bf16[2,256,256]{2,1,0:T(8,128)(2,1)} %constant.14.clone.there) | copy-start | bytes 786436
  30.5 1.2 %copy-start.2 = (f32[2,2,64,128]{3,2,1,0:T(8,128)S(1)}, f32[2,2,64,128]{3,2,1,0:T(8,128)}, u32[]{:S(2)}) copy-start(f32[2,2,64,128]{3,2,1,0:T(8,128)} %constant.17.clone.twists) | copy-start | bytes 393220
  30.5 1.2 %copy-start.3 = (bf16[2,2,128,128]{3,2,1,0:T(8,128)(2,1)S(1)}, bf16[2,2,128,128]{3,2,1,0:T(8,128)(2,1)}, u32[]{:S(2)}) copy-start(bf16[2,2,128,128]{3,2,1,0:T(8,128)(2,1)} %constant.16.clone.last) | copy-start | bytes 393220
  30.5 1.2 %copy-start.4 = (bf16[2,128,192]{2,1,0:T(8,128)(2,1)S(1)}, bf16[2,128,192]{2,1,0:T(8,128)(2,1)}, u32[]{:S(2)}) copy-start(bf16[2,128,192]{2,1,0:T(8,128)(2,1)} %constant.13.clone.far) | copy-start | bytes 294916
  33.6 1.6 %collective-permute-start.10 = (f32[512,128]{1,0:T(8,128)S(1)}, f32[512,128]{1,0:T(8,128)S(1)}, u32[]{:S(2)}, u32[]{:S(2)}) collective-permute-start(f32[512,128]{1,0:T(8,128)S(1)} %get-tuple-element.49), channel_id=1, source_target_pairs={{0,1},{1,0},{2,3},{3,2},{4,5},{5,4},{6,7},{7,6},{8,9},{9,8},{10,11... | collective-permute-start | bytes 786440 | tf_op jit(solution)/shard_map/ppermute | solution.py:597
  35.3 8.5 %collective-permute-start.11 = (f32[256,128]{1,0:T(8,128)S(1)}, f32[256,128]{1,0:T(8,128)S(1)}, u32[]{:S(2)}, u32[]{:S(2)}) collective-permute-start(f32[256,128]{1,0:T(8,128)S(1)} %get-tuple-element.50), channel_id=1, source_target_pairs={{0,0},{1,2},{2,8},{3,10},{4,4},{5,6},{6,12},{7,14},{8,1},{9,3},{10... | collective-permute-start | bytes 393224 | tf_op jit(solution)/shard_map/ppermute | solution.py:598
  38.5 13.1 %collective-permute-start.12 = (f32[256,128]{1,0:T(8,128)S(1)}, f32[256,128]{1,0:T(8,128)S(1)}, u32[]{:S(2)}, u32[]{:S(2)}) collective-permute-start(f32[256,128]{1,0:T(8,128)S(1)} %get-tuple-element.53), channel_id=1, source_target_pairs={{0,4},{1,6},{2,12},{3,14},{4,0},{5,2},{6,8},{7,10},{8,5},{9,7},{10... | collective-permute-start | bytes 393224 | tf_op jit(solution)/shard_map/ppermute | solution.py:598
  42.1 9.6 %collective-permute-start.13 = (f32[256,128]{1,0:T(8,128)S(1)}, f32[256,128]{1,0:T(8,128)S(1)}, u32[]{:S(2)}, u32[]{:S(2)}) collective-permute-start(f32[256,128]{1,0:T(8,128)S(1)} %get-tuple-element.56), channel_id=1, source_target_pairs={{0,8},{1,10},{2,0},{3,2},{4,12},{5,14},{6,4},{7,6},{8,9},{9,11},{1... | collective-permute-start | bytes 393224 | tf_op jit(solution)/shard_map/ppermute | solution.py:598
  42.1 12.0 %collective-permute-start.14 = (f32[256,128]{1,0:T(8,128)S(1)}, f32[256,128]{1,0:T(8,128)S(1)}, u32[]{:S(2)}, u32[]{:S(2)}) collective-permute-start(f32[256,128]{1,0:T(8,128)S(1)} %get-tuple-element.59), channel_id=1, source_target_pairs={{0,12},{1,14},{2,4},{3,6},{4,8},{5,10},{6,0},{7,2},{8,13},{9,15},{... | collective-permute-start | bytes 393224 | tf_op jit(solution)/shard_map/ppermute | solution.py:598

commit v9 on v8

--- a/solution.py
+++ b/solution.py
@@ -483,20 +483,17 @@
             message[line * PART : (line + 1) * PART, :] = keep[read, :] * keep_factor + got[read, :] * got_factor
 
 
-def tile_kernel(message, re_tile, im_tile):
-    for part, tile in enumerate((re_tile, im_tile)):
+def place_kernel(step, message, *refs):
+    outs, (tiles, sems) = refs[-4:-2], refs[-2:]
+    sender = crossed((lax.axis_index("az") >> 1) ^ step)
+    rows = pl.ds(pl.multiple_of(sender * OUT_BINS, 8), OUT_BINS)
+    copies = []
+    for part, out in enumerate(outs):
         for row in range(PART):
-            tile[:, row * FACTOR : (row + 1) * FACTOR] = message[pl.ds(part * PART + row, OUT_BINS, stride=2 * PART), :]
-
-
-def place_kernel(*refs):
-    tiles, (out_re, out_im, sems) = refs[:-3], refs[-3:]
-    place = lax.axis_index("az")
-    copies = []
-    for at, tile in enumerate(tiles):
-        sender = crossed((place >> 1) ^ (at // 2))
-        rows = pl.ds(pl.multiple_of(sender * OUT_BINS, 8), OUT_BINS)
-        copies.append(pltpu.make_async_copy(tile, (out_re, out_im)[at % 2].at[rows], sems.at[at]))
+            tiles[part, :, row * FACTOR : (row + 1) * FACTOR] = message[
+                pl.ds(part * PART + row, OUT_BINS, stride=2 * PART), :
+            ]
+        copies.append(pltpu.make_async_copy(tiles.at[part], out.at[rows], sems.at[part]))
         copies[-1].start()
     for copy in copies:
         copy.wait()
@@ -596,19 +593,20 @@
     )
     sent = kernel_call(join_kernel, "join", [array(2 * OUT_BINS * PART, FACTOR)] * half, [keep, swap(give)])
     results = [lax.ppermute(message, ("az", "rg"), route) for message, route in zip(sent, routes_back)]
-    tiles = []
-    for message in results:
-        tiles += kernel_call(tile_kernel, "tile", [array(OUT_BINS, samples)] * 2, [message])
-    return pl.pallas_call(
-        place_kernel,
-        out_shape=[array(bins, samples)] * 2,
-        in_specs=[VMEM] * len(tiles),
-        out_specs=[anywhere] * 2,
-        scratch_shapes=[pltpu.SemaphoreType.DMA((len(tiles),))],
-        compiler_params=pltpu.CompilerParams(vmem_limit_bytes=8 * 1024 * 1024),
-        cost_estimate=pl.CostEstimate(flops=1, bytes_accessed=1, transcendentals=0),
-        name="place",
-    )(*tiles)
+    images = []
+    for step, message in enumerate(results):
+        images = pl.pallas_call(
+            functools.partial(place_kernel, step),
+            out_shape=[array(bins, samples)] * 2,
+            in_specs=[VMEM] + [anywhere] * len(images),
+            out_specs=[anywhere] * 2,
+            scratch_shapes=[pltpu.VMEM((2, OUT_BINS, samples), jnp.float32), pltpu.SemaphoreType.DMA((2,))],
+            input_output_aliases={1: 0, 2: 1} if images else {},
+            compiler_params=pltpu.CompilerParams(vmem_limit_bytes=8 * 1024 * 1024),
+            cost_estimate=pl.CostEstimate(flops=1, bytes_accessed=1, transcendentals=0),
+            name="place",
+        )(message, *images)
+    return images
 
 
 def solution(mesh):

time: 55.3 us -> 55.1 us (level)
  waiting for transfers between devices: 28.6 us -> 26.7 us
  Pallas kernels: 6.21 us -> 7.93 us
    pallas_call x1 -> x4, Pallas kernels: 0.86 us -> 2.91 us  [transposed_shards(): pl.pallas_call(functools.partial(place_kernel, step), out_shape=[array(bi...]
    ppermute x4, waiting for transfers between devices: 11.7 us -> 9.73 us  [transposed_shards(): lax.ppermute(message, ('az', 'rg'), route)]
    pallas_call x9 -> x5, Pallas kernels: 4.67 us -> 4.35 us  [kernel_call(): pl.pallas_call(body, out_shape=out_shape, in_specs=specs, out_specs=jax.t...]
  transfers between devices with their start and end apart: 15 -> 15, of which waited for: 9 -> 9; matrix products, arithmetic and copies ran while one was open for 2% -> 2% of each run, Pallas kernels for 4% -> 8%
where the time goes in v9:
time: 55.1 us; the launch traced here: 54.8 us
  waiting for transfers between devices  26.7 us (48%)
  starting transfers between devices  17.4 us (32%)
  Pallas kernels  7.93 us (14%)
  local copies, waits for them, and re-layouts  2.05 us (4%)
  between operations  0.82 us (1%)
    ppermute x4, waiting for transfers between devices, transposed_shards(): lax.ppermute(messages[step], ('az', 'rg'), routes[step])  13.6 us
    ppermute x4, waiting for transfers between devices, transposed_shards(): lax.ppermute(message, ('az', 'rg'), route)  9.73 us
    ppermute x4, starting transfers between devices, transposed_shards(): lax.ppermute(messages[step], ('az', 'rg'), routes[step])  8.37 us
    ppermute x4, starting transfers between devices, transposed_shards(): lax.ppermute(message, ('az', 'rg'), route)  6.86 us
    pallas_call x5, Pallas kernels, kernel_call(): pl.pallas_call(body, out_shape=out_shape, in_specs=specs, out_specs=jax.t...  4.35 us
    pallas_call x4, Pallas kernels, transposed_shards(): pl.pallas_call(functools.partial(place_kernel, step), out_shape=[array(bi...  2.91 us
    ppermute x1, waiting for transfers between devices, transposed_shards(): swap(give)  1.2 us
    ppermute x1, waiting for transfers between devices, transposed_shards(): swap(taps)  1.17 us
  transfers between devices with their start and end apart: 15, of which 9 were waited for; matrix products, arithmetic and copies ran while one was open for 2% of the time, Pallas kernels for 8%

profile of v9, /device:TPU:13, one launch (start us, length us, event | category | flops | bytes accessed | tf_op | source)
XLA Modules:
  0.0 54.8 jit_solution(281249272400297666)
XLA Ops:
  0.6 0.7 %collective-permute-start = (f32[32,2048]{1,0:T(8,128)}, f32[32,2048]{1,0:T(8,128)S(1)}, u32[]{:S(2)}, u32[]{:S(2)}) collective-permute-start(f32[32,2048]{1,0:T(8,128)} %param.12), channel_id=1, source_target_pairs={{0,1},{1,0},{2,3},{3,2},{4,5},{5,4},{6,7},{7,6},{8,9},{9,8},{10,11... | collective-permute-start | bytes 786440 | tf_op jit(solution)/shard_map/ppermute | solution.py:532
  1.4 0.1 collective-permute-start.1
  1.5 0.4 collective-permute-start.2
  2.0 1.0 %reshape.10.re_lines = f32[512,128]{1,0:T(8,128)S(1)} reshape(f32[32,2048]{1,0:T(8,128)} %param.12) | data formatting | bytes 524288 | tf_op jit(solution)/shard_map/reshape | solution.py:534
  3.1 0.1 collective-permute-done.2.ref_other
  3.2 0.5 copy-done.6
  3.7 0.7 %pack.1 = (f32[488,128]{1,0:T(8,128)S(1)}, f32[488,128]{1,0:T(8,128)S(1)}, f32[488,128]{1,0:T(8,128)S(1)}, f32[488,128]{1,0:T(8,128)S(1)}) custom-call(f32[512,128]{1,0:T(8,128)S(1)} %reshape.10.re_lines, f32[512,128]{1,0:T(8,128)S(1)} %reshape.11.im_lines, f32[32,2048]{1,0:T(8,128)S(1)} %collective-permute-done.re_other, ...), custom_call_target="tpu_custom_call" | custom-call | flops 1 | bytes 1 | tf_op jit(solution)/shard_map/pack/pallas_call | solution.py:537
  4.4 3.6 %collective-permute-start.4 = (f32[488,128]{1,0:T(8,128)S(1)}, f32[488,128]{1,0:T(8,128)S(1)}, u32[]{:S(2)}, u32[]{:S(2)}) collective-permute-start(f32[488,128]{1,0:T(8,128)S(1)} %get-tuple-element.30), channel_id=1, source_target_pairs={{0,8},{1,10},{2,9},{3,11},{4,12},{5,14},{6,13},{7,15},{8,0},{9,2},... | collective-permute-start | bytes 749576 | tf_op jit(solution)/shard_map/ppermute | solution.py:577
  8.0 2.4 %collective-permute-start.6 = (f32[488,128]{1,0:T(8,128)S(1)}, f32[488,128]{1,0:T(8,128)S(1)}, u32[]{:S(2)}, u32[]{:S(2)}) collective-permute-start(f32[488,128]{1,0:T(8,128)S(1)} %get-tuple-element.32), channel_id=1, source_target_pairs={{0,4},{1,6},{2,5},{3,7},{4,0},{5,2},{6,1},{7,3},{8,12},{9,14},{10,... | collective-permute-start | bytes 749576 | tf_op jit(solution)/shard_map/ppermute | solution.py:577
  10.4 2.3 %collective-permute-start.7 = (f32[488,128]{1,0:T(8,128)S(1)}, f32[488,128]{1,0:T(8,128)S(1)}, u32[]{:S(2)}, u32[]{:S(2)}) collective-permute-start(f32[488,128]{1,0:T(8,128)S(1)} %get-tuple-element.33), channel_id=1, source_target_pairs={{0,0},{1,2},{2,1},{3,3},{4,4},{5,6},{6,5},{7,7},{8,8},{9,10},{10,9... | collective-permute-start | bytes 749576 | tf_op jit(solution)/shard_map/ppermute | solution.py:577
  12.9 1.2 %collective-permute-done.8.taps_other = f32[32,8]{1,0:T(8,128)S(1)} collective-permute-done((f32[32,8]{1,0:T(8,128)S(1)}, f32[32,8]{1,0:T(8,128)S(1)}, u32[]{:S(2)}, u32[]{:S(2)}) %collective-permute-start.8) | collective-permute-done | bytes 1056 | tf_op jit(solution)/shard_map/ppermute | solution.py:532
  14.1 1.9 %phase.1 = (f32[15,2,64,128]{3,2,1,0:T(8,128)S(1)}, f32[64,128]{1,0:T(8,128)S(1)}, f32[2,8,128]{2,1,0:T(8,128)S(1)}) custom-call(s32[2]{0:T(128)S(1)} %copy-done.7, s32[2]{0:T(128)S(1)} %collective-permute-done.3.other_offsets.off_other, s32[2]{0:T(128)S(1)} %copy-done.8, f32[32,8]{1,0:T(8,128)S(1)} %copy.21.taps_own, ...), custom_call_target="tpu_custom_call" | custom-call | bytes 1000000 | tf_op jit(solution)/shard_map/phase/pallas_call | solution.py:508
  16.0 8.2 %collective-permute-done.4.refs_0_ = f32[488,128]{1,0:T(8,128)S(1)} collective-permute-done((f32[488,128]{1,0:T(8,128)S(1)}, f32[488,128]{1,0:T(8,128)S(1)}, u32[]{:S(2)}, u32[]{:S(2)}) %collective-permute-start.4) | collective-permute-done | bytes 249888 | tf_op jit(solution)/shard_map/ppermute | solution.py:577
  24.2 5.4 %collective-permute-done.5.refs_1_ = f32[488,128]{1,0:T(8,128)S(1)} collective-permute-done((f32[488,128]{1,0:T(8,128)S(1)}, f32[488,128]{1,0:T(8,128)S(1)}, u32[]{:S(2)}, u32[]{:S(2)}) %collective-permute-start.5) | collective-permute-done | bytes 249888 | tf_op jit(solution)/shard_map/ppermute | solution.py:577
  29.6 0.2 parity.1
  29.7 0.4 collective-permute-start.9
  30.1 0.3 copy-done.5
  30.5 0.3 near.2.partial
  30.8 0.9 %collective-permute-done.9.got = f32[992,128]{1,0:T(8,128)S(1)} collective-permute-done((f32[992,128]{1,0:T(8,128)S(1)}, f32[992,128]{1,0:T(8,128)S(1)}, u32[]{:S(2)}, u32[]{:S(2)}) %collective-permute-start.9) | collective-permute-done | bytes 507936 | tf_op jit(solution)/shard_map/ppermute | solution.py:582
  31.7 1.9 %band.1 = (f32[512,128]{1,0:T(8,128)S(1)}, f32[512,128]{1,0:T(8,128)S(1)}) custom-call(f32[4,128,512]{2,1,0:T(8,128)S(1)} %near.2.partial, f32[992,128]{1,0:T(8,128)S(1)} %get-tuple-element.41.keep, f32[992,128]{1,0:T(8,128)S(1)} %collective-permute-done.9.got, f32[15,2,64,128]{3,2,1,0:T(8,128)S(1)} %get-tuple-element.43.phase, ...), custom_call_target="tpu_custom_call" | custom-call | bytes 1000000 | tf_op jit(solution)/shard_map/band/pallas_call | solution.py:508
  33.6 0.4 collective-permute-start.10
  34.0 1.2 %collective-permute-done.10.got = f32[512,128]{1,0:T(8,128)S(1)} collective-permute-done((f32[512,128]{1,0:T(8,128)S(1)}, f32[512,128]{1,0:T(8,128)S(1)}, u32[]{:S(2)}, u32[]{:S(2)}) %collective-permute-start.10) | collective-permute-done | bytes 262176 | tf_op jit(solution)/shard_map/ppermute | solution.py:594
  35.3 3.2 %collective-permute-start.14 = (f32[256,128]{1,0:T(8,128)S(1)}, f32[256,128]{1,0:T(8,128)S(1)}, u32[]{:S(2)}, u32[]{:S(2)}) collective-permute-start(f32[256,128]{1,0:T(8,128)S(1)} %get-tuple-element.51), channel_id=1, source_target_pairs={{0,0},{1,2},{2,8},{3,10},{4,4},{5,6},{6,12},{7,14},{8,1},{9,3},{10... | collective-permute-start | bytes 393224 | tf_op jit(solution)/shard_map/ppermute | solution.py:595
  38.5 3.5 %collective-permute-start.13 = (f32[256,128]{1,0:T(8,128)S(1)}, f32[256,128]{1,0:T(8,128)S(1)}, u32[]{:S(2)}, u32[]{:S(2)}) collective-permute-start(f32[256,128]{1,0:T(8,128)S(1)} %get-tuple-element.50), channel_id=1, source_target_pairs={{0,4},{1,6},{2,12},{3,14},{4,0},{5,2},{6,8},{7,10},{8,5},{9,7},{10... | collective-permute-start | bytes 393224 | tf_op jit(solution)/shard_map/ppermute | solution.py:595
  42.1 0.1 collective-permute-start.11
  42.2 1.6 %collective-permute-done.14.message = f32[256,128]{1,0:T(8,128)S(1)} collective-permute-done((f32[256,128]{1,0:T(8,128)S(1)}, f32[256,128]{1,0:T(8,128)S(1)}, u32[]{:S(2)}, u32[]{:S(2)}) %collective-permute-start.14) | collective-permute-done | bytes 131104 | tf_op jit(solution)/shard_map/ppermute | solution.py:595
  43.8 0.7 %place.4 = (f32[32,2048]{1,0:T(8,128)}, f32[32,2048]{1,0:T(8,128)}) custom-call(f32[256,128]{1,0:T(8,128)S(1)} %collective-permute-done.14.message), custom_call_target="tpu_custom_call" | custom-call | flops 1 | bytes 1 | tf_op jit(solution)/shard_map/place/pallas_call | solution.py:598
  44.5 7.1 %collective-permute-done.13.message = f32[256,128]{1,0:T(8,128)S(1)} collective-permute-done((f32[256,128]{1,0:T(8,128)S(1)}, f32[256,128]{1,0:T(8,128)S(1)}, u32[]{:S(2)}, u32[]{:S(2)}) %collective-permute-start.13) | collective-permute-done | bytes 131104 | tf_op jit(solution)/shard_map/ppermute | solution.py:595
  51.6 0.7 %place.5 = (f32[32,2048]{1,0:T(8,128)}, f32[32,2048]{1,0:T(8,128)}) custom-call(f32[256,128]{1,0:T(8,128)S(1)} %collective-permute-done.13.message, f32[32,2048]{1,0:T(8,128)} %get-tuple-element.52.refs_0_, f32[32,2048]{1,0:T(8,128)} %get-tuple-element.53.refs_1_), custom_call_target="tpu_custom_call", output_to_operand_aliasing={{0}: (1, {}), {1}: (2, {})} | custom-call | flops 1 | bytes 1 | tf_op jit(solution)/shard_map/place/pallas_call | solution.py:598
  52.3 0.7 %place.6 = (f32[32,2048]{1,0:T(8,128)}, f32[32,2048]{1,0:T(8,128)}) custom-call(f32[256,128]{1,0:T(8,128)S(1)} %collective-permute-done.12.message, f32[32,2048]{1,0:T(8,128)} %get-tuple-element.54.refs_0_, f32[32,2048]{1,0:T(8,128)} %get-tuple-element.55.refs_1_), custom_call_target="tpu_custom_call", output_to_operand_aliasing={{0}: (1, {}), {1}: (2, {})} | custom-call | flops 1 | bytes 1 | tf_op jit(solution)/shard_map/place/pallas_call | solution.py:598
  53.1 1.0 %collective-permute-done.11.message = f32[256,128]{1,0:T(8,128)S(1)} collective-permute-done((f32[256,128]{1,0:T(8,128)S(1)}, f32[256,128]{1,0:T(8,128)S(1)}, u32[]{:S(2)}, u32[]{:S(2)}) %collective-permute-start.11) | collective-permute-done | bytes 131104 | tf_op jit(solution)/shard_map/ppermute | solution.py:595
  54.1 0.7 %place.7 = (f32[32,2048]{1,0:T(8,128)}, f32[32,2048]{1,0:T(8,128)}) custom-call(f32[256,128]{1,0:T(8,128)S(1)} %collective-permute-done.11.message, f32[32,2048]{1,0:T(8,128)} %get-tuple-element.56.refs_0_, f32[32,2048]{1,0:T(8,128)} %get-tuple-element.57.refs_1_), custom_call_target="tpu_custom_call", output_to_operand_aliasing={{0}: (1, {}), {1}: (2, {})} | custom-call | flops 1 | bytes 1 | tf_op jit(solution)/shard_map/place/pallas_call | solution.py:598
  (33 shorter events, 0.3 us)
Async XLA Ops:
  0.6 1.3 %copy-start.7 = (s32[2]{0:T(128)S(1)}, s32[2]{0:T(128)}, u32[]{:S(2)}) copy-start(s32[2]{0:T(128)} %off_own.1) | copy-start | bytes 28
  0.6 2.5 %collective-permute-start = (f32[32,2048]{1,0:T(8,128)}, f32[32,2048]{1,0:T(8,128)S(1)}, u32[]{:S(2)}, u32[]{:S(2)}) collective-permute-start(f32[32,2048]{1,0:T(8,128)} %param.12), channel_id=1, source_target_pairs={{0,1},{1,0},{2,3},{3,2},{4,5},{5,4},{6,7},{7,6},{8,9},{9,8},{10,11... | collective-permute-start | bytes 786440 | tf_op jit(solution)/shard_map/ppermute | solution.py:532
  1.4 1.8 %collective-permute-start.1 = (f32[32,2048]{1,0:T(8,128)}, f32[32,2048]{1,0:T(8,128)S(1)}, u32[]{:S(2)}, u32[]{:S(2)}) collective-permute-start(f32[32,2048]{1,0:T(8,128)} %param.13), channel_id=1, source_target_pairs={{0,1},{1,0},{2,3},{3,2},{4,5},{5,4},{6,7},{7,6},{8,9},{9,8},{10,11... | collective-permute-start | bytes 786440 | tf_op jit(solution)/shard_map/ppermute | solution.py:532
  1.5 1.5 %copy-start.9 = (f32[32,2048]{1,0:T(8,128)S(1)}, f32[32,2048]{1,0:T(8,128)}, u32[]{:S(2)}) copy-start(f32[32,2048]{1,0:T(8,128)} %param.13) | copy-start | bytes 786436
  1.5 1.7 %collective-permute-start.2 = (f32[32,64]{1,0:T(8,128)}, f32[32,64]{1,0:T(8,128)S(1)}, u32[]{:S(2)}, u32[]{:S(2)}) collective-permute-start(f32[32,64]{1,0:T(8,128)} %bitcast.3), channel_id=1, source_target_pairs={{0,1},{1,0},{2,3},{3,2},{4,5},{5,4},{6,7},{7,6},{8,9},{9,8},{10,11... | collective-permute-start | bytes 24584 | tf_op jit(solution)/shard_map/ppermute | solution.py:532
  1.9 1.2 %collective-permute-start.3 = (s32[2]{0:T(128)S(1)}, s32[2]{0:T(128)S(1)}, u32[]{:S(2)}, u32[]{:S(2)}) collective-permute-start(s32[2]{0:T(128)S(1)} %copy-done.7), channel_id=1, source_target_pairs={{0,1},{1,0},{2,3},{3,2},{4,5},{5,4},{6,7},{7,6},{8,9},{9,8},{10,11... | collective-permute-start | bytes 32 | tf_op jit(solution)/shard_map/ppermute | solution.py:531
  3.0 0.7 %copy-start.6 = (f32[1,64,32]{1,2,0:T(8,128)S(1)}, f32[1,64,32]{1,2,0:T(8,128)}, u32[]{:S(2)}) copy-start(f32[1,64,32]{1,2,0:T(8,128)} %param.14) | copy-start | bytes 24580
  4.4 8.4 %copy-start.10 = (f32[32,8]{0,1:T(8,128)S(1)}, f32[32,8]{0,1:T(8,128)}, u32[]{:S(2)}) copy-start(f32[32,8]{0,1:T(8,128)} %param.17) | copy-start | bytes 3076
  4.4 19.8 %collective-permute-start.4 = (f32[488,128]{1,0:T(8,128)S(1)}, f32[488,128]{1,0:T(8,128)S(1)}, u32[]{:S(2)}, u32[]{:S(2)}) collective-permute-start(f32[488,128]{1,0:T(8,128)S(1)} %get-tuple-element.30), channel_id=1, source_target_pairs={{0,8},{1,10},{2,9},{3,11},{4,12},{5,14},{6,13},{7,15},{8,0},{9,2},... | collective-permute-start | bytes 749576 | tf_op jit(solution)/shard_map/ppermute | solution.py:577
  8.0 21.5 %collective-permute-start.5 = (f32[488,128]{1,0:T(8,128)S(1)}, f32[488,128]{1,0:T(8,128)S(1)}, u32[]{:S(2)}, u32[]{:S(2)}) collective-permute-start(f32[488,128]{1,0:T(8,128)S(1)} %get-tuple-element.31), channel_id=1, source_target_pairs={{0,12},{1,14},{2,13},{3,15},{4,8},{5,10},{6,9},{7,11},{8,4},{9,6},... | collective-permute-start | bytes 749576 | tf_op jit(solution)/shard_map/ppermute | solution.py:577
  8.0 21.5 %collective-permute-start.6 = (f32[488,128]{1,0:T(8,128)S(1)}, f32[488,128]{1,0:T(8,128)S(1)}, u32[]{:S(2)}, u32[]{:S(2)}) collective-permute-start(f32[488,128]{1,0:T(8,128)S(1)} %get-tuple-element.32), channel_id=1, source_target_pairs={{0,4},{1,6},{2,5},{3,7},{4,0},{5,2},{6,1},{7,3},{8,12},{9,14},{10,... | collective-permute-start | bytes 749576 | tf_op jit(solution)/shard_map/ppermute | solution.py:577
  10.4 3.6 %copy-start.8 = (s32[2]{0:T(128)S(1)}, s32[2]{0:T(128)}, u32[]{:S(2)}) copy-start(s32[2]{0:T(128)} %owners.1) | copy-start | bytes 28
  10.4 19.1 %collective-permute-start.7 = (f32[488,128]{1,0:T(8,128)S(1)}, f32[488,128]{1,0:T(8,128)S(1)}, u32[]{:S(2)}, u32[]{:S(2)}) collective-permute-start(f32[488,128]{1,0:T(8,128)S(1)} %get-tuple-element.33), channel_id=1, source_target_pairs={{0,0},{1,2},{2,1},{3,3},{4,4},{5,6},{6,5},{7,7},{8,8},{9,10},{10,9... | collective-permute-start | bytes 749576 | tf_op jit(solution)/shard_map/ppermute | solution.py:577
  12.9 1.2 %collective-permute-start.8 = (f32[32,8]{1,0:T(8,128)S(1)}, f32[32,8]{1,0:T(8,128)S(1)}, u32[]{:S(2)}, u32[]{:S(2)}) collective-permute-start(f32[32,8]{1,0:T(8,128)S(1)} %copy.21.taps_own), channel_id=1, source_target_pairs={{0,1},{1,0},{2,3},{3,2},{4,5},{5,4},{6,7},{7,6},{8,9},{9,8},{10,11... | collective-permute-start | bytes 3080 | tf_op jit(solution)/shard_map/ppermute | solution.py:532
  29.6 0.9 %copy-start.5 = (bf16[2,128,192]{2,1,0:T(8,128)(2,1)S(1)}, bf16[2,128,192]{2,1,0:T(8,128)(2,1)}, u32[]{:S(2)}) copy-start(bf16[2,128,192]{2,1,0:T(8,128)(2,1)} %constant.12.clone.near) | copy-start | bytes 294916
  29.7 2.0 %collective-permute-start.9 = (f32[992,128]{1,0:T(8,128)S(1)}, f32[992,128]{1,0:T(8,128)S(1)}, u32[]{:S(2)}, u32[]{:S(2)}) collective-permute-start(f32[992,128]{1,0:T(8,128)S(1)} %get-tuple-element.42), channel_id=1, source_target_pairs={{0,1},{1,0},{2,3},{3,2},{4,5},{5,4},{6,7},{7,6},{8,9},{9,8},{10,11... | collective-permute-start | bytes 1523720 | tf_op jit(solution)/shard_map/ppermute | solution.py:582
  30.5 1.2 %copy-start = (bf16[2,256,256]{2,1,0:T(8,128)(2,1)S(1)}, bf16[2,256,256]{2,1,0:T(8,128)(2,1)}, u32[]{:S(2)}) copy-start(bf16[2,256,256]{2,1,0:T(8,128)(2,1)} %constant.15.clone.back) | copy-start | bytes 786436
  30.5 1.2 %copy-start.1 = (bf16[2,256,256]{2,1,0:T(8,128)(2,1)S(1)}, bf16[2,256,256]{2,1,0:T(8,128)(2,1)}, u32[]{:S(2)}) copy-start(bf16[2,256,256]{2,1,0:T(8,128)(2,1)} %constant.14.clone.there) | copy-start | bytes 786436
  30.5 1.2 %copy-start.2 = (f32[2,2,64,128]{3,2,1,0:T(8,128)S(1)}, f32[2,2,64,128]{3,2,1,0:T(8,128)}, u32[]{:S(2)}) copy-start(f32[2,2,64,128]{3,2,1,0:T(8,128)} %constant.17.clone.twists) | copy-start | bytes 393220
  30.5 1.2 %copy-start.3 = (bf16[2,2,128,128]{3,2,1,0:T(8,128)(2,1)S(1)}, bf16[2,2,128,128]{3,2,1,0:T(8,128)(2,1)}, u32[]{:S(2)}) copy-start(bf16[2,2,128,128]{3,2,1,0:T(8,128)(2,1)} %constant.16.clone.last) | copy-start | bytes 393220
  30.5 1.2 %copy-start.4 = (bf16[2,128,192]{2,1,0:T(8,128)(2,1)S(1)}, bf16[2,128,192]{2,1,0:T(8,128)(2,1)}, u32[]{:S(2)}) copy-start(bf16[2,128,192]{2,1,0:T(8,128)(2,1)} %constant.13.clone.far) | copy-start | bytes 294916
  33.6 1.6 %collective-permute-start.10 = (f32[512,128]{1,0:T(8,128)S(1)}, f32[512,128]{1,0:T(8,128)S(1)}, u32[]{:S(2)}, u32[]{:S(2)}) collective-permute-start(f32[512,128]{1,0:T(8,128)S(1)} %get-tuple-element.47), channel_id=1, source_target_pairs={{0,1},{1,0},{2,3},{3,2},{4,5},{5,4},{6,7},{7,6},{8,9},{9,8},{10,11... | collective-permute-start | bytes 786440 | tf_op jit(solution)/shard_map/ppermute | solution.py:594
  35.3 8.5 %collective-permute-start.14 = (f32[256,128]{1,0:T(8,128)S(1)}, f32[256,128]{1,0:T(8,128)S(1)}, u32[]{:S(2)}, u32[]{:S(2)}) collective-permute-start(f32[256,128]{1,0:T(8,128)S(1)} %get-tuple-element.51), channel_id=1, source_target_pairs={{0,0},{1,2},{2,8},{3,10},{4,4},{5,6},{6,12},{7,14},{8,1},{9,3},{10... | collective-permute-start | bytes 393224 | tf_op jit(solution)/shard_map/ppermute | solution.py:595
  38.5 13.1 %collective-permute-start.13 = (f32[256,128]{1,0:T(8,128)S(1)}, f32[256,128]{1,0:T(8,128)S(1)}, u32[]{:S(2)}, u32[]{:S(2)}) collective-permute-start(f32[256,128]{1,0:T(8,128)S(1)} %get-tuple-element.50), channel_id=1, source_target_pairs={{0,4},{1,6},{2,12},{3,14},{4,0},{5,2},{6,8},{7,10},{8,5},{9,7},{10... | collective-permute-start | bytes 393224 | tf_op jit(solution)/shard_map/ppermute | solution.py:595
  42.1 10.3 %collective-permute-start.12 = (f32[256,128]{1,0:T(8,128)S(1)}, f32[256,128]{1,0:T(8,128)S(1)}, u32[]{:S(2)}, u32[]{:S(2)}) collective-permute-start(f32[256,128]{1,0:T(8,128)S(1)} %get-tuple-element.49), channel_id=1, source_target_pairs={{0,8},{1,10},{2,0},{3,2},{4,12},{5,14},{6,4},{7,6},{8,9},{9,11},{1... | collective-permute-start | bytes 393224 | tf_op jit(solution)/shard_map/ppermute | solution.py:595
  42.1 12.0 %collective-permute-start.11 = (f32[256,128]{1,0:T(8,128)S(1)}, f32[256,128]{1,0:T(8,128)S(1)}, u32[]{:S(2)}, u32[]{:S(2)}) collective-permute-start(f32[256,128]{1,0:T(8,128)S(1)} %get-tuple-element.48), channel_id=1, source_target_pairs={{0,12},{1,14},{2,4},{3,6},{4,8},{5,10},{6,0},{7,2},{8,13},{9,15},{... | collective-permute-start | bytes 393224 | tf_op jit(solution)/shard_map/ppermute | solution.py:595

commit v10 on v9

--- a/solution.py
+++ b/solution.py
@@ -170,7 +170,7 @@
 WINDOW = OUT_BINS + TAPS - 1
 REF_LINES = 8
 EDGE = 16
-STEPS = (2, 3, 1, 0)
+STEPS = (3, 2, 1, 0)
 
 
 def split_bf16(value):

time: 55.1 us -> 56.8 us (1.031)
  the two profiles are of different devices: /device:TPU:13 before, /device:TPU:1 now
where the time goes in v10:
time: 56.8 us; the launch traced here: 56.6 us
  waiting for transfers between devices  26.1 us (46%)
  starting transfers between devices  19.7 us (35%)
  Pallas kernels  7.94 us (14%)
  local copies, waits for them, and re-layouts  2.04 us (4%)
  between operations  0.83 us (1%)
    ppermute x4, waiting for transfers between devices, transposed_shards(): lax.ppermute(messages[step], ('az', 'rg'), routes[step])  14.1 us
    ppermute x4, starting transfers between devices, transposed_shards(): lax.ppermute(messages[step], ('az', 'rg'), routes[step])  9.56 us
    ppermute x4, waiting for transfers between devices, transposed_shards(): lax.ppermute(message, ('az', 'rg'), route)  8.64 us
    ppermute x4, starting transfers between devices, transposed_shards(): lax.ppermute(message, ('az', 'rg'), route)  8.13 us
    pallas_call x5, Pallas kernels, kernel_call(): pl.pallas_call(body, out_shape=out_shape, in_specs=specs, out_specs=jax.t...  4.35 us
    pallas_call x4, Pallas kernels, transposed_shards(): pl.pallas_call(functools.partial(place_kernel, step), out_shape=[array(bi...  2.91 us
    ppermute x1, waiting for transfers between devices, transposed_shards(): swap(taps)  1.17 us
    ppermute x1, waiting for transfers between devices, transposed_shards(): swap(give)  1.16 us
  transfers between devices with their start and end apart: 15, of which 6 were waited for; matrix products, arithmetic and copies ran while one was open for 2% of the time, Pallas kernels for 8%

profile of v10, /device:TPU:1, one launch (start us, length us, event | category | flops | bytes accessed | tf_op | source)
XLA Modules:
  0.0 56.6 jit_solution(9331174228131816518)
XLA Ops:
  0.6 0.1 collective-permute-start
  0.8 0.5 collective-permute-start.1
  1.2 0.1 collective-permute-start.2
  1.3 0.4 collective-permute-start.3
  1.7 1.0 %reshape.10.re_lines = f32[512,128]{1,0:T(8,128)S(1)} reshape(f32[32,2048]{1,0:T(8,128)} %param.12) | data formatting | bytes 524288 | tf_op jit(solution)/shard_map/reshape | solution.py:534
  2.9 0.6 %copy-done.6 = f32[1,64,32]{1,2,0:T(8,128)S(1)} copy-done((f32[1,64,32]{1,2,0:T(8,128)S(1)}, f32[1,64,32]{1,2,0:T(8,128)}, u32[]{:S(2)}) %copy-start.6) | copy-done | bytes 8216
  3.5 0.7 %pack.1 = (f32[488,128]{1,0:T(8,128)S(1)}, f32[488,128]{1,0:T(8,128)S(1)}, f32[488,128]{1,0:T(8,128)S(1)}, f32[488,128]{1,0:T(8,128)S(1)}) custom-call(f32[512,128]{1,0:T(8,128)S(1)} %reshape.10.re_lines, f32[512,128]{1,0:T(8,128)S(1)} %reshape.11.im_lines, f32[32,2048]{1,0:T(8,128)S(1)} %collective-permute-done.re_other, ...), custom_call_target="tpu_custom_call" | custom-call | flops 1 | bytes 1 | tf_op jit(solution)/shard_map/pack/pallas_call | solution.py:537
  4.2 5.7 %collective-permute-start.4 = (f32[488,128]{1,0:T(8,128)S(1)}, f32[488,128]{1,0:T(8,128)S(1)}, u32[]{:S(2)}, u32[]{:S(2)}) collective-permute-start(f32[488,128]{1,0:T(8,128)S(1)} %get-tuple-element.30), channel_id=1, source_target_pairs={{0,12},{1,14},{2,13},{3,15},{4,8},{5,10},{6,9},{7,11},{8,4},{9,6},... | collective-permute-start | bytes 749576 | tf_op jit(solution)/shard_map/ppermute | solution.py:577
  9.9 1.4 %collective-permute-start.6 = (f32[488,128]{1,0:T(8,128)S(1)}, f32[488,128]{1,0:T(8,128)S(1)}, u32[]{:S(2)}, u32[]{:S(2)}) collective-permute-start(f32[488,128]{1,0:T(8,128)S(1)} %get-tuple-element.32), channel_id=1, source_target_pairs={{0,4},{1,6},{2,5},{3,7},{4,0},{5,2},{6,1},{7,3},{8,12},{9,14},{10,... | collective-permute-start | bytes 749576 | tf_op jit(solution)/shard_map/ppermute | solution.py:577
  11.3 2.4 %collective-permute-start.7 = (f32[488,128]{1,0:T(8,128)S(1)}, f32[488,128]{1,0:T(8,128)S(1)}, u32[]{:S(2)}, u32[]{:S(2)}) collective-permute-start(f32[488,128]{1,0:T(8,128)S(1)} %get-tuple-element.33), channel_id=1, source_target_pairs={{0,0},{1,2},{2,1},{3,3},{4,4},{5,6},{6,5},{7,7},{8,8},{9,10},{10,9... | collective-permute-start | bytes 749576 | tf_op jit(solution)/shard_map/ppermute | solution.py:577
  13.7 0.1 copy.21.taps_own
  13.8 1.2 %collective-permute-done.8.taps_other = f32[32,8]{1,0:T(8,128)S(1)} collective-permute-done((f32[32,8]{1,0:T(8,128)S(1)}, f32[32,8]{1,0:T(8,128)S(1)}, u32[]{:S(2)}, u32[]{:S(2)}) %collective-permute-start.8) | collective-permute-done | bytes 1056 | tf_op jit(solution)/shard_map/ppermute | solution.py:532
  15.0 1.9 %phase.1 = (f32[15,2,64,128]{3,2,1,0:T(8,128)S(1)}, f32[64,128]{1,0:T(8,128)S(1)}, f32[2,8,128]{2,1,0:T(8,128)S(1)}) custom-call(s32[2]{0:T(128)S(1)} %copy-done.7, s32[2]{0:T(128)S(1)} %collective-permute-done.3.other_offsets.off_other, s32[2]{0:T(128)S(1)} %copy-done.8, f32[32,8]{1,0:T(8,128)S(1)} %copy.21.taps_own, ...), custom_call_target="tpu_custom_call" | custom-call | bytes 1000000 | tf_op jit(solution)/shard_map/phase/pallas_call | solution.py:508
  16.9 14.1 %collective-permute-done.5.refs_1_ = f32[488,128]{1,0:T(8,128)S(1)} collective-permute-done((f32[488,128]{1,0:T(8,128)S(1)}, f32[488,128]{1,0:T(8,128)S(1)}, u32[]{:S(2)}, u32[]{:S(2)}) %collective-permute-start.5) | collective-permute-done | bytes 249888 | tf_op jit(solution)/shard_map/ppermute | solution.py:577
  31.1 0.2 parity.1
  31.2 0.5 collective-permute-start.9
  31.7 0.3 copy-done.5
  32.0 0.3 near.2.partial
  32.3 0.9 %collective-permute-done.9.got = f32[992,128]{1,0:T(8,128)S(1)} collective-permute-done((f32[992,128]{1,0:T(8,128)S(1)}, f32[992,128]{1,0:T(8,128)S(1)}, u32[]{:S(2)}, u32[]{:S(2)}) %collective-permute-start.9) | collective-permute-done | bytes 507936 | tf_op jit(solution)/shard_map/ppermute | solution.py:582
  33.2 1.9 %band.1 = (f32[512,128]{1,0:T(8,128)S(1)}, f32[512,128]{1,0:T(8,128)S(1)}) custom-call(f32[4,128,512]{2,1,0:T(8,128)S(1)} %near.2.partial, f32[992,128]{1,0:T(8,128)S(1)} %get-tuple-element.41.keep, f32[992,128]{1,0:T(8,128)S(1)} %collective-permute-done.9.got, f32[15,2,64,128]{3,2,1,0:T(8,128)S(1)} %get-tuple-element.43.phase, ...), custom_call_target="tpu_custom_call" | custom-call | bytes 1000000 | tf_op jit(solution)/shard_map/band/pallas_call | solution.py:508
  35.1 0.4 collective-permute-start.10
  35.6 1.2 %collective-permute-done.10.got = f32[512,128]{1,0:T(8,128)S(1)} collective-permute-done((f32[512,128]{1,0:T(8,128)S(1)}, f32[512,128]{1,0:T(8,128)S(1)}, u32[]{:S(2)}, u32[]{:S(2)}) %collective-permute-start.10) | collective-permute-done | bytes 262176 | tf_op jit(solution)/shard_map/ppermute | solution.py:594
  36.8 0.1 join.1
  36.8 3.6 %collective-permute-start.14 = (f32[256,128]{1,0:T(8,128)S(1)}, f32[256,128]{1,0:T(8,128)S(1)}, u32[]{:S(2)}, u32[]{:S(2)}) collective-permute-start(f32[256,128]{1,0:T(8,128)S(1)} %get-tuple-element.51), channel_id=1, source_target_pairs={{0,0},{1,2},{2,8},{3,10},{4,4},{5,6},{6,12},{7,14},{8,1},{9,3},{10... | collective-permute-start | bytes 393224 | tf_op jit(solution)/shard_map/ppermute | solution.py:595
  40.5 2.3 %collective-permute-start.13 = (f32[256,128]{1,0:T(8,128)S(1)}, f32[256,128]{1,0:T(8,128)S(1)}, u32[]{:S(2)}, u32[]{:S(2)}) collective-permute-start(f32[256,128]{1,0:T(8,128)S(1)} %get-tuple-element.50), channel_id=1, source_target_pairs={{0,4},{1,6},{2,12},{3,14},{4,0},{5,2},{6,8},{7,10},{8,5},{9,7},{10... | collective-permute-start | bytes 393224 | tf_op jit(solution)/shard_map/ppermute | solution.py:595
  42.7 2.2 %collective-permute-start.11 = (f32[256,128]{1,0:T(8,128)S(1)}, f32[256,128]{1,0:T(8,128)S(1)}, u32[]{:S(2)}, u32[]{:S(2)}) collective-permute-start(f32[256,128]{1,0:T(8,128)S(1)} %get-tuple-element.48), channel_id=1, source_target_pairs={{0,12},{1,14},{2,4},{3,6},{4,8},{5,10},{6,0},{7,2},{8,13},{9,15},{... | collective-permute-start | bytes 393224 | tf_op jit(solution)/shard_map/ppermute | solution.py:595
  45.0 5.3 %collective-permute-done.14.message = f32[256,128]{1,0:T(8,128)S(1)} collective-permute-done((f32[256,128]{1,0:T(8,128)S(1)}, f32[256,128]{1,0:T(8,128)S(1)}, u32[]{:S(2)}, u32[]{:S(2)}) %collective-permute-start.14) | collective-permute-done | bytes 131104 | tf_op jit(solution)/shard_map/ppermute | solution.py:595
  50.3 0.7 %place.4 = (f32[32,2048]{1,0:T(8,128)}, f32[32,2048]{1,0:T(8,128)}) custom-call(f32[256,128]{1,0:T(8,128)S(1)} %collective-permute-done.14.message), custom_call_target="tpu_custom_call" | custom-call | flops 1 | bytes 1 | tf_op jit(solution)/shard_map/place/pallas_call | solution.py:598
  51.0 0.7 %place.5 = (f32[32,2048]{1,0:T(8,128)}, f32[32,2048]{1,0:T(8,128)}) custom-call(f32[256,128]{1,0:T(8,128)S(1)} %collective-permute-done.13.message, f32[32,2048]{1,0:T(8,128)} %get-tuple-element.52.refs_0_, f32[32,2048]{1,0:T(8,128)} %get-tuple-element.53.refs_1_), custom_call_target="tpu_custom_call", output_to_operand_aliasing={{0}: (1, {}), {1}: (2, {})} | custom-call | flops 1 | bytes 1 | tf_op jit(solution)/shard_map/place/pallas_call | solution.py:598
  51.7 3.3 %collective-permute-done.12.message = f32[256,128]{1,0:T(8,128)S(1)} collective-permute-done((f32[256,128]{1,0:T(8,128)S(1)}, f32[256,128]{1,0:T(8,128)S(1)}, u32[]{:S(2)}, u32[]{:S(2)}) %collective-permute-start.12) | collective-permute-done | bytes 131104 | tf_op jit(solution)/shard_map/ppermute | solution.py:595
  55.1 0.7 %place.6 = (f32[32,2048]{1,0:T(8,128)}, f32[32,2048]{1,0:T(8,128)}) custom-call(f32[256,128]{1,0:T(8,128)S(1)} %collective-permute-done.12.message, f32[32,2048]{1,0:T(8,128)} %get-tuple-element.54.refs_0_, f32[32,2048]{1,0:T(8,128)} %get-tuple-element.55.refs_1_), custom_call_target="tpu_custom_call", output_to_operand_aliasing={{0}: (1, {}), {1}: (2, {})} | custom-call | flops 1 | bytes 1 | tf_op jit(solution)/shard_map/place/pallas_call | solution.py:598
  55.8 0.7 %place.7 = (f32[32,2048]{1,0:T(8,128)}, f32[32,2048]{1,0:T(8,128)}) custom-call(f32[256,128]{1,0:T(8,128)S(1)} %collective-permute-done.11.message, f32[32,2048]{1,0:T(8,128)} %get-tuple-element.56.refs_0_, f32[32,2048]{1,0:T(8,128)} %get-tuple-element.57.refs_1_), custom_call_target="tpu_custom_call", output_to_operand_aliasing={{0}: (1, {}), {1}: (2, {})} | custom-call | flops 1 | bytes 1 | tf_op jit(solution)/shard_map/place/pallas_call | solution.py:598
  (33 shorter events, 0.2 us)
Async XLA Ops:
  0.6 0.7 %copy-start.7 = (s32[2]{0:T(128)S(1)}, s32[2]{0:T(128)}, u32[]{:S(2)}) copy-start(s32[2]{0:T(128)} %off_own.1) | copy-start | bytes 28
  0.6 2.2 %collective-permute-start = (f32[32,2048]{1,0:T(8,128)}, f32[32,2048]{1,0:T(8,128)S(1)}, u32[]{:S(2)}, u32[]{:S(2)}) collective-permute-start(f32[32,2048]{1,0:T(8,128)} %param.12), channel_id=1, source_target_pairs={{0,1},{1,0},{2,3},{3,2},{4,5},{5,4},{6,7},{7,6},{8,9},{9,8},{10,11... | collective-permute-start | bytes 786440 | tf_op jit(solution)/shard_map/ppermute | solution.py:532
  0.8 2.1 %collective-permute-start.1 = (f32[32,2048]{1,0:T(8,128)}, f32[32,2048]{1,0:T(8,128)S(1)}, u32[]{:S(2)}, u32[]{:S(2)}) collective-permute-start(f32[32,2048]{1,0:T(8,128)} %param.13), channel_id=1, source_target_pairs={{0,1},{1,0},{2,3},{3,2},{4,5},{5,4},{6,7},{7,6},{8,9},{9,8},{10,11... | collective-permute-start | bytes 786440 | tf_op jit(solution)/shard_map/ppermute | solution.py:532
  1.2 1.5 %copy-start.9 = (f32[32,2048]{1,0:T(8,128)S(1)}, f32[32,2048]{1,0:T(8,128)}, u32[]{:S(2)}) copy-start(f32[32,2048]{1,0:T(8,128)} %param.13) | copy-start | bytes 786436
  1.2 1.6 %collective-permute-start.2 = (f32[32,64]{1,0:T(8,128)}, f32[32,64]{1,0:T(8,128)S(1)}, u32[]{:S(2)}, u32[]{:S(2)}) collective-permute-start(f32[32,64]{1,0:T(8,128)} %bitcast.3), channel_id=1, source_target_pairs={{0,1},{1,0},{2,3},{3,2},{4,5},{5,4},{6,7},{7,6},{8,9},{9,8},{10,11... | collective-permute-start | bytes 24584 | tf_op jit(solution)/shard_map/ppermute | solution.py:532
  1.3 1.5 %collective-permute-start.3 = (s32[2]{0:T(128)S(1)}, s32[2]{0:T(128)S(1)}, u32[]{:S(2)}, u32[]{:S(2)}) collective-permute-start(s32[2]{0:T(128)S(1)} %copy-done.7), channel_id=1, source_target_pairs={{0,1},{1,0},{2,3},{3,2},{4,5},{5,4},{6,7},{7,6},{8,9},{9,8},{10,11... | collective-permute-start | bytes 32 | tf_op jit(solution)/shard_map/ppermute | solution.py:531
  2.7 0.7 %copy-start.6 = (f32[1,64,32]{1,2,0:T(8,128)S(1)}, f32[1,64,32]{1,2,0:T(8,128)}, u32[]{:S(2)}) copy-start(f32[1,64,32]{1,2,0:T(8,128)} %param.14) | copy-start | bytes 24580
  4.1 9.6 %copy-start.10 = (f32[32,8]{0,1:T(8,128)S(1)}, f32[32,8]{0,1:T(8,128)}, u32[]{:S(2)}) copy-start(f32[32,8]{0,1:T(8,128)} %param.17) | copy-start | bytes 3076
  4.2 12.8 %collective-permute-start.4 = (f32[488,128]{1,0:T(8,128)S(1)}, f32[488,128]{1,0:T(8,128)S(1)}, u32[]{:S(2)}, u32[]{:S(2)}) collective-permute-start(f32[488,128]{1,0:T(8,128)S(1)} %get-tuple-element.30), channel_id=1, source_target_pairs={{0,12},{1,14},{2,13},{3,15},{4,8},{5,10},{6,9},{7,11},{8,4},{9,6},... | collective-permute-start | bytes 749576 | tf_op jit(solution)/shard_map/ppermute | solution.py:577
  9.9 21.2 %collective-permute-start.5 = (f32[488,128]{1,0:T(8,128)S(1)}, f32[488,128]{1,0:T(8,128)S(1)}, u32[]{:S(2)}, u32[]{:S(2)}) collective-permute-start(f32[488,128]{1,0:T(8,128)S(1)} %get-tuple-element.31), channel_id=1, source_target_pairs={{0,8},{1,10},{2,9},{3,11},{4,12},{5,14},{6,13},{7,15},{8,0},{9,2},... | collective-permute-start | bytes 749576 | tf_op jit(solution)/shard_map/ppermute | solution.py:577
  9.9 21.2 %collective-permute-start.6 = (f32[488,128]{1,0:T(8,128)S(1)}, f32[488,128]{1,0:T(8,128)S(1)}, u32[]{:S(2)}, u32[]{:S(2)}) collective-permute-start(f32[488,128]{1,0:T(8,128)S(1)} %get-tuple-element.32), channel_id=1, source_target_pairs={{0,4},{1,6},{2,5},{3,7},{4,0},{5,2},{6,1},{7,3},{8,12},{9,14},{10,... | collective-permute-start | bytes 749576 | tf_op jit(solution)/shard_map/ppermute | solution.py:577
  11.3 3.7 %copy-start.8 = (s32[2]{0:T(128)S(1)}, s32[2]{0:T(128)}, u32[]{:S(2)}) copy-start(s32[2]{0:T(128)} %owners.1) | copy-start | bytes 28
  11.3 19.8 %collective-permute-start.7 = (f32[488,128]{1,0:T(8,128)S(1)}, f32[488,128]{1,0:T(8,128)S(1)}, u32[]{:S(2)}, u32[]{:S(2)}) collective-permute-start(f32[488,128]{1,0:T(8,128)S(1)} %get-tuple-element.33), channel_id=1, source_target_pairs={{0,0},{1,2},{2,1},{3,3},{4,4},{5,6},{6,5},{7,7},{8,8},{9,10},{10,9... | collective-permute-start | bytes 749576 | tf_op jit(solution)/shard_map/ppermute | solution.py:577
  13.8 1.2 %collective-permute-start.8 = (f32[32,8]{1,0:T(8,128)S(1)}, f32[32,8]{1,0:T(8,128)S(1)}, u32[]{:S(2)}, u32[]{:S(2)}) collective-permute-start(f32[32,8]{1,0:T(8,128)S(1)} %copy.21.taps_own), channel_id=1, source_target_pairs={{0,1},{1,0},{2,3},{3,2},{4,5},{5,4},{6,7},{7,6},{8,9},{9,8},{10,11... | collective-permute-start | bytes 3080 | tf_op jit(solution)/shard_map/ppermute | solution.py:532
  31.1 0.9 %copy-start.5 = (bf16[2,128,192]{2,1,0:T(8,128)(2,1)S(1)}, bf16[2,128,192]{2,1,0:T(8,128)(2,1)}, u32[]{:S(2)}) copy-start(bf16[2,128,192]{2,1,0:T(8,128)(2,1)} %constant.12.clone.near) | copy-start | bytes 294916
  31.2 2.0 %collective-permute-start.9 = (f32[992,128]{1,0:T(8,128)S(1)}, f32[992,128]{1,0:T(8,128)S(1)}, u32[]{:S(2)}, u32[]{:S(2)}) collective-permute-start(f32[992,128]{1,0:T(8,128)S(1)} %get-tuple-element.42), channel_id=1, source_target_pairs={{0,1},{1,0},{2,3},{3,2},{4,5},{5,4},{6,7},{7,6},{8,9},{9,8},{10,11... | collective-permute-start | bytes 1523720 | tf_op jit(solution)/shard_map/ppermute | solution.py:582
  32.0 1.2 %copy-start = (bf16[2,256,256]{2,1,0:T(8,128)(2,1)S(1)}, bf16[2,256,256]{2,1,0:T(8,128)(2,1)}, u32[]{:S(2)}) copy-start(bf16[2,256,256]{2,1,0:T(8,128)(2,1)} %constant.15.clone.back) | copy-start | bytes 786436
  32.0 1.2 %copy-start.1 = (bf16[2,256,256]{2,1,0:T(8,128)(2,1)S(1)}, bf16[2,256,256]{2,1,0:T(8,128)(2,1)}, u32[]{:S(2)}) copy-start(bf16[2,256,256]{2,1,0:T(8,128)(2,1)} %constant.14.clone.there) | copy-start | bytes 786436
  32.0 1.2 %copy-start.2 = (f32[2,2,64,128]{3,2,1,0:T(8,128)S(1)}, f32[2,2,64,128]{3,2,1,0:T(8,128)}, u32[]{:S(2)}) copy-start(f32[2,2,64,128]{3,2,1,0:T(8,128)} %constant.17.clone.twists) | copy-start | bytes 393220
  32.0 1.2 %copy-start.3 = (bf16[2,2,128,128]{3,2,1,0:T(8,128)(2,1)S(1)}, bf16[2,2,128,128]{3,2,1,0:T(8,128)(2,1)}, u32[]{:S(2)}) copy-start(bf16[2,2,128,128]{3,2,1,0:T(8,128)(2,1)} %constant.16.clone.last) | copy-start | bytes 393220
  32.0 1.2 %copy-start.4 = (bf16[2,128,192]{2,1,0:T(8,128)(2,1)S(1)}, bf16[2,128,192]{2,1,0:T(8,128)(2,1)}, u32[]{:S(2)}) copy-start(bf16[2,128,192]{2,1,0:T(8,128)(2,1)} %constant.13.clone.far) | copy-start | bytes 294916
  35.1 1.6 %collective-permute-start.10 = (f32[512,128]{1,0:T(8,128)S(1)}, f32[512,128]{1,0:T(8,128)S(1)}, u32[]{:S(2)}, u32[]{:S(2)}) collective-permute-start(f32[512,128]{1,0:T(8,128)S(1)} %get-tuple-element.47), channel_id=1, source_target_pairs={{0,1},{1,0},{2,3},{3,2},{4,5},{5,4},{6,7},{7,6},{8,9},{9,8},{10,11... | collective-permute-start | bytes 786440 | tf_op jit(solution)/shard_map/ppermute | solution.py:594
  36.8 13.4 %collective-permute-start.14 = (f32[256,128]{1,0:T(8,128)S(1)}, f32[256,128]{1,0:T(8,128)S(1)}, u32[]{:S(2)}, u32[]{:S(2)}) collective-permute-start(f32[256,128]{1,0:T(8,128)S(1)} %get-tuple-element.51), channel_id=1, source_target_pairs={{0,0},{1,2},{2,8},{3,10},{4,4},{5,6},{6,12},{7,14},{8,1},{9,3},{10... | collective-permute-start | bytes 393224 | tf_op jit(solution)/shard_map/ppermute | solution.py:595
  40.5 10.5 %collective-permute-start.13 = (f32[256,128]{1,0:T(8,128)S(1)}, f32[256,128]{1,0:T(8,128)S(1)}, u32[]{:S(2)}, u32[]{:S(2)}) collective-permute-start(f32[256,128]{1,0:T(8,128)S(1)} %get-tuple-element.50), channel_id=1, source_target_pairs={{0,4},{1,6},{2,12},{3,14},{4,0},{5,2},{6,8},{7,10},{8,5},{9,7},{10... | collective-permute-start | bytes 393224 | tf_op jit(solution)/shard_map/ppermute | solution.py:595
  42.7 12.4 %collective-permute-start.12 = (f32[256,128]{1,0:T(8,128)S(1)}, f32[256,128]{1,0:T(8,128)S(1)}, u32[]{:S(2)}, u32[]{:S(2)}) collective-permute-start(f32[256,128]{1,0:T(8,128)S(1)} %get-tuple-element.49), channel_id=1, source_target_pairs={{0,8},{1,10},{2,0},{3,2},{4,12},{5,14},{6,4},{7,6},{8,9},{9,11},{1... | collective-permute-start | bytes 393224 | tf_op jit(solution)/shard_map/ppermute | solution.py:595
  42.7 13.1 %collective-permute-start.11 = (f32[256,128]{1,0:T(8,128)S(1)}, f32[256,128]{1,0:T(8,128)S(1)}, u32[]{:S(2)}, u32[]{:S(2)}) collective-permute-start(f32[256,128]{1,0:T(8,128)S(1)} %get-tuple-element.48), channel_id=1, source_target_pairs={{0,12},{1,14},{2,4},{3,6},{4,8},{5,10},{6,0},{7,2},{8,13},{9,15},{... | collective-permute-start | bytes 393224 | tf_op jit(solution)/shard_map/ppermute | solution.py:595

commit v11 on v9

--- a/solution.py
+++ b/solution.py
@@ -171,6 +171,7 @@
 REF_LINES = 8
 EDGE = 16
 STEPS = (2, 3, 1, 0)
+STEPS_BACK = (1, 0, 3, 2)
 
 
 def split_bf16(value):
@@ -594,7 +595,7 @@
     sent = kernel_call(join_kernel, "join", [array(2 * OUT_BINS * PART, FACTOR)] * half, [keep, swap(give)])
     results = [lax.ppermute(message, ("az", "rg"), route) for message, route in zip(sent, routes_back)]
     images = []
-    for step, message in enumerate(results):
+    for step in STEPS_BACK:
         images = pl.pallas_call(
             functools.partial(place_kernel, step),
             out_shape=[array(bins, samples)] * 2,
@@ -605,7 +606,7 @@
             compiler_params=pltpu.CompilerParams(vmem_limit_bytes=8 * 1024 * 1024),
             cost_estimate=pl.CostEstimate(flops=1, bytes_accessed=1, transcendentals=0),
             name="place",
-        )(message, *images)
+        )(results[step], *images)
     return images
 
 

time: 55.1 us -> 58.1 us (1.054)
  the two profiles are of different devices: /device:TPU:13 before, /device:TPU:1 now
where the time goes in v11:
time: 58.1 us; the launch traced here: 57.8 us
  starting transfers between devices  23.8 us (41%)
  waiting for transfers between devices  22.8 us (39%)
  Pallas kernels  7.93 us (14%)
  local copies, waits for them, and re-layouts  2.43 us (4%)
  between operations  0.83 us (1%)
    ppermute x4, starting transfers between devices, transposed_shards(): lax.ppermute(message, ('az', 'rg'), route)  13 us
    ppermute x4, waiting for transfers between devices, transposed_shards(): lax.ppermute(messages[step], ('az', 'rg'), routes[step])  10.1 us
    ppermute x4, starting transfers between devices, transposed_shards(): lax.ppermute(messages[step], ('az', 'rg'), routes[step])  9.48 us
    ppermute x4, waiting for transfers between devices, transposed_shards(): lax.ppermute(message, ('az', 'rg'), route)  9.18 us
    pallas_call x5, Pallas kernels, kernel_call(): pl.pallas_call(body, out_shape=out_shape, in_specs=specs, out_specs=jax.t...  4.35 us
    pallas_call x4, Pallas kernels, transposed_shards(): pl.pallas_call(functools.partial(place_kernel, step), out_shape=[array(bi...  2.91 us
    ppermute x1, waiting for transfers between devices, transposed_shards(): swap(give)  1.41 us
    unnamed x23, local copies, waits for them, and re-layouts  1.39 us
  transfers between devices with their start and end apart: 15, of which 7 were waited for; matrix products, arithmetic and copies ran while one was open for 2% of the time, Pallas kernels for 8%

profile of v11, /device:TPU:1, one launch (start us, length us, event | category | flops | bytes accessed | tf_op | source)
XLA Modules:
  0.0 57.8 jit_solution(3588989364144785252)
XLA Ops:
  0.6 0.1 collective-permute-start
  0.8 0.5 collective-permute-start.1
  1.2 0.1 collective-permute-start.2
  1.3 0.4 collective-permute-start.3
  1.7 1.0 %reshape.10.re_lines = f32[512,128]{1,0:T(8,128)S(1)} reshape(f32[32,2048]{1,0:T(8,128)} %param.12) | data formatting | bytes 524288 | tf_op jit(solution)/shard_map/reshape | solution.py:535
  2.9 0.6 %copy-done.6 = f32[1,64,32]{1,2,0:T(8,128)S(1)} copy-done((f32[1,64,32]{1,2,0:T(8,128)S(1)}, f32[1,64,32]{1,2,0:T(8,128)}, u32[]{:S(2)}) %copy-start.6) | copy-done | bytes 8216
  3.5 0.7 %pack.1 = (f32[488,128]{1,0:T(8,128)S(1)}, f32[488,128]{1,0:T(8,128)S(1)}, f32[488,128]{1,0:T(8,128)S(1)}, f32[488,128]{1,0:T(8,128)S(1)}) custom-call(f32[512,128]{1,0:T(8,128)S(1)} %reshape.10.re_lines, f32[512,128]{1,0:T(8,128)S(1)} %reshape.11.im_lines, f32[32,2048]{1,0:T(8,128)S(1)} %collective-permute-done.re_other, ...), custom_call_target="tpu_custom_call" | custom-call | flops 1 | bytes 1 | tf_op jit(solution)/shard_map/pack/pallas_call | solution.py:538
  4.2 4.7 %collective-permute-start.4 = (f32[488,128]{1,0:T(8,128)S(1)}, f32[488,128]{1,0:T(8,128)S(1)}, u32[]{:S(2)}, u32[]{:S(2)}) collective-permute-start(f32[488,128]{1,0:T(8,128)S(1)} %get-tuple-element.30), channel_id=1, source_target_pairs={{0,8},{1,10},{2,9},{3,11},{4,12},{5,14},{6,13},{7,15},{8,0},{9,2},... | collective-permute-start | bytes 749576 | tf_op jit(solution)/shard_map/ppermute | solution.py:578
  8.8 1.1 %collective-permute-start.5 = (f32[488,128]{1,0:T(8,128)S(1)}, f32[488,128]{1,0:T(8,128)S(1)}, u32[]{:S(2)}, u32[]{:S(2)}) collective-permute-start(f32[488,128]{1,0:T(8,128)S(1)} %get-tuple-element.31), channel_id=1, source_target_pairs={{0,12},{1,14},{2,13},{3,15},{4,8},{5,10},{6,9},{7,11},{8,4},{9,6},... | collective-permute-start | bytes 749576 | tf_op jit(solution)/shard_map/ppermute | solution.py:578
  9.9 0.4 collective-permute-start.6
  10.4 3.3 %collective-permute-start.7 = (f32[488,128]{1,0:T(8,128)S(1)}, f32[488,128]{1,0:T(8,128)S(1)}, u32[]{:S(2)}, u32[]{:S(2)}) collective-permute-start(f32[488,128]{1,0:T(8,128)S(1)} %get-tuple-element.33), channel_id=1, source_target_pairs={{0,0},{1,2},{2,1},{3,3},{4,4},{5,6},{6,5},{7,7},{8,8},{9,10},{10,9... | collective-permute-start | bytes 749576 | tf_op jit(solution)/shard_map/ppermute | solution.py:578
  13.7 1.2 %collective-permute-done.8.taps_other = f32[32,8]{1,0:T(8,128)S(1)} collective-permute-done((f32[32,8]{1,0:T(8,128)S(1)}, f32[32,8]{1,0:T(8,128)S(1)}, u32[]{:S(2)}, u32[]{:S(2)}) %collective-permute-start.8) | collective-permute-done | bytes 1056 | tf_op jit(solution)/shard_map/ppermute | solution.py:533
  14.9 1.9 %phase.1 = (f32[15,2,64,128]{3,2,1,0:T(8,128)S(1)}, f32[64,128]{1,0:T(8,128)S(1)}, f32[2,8,128]{2,1,0:T(8,128)S(1)}) custom-call(s32[2]{0:T(128)S(1)} %copy-done.7, s32[2]{0:T(128)S(1)} %collective-permute-done.3.other_offsets.off_other, s32[2]{0:T(128)S(1)} %copy-done.8, f32[32,8]{1,0:T(8,128)S(1)} %copy.21.taps_own, ...), custom_call_target="tpu_custom_call" | custom-call | bytes 1000000 | tf_op jit(solution)/shard_map/phase/pallas_call | solution.py:509
  16.8 9.3 %collective-permute-done.4.refs_0_ = f32[488,128]{1,0:T(8,128)S(1)} collective-permute-done((f32[488,128]{1,0:T(8,128)S(1)}, f32[488,128]{1,0:T(8,128)S(1)}, u32[]{:S(2)}, u32[]{:S(2)}) %collective-permute-start.4) | collective-permute-done | bytes 249888 | tf_op jit(solution)/shard_map/ppermute | solution.py:578
  26.1 0.8 %collective-permute-done.6.refs_2_ = f32[488,128]{1,0:T(8,128)S(1)} collective-permute-done((f32[488,128]{1,0:T(8,128)S(1)}, f32[488,128]{1,0:T(8,128)S(1)}, u32[]{:S(2)}, u32[]{:S(2)}) %collective-permute-start.6) | collective-permute-done | bytes 249888 | tf_op jit(solution)/shard_map/ppermute | solution.py:578
  27.0 0.2 parity.1
  27.2 0.7 %copy-done.5 = bf16[2,128,192]{2,1,0:T(8,128)(2,1)S(1)} copy-done((bf16[2,128,192]{2,1,0:T(8,128)(2,1)S(1)}, bf16[2,128,192]{2,1,0:T(8,128)(2,1)}, u32[]{:S(2)}) %copy-start.5) | copy-done | bytes 98328
  27.9 0.3 near.2.partial
  28.2 0.9 %collective-permute-done.9.got = f32[992,128]{1,0:T(8,128)S(1)} collective-permute-done((f32[992,128]{1,0:T(8,128)S(1)}, f32[992,128]{1,0:T(8,128)S(1)}, u32[]{:S(2)}, u32[]{:S(2)}) %collective-permute-start.9) | collective-permute-done | bytes 507936 | tf_op jit(solution)/shard_map/ppermute | solution.py:583
  29.1 1.9 %band.1 = (f32[512,128]{1,0:T(8,128)S(1)}, f32[512,128]{1,0:T(8,128)S(1)}) custom-call(f32[4,128,512]{2,1,0:T(8,128)S(1)} %near.2.partial, f32[992,128]{1,0:T(8,128)S(1)} %get-tuple-element.41.keep, f32[992,128]{1,0:T(8,128)S(1)} %collective-permute-done.9.got, f32[15,2,64,128]{3,2,1,0:T(8,128)S(1)} %get-tuple-element.43.phase, ...), custom_call_target="tpu_custom_call" | custom-call | bytes 1000000 | tf_op jit(solution)/shard_map/band/pallas_call | solution.py:509
  31.0 0.2 collective-permute-start.10
  31.2 1.4 %collective-permute-done.10.got = f32[512,128]{1,0:T(8,128)S(1)} collective-permute-done((f32[512,128]{1,0:T(8,128)S(1)}, f32[512,128]{1,0:T(8,128)S(1)}, u32[]{:S(2)}, u32[]{:S(2)}) %collective-permute-start.10) | collective-permute-done | bytes 262176 | tf_op jit(solution)/shard_map/ppermute | solution.py:595
  32.7 5.5 %collective-permute-start.14 = (f32[256,128]{1,0:T(8,128)S(1)}, f32[256,128]{1,0:T(8,128)S(1)}, u32[]{:S(2)}, u32[]{:S(2)}) collective-permute-start(f32[256,128]{1,0:T(8,128)S(1)} %get-tuple-element.51), channel_id=1, source_target_pairs={{0,4},{1,6},{2,12},{3,14},{4,0},{5,2},{6,8},{7,10},{8,5},{9,7},{10... | collective-permute-start | bytes 393224 | tf_op jit(solution)/shard_map/ppermute | solution.py:596
  38.2 1.9 %collective-permute-start.13 = (f32[256,128]{1,0:T(8,128)S(1)}, f32[256,128]{1,0:T(8,128)S(1)}, u32[]{:S(2)}, u32[]{:S(2)}) collective-permute-start(f32[256,128]{1,0:T(8,128)S(1)} %get-tuple-element.50), channel_id=1, source_target_pairs={{0,0},{1,2},{2,8},{3,10},{4,4},{5,6},{6,12},{7,14},{8,1},{9,3},{10... | collective-permute-start | bytes 393224 | tf_op jit(solution)/shard_map/ppermute | solution.py:596
  40.1 3.6 %collective-permute-start.12 = (f32[256,128]{1,0:T(8,128)S(1)}, f32[256,128]{1,0:T(8,128)S(1)}, u32[]{:S(2)}, u32[]{:S(2)}) collective-permute-start(f32[256,128]{1,0:T(8,128)S(1)} %get-tuple-element.49), channel_id=1, source_target_pairs={{0,12},{1,14},{2,4},{3,6},{4,8},{5,10},{6,0},{7,2},{8,13},{9,15},{... | collective-permute-start | bytes 393224 | tf_op jit(solution)/shard_map/ppermute | solution.py:596
  43.7 2.0 %collective-permute-start.11 = (f32[256,128]{1,0:T(8,128)S(1)}, f32[256,128]{1,0:T(8,128)S(1)}, u32[]{:S(2)}, u32[]{:S(2)}) collective-permute-start(f32[256,128]{1,0:T(8,128)S(1)} %get-tuple-element.48), channel_id=1, source_target_pairs={{0,8},{1,10},{2,0},{3,2},{4,12},{5,14},{6,4},{7,6},{8,9},{9,11},{1... | collective-permute-start | bytes 393224 | tf_op jit(solution)/shard_map/ppermute | solution.py:596
  45.7 0.7 %place.4 = (f32[32,2048]{1,0:T(8,128)}, f32[32,2048]{1,0:T(8,128)}) custom-call(f32[256,128]{1,0:T(8,128)S(1)} %collective-permute-done.14.message), custom_call_target="tpu_custom_call" | custom-call | flops 1 | bytes 1 | tf_op jit(solution)/shard_map/place/pallas_call | solution.py:599
  46.4 2.4 %collective-permute-done.13.message = f32[256,128]{1,0:T(8,128)S(1)} collective-permute-done((f32[256,128]{1,0:T(8,128)S(1)}, f32[256,128]{1,0:T(8,128)S(1)}, u32[]{:S(2)}, u32[]{:S(2)}) %collective-permute-start.13) | collective-permute-done | bytes 131104 | tf_op jit(solution)/shard_map/ppermute | solution.py:596
  48.8 0.7 %place.5 = (f32[32,2048]{1,0:T(8,128)}, f32[32,2048]{1,0:T(8,128)}) custom-call(f32[256,128]{1,0:T(8,128)S(1)} %collective-permute-done.13.message, f32[32,2048]{1,0:T(8,128)} %get-tuple-element.52.refs_0_, f32[32,2048]{1,0:T(8,128)} %get-tuple-element.53.refs_1_), custom_call_target="tpu_custom_call", output_to_operand_aliasing={{0}: (1, {}), {1}: (2, {})} | custom-call | flops 1 | bytes 1 | tf_op jit(solution)/shard_map/place/pallas_call | solution.py:599
  49.6 0.7 %place.6 = (f32[32,2048]{1,0:T(8,128)}, f32[32,2048]{1,0:T(8,128)}) custom-call(f32[256,128]{1,0:T(8,128)S(1)} %collective-permute-done.12.message, f32[32,2048]{1,0:T(8,128)} %get-tuple-element.54.refs_0_, f32[32,2048]{1,0:T(8,128)} %get-tuple-element.55.refs_1_), custom_call_target="tpu_custom_call", output_to_operand_aliasing={{0}: (1, {}), {1}: (2, {})} | custom-call | flops 1 | bytes 1 | tf_op jit(solution)/shard_map/place/pallas_call | solution.py:599
  50.3 6.8 %collective-permute-done.11.message = f32[256,128]{1,0:T(8,128)S(1)} collective-permute-done((f32[256,128]{1,0:T(8,128)S(1)}, f32[256,128]{1,0:T(8,128)S(1)}, u32[]{:S(2)}, u32[]{:S(2)}) %collective-permute-start.11) | collective-permute-done | bytes 131104 | tf_op jit(solution)/shard_map/ppermute | solution.py:596
  57.1 0.7 %place.7 = (f32[32,2048]{1,0:T(8,128)}, f32[32,2048]{1,0:T(8,128)}) custom-call(f32[256,128]{1,0:T(8,128)S(1)} %collective-permute-done.11.message, f32[32,2048]{1,0:T(8,128)} %get-tuple-element.56.refs_0_, f32[32,2048]{1,0:T(8,128)} %get-tuple-element.57.refs_1_), custom_call_target="tpu_custom_call", output_to_operand_aliasing={{0}: (1, {}), {1}: (2, {})} | custom-call | flops 1 | bytes 1 | tf_op jit(solution)/shard_map/place/pallas_call | solution.py:599
  (33 shorter events, 0.4 us)
Async XLA Ops:
  0.6 0.7 %copy-start.7 = (s32[2]{0:T(128)S(1)}, s32[2]{0:T(128)}, u32[]{:S(2)}) copy-start(s32[2]{0:T(128)} %off_own.1) | copy-start | bytes 28
  0.6 2.2 %collective-permute-start = (f32[32,2048]{1,0:T(8,128)}, f32[32,2048]{1,0:T(8,128)S(1)}, u32[]{:S(2)}, u32[]{:S(2)}) collective-permute-start(f32[32,2048]{1,0:T(8,128)} %param.12), channel_id=1, source_target_pairs={{0,1},{1,0},{2,3},{3,2},{4,5},{5,4},{6,7},{7,6},{8,9},{9,8},{10,11... | collective-permute-start | bytes 786440 | tf_op jit(solution)/shard_map/ppermute | solution.py:533
  0.8 2.1 %collective-permute-start.1 = (f32[32,2048]{1,0:T(8,128)}, f32[32,2048]{1,0:T(8,128)S(1)}, u32[]{:S(2)}, u32[]{:S(2)}) collective-permute-start(f32[32,2048]{1,0:T(8,128)} %param.13), channel_id=1, source_target_pairs={{0,1},{1,0},{2,3},{3,2},{4,5},{5,4},{6,7},{7,6},{8,9},{9,8},{10,11... | collective-permute-start | bytes 786440 | tf_op jit(solution)/shard_map/ppermute | solution.py:533
  1.2 1.5 %copy-start.9 = (f32[32,2048]{1,0:T(8,128)S(1)}, f32[32,2048]{1,0:T(8,128)}, u32[]{:S(2)}) copy-start(f32[32,2048]{1,0:T(8,128)} %param.13) | copy-start | bytes 786436
  1.2 1.6 %collective-permute-start.2 = (f32[32,64]{1,0:T(8,128)}, f32[32,64]{1,0:T(8,128)S(1)}, u32[]{:S(2)}, u32[]{:S(2)}) collective-permute-start(f32[32,64]{1,0:T(8,128)} %bitcast.3), channel_id=1, source_target_pairs={{0,1},{1,0},{2,3},{3,2},{4,5},{5,4},{6,7},{7,6},{8,9},{9,8},{10,11... | collective-permute-start | bytes 24584 | tf_op jit(solution)/shard_map/ppermute | solution.py:533
  1.3 1.5 %collective-permute-start.3 = (s32[2]{0:T(128)S(1)}, s32[2]{0:T(128)S(1)}, u32[]{:S(2)}, u32[]{:S(2)}) collective-permute-start(s32[2]{0:T(128)S(1)} %copy-done.7), channel_id=1, source_target_pairs={{0,1},{1,0},{2,3},{3,2},{4,5},{5,4},{6,7},{7,6},{8,9},{9,8},{10,11... | collective-permute-start | bytes 32 | tf_op jit(solution)/shard_map/ppermute | solution.py:532
  2.7 0.7 %copy-start.6 = (f32[1,64,32]{1,2,0:T(8,128)S(1)}, f32[1,64,32]{1,2,0:T(8,128)}, u32[]{:S(2)}) copy-start(f32[1,64,32]{1,2,0:T(8,128)} %param.14) | copy-start | bytes 24580
  4.1 9.5 %copy-start.10 = (f32[32,8]{0,1:T(8,128)S(1)}, f32[32,8]{0,1:T(8,128)}, u32[]{:S(2)}) copy-start(f32[32,8]{0,1:T(8,128)} %param.17) | copy-start | bytes 3076
  4.2 22.0 %collective-permute-start.4 = (f32[488,128]{1,0:T(8,128)S(1)}, f32[488,128]{1,0:T(8,128)S(1)}, u32[]{:S(2)}, u32[]{:S(2)}) collective-permute-start(f32[488,128]{1,0:T(8,128)S(1)} %get-tuple-element.30), channel_id=1, source_target_pairs={{0,8},{1,10},{2,9},{3,11},{4,12},{5,14},{6,13},{7,15},{8,0},{9,2},... | collective-permute-start | bytes 749576 | tf_op jit(solution)/shard_map/ppermute | solution.py:578
  8.8 17.3 %collective-permute-start.5 = (f32[488,128]{1,0:T(8,128)S(1)}, f32[488,128]{1,0:T(8,128)S(1)}, u32[]{:S(2)}, u32[]{:S(2)}) collective-permute-start(f32[488,128]{1,0:T(8,128)S(1)} %get-tuple-element.31), channel_id=1, source_target_pairs={{0,12},{1,14},{2,13},{3,15},{4,8},{5,10},{6,9},{7,11},{8,4},{9,6},... | collective-permute-start | bytes 749576 | tf_op jit(solution)/shard_map/ppermute | solution.py:578
  9.9 17.0 %collective-permute-start.6 = (f32[488,128]{1,0:T(8,128)S(1)}, f32[488,128]{1,0:T(8,128)S(1)}, u32[]{:S(2)}, u32[]{:S(2)}) collective-permute-start(f32[488,128]{1,0:T(8,128)S(1)} %get-tuple-element.32), channel_id=1, source_target_pairs={{0,4},{1,6},{2,5},{3,7},{4,0},{5,2},{6,1},{7,3},{8,12},{9,14},{10,... | collective-permute-start | bytes 749576 | tf_op jit(solution)/shard_map/ppermute | solution.py:578
  10.4 4.6 %copy-start.8 = (s32[2]{0:T(128)S(1)}, s32[2]{0:T(128)}, u32[]{:S(2)}) copy-start(s32[2]{0:T(128)} %owners.1) | copy-start | bytes 28
  10.4 16.6 %collective-permute-start.7 = (f32[488,128]{1,0:T(8,128)S(1)}, f32[488,128]{1,0:T(8,128)S(1)}, u32[]{:S(2)}, u32[]{:S(2)}) collective-permute-start(f32[488,128]{1,0:T(8,128)S(1)} %get-tuple-element.33), channel_id=1, source_target_pairs={{0,0},{1,2},{2,1},{3,3},{4,4},{5,6},{6,5},{7,7},{8,8},{9,10},{10,9... | collective-permute-start | bytes 749576 | tf_op jit(solution)/shard_map/ppermute | solution.py:578
  13.7 1.2 %collective-permute-start.8 = (f32[32,8]{1,0:T(8,128)S(1)}, f32[32,8]{1,0:T(8,128)S(1)}, u32[]{:S(2)}, u32[]{:S(2)}) collective-permute-start(f32[32,8]{1,0:T(8,128)S(1)} %copy.21.taps_own), channel_id=1, source_target_pairs={{0,1},{1,0},{2,3},{3,2},{4,5},{5,4},{6,7},{7,6},{8,9},{9,8},{10,11... | collective-permute-start | bytes 3080 | tf_op jit(solution)/shard_map/ppermute | solution.py:533
  27.0 0.9 %copy-start.5 = (bf16[2,128,192]{2,1,0:T(8,128)(2,1)S(1)}, bf16[2,128,192]{2,1,0:T(8,128)(2,1)}, u32[]{:S(2)}) copy-start(bf16[2,128,192]{2,1,0:T(8,128)(2,1)} %constant.12.clone.near) | copy-start | bytes 294916
  27.1 2.0 %collective-permute-start.9 = (f32[992,128]{1,0:T(8,128)S(1)}, f32[992,128]{1,0:T(8,128)S(1)}, u32[]{:S(2)}, u32[]{:S(2)}) collective-permute-start(f32[992,128]{1,0:T(8,128)S(1)} %get-tuple-element.42), channel_id=1, source_target_pairs={{0,1},{1,0},{2,3},{3,2},{4,5},{5,4},{6,7},{7,6},{8,9},{9,8},{10,11... | collective-permute-start | bytes 1523720 | tf_op jit(solution)/shard_map/ppermute | solution.py:583
  27.9 1.2 %copy-start = (bf16[2,256,256]{2,1,0:T(8,128)(2,1)S(1)}, bf16[2,256,256]{2,1,0:T(8,128)(2,1)}, u32[]{:S(2)}) copy-start(bf16[2,256,256]{2,1,0:T(8,128)(2,1)} %constant.15.clone.back) | copy-start | bytes 786436
  27.9 1.2 %copy-start.1 = (bf16[2,256,256]{2,1,0:T(8,128)(2,1)S(1)}, bf16[2,256,256]{2,1,0:T(8,128)(2,1)}, u32[]{:S(2)}) copy-start(bf16[2,256,256]{2,1,0:T(8,128)(2,1)} %constant.14.clone.there) | copy-start | bytes 786436
  27.9 1.2 %copy-start.2 = (f32[2,2,64,128]{3,2,1,0:T(8,128)S(1)}, f32[2,2,64,128]{3,2,1,0:T(8,128)}, u32[]{:S(2)}) copy-start(f32[2,2,64,128]{3,2,1,0:T(8,128)} %constant.17.clone.twists) | copy-start | bytes 393220
  27.9 1.2 %copy-start.3 = (bf16[2,2,128,128]{3,2,1,0:T(8,128)(2,1)S(1)}, bf16[2,2,128,128]{3,2,1,0:T(8,128)(2,1)}, u32[]{:S(2)}) copy-start(bf16[2,2,128,128]{3,2,1,0:T(8,128)(2,1)} %constant.16.clone.last) | copy-start | bytes 393220
  27.9 1.2 %copy-start.4 = (bf16[2,128,192]{2,1,0:T(8,128)(2,1)S(1)}, bf16[2,128,192]{2,1,0:T(8,128)(2,1)}, u32[]{:S(2)}) copy-start(bf16[2,128,192]{2,1,0:T(8,128)(2,1)} %constant.13.clone.far) | copy-start | bytes 294916
  31.0 1.6 %collective-permute-start.10 = (f32[512,128]{1,0:T(8,128)S(1)}, f32[512,128]{1,0:T(8,128)S(1)}, u32[]{:S(2)}, u32[]{:S(2)}) collective-permute-start(f32[512,128]{1,0:T(8,128)S(1)} %get-tuple-element.47), channel_id=1, source_target_pairs={{0,1},{1,0},{2,3},{3,2},{4,5},{5,4},{6,7},{7,6},{8,9},{9,8},{10,11... | collective-permute-start | bytes 786440 | tf_op jit(solution)/shard_map/ppermute | solution.py:595
  32.7 13.0 %collective-permute-start.14 = (f32[256,128]{1,0:T(8,128)S(1)}, f32[256,128]{1,0:T(8,128)S(1)}, u32[]{:S(2)}, u32[]{:S(2)}) collective-permute-start(f32[256,128]{1,0:T(8,128)S(1)} %get-tuple-element.51), channel_id=1, source_target_pairs={{0,4},{1,6},{2,12},{3,14},{4,0},{5,2},{6,8},{7,10},{8,5},{9,7},{10... | collective-permute-start | bytes 393224 | tf_op jit(solution)/shard_map/ppermute | solution.py:596
  38.2 10.6 %collective-permute-start.13 = (f32[256,128]{1,0:T(8,128)S(1)}, f32[256,128]{1,0:T(8,128)S(1)}, u32[]{:S(2)}, u32[]{:S(2)}) collective-permute-start(f32[256,128]{1,0:T(8,128)S(1)} %get-tuple-element.50), channel_id=1, source_target_pairs={{0,0},{1,2},{2,8},{3,10},{4,4},{5,6},{6,12},{7,14},{8,1},{9,3},{10... | collective-permute-start | bytes 393224 | tf_op jit(solution)/shard_map/ppermute | solution.py:596
  40.1 9.5 %collective-permute-start.12 = (f32[256,128]{1,0:T(8,128)S(1)}, f32[256,128]{1,0:T(8,128)S(1)}, u32[]{:S(2)}, u32[]{:S(2)}) collective-permute-start(f32[256,128]{1,0:T(8,128)S(1)} %get-tuple-element.49), channel_id=1, source_target_pairs={{0,12},{1,14},{2,4},{3,6},{4,8},{5,10},{6,0},{7,2},{8,13},{9,15},{... | collective-permute-start | bytes 393224 | tf_op jit(solution)/shard_map/ppermute | solution.py:596
  43.7 13.4 %collective-permute-start.11 = (f32[256,128]{1,0:T(8,128)S(1)}, f32[256,128]{1,0:T(8,128)S(1)}, u32[]{:S(2)}, u32[]{:S(2)}) collective-permute-start(f32[256,128]{1,0:T(8,128)S(1)} %get-tuple-element.48), channel_id=1, source_target_pairs={{0,8},{1,10},{2,0},{3,2},{4,12},{5,14},{6,4},{7,6},{8,9},{9,11},{1... | collective-permute-start | bytes 393224 | tf_op jit(solution)/shard_map/ppermute | solution.py:596
